TPU v7x, 32 devices: a whole 2x2x4 slice. The times are simulated.
32 devices in a mesh: fsdp: 8 (over y, x, core), rep: 4 (over z).
Axes of the slice: x: 2, y: 2, z: 4, core: 2. Of those that a mesh axis runs over, the one named last changes fastest.
Arguments:
- tokens: bfloat16 [13312, 768], P(('fsdp', 'rep')), may hold values from -6 to 6
- starts: int32 [32, 4], P(('fsdp', 'rep')), may hold values from 0 to 415, as said below
- routes: int32 [13312, 1], P(('fsdp', 'rep')), may hold values from 0 to 2; in each aligned block of 416 rows (0 to 415, 416 to 831, ...) at most 208 rows name the same one
- norm1_gain: bfloat16 [768], P('fsdp'), may hold values from 0.5 to 1.5
- norm1_bias: bfloat16 [768], P('fsdp'), may hold values from -1 to 1
- query_weight: bfloat16 [768, 768], P('fsdp'), may hold values from -0.21875 to 0.21875
- query_bias: bfloat16 [768], P('fsdp'), may hold values from -1.5 to 1.5
- key_weight: bfloat16 [768, 768], P('fsdp'), may hold values from -0.21875 to 0.21875
- value_weight: bfloat16 [768, 768], P('fsdp'), may hold values from -0.21875 to 0.21875
- value_bias: bfloat16 [768], P('fsdp'), may hold values from -1 to 1
- out_weight: bfloat16 [768, 768], P('fsdp'), may hold values from -2 to 2
- out_bias: bfloat16 [768], P('fsdp'), may hold values from -1 to 1
- norm2_gain: bfloat16 [768], P('fsdp'), may hold values from 0.5 to 1.5
- norm2_bias: bfloat16 [768], P('fsdp'), may hold values from -1 to 1
- expert_in: bfloat16 [3, 768, 3072], P(None, 'fsdp'), may hold values from -0.21875 to 0.21875
- expert_in_bias: bfloat16 [3, 3072], P(None, 'fsdp'), may hold values from -1 to 1
- expert_out: bfloat16 [3, 3072, 768], P(None, 'fsdp'), may hold values from -0.109375 to 0.109375
- expert_out_bias: bfloat16 [3, 768], P(None, 'fsdp'), may hold values from -1 to 1
- cotangent: bfloat16 [13312, 768], P(('fsdp', 'rep')), may hold values from -6 to 6
Outputs:
- output: bfloat16 [13312, 768], P(('fsdp', 'rep'))
- input_grad: float32 [13312, 768], P(('fsdp', 'rep'))
- grad_norm1_gain: float32 [768], P('fsdp')
- grad_norm1_bias: float32 [768], P('fsdp')
- grad_query_weight: float32 [768, 768], P('fsdp')
- grad_query_bias: float32 [768], P('fsdp')
- grad_key_weight: float32 [768, 768], P('fsdp')
- grad_value_weight: float32 [768, 768], P('fsdp')
- grad_value_bias: float32 [768], P('fsdp')
- grad_out_weight: float32 [768, 768], P('fsdp')
- grad_out_bias: float32 [768], P('fsdp')
- grad_norm2_gain: float32 [768], P('fsdp')
- grad_norm2_bias: float32 [768], P('fsdp')
- grad_expert_in: float32 [3, 768, 3072], P(None, 'fsdp')
- grad_expert_in_bias: float32 [3, 3072], P(None, 'fsdp')
- grad_expert_out: float32 [3, 3072, 768], P(None, 'fsdp')
- grad_expert_out_bias: float32 [3, 768], P(None, 'fsdp')
Inputs may be any that keep to these rules, and one draw needn't show every extreme that they name: Each row's first start is 0 and its starts rise strictly. `routes`: in each aligned block of 416 tokens (the tokens of one device) no expert is named by more than 208 tokens, and in some blocks one expert is named by exactly 208.
All inputs are finite; a program needn't handle non-finite values.
Results may differ from a plain program's by a relative error of at most 0.017.
Values may be sent and summed in bfloat16 or wider, within the bound.
No kernel may reach another device: no remote copies, remote signals or barrier semaphores. Data moves between devices by JAX's collectives and lax.ppermute only.
A program may use at most 256 MiB of HBM per device.

v0:
```python
import jax
import jax.numpy as jnp
from jax import lax
from jax.sharding import PartitionSpec as P

HEAD = 64
EXPERTS = 3
CAP = 208


EPSILON = 1e-05
MASKED = -1000000000.0


def normalize(inputs, gain, shift):
    mean = jnp.mean(inputs, -1, keepdims=True)
    centred = inputs - mean
    inverse = lax.rsqrt(jnp.mean(centred * centred, -1, keepdims=True) + EPSILON)
    return centred * inverse * gain + shift


def norm_back(inputs, gain, gradient):
    mean = jnp.mean(inputs, -1, keepdims=True)
    centred = inputs - mean
    inverse = lax.rsqrt(jnp.mean(centred * centred, -1, keepdims=True) + EPSILON)
    normed = centred * inverse
    grad_normed = gradient * gain
    grad_inputs = inverse * (
        grad_normed
        - jnp.mean(grad_normed, -1, keepdims=True)
        - normed * jnp.mean(grad_normed * normed, -1, keepdims=True)
    )
    return (grad_inputs, jnp.sum(gradient * normed, 0), jnp.sum(gradient, 0))


def gelu_exact(inputs):
    return 0.5 * inputs * (1.0 + lax.erf(inputs * 0.7071067811865476))


def gelu_slope(inputs):
    return (
        0.5 * (1.0 + lax.erf(inputs * 0.7071067811865476))
        + inputs * jnp.exp(-0.5 * inputs * inputs) * 0.3989422804014327
    )


def per_device(
    tokens,
    starts,
    routes,
    norm1_gain,
    norm1_bias,
    query_weight,
    query_bias,
    key_weight,
    value_weight,
    value_bias,
    out_weight,
    out_bias,
    norm2_gain,
    norm2_bias,
    expert_in,
    expert_in_bias,
    expert_out,
    expert_out_bias,
    cotangent,
):
    seq_rows = starts.shape[0]
    tok_count = tokens.shape[0]
    seq_len = tok_count // seq_rows
    model_width = tokens.shape[1]
    head_count = model_width // HEAD
    head_shape = (seq_rows, seq_len, head_count, HEAD)
    scale_factor = HEAD ** (-0.5)
    gain_one, shift_one, w_query, b_query, w_key, w_value, b_value, w_out, b_out = (
        lax.all_gather(norm1_gain, "fsdp", axis=0, tiled=True),
        lax.all_gather(norm1_bias, "fsdp", axis=0, tiled=True),
        lax.all_gather(query_weight, "fsdp", axis=0, tiled=True),
        lax.all_gather(query_bias, "fsdp", axis=0, tiled=True),
        lax.all_gather(key_weight, "fsdp", axis=0, tiled=True),
        lax.all_gather(value_weight, "fsdp", axis=0, tiled=True),
        lax.all_gather(value_bias, "fsdp", axis=0, tiled=True),
        lax.all_gather(out_weight, "fsdp", axis=0, tiled=True),
        lax.all_gather(out_bias, "fsdp", axis=0, tiled=True),
    )
    resid_in = tokens.astype(jnp.float32)
    normed_one = normalize(
        resid_in, gain_one.astype(jnp.float32), shift_one.astype(jnp.float32)
    ).astype(jnp.bfloat16)
    queries = (
        (
            jnp.dot(normed_one, w_query, preferred_element_type=jnp.float32)
            + b_query.astype(jnp.float32)
        )
        .astype(jnp.bfloat16)
        .reshape(head_shape)
    )
    keys_mat = (
        jnp.dot(normed_one, w_key, preferred_element_type=jnp.float32)
        .astype(jnp.bfloat16)
        .reshape(head_shape)
    )
    values = (
        (
            jnp.dot(normed_one, w_value, preferred_element_type=jnp.float32)
            + b_value.astype(jnp.float32)
        )
        .astype(jnp.bfloat16)
        .reshape(head_shape)
    )
    position = jnp.arange(seq_len, dtype=jnp.int32)
    segment = jnp.sum((position[None, :, None] >= starts[:, None, :]).astype(jnp.int32), -1)
    same_seg = (segment[:, :, None] == segment[:, None, :])[:, None]

    def scores_of(query_part, key_part):
        raw_scores = (
            jnp.einsum("rqhd,rkhd->rhqk", query_part, key_part, preferred_element_type=jnp.float32)
            * scale_factor
        )
        return jnp.where(same_seg, raw_scores, MASKED)

    scores = scores_of(queries, keys_mat)
    row_max = jnp.max(scores, -1, keepdims=True)
    exp_scores = jnp.exp(scores - row_max)
    row_total = jnp.sum(exp_scores, -1, keepdims=True)
    log_total = row_max + jnp.log(row_total)
    probs_low = (exp_scores / row_total).astype(jnp.bfloat16)
    mixed = jnp.einsum("rhqk,rkhd->rqhd", probs_low, values, preferred_element_type=jnp.float32)
    mixed = mixed.reshape(tok_count, model_width).astype(jnp.bfloat16)
    hidden = (
        resid_in
        + jnp.dot(mixed, w_out, preferred_element_type=jnp.float32)
        + b_out.astype(jnp.float32)
    )
    gain_two, shift_two, w_in, b_in, w_down, b_down = (
        lax.all_gather(norm2_gain, "fsdp", axis=0, tiled=True),
        lax.all_gather(norm2_bias, "fsdp", axis=0, tiled=True),
        lax.all_gather(expert_in, "fsdp", axis=1, tiled=True),
        lax.all_gather(expert_in_bias, "fsdp", axis=1, tiled=True),
        lax.all_gather(expert_out, "fsdp", axis=1, tiled=True),
        lax.all_gather(expert_out_bias, "fsdp", axis=1, tiled=True),
    )
    normed_two = normalize(
        hidden, gain_two.astype(jnp.float32), shift_two.astype(jnp.float32)
    ).astype(jnp.bfloat16)
    route_ids = routes[:, 0]
    member = (route_ids[:, None] == jnp.arange(EXPERTS, dtype=jnp.int32)[None, :]).astype(jnp.int32)
    rank = jnp.sum(jnp.cumsum(member, 0) * member, 1) - 1
    slot_ids = route_ids * CAP + rank
    packed = (
        jnp.zeros((EXPERTS * CAP, model_width), jnp.bfloat16)
        .at[slot_ids]
        .set(normed_two)
        .reshape(EXPERTS, CAP, model_width)
    )
    pre_act = (
        jnp.einsum("ecd,edf->ecf", packed, w_in, preferred_element_type=jnp.float32)
        + b_in.astype(jnp.float32)[:, None, :]
    )
    act_low = gelu_exact(pre_act).astype(jnp.bfloat16)
    result = (
        jnp.einsum("ecf,efd->ecd", act_low, w_down, preferred_element_type=jnp.float32)
        + b_down.astype(jnp.float32)[:, None, :]
    )
    routed = result.reshape(EXPERTS * CAP, model_width)[slot_ids]
    output = (hidden + routed).astype(jnp.bfloat16)
    gain_two_back, w_in_back, w_down_back = (
        lax.all_gather(norm2_gain, "fsdp", axis=0, tiled=True),
        lax.all_gather(expert_in, "fsdp", axis=1, tiled=True),
        lax.all_gather(expert_out, "fsdp", axis=1, tiled=True),
    )
    grad_output = cotangent.astype(jnp.float32)
    grad_packed = (
        jnp.zeros((EXPERTS * CAP, model_width), jnp.bfloat16)
        .at[slot_ids]
        .set(cotangent)
        .reshape(EXPERTS, CAP, model_width)
    )
    grad_down_bias = jnp.sum(grad_packed.astype(jnp.float32), 1)
    grad_down = jnp.einsum("ecf,ecd->efd", act_low, grad_packed, preferred_element_type=jnp.float32)
    grad_act = jnp.einsum(
        "ecd,efd->ecf", grad_packed, w_down_back, preferred_element_type=jnp.float32
    )
    grad_pre = (grad_act * gelu_slope(pre_act)).astype(jnp.bfloat16)
    grad_in_bias = jnp.sum(grad_pre.astype(jnp.float32), 1)
    grad_in = jnp.einsum("ecd,ecf->edf", packed, grad_pre, preferred_element_type=jnp.float32)
    grad_slots = jnp.einsum(
        "ecf,edf->ecd", grad_pre, w_in_back, preferred_element_type=jnp.float32
    ).reshape(EXPERTS * CAP, model_width)
    grad_normed_two = grad_slots[slot_ids]
    grad_from_norm, grad_gain_two, grad_shift_two = norm_back(
        hidden, gain_two_back.astype(jnp.float32), grad_normed_two
    )
    grad_hidden = grad_output + grad_from_norm
    column_in, column_down = (
        lax.psum_scatter(
            grad_in.astype(jnp.bfloat16), "rep", scatter_dimension=2, tiled=True
        ).astype(jnp.float32),
        lax.psum_scatter(
            grad_down.astype(jnp.bfloat16), "rep", scatter_dimension=2, tiled=True
        ).astype(jnp.float32),
    )
    share_in, share_down, part_gain_two, part_shift_two, part_in_bias, part_down_bias = (
        lax.psum_scatter(column_in, "fsdp", scatter_dimension=1, tiled=True),
        lax.psum_scatter(column_down, "fsdp", scatter_dimension=1, tiled=True),
        lax.psum_scatter(grad_gain_two, "fsdp", scatter_dimension=0, tiled=True),
        lax.psum_scatter(grad_shift_two, "fsdp", scatter_dimension=0, tiled=True),
        lax.psum_scatter(grad_in_bias, "fsdp", scatter_dimension=1, tiled=True),
        lax.psum_scatter(grad_down_bias, "fsdp", scatter_dimension=1, tiled=True),
    )
    sum_in, sum_down, stack_gain_two, stack_shift_two, stack_in_bias, stack_down_bias = (
        lax.all_gather(share_in.astype(jnp.bfloat16), "rep", axis=2, tiled=True).astype(
            share_in.dtype
        ),
        lax.all_gather(share_down.astype(jnp.bfloat16), "rep", axis=2, tiled=True).astype(
            share_down.dtype
        ),
        lax.all_gather(part_gain_two[None].astype(jnp.bfloat16), "rep", axis=0, tiled=True).astype(
            jnp.float32
        ),
        lax.all_gather(part_shift_two[None].astype(jnp.bfloat16), "rep", axis=0, tiled=True).astype(
            jnp.float32
        ),
        lax.all_gather(part_in_bias[None].astype(jnp.bfloat16), "rep", axis=0, tiled=True).astype(
            jnp.float32
        ),
        lax.all_gather(part_down_bias[None].astype(jnp.bfloat16), "rep", axis=0, tiled=True).astype(
            jnp.float32
        ),
    )
    sum_gain_two = jnp.sum(stack_gain_two, 0)
    sum_shift_two = jnp.sum(stack_shift_two, 0)
    sum_in_bias = jnp.sum(stack_in_bias, 0)
    sum_down_bias = jnp.sum(stack_down_bias, 0)
    gain_one_back, w_query_back, w_key_back, w_value_back, w_out_back = (
        lax.all_gather(norm1_gain, "fsdp", axis=0, tiled=True),
        lax.all_gather(query_weight, "fsdp", axis=0, tiled=True),
        lax.all_gather(key_weight, "fsdp", axis=0, tiled=True),
        lax.all_gather(value_weight, "fsdp", axis=0, tiled=True),
        lax.all_gather(out_weight, "fsdp", axis=0, tiled=True),
    )
    grad_branch = grad_hidden.astype(jnp.bfloat16)
    grad_out_bias = jnp.sum(grad_branch.astype(jnp.float32), 0)
    grad_out_weight = jnp.einsum(
        "td,te->de", mixed, grad_branch, preferred_element_type=jnp.float32
    )
    grad_mixed = (
        jnp.einsum("te,de->td", grad_branch, w_out_back, preferred_element_type=jnp.float32)
        .astype(jnp.bfloat16)
        .reshape(head_shape)
    )
    scores_again = scores_of(queries, keys_mat)
    probs = jnp.exp(scores_again - log_total)
    probs_again = probs.astype(jnp.bfloat16)
    grad_values = jnp.einsum(
        "rhqk,rqhd->rkhd", probs_again, grad_mixed, preferred_element_type=jnp.float32
    )
    grad_values = grad_values.astype(jnp.bfloat16).reshape(tok_count, model_width)
    grad_probs = jnp.einsum(
        "rqhd,rkhd->rhqk", grad_mixed, values, preferred_element_type=jnp.float32
    )
    grad_scores = (probs * (grad_probs - jnp.sum(grad_probs * probs, -1, keepdims=True))).astype(
        jnp.bfloat16
    )
    grad_queries = (
        (
            jnp.einsum("rhqk,rkhd->rqhd", grad_scores, keys_mat, preferred_element_type=jnp.float32)
            * scale_factor
        )
        .astype(jnp.bfloat16)
        .reshape(tok_count, model_width)
    )
    grad_keys = (
        (
            jnp.einsum("rhqk,rqhd->rkhd", grad_scores, queries, preferred_element_type=jnp.float32)
            * scale_factor
        )
        .astype(jnp.bfloat16)
        .reshape(tok_count, model_width)
    )
    grad_query_bias = jnp.sum(grad_queries.astype(jnp.float32), 0)
    grad_value_bias = jnp.sum(grad_values.astype(jnp.float32), 0)
    grad_query_weight = jnp.einsum(
        "td,te->de", normed_one, grad_queries, preferred_element_type=jnp.float32
    )
    grad_key_weight = jnp.einsum(
        "td,te->de", normed_one, grad_keys, preferred_element_type=jnp.float32
    )
    grad_value_weight = jnp.einsum(
        "td,te->de", normed_one, grad_values, preferred_element_type=jnp.float32
    )
    grad_normed_one = (
        jnp.einsum("te,de->td", grad_queries, w_query_back, preferred_element_type=jnp.float32)
        + jnp.einsum("te,de->td", grad_keys, w_key_back, preferred_element_type=jnp.float32)
        + jnp.einsum("te,de->td", grad_values, w_value_back, preferred_element_type=jnp.float32)
    )
    grad_from_first, grad_gain_one, grad_shift_one = norm_back(
        resid_in, gain_one_back.astype(jnp.float32), grad_normed_one
    )
    input_grad = grad_hidden + grad_from_first
    column_query, column_key, column_value, column_out = (
        lax.psum_scatter(
            grad_query_weight.astype(jnp.bfloat16), "rep", scatter_dimension=1, tiled=True
        ).astype(jnp.float32),
        lax.psum_scatter(
            grad_key_weight.astype(jnp.bfloat16), "rep", scatter_dimension=1, tiled=True
        ).astype(jnp.float32),
        lax.psum_scatter(
            grad_value_weight.astype(jnp.bfloat16), "rep", scatter_dimension=1, tiled=True
        ).astype(jnp.float32),
        lax.psum_scatter(
            grad_out_weight.astype(jnp.bfloat16), "rep", scatter_dimension=1, tiled=True
        ).astype(jnp.float32),
    )
    (
        share_query,
        share_key,
        share_value,
        share_out,
        part_gain_one,
        part_shift_one,
        part_query_bias,
        part_value_bias,
        part_out_bias,
    ) = (
        lax.psum_scatter(column_query, "fsdp", scatter_dimension=0, tiled=True),
        lax.psum_scatter(column_key, "fsdp", scatter_dimension=0, tiled=True),
        lax.psum_scatter(column_value, "fsdp", scatter_dimension=0, tiled=True),
        lax.psum_scatter(column_out, "fsdp", scatter_dimension=0, tiled=True),
        lax.psum_scatter(grad_gain_one, "fsdp", scatter_dimension=0, tiled=True),
        lax.psum_scatter(grad_shift_one, "fsdp", scatter_dimension=0, tiled=True),
        lax.psum_scatter(grad_query_bias, "fsdp", scatter_dimension=0, tiled=True),
        lax.psum_scatter(grad_value_bias, "fsdp", scatter_dimension=0, tiled=True),
        lax.psum_scatter(grad_out_bias, "fsdp", scatter_dimension=0, tiled=True),
    )
    (
        sum_query,
        sum_key,
        sum_value,
        sum_out,
        stack_gain_one,
        stack_shift_one,
        stack_query_bias,
        stack_value_bias,
        stack_out_bias,
    ) = (
        lax.all_gather(share_query.astype(jnp.bfloat16), "rep", axis=1, tiled=True).astype(
            share_query.dtype
        ),
        lax.all_gather(share_key.astype(jnp.bfloat16), "rep", axis=1, tiled=True).astype(
            share_key.dtype
        ),
        lax.all_gather(share_value.astype(jnp.bfloat16), "rep", axis=1, tiled=True).astype(
            share_value.dtype
        ),
        lax.all_gather(share_out.astype(jnp.bfloat16), "rep", axis=1, tiled=True).astype(
            share_out.dtype
        ),
        lax.all_gather(part_gain_one[None].astype(jnp.bfloat16), "rep", axis=0, tiled=True).astype(
            jnp.float32
        ),
        lax.all_gather(part_shift_one[None].astype(jnp.bfloat16), "rep", axis=0, tiled=True).astype(
            jnp.float32
        ),
        lax.all_gather(
            part_query_bias[None].astype(jnp.bfloat16), "rep", axis=0, tiled=True
        ).astype(jnp.float32),
        lax.all_gather(
            part_value_bias[None].astype(jnp.bfloat16), "rep", axis=0, tiled=True
        ).astype(jnp.float32),
        lax.all_gather(part_out_bias[None].astype(jnp.bfloat16), "rep", axis=0, tiled=True).astype(
            jnp.float32
        ),
    )
    sum_gain_one = jnp.sum(stack_gain_one, 0)
    sum_shift_one = jnp.sum(stack_shift_one, 0)
    sum_query_bias = jnp.sum(stack_query_bias, 0)
    sum_value_bias = jnp.sum(stack_value_bias, 0)
    sum_out_bias = jnp.sum(stack_out_bias, 0)
    return (
        output,
        input_grad,
        sum_gain_one,
        sum_shift_one,
        sum_query,
        sum_query_bias,
        sum_key,
        sum_value,
        sum_value_bias,
        sum_out,
        sum_out_bias,
        sum_gain_two,
        sum_shift_two,
        sum_in,
        sum_in_bias,
        sum_down,
        sum_down_bias,
    )


def solution(mesh):
    in_specs = (
        P(("fsdp", "rep"), None),
        P(("fsdp", "rep"), None),
        P(("fsdp", "rep"), None),
        P("fsdp"),
        P("fsdp"),
        P("fsdp", None),
        P("fsdp"),
        P("fsdp", None),
        P("fsdp", None),
        P("fsdp"),
        P("fsdp", None),
        P("fsdp"),
        P("fsdp"),
        P("fsdp"),
        P(None, "fsdp", None),
        P(None, "fsdp"),
        P(None, "fsdp", None),
        P(None, "fsdp"),
        P(("fsdp", "rep"), None),
    )
    out_specs = (
        P(("fsdp", "rep"), None),
        P(("fsdp", "rep"), None),
        P("fsdp"),
        P("fsdp"),
        P("fsdp", None),
        P("fsdp"),
        P("fsdp", None),
        P("fsdp", None),
        P("fsdp"),
        P("fsdp", None),
        P("fsdp"),
        P("fsdp"),
        P("fsdp"),
        P(None, "fsdp", None),
        P(None, "fsdp"),
        P(None, "fsdp", None),
        P(None, "fsdp"),
    )
    return jax.shard_map(
        per_device, mesh=mesh, in_specs=in_specs, out_specs=out_specs, check_vma=False
    )
```

profile of v0, /device:TPU:0, one launch (start us, length us, event | category | flops | bytes accessed | tf_op | source)
XLA Modules:
  0.0 1307.9 jit_solution(16431922186727558115)
XLA Ops:
  14.2 25.8 %all-reduce.23 = (bf16[768]{0:T(1024)(128)(2,1)S(1)}, bf16[768]{0:T(1024)(128)(2,1)S(1)}, bf16[768]{0:T(1024)(128)(2,1)S(1)}, bf16[768]{0:T(1024)(128)(2,1)S(1)}...) all-reduce(bf16[768]{0:T(1024)(128)(2,1)S(1)} %dynamic-update-slice, ...), channel_id=1, replica_groups=mesh['fsdp'=8,'rep'=4] {'fsdp'}, use_global_device_ids=true, to_apply=%add.2 | all-reduce | flops 5376 | bytes 21504
  41.6 7.9 all_gather.110
  49.6 3.2 scatter_custom_fusion.1
  54.3 2.0 fusion.24
  56.7 6.2 all-gather.21.cloned.1.call-done
  62.9 2.9 fusion.23
  67.1 21.7 %all-gather.25.cloned.1.call-done = bf16[768,768]{1,0:T(8,128)(2,1)} async-done(((bf16[96,768]{1,0:T(8,128)(2,1)}), bf16[768,768]{1,0:T(8,128)(2,1)}) %all-gather.25.cloned.1.call-update) | async-done | bytes 1179664 | tf_op jit(solution)/shard_map/all_gather | solution.py:80
  88.8 2.9 convolution_convert_fusion.7
  93.1 3.1 fusion.51
  97.9 2.1 copy-done
  100.2 2.8 fusion.19
  103.0 11.7 all-gather.27.cloned.1.call-done
  114.7 2.3 fusion.52
  117.7 2.9 scatter_custom_fusion
  120.6 74.6 %all-gather.29.cloned.1.call-done = bf16[3,768,3072]{2,1,0:T(8,128)(2,1)} async-done(((bf16[3,96,3072]{2,1,0:T(8,128)(2,1)}), bf16[3,768,3072]{2,1,0:T(8,128)(2,1)}) %all-gather.29.cloned.1.call-update) | async-done | bytes 14155792 | tf_op jit(solution)/shard_map/all_gather | solution.py:138
  195.2 9.2 multiply_convert_fusion.1
  204.5 9.7 convolution_convert_fusion
  214.2 61.6 %all-gather.31.cloned.1.call-done = bf16[3,3072,768]{2,1,0:T(8,128)(2,1)} async-done(((bf16[3,384,768]{2,1,0:T(8,128)(2,1)}), bf16[3,3072,768]{2,1,0:T(8,128)(2,1)}) %all-gather.31.cloned.1.call-update) | async-done | bytes 14155792 | tf_op jit(solution)/shard_map/all_gather | solution.py:140
  275.8 11.3 convert_reduce_fusion
  287.1 9.2 convolution_convert_fusion.1
  297.0 9.2 all-gather.9
  306.4 10.9 fusion.53
  317.2 2.5 gather_fusion.1
  319.7 9.3 convolution_add_fusion
  329.0 2.5 gather_fusion
  331.6 2.1 multiply_reduce_fusion.1
  333.8 2.6 convert_reduce_fusion.5
  340.8 5.8 convert_reduce_fusion.3
  349.6 8.0 multiply_reduce_fusion
  357.7 12.3 multiply_convert_fusion
  369.9 3.6 convert_reduce_fusion.4
  377.5 4.0 multiply_convert_fusion.2
  384.4 131.0 %reduce-scatter.39.cloned.1.call-done = bf16[3,3072,192]{1,2,0:T(8,128)(2,1)} async-done(((bf16[3,3072,768]{1,2,0:T(8,128)(2,1)}), bf16[3,3072,192]{1,2,0:T(8,128)(2,1)}) %reduce-scatter.39.cloned.1.call-update) | async-done | bytes 3538960 | tf_op jit(solution)/shard_map/reduce_scatter | solution.py:199
  515.5 240.6 %reduce-scatter.35.cloned.1.call-done = bf16[3,768,768]{2,1,0:T(8,128)(2,1)} async-done(((bf16[3,768,3072]{2,1,0:T(8,128)(2,1)}), bf16[3,768,768]{2,1,0:T(8,128)(2,1)}) %reduce-scatter.35.cloned.1.call-update) | async-done | bytes 3538960 | tf_op jit(solution)/shard_map/reduce_scatter | solution.py:196
  760.4 28.2 %reduce-scatter.33.cloned.1.call-done = bf16[768,192]{0,1:T(8,128)(2,1)} async-done(((bf16[768,768]{0,1:T(8,128)(2,1)}), bf16[768,192]{0,1:T(8,128)(2,1)}) %reduce-scatter.33.cloned.1.call-update) | async-done | bytes 294928 | tf_op jit(solution)/shard_map/reduce_scatter | solution.py:311
  788.7 2.0 copy.119
  790.8 28.0 %reduce-scatter.31.cloned.1.call-done = bf16[768,192]{0,1:T(8,128)(2,1)} async-done(((bf16[768,768]{0,1:T(8,128)(2,1)}), bf16[768,192]{0,1:T(8,128)(2,1)}) %reduce-scatter.31.cloned.1.call-update) | async-done | bytes 294928 | tf_op jit(solution)/shard_map/reduce_scatter | solution.py:308
  818.8 2.0 copy.117
  820.9 28.7 %reduce-scatter.27.cloned.1.call-done = bf16[768,192]{0,1:T(8,128)(2,1)} async-done(((bf16[768,768]{0,1:T(8,128)(2,1)}), bf16[768,192]{0,1:T(8,128)(2,1)}) %reduce-scatter.27.cloned.1.call-update) | async-done | bytes 294928 | tf_op jit(solution)/shard_map/reduce_scatter | solution.py:302
  849.6 2.0 copy.113
  851.7 28.5 %reduce-scatter.29.cloned.1.call-done = bf16[768,192]{0,1:T(8,128)(2,1)} async-done(((bf16[768,768]{0,1:T(8,128)(2,1)}), bf16[768,192]{0,1:T(8,128)(2,1)}) %reduce-scatter.29.cloned.1.call-update) | async-done | bytes 294928 | tf_op jit(solution)/shard_map/reduce_scatter | solution.py:305
  880.3 2.0 copy.115
  882.3 48.2 %reduce-scatter.41.cloned.1.call-done = bf16[3,384,192]{1,2,0:T(8,128)(2,1)} async-done(((bf16[3,3072,192]{1,2,0:T(8,128)(2,1)}), bf16[3,384,192]{1,2,0:T(8,128)(2,1)}) %reduce-scatter.41.cloned.1.call-update) | async-done | bytes 442384 | tf_op jit(solution)/shard_map/reduce_scatter | solution.py:205
  930.6 51.4 %reduce-scatter.37.cloned.1.call-done = bf16[3,96,768]{2,1,0:T(8,128)(2,1)} async-done(((bf16[3,768,768]{2,1,0:T(8,128)(2,1)}), bf16[3,96,768]{2,1,0:T(8,128)(2,1)}) %reduce-scatter.37.cloned.1.call-update) | async-done | bytes 442384 | tf_op jit(solution)/shard_map/reduce_scatter | solution.py:204
  983.9 34.8 %reduce-scatter.53.cloned.1.call-done = f32[96,3]{1,0:T(8,128)} async-done(((f32[768,3]{1,0:T(8,128)}), f32[96,3]{1,0:T(8,128)}) %reduce-scatter.53.cloned.1.call-update) | async-done | bytes 1168
  1019.6 10.9 all-gather.11
  1031.2 2.3 fusion.54
  1035.1 2.2 fusion.31
  1037.4 22.7 %all-reduce.22 = (bf16[768]{0:T(1024)(128)(2,1)S(1)}, bf16[768]{0:T(1024)(128)(2,1)S(1)}, bf16[768]{0:T(1024)(128)(2,1)S(1)}, bf16[768]{0:T(1024)(128)(2,1)S(1)}...) all-reduce(f32[768]{0:T(1024)S(1)} %get-tuple-element.104, ...), channel_id=11, replica_groups=mesh['fsdp'=8,'rep'=4] {'fsdp'}, use_global_device_ids=true, to_apply=%region_18.19.clone | all-reduce | flops 5376 | bytes 32256
  1062.1 8.5 all-reduce.24
  1074.9 2.8 fusion.30
  1078.8 13.1 all-gather.10
  1092.4 6.7 reduce-scatter.49.cloned.1.call-done
  1100.2 13.6 %all_gather.120 = bf16[96,768]{0,1:T(8,128)(2,1)S(1)} all-gather(bf16[96,192]{0,1:T(8,128)(2,1)S(1)} %copy.120), channel_id=1, replica_groups=mesh['fsdp'=8,'rep'=4] {'rep'}, dimensions={1}, use_global_device_ids=true | all-gather | bytes 184320 | tf_op jit(solution)/shard_map/all_gather | solution.py:356
  1114.6 22.5 %reduce-scatter.47.cloned.1.call-done = f32[96,192]{1,0:T(8,128)} async-done(((f32[768,192]{1,0:T(8,128)}), f32[96,192]{1,0:T(8,128)}) %reduce-scatter.47.cloned.1.call-update) | async-done | bytes 73744
  1138.2 13.6 %all_gather.118 = bf16[96,768]{0,1:T(8,128)(2,1)S(1)} all-gather(bf16[96,192]{0,1:T(8,128)(2,1)S(1)} %copy.118), channel_id=1, replica_groups=mesh['fsdp'=8,'rep'=4] {'rep'}, dimensions={1}, use_global_device_ids=true | all-gather | bytes 184320 | tf_op jit(solution)/shard_map/all_gather | solution.py:353
  1152.7 22.7 %reduce-scatter.43.cloned.1.call-done = f32[96,192]{1,0:T(8,128)} async-done(((f32[768,192]{1,0:T(8,128)}), f32[96,192]{1,0:T(8,128)}) %reduce-scatter.43.cloned.1.call-update) | async-done | bytes 73744
  1176.3 13.6 %all_gather.115 = bf16[96,768]{0,1:T(8,128)(2,1)S(1)} all-gather(bf16[96,192]{0,1:T(8,128)(2,1)S(1)} %copy.114), channel_id=1, replica_groups=mesh['fsdp'=8,'rep'=4] {'rep'}, dimensions={1}, use_global_device_ids=true | all-gather | bytes 184320 | tf_op jit(solution)/shard_map/all_gather | solution.py:347
  1190.8 23.1 %reduce-scatter.45.cloned.1.call-done = f32[96,192]{1,0:T(8,128)} async-done(((f32[768,192]{1,0:T(8,128)}), f32[96,192]{1,0:T(8,128)}) %reduce-scatter.45.cloned.1.call-update) | async-done | bytes 73744
  1215.0 14.4 %all_gather.117 = bf16[96,768]{0,1:T(8,128)(2,1)S(1)} all-gather(bf16[96,192]{0,1:T(8,128)(2,1)S(1)} %copy.116), channel_id=1, replica_groups=mesh['fsdp'=8,'rep'=4] {'rep'}, dimensions={1}, use_global_device_ids=true | all-gather | bytes 184320 | tf_op jit(solution)/shard_map/all_gather | solution.py:350
  1230.2 26.3 %all-gather.35.cloned.1.call-done = bf16[3,384,768]{1,2,0:T(8,128)(2,1)} async-done(((bf16[3,384,192]{1,2,0:T(8,128)(2,1)}), bf16[3,384,768]{1,2,0:T(8,128)(2,1)}) %all-gather.35.cloned.1.call-update) | async-done | bytes 1769488 | tf_op jit(solution)/shard_map/all_gather | solution.py:215
  1256.4 4.0 copy.108
  1260.5 36.7 %all-gather.33.cloned.1.call-done = bf16[3,96,3072]{2,1,0:T(8,128)(2,1)} async-done(((bf16[3,96,768]{2,1,0:T(8,128)(2,1)}), bf16[3,96,3072]{2,1,0:T(8,128)(2,1)}) %all-gather.33.cloned.1.call-update) | async-done | bytes 1769488 | tf_op jit(solution)/shard_map/all_gather | solution.py:212
  1297.2 3.7 convert_element_type.380
  (249 shorter events, 53.6 us)
Async XLA Ops:
  7.2 47.2 %all-gather.23.cloned.1.call-start = ((), (), s32[]{:S(2)}) async-start(), calls=%async_computation.15 | async-start | bytes 1327104 | tf_op jit(solution)/shard_map/all_gather | solution.py:78
  7.9 54.9 %all-gather.21.cloned.1.call-start = ((), (), s32[]{:S(2)}) async-start(), calls=%async_computation.14 | async-start | bytes 1327104 | tf_op jit(solution)/shard_map/all_gather | solution.py:81
  8.7 80.2 %all-gather.25.cloned.1.call-start = ((), (), s32[]{:S(2)}) async-start(), calls=%async_computation.16 | async-start | bytes 1327104 | tf_op jit(solution)/shard_map/all_gather | solution.py:80
  9.4 105.3 %all-gather.27.cloned.1.call-start = ((), (), s32[]{:S(2)}) async-start(), calls=%async_computation.17 | async-start | bytes 1327104 | tf_op jit(solution)/shard_map/all_gather | solution.py:83
  10.0 185.2 %all-gather.29.cloned.1.call-start = ((), (), s32[]{:S(2)}) async-start(), calls=%async_computation.18 | async-start | bytes 15925248 | tf_op jit(solution)/shard_map/all_gather | solution.py:138
  10.6 2.0 copy-start.36
  10.6 2.2 copy-start.37
  10.6 2.5 copy-start.38
  10.6 2.7 copy-start.39
  10.6 2.9 copy-start.40
  10.6 3.1 copy-start.41
  10.6 3.4 copy-start.42
  10.7 29.5 %copy-start.24 = (s32[416,1]{0,1:T(1,128)S(1)}, s32[416,1]{0,1:T(1,128)}, u32[]{:S(2)}) copy-start(s32[416,1]{0,1:T(1,128)} %param.21) | copy-start | bytes 4996
  10.7 30.9 %copy-start.31 = (bf16[3,384]{1,0:T(4,128)(2,1)S(1)}, bf16[3,384]{1,0:T(4,128)(2,1)}, u32[]{:S(2)}) copy-start(bf16[3,384]{1,0:T(4,128)(2,1)} %param.34) | copy-start | bytes 6916
  10.7 42.2 %copy-start.34 = (s32[1,4]{1,0:T(1,128)S(1)}, s32[1,4]{1,0:T(1,128)}, u32[]{:S(2)}) copy-start(s32[1,4]{1,0:T(1,128)} %param.20) | copy-start | bytes 52
  10.7 42.3 %copy-start.8 = (bf16[416,768]{1,0:T(8,128)(2,1)S(1)}, bf16[416,768]{1,0:T(8,128)(2,1)}, u32[]{:S(2)}) copy-start(bf16[416,768]{1,0:T(8,128)(2,1)} %param.19) | copy-start | bytes 1916932
  10.7 265.1 %all-gather.31.cloned.1.call-start = ((), (), s32[]{:S(2)}) async-start(), calls=%async_computation.19 | async-start | bytes 15925248 | tf_op jit(solution)/shard_map/all_gather | solution.py:140
  11.3 504.1 %reduce-scatter.39.cloned.1.call-start = ((), (), s32[]{:S(2)}) async-start(), calls=%async_computation.27 | async-start | bytes 17694720 | tf_op jit(solution)/shard_map/reduce_scatter | solution.py:199
  40.1 48.8 %copy-start.29 = (f32[768]{0:T(1024)}, f32[768]{0:T(1024)S(1)}, u32[]{:S(2)}) copy-start(f32[768]{0:T(1024)S(1)} %convert_element_type.301) | copy-start | bytes 9220
  49.6 3.4 copy-start.27
  52.8 223.0 %copy-start.2 = (bf16[624,768]{1,0:T(8,128)(2,1)}, bf16[624,768]{1,0:T(8,128)(2,1)S(1)}, u32[]{:S(2)}) copy-start(bf16[624,768]{1,0:T(8,128)(2,1)S(1)} %scatter_custom_fusion.1) | copy-start | bytes 2875396
  53.5 35.4 %copy-start.25 = (f32[416]{0:T(512)}, f32[416]{0:T(512)S(1)}, u32[]{:S(2)}) copy-start(f32[416]{0:T(512)S(1)} %add_rsqrt_fusion.1) | copy-start | bytes 4996
  56.7 36.4 %copy-start.4 = (bf16[416,768]{0,1:T(8,128)(2,1)}, bf16[416,768]{0,1:T(8,128)(2,1)S(1)}, u32[]{:S(2)}) copy-start(bf16[416,768]{0,1:T(8,128)(2,1)S(1)} %copy.96) | copy-start | bytes 1916932
  67.1 30.8 %copy-start.12 = (bf16[416,768]{0,1:T(8,128)(2,1)}, bf16[416,768]{0,1:T(8,128)(2,1)S(1)}, u32[]{:S(2)}) copy-start(bf16[416,768]{0,1:T(8,128)(2,1)S(1)} %copy.95) | copy-start | bytes 1916932
  93.1 3.1 copy-start.6
  96.2 3.8 copy-start
  96.2 4.0 copy-start.20
  97.8 5.2 copy-start.22
  100.2 14.5 %copy-start.9 = (bf16[416,768]{1,0:T(8,128)(2,1)S(1)}, bf16[416,768]{1,0:T(8,128)(2,1)}, u32[]{:S(2)}) copy-start(bf16[416,768]{1,0:T(8,128)(2,1)} %param.19) | copy-start | bytes 1916932
  214.2 541.9 %reduce-scatter.35.cloned.1.call-start = ((), (), s32[]{:S(2)}) async-start(), calls=%async_computation.24 | async-start | bytes 17694720 | tf_op jit(solution)/shard_map/reduce_scatter | solution.py:196
  296.4 492.3 %reduce-scatter.33.cloned.1.call-start = ((), (), s32[]{:S(2)}) async-start(), calls=%async_computation.23 | async-start | bytes 1474560 | tf_op jit(solution)/shard_map/reduce_scatter | solution.py:311
  331.5 2.1 copy-start.1
  331.5 2.2 copy-start.11
  333.8 2.6 copy-start.43
  336.4 2.2 copy-start.21
  336.4 2.2 copy-start.23
  338.3 480.5 %reduce-scatter.31.cloned.1.call-start = ((), (), s32[]{:S(2)}) async-start(), calls=%async_computation.22 | async-start | bytes 1474560 | tf_op jit(solution)/shard_map/reduce_scatter | solution.py:308
  340.8 6.7 copy-start.10
  340.8 6.7 copy-start.26
  340.8 6.7 copy-start.30
  346.6 0.9 copy-start.18
  349.6 500.0 %reduce-scatter.27.cloned.1.call-start = ((), (), s32[]{:S(2)}) async-start(), calls=%async_computation.20 | async-start | bytes 1474560 | tf_op jit(solution)/shard_map/reduce_scatter | solution.py:302
  357.7 12.3 copy-start.7
  373.5 0.9 copy-start.13
  376.4 1.1 copy-start.5
  376.4 503.9 %reduce-scatter.29.cloned.1.call-start = ((), (), s32[]{:S(2)}) async-start(), calls=%async_computation.21 | async-start | bytes 1474560 | tf_op jit(solution)/shard_map/reduce_scatter | solution.py:305
  381.5 0.9 copy-start.15
  384.4 546.2 %reduce-scatter.41.cloned.1.call-start = ((), (), s32[]{:S(2)}) async-start(), calls=%async_computation.28 | async-start | bytes 3981312 | tf_op jit(solution)/shard_map/reduce_scatter | solution.py:205
  515.4 466.6 %reduce-scatter.37.cloned.1.call-start = ((), (), s32[]{:S(2)}) async-start(), calls=%async_computation.25 | async-start | bytes 3981312 | tf_op jit(solution)/shard_map/reduce_scatter | solution.py:204
  756.1 1.2 copy-start.3
  756.1 262.6 %reduce-scatter.53.cloned.1.call-start = ((), (), s32[]{:S(2)}) async-start(), calls=%async_computation.35 | async-start | bytes 442368
  758.4 319.3 %reduce-scatter.51.cloned.1.call-start = ((), (), s32[]{:S(2)}) async-start(), calls=%async_computation.34 | async-start | bytes 1769472
  760.2 339.0 %reduce-scatter.49.cloned.1.call-start = ((), (), s32[]{:S(2)}) async-start(), calls=%async_computation.33 | async-start | bytes 884736
  790.7 346.4 %reduce-scatter.47.cloned.1.call-start = ((), (), s32[]{:S(2)}) async-start(), calls=%async_computation.32 | async-start | bytes 884736
  820.8 354.5 %reduce-scatter.43.cloned.1.call-start = ((), (), s32[]{:S(2)}) async-start(), calls=%async_computation.30 | async-start | bytes 884736
  851.7 130.4 %copy-start.44 = (u32[32]{0:T(128)S(1)}, u32[32]{0:T(128)}, u32[]{:S(2)}) copy-start(u32[32]{0:T(128)} %constant.89) | copy-start | bytes 388
  851.7 179.6 %copy-start.14 = (bf16[12,64,416]{2,1,0:T(8,128)(2,1)S(1)}, bf16[12,64,416]{2,1,0:T(8,128)(2,1)}, u32[]{:S(2)}) copy-start(bf16[12,64,416]{2,1,0:T(8,128)(2,1)} %copy-done.13) | copy-start | bytes 1916932
  851.7 362.3 %reduce-scatter.45.cloned.1.call-start = ((), (), s32[]{:S(2)}) async-start(), calls=%async_computation.31 | async-start | bytes 884736
  882.3 374.1 %all-gather.35.cloned.1.call-start = ((), (), s32[]{:S(2)}) async-start(), calls=%async_computation.29 | async-start | bytes 2211840 | tf_op jit(solution)/shard_map/all_gather | solution.py:215
  930.6 366.6 %all-gather.33.cloned.1.call-start = ((), (), s32[]{:S(2)}) async-start(), calls=%async_computation.26 | async-start | bytes 2211840 | tf_op jit(solution)/shard_map/all_gather | solution.py:212
  1031.2 2.3 copy-start.16
  1031.2 2.3 copy-start.17
  1033.6 1.1 copy-start.19
  1033.6 1.5 copy-start.35
  (3 other events, 2.1 us)
Sparse Core Ops, SparseCore 0:
  9.9 26.9 all-gather.22
  38.7 24.0 all-gather.20
  64.7 24.0 all-gather.24
  90.6 24.0 all-gather.26
  116.4 78.7 all-gather.28
  197.0 78.7 all-gather.30
  278.2 237.2 reduce-scatter.38
  517.8 238.2 reduce-scatter.34
  758.4 30.2 reduce-scatter.32
  790.8 27.8 reduce-scatter.30
  821.7 27.8 reduce-scatter.26
  852.3 27.8 reduce-scatter.28
  883.7 46.7 reduce-scatter.40
  933.9 48.0 reduce-scatter.36
  984.9 33.7 reduce-scatter.52
  1022.5 38.5 reduce-scatter.50
  1064.1 35.0 reduce-scatter.48
  1102.2 34.9 reduce-scatter.46
  1140.3 34.9 reduce-scatter.42
  1178.9 35.0 reduce-scatter.44
  1215.5 40.8 all-gather.34
  1258.0 39.1 all-gather.32
where the time goes:
time: 1310 us
  waiting for transfers between devices  937 us (72%)
  blocking collectives  153 us (12%)
  matrix products  112 us (9%)
  local copies, waits for them, and re-layouts  50.5 us (4%)
  other arithmetic  36.1 us (3%)
  between operations  17.2 us (1%)
    reduce_scatter x1, waiting for transfers between devices, per_device(): lax.psum_scatter(grad_in.astype(jnp.bfloat16), 'rep', scatter_dimension=2...  241 us
    reduce_scatter x1, waiting for transfers between devices, per_device(): lax.psum_scatter(grad_down.astype(jnp.bfloat16), 'rep', scatter_dimension...  131 us
    unnamed x28, waiting for transfers between devices  114 us
    all_gather x1, waiting for transfers between devices, per_device(): lax.all_gather(expert_in, 'fsdp', axis=1, tiled=True)  74.6 us
    all_gather x1, waiting for transfers between devices, per_device(): lax.all_gather(expert_out, 'fsdp', axis=1, tiled=True)  61.6 us
    unnamed x3, blocking collectives  57 us
    reduce_scatter x1, waiting for transfers between devices, per_device(): lax.psum_scatter(column_in, 'fsdp', scatter_dimension=1, tiled=True)  51.4 us
    reduce_scatter x1, waiting for transfers between devices, per_device(): lax.psum_scatter(column_down, 'fsdp', scatter_dimension=1, tiled=True)  48.2 us
  transfers between devices with their start and end apart: 22, of which 20 were waited for; matrix products, arithmetic and copies ran while one was open for 14% of the time, Pallas kernels for 0%

commit v1 on v0

--- a/solution.py
+++ b/solution.py
@@ -1,6 +1,8 @@
 import jax
 import jax.numpy as jnp
 from jax import lax
+from jax.experimental import pallas as pl
+from jax.experimental.pallas import tpu as pltpu
 from jax.sharding import PartitionSpec as P
 
 HEAD = 64
@@ -44,7 +46,7 @@
     )
 
 
-def per_device(
+def per_device_weights(
     tokens,
     starts,
     routes,
@@ -398,6 +400,356 @@
     )
 
 
+def dot_nn(a,b): return lax.dot_general(a,b,(((1,),(0,)),((),())),preferred_element_type=jnp.float32)
+def dot_nt(a,b): return lax.dot_general(a,b,(((1,),(1,)),((),())),preferred_element_type=jnp.float32)
+def dot_tn(a,b): return lax.dot_general(a,b,(((0,),(0,)),((),())),preferred_element_type=jnp.float32)
+
+def moe_kernel(n, cap, meta, *refs):
+    E=3
+    xin=refs[:n]; gin=refs[n:2*n]
+    w_in,w_out,b_in=refs[2*n:2*n+3]
+    res_e,res_o,dsl_e,dsl_o,gwo,gwi,gb=refs[2*n+3:2*n+10]
+    X,G,R,S,XS,GS,ACT,DP,sem,osem=refs[2*n+10:]
+    copies=[]
+    for j in range(n):
+        for src,dst,k in ((xin[j],X,0),(gin[j],G,1)):
+            c=pltpu.make_async_copy(src,dst.at[j],sem.at[k,j]); c.start(); copies.append(c)
+    def zero(j,c):
+        R[j]=jnp.zeros_like(R[j]); S[j]=jnp.zeros_like(S[j]); return c
+    lax.fori_loop(0,n,zero,0)
+    for c in copies: c.wait()
+    T=2*cap
+    for e in range(E):
+        def tile(t,carry):
+            base=pl.multiple_of(t*T,T)
+            masks=[];starts=[]
+            for q in range(2):
+                j=2*t+q
+                st=pl.multiple_of(meta[j,3*e],16); lo=meta[j,3*e+1]; hi=meta[j,3*e+2]
+                row=lax.broadcasted_iota(jnp.int32,(cap,1),0)
+                m=(row>=lo)&(row<hi)
+                masks.append(m);starts.append(st)
+                XS[pl.ds(base+q*cap,cap),:]=X[j,pl.ds(st,cap),:]
+                g=G[j,pl.ds(st,cap),:]
+                GS[pl.ds(base+q*cap,cap),:]=jnp.where(m,g,jnp.zeros_like(g))
+            xs=XS[pl.ds(base,T),:]
+            gs=GS[pl.ds(base,T),:]
+            pre=dot_nn(xs,w_in[e])+b_in[e]
+            cdf=0.5*(1.0+lax.erf(pre*0.7071067811865476))
+            act=(pre*cdf).astype(jnp.bfloat16)
+            slope=cdf+pre*jnp.exp(-0.5*pre*pre)*0.3989422804014327
+            da=dot_nt(gs,w_out[e])
+            dp=(da*slope).astype(jnp.bfloat16)
+            ACT[pl.ds(base,T),:]=act
+            DP[pl.ds(base,T),:]=dp
+            ds=dot_nt(dp,w_in[e]).astype(jnp.bfloat16)
+            rs=dot_nn(act,w_out[e]).astype(jnp.bfloat16)
+            for q in range(2):
+                j=2*t+q
+                for dst,v in ((R,rs),(S,ds)):
+                    old=dst[j,pl.ds(starts[q],cap),:]
+                    dst[j,pl.ds(starts[q],cap),:]=jnp.where(masks[q],v[q*cap:(q+1)*cap],old)
+            return carry
+        lax.fori_loop(0,n//2,tile,0)
+        gwo[e]=dot_tn(ACT[...],GS[...]).astype(jnp.bfloat16)
+        gwi[e]=dot_tn(XS[...],DP[...]).astype(jnp.bfloat16)
+        gb[e]=jnp.sum(DP[...].astype(jnp.float32),0,keepdims=True)
+    outs=[]
+    for j in range(n):
+        for k,(src,de,do) in enumerate(((S,dsl_e,dsl_o),(R,res_e,res_o))):
+            dst=(de if j%2==0 else do).at[j//2]
+            c=pltpu.make_async_copy(src.at[j],dst,osem.at[k,j]); c.start(); outs.append(c)
+    for c in outs: c.wait()
+
+def moe(meta,xs,gs,w_in,w_out,b_in,cap):
+    n=len(xs); rows,d=xs[0].shape; E,_,f=w_in.shape
+    bf=jnp.bfloat16
+    any_=pl.BlockSpec(memory_space=pl.ANY); vm=pl.BlockSpec(memory_space=pltpu.VMEM)
+    sd=jax.ShapeDtypeStruct
+    return pl.pallas_call(
+        lambda *r: moe_kernel(n,cap,*r),
+        out_shape=(sd((n//2,rows,d),bf),)*4+(sd((E,f,d),bf),sd((E,d,f),bf),sd((E,1,f),jnp.float32)),
+        in_specs=[pl.BlockSpec(memory_space=pltpu.SMEM)]+[any_]*(2*n)+[vm]*3,
+        out_specs=(any_,)*4+(vm,)*3,
+        scratch_shapes=[pltpu.VMEM((n,rows,d),bf)]*4+[pltpu.VMEM((n*cap,d),bf)]*2+[pltpu.VMEM((n*cap,f),bf)]*2+[pltpu.SemaphoreType.DMA((2,n)),pltpu.SemaphoreType.DMA((2,n))],
+        compiler_params=pltpu.CompilerParams(vmem_limit_bytes=60*1024*1024),
+        name="moe",
+    )(meta,*xs,*gs,w_in,w_out,b_in)
+
+
+ROWS16 = 16
+LANES = 128
+BF = jnp.bfloat16
+F32 = jnp.float32
+
+
+def swap(v, n, mask, axis="fsdp"):
+    return lax.ppermute(v, axis, [(i, i ^ mask) for i in range(n)])
+
+
+def gather_pieces(v, n):
+    pieces = {0: v, 1: swap(v, n, 1)}
+    for m in range(2, n, 2):
+        pieces[m] = swap(v, n, m)
+        pieces[m ^ 1] = swap(pieces[m], n, 1)
+    return [pieces[m] for m in range(n)]
+
+
+def scatter_sum(even, odd, n):
+    other = swap(odd, n, 1)
+    terms = [(even[i].astype(F32) + other[i].astype(F32)).astype(BF) for i in range(n // 2)]
+    total = terms[0].astype(F32)
+    for i in range(1, n // 2):
+        total = total + swap(terms[i], n, 2 * i).astype(F32)
+    return total
+
+
+def line_sum(v):
+    idx = lax.axis_index("rep")
+    inward = lax.ppermute(v, "rep", [(0, 1), (3, 2)])
+    part = (v.astype(F32) + inward.astype(F32)).astype(BF)
+    across = lax.ppermute(part, "rep", [(1, 2), (2, 1)])
+    total = (part.astype(F32) + across.astype(F32)).astype(BF)
+    outward = lax.ppermute(total, "rep", [(1, 0), (2, 3)])
+    return jnp.where((idx == 0) | (idx == 3), outward, total).astype(F32)
+
+
+def per_device_tokens(
+    n,
+    tokens,
+    starts,
+    routes,
+    norm1_gain,
+    norm1_bias,
+    query_weight,
+    query_bias,
+    key_weight,
+    value_weight,
+    value_bias,
+    out_weight,
+    out_bias,
+    norm2_gain,
+    norm2_bias,
+    expert_in,
+    expert_in_bias,
+    expert_out,
+    expert_out_bias,
+    cotangent,
+):
+    me = lax.axis_index("fsdp")
+    seq_rows = starts.shape[0]
+    tok_count, width = tokens.shape
+    seq_len = tok_count // seq_rows
+    shard = width // n
+    ff_shard = expert_out.shape[1]
+    head_count = width // HEAD
+    head_shape = (seq_rows, seq_len, head_count, HEAD)
+    scale_factor = HEAD ** (-0.5)
+
+    vectors = jnp.stack(
+        [norm1_gain, norm1_bias, query_bias, value_bias, out_bias, norm2_gain, norm2_bias], 1
+    )
+    vectors = jnp.concatenate([vectors, expert_out_bias.T], 1)
+    n_vec = vectors.shape[1]
+    pad = jnp.zeros((shard, LANES - n_vec), BF)
+    first = jnp.concatenate([query_weight, key_weight, value_weight, vectors, pad], 1)
+
+    def assemble(v):
+        whole = jnp.zeros((width, v.shape[1]), v.dtype)
+        for m, piece in enumerate(gather_pieces(v, n)):
+            whole = lax.dynamic_update_slice(whole, piece, ((me ^ m) * shard, 0))
+        return whole
+
+    first_all = assemble(first)
+    w_qkv = first_all[:, : 3 * width]
+    vec = first_all[:, 3 * width : 3 * width + n_vec].T.astype(F32)
+    gain_one, shift_one, b_query, b_value, b_out, gain_two, shift_two = (vec[i] for i in range(7))
+    b_down = vec[7:]
+    w_out = assemble(out_weight)
+
+    route_ids = routes[:, 0]
+    member = (route_ids[:, None] == jnp.arange(EXPERTS, dtype=jnp.int32)[None, :]).astype(jnp.int32)
+    rank = jnp.sum(jnp.cumsum(member, 0) * member, 1) - 1
+    counts = jnp.sum(member, 0)
+    padded = (counts + ROWS16 - 1) // ROWS16 * ROWS16
+    base = jnp.cumsum(padded) - padded
+    slots = tok_count + ROWS16 * (EXPERTS - 1)
+    position = jnp.sum(member * base[None, :], 1) + rank
+    place = (jnp.arange(slots, dtype=jnp.int32)[:, None] == position[None, :]).astype(BF)
+    begin = jnp.minimum(base, slots - CAP)
+    meta = jnp.stack([begin, base - begin, base - begin + padded], 1).reshape(1, 3 * EXPERTS)
+    meta_all = lax.all_gather(meta, "fsdp", axis=0, tiled=True)
+    meta_rel = jnp.take(meta_all, me ^ jnp.arange(n), axis=0)
+
+    def sort(v):
+        return jnp.dot(place, v, preferred_element_type=F32).astype(BF)
+
+    def unsort(v):
+        return lax.dot_general(
+            place, v.astype(BF), (((0,), (0,)), ((), ())), preferred_element_type=F32
+        )
+
+    grad_pieces = gather_pieces(sort(cotangent), n)
+
+    w_in = jnp.zeros((EXPERTS, width, ff_shard), BF)
+    for m in range(n):
+        piece = lax.dynamic_slice(
+            expert_in, (0, 0, (me ^ m) * ff_shard), (EXPERTS, shard, ff_shard)
+        )
+        if m:
+            piece = swap(piece, n, m)
+        w_in = lax.dynamic_update_slice(w_in, piece, (0, (me ^ m) * shard, 0))
+
+    resid_in = tokens.astype(F32)
+    normed_one = normalize(resid_in, gain_one, shift_one).astype(BF)
+    qkv = jnp.dot(normed_one, w_qkv, preferred_element_type=F32)
+    queries = (qkv[:, :width] + b_query).astype(BF).reshape(head_shape)
+    keys_mat = qkv[:, width : 2 * width].astype(BF).reshape(head_shape)
+    values = (qkv[:, 2 * width :] + b_value).astype(BF).reshape(head_shape)
+    pos = jnp.arange(seq_len, dtype=jnp.int32)
+    segment = jnp.sum((pos[None, :, None] >= starts[:, None, :]).astype(jnp.int32), -1)
+    same_seg = (segment[:, :, None] == segment[:, None, :])[:, None]
+
+    def scores_of(query_part, key_part):
+        raw_scores = (
+            jnp.einsum("rqhd,rkhd->rhqk", query_part, key_part, preferred_element_type=F32)
+            * scale_factor
+        )
+        return jnp.where(same_seg, raw_scores, MASKED)
+
+    scores = scores_of(queries, keys_mat)
+    row_max = jnp.max(scores, -1, keepdims=True)
+    exp_scores = jnp.exp(scores - row_max)
+    row_total = jnp.sum(exp_scores, -1, keepdims=True)
+    log_total = row_max + jnp.log(row_total)
+    probs_low = (exp_scores / row_total).astype(BF)
+    mixed = jnp.einsum("rhqk,rkhd->rqhd", probs_low, values, preferred_element_type=F32)
+    mixed = mixed.reshape(tok_count, width).astype(BF)
+    hidden = resid_in + jnp.dot(mixed, w_out, preferred_element_type=F32) + b_out
+    normed_two = normalize(hidden, gain_two, shift_two).astype(BF)
+
+    token_pieces = gather_pieces(sort(normed_two), n)
+    res_e, res_o, dsl_e, dsl_o, g_down, g_in, g_in_bias = moe(
+        meta_rel,
+        token_pieces,
+        grad_pieces,
+        w_in,
+        expert_out,
+        expert_in_bias.astype(F32)[:, None, :],
+        CAP,
+    )
+    grad_normed_two = unsort(scatter_sum(dsl_e, dsl_o, n))
+    routed = unsort(scatter_sum(res_e, res_o, n)) + jnp.dot(
+        member.astype(F32), b_down, precision=lax.Precision.HIGHEST
+    )
+    output = (hidden + routed).astype(BF)
+
+    grad_output = cotangent.astype(F32)
+    g_down_bias = lax.dot_general(
+        member.astype(BF), cotangent, (((0,), (0,)), ((), ())), preferred_element_type=F32
+    )
+    grad_from_norm, g_gain_two, g_shift_two = norm_back(hidden, gain_two, grad_normed_two)
+    grad_hidden = grad_output + grad_from_norm
+
+    sum_down = jnp.stack([line_sum(g_down[e]) for e in range(EXPERTS)])
+    sum_in_bias = line_sum(g_in_bias[:, 0].astype(BF))
+    mine = jnp.zeros((EXPERTS, shard, n * ff_shard), BF)
+    for m in range(n):
+        piece = lax.dynamic_slice(g_in, (0, (me ^ m) * shard, 0), (EXPERTS, shard, ff_shard))
+        if m:
+            piece = swap(piece, n, m)
+        mine = lax.dynamic_update_slice(mine, piece, (0, 0, (me ^ m) * ff_shard))
+    sum_in = jnp.stack([line_sum(mine[e]) for e in range(EXPERTS)])
+
+    grad_branch = grad_hidden.astype(BF)
+    g_out_bias = jnp.sum(grad_branch.astype(F32), 0)
+    g_out_weight = jnp.einsum("td,te->de", mixed, grad_branch, preferred_element_type=F32)
+
+    def shares(v):
+        even = [
+            lax.dynamic_slice(v, ((me ^ m) * shard, 0), (shard, v.shape[1]))
+            for m in range(0, n, 2)
+        ]
+        odd = [
+            lax.dynamic_slice(v, ((me ^ m) * shard, 0), (shard, v.shape[1]))
+            for m in range(1, n, 2)
+        ]
+        return even, jnp.stack(odd)
+
+    sum_out = line_sum(scatter_sum(*shares(g_out_weight.astype(BF)), n).astype(BF))
+
+    grad_mixed = (
+        jnp.einsum("te,de->td", grad_branch, w_out, preferred_element_type=F32)
+        .astype(BF)
+        .reshape(head_shape)
+    )
+    scores_again = scores_of(queries, keys_mat)
+    probs = jnp.exp(scores_again - log_total)
+    probs_again = probs.astype(BF)
+    grad_values = jnp.einsum("rhqk,rqhd->rkhd", probs_again, grad_mixed, preferred_element_type=F32)
+    grad_values = grad_values.astype(BF).reshape(tok_count, width)
+    grad_probs = jnp.einsum("rqhd,rkhd->rhqk", grad_mixed, values, preferred_element_type=F32)
+    grad_scores = (probs * (grad_probs - jnp.sum(grad_probs * probs, -1, keepdims=True))).astype(BF)
+    grad_queries = (
+        (
+            jnp.einsum("rhqk,rkhd->rqhd", grad_scores, keys_mat, preferred_element_type=F32)
+            * scale_factor
+        )
+        .astype(BF)
+        .reshape(tok_count, width)
+    )
+    grad_keys = (
+        (
+            jnp.einsum("rhqk,rqhd->rkhd", grad_scores, queries, preferred_element_type=F32)
+            * scale_factor
+        )
+        .astype(BF)
+        .reshape(tok_count, width)
+    )
+    g_query_bias = jnp.sum(grad_queries.astype(F32), 0)
+    g_value_bias = jnp.sum(grad_values.astype(F32), 0)
+    grad_qkv = jnp.concatenate([grad_queries, grad_keys, grad_values], 1)
+    g_qkv_weight = jnp.einsum("td,te->de", normed_one, grad_qkv, preferred_element_type=F32)
+    grad_normed_one = jnp.einsum("te,de->td", grad_qkv, w_qkv, preferred_element_type=F32)
+    grad_from_first, g_gain_one, g_shift_one = norm_back(resid_in, gain_one, grad_normed_one)
+    input_grad = grad_hidden + grad_from_first
+
+    g_vec = jnp.stack(
+        [g_gain_one, g_shift_one, g_query_bias, g_value_bias, g_out_bias, g_gain_two, g_shift_two], 1
+    )
+    g_vec = jnp.concatenate([g_vec, g_down_bias.T], 1).astype(BF)
+    last = jnp.concatenate(
+        [g_qkv_weight.astype(BF), g_vec, jnp.zeros((width, LANES - n_vec), BF)], 1
+    )
+    sum_last = line_sum(scatter_sum(*shares(last), n).astype(BF))
+    sum_vec = sum_last[:, 3 * width : 3 * width + n_vec].T
+    return (
+        output,
+        input_grad,
+        sum_vec[0],
+        sum_vec[1],
+        sum_last[:, :width],
+        sum_vec[2],
+        sum_last[:, width : 2 * width],
+        sum_last[:, 2 * width : 3 * width],
+        sum_vec[3],
+        sum_out,
+        sum_vec[4],
+        sum_vec[5],
+        sum_vec[6],
+        sum_in,
+        sum_in_bias,
+        sum_down,
+        sum_vec[7:],
+    )
+
+
+def plan_of(n, replicas):
+    if n == 8 and replicas == 4:
+        return lambda *args: per_device_tokens(n, *args)
+    return per_device_weights
+
+
 def solution(mesh):
     in_specs = (
         P(("fsdp", "rep"), None),
@@ -439,6 +791,7 @@
         P(None, "fsdp", None),
         P(None, "fsdp"),
     )
+    per_device = plan_of(mesh.shape["fsdp"], mesh.shape["rep"])
     return jax.shard_map(
         per_device, mesh=mesh, in_specs=in_specs, out_specs=out_specs, check_vma=False
     )

time: 1310 us -> 668 us (0.51)
  waiting for transfers between devices: 937 us -> 292 us
  blocking collectives: 153 us -> 18.1 us
  starting transfers between devices: 1.26 us -> 84.6 us
  local copies, waits for them, and re-layouts: 50.5 us -> 131 us
  matrix products: 112 us -> 52.6 us
  Pallas kernels: 0 us -> 37.8 us
  between operations: 17.2 us -> 2.5 us
    reduce_scatter x8 -> x0, waiting for transfers between devices: 585 us -> none  [the longest x1 241 us: per_device(): lax.psum_scatter(grad_in.astype(jnp.bfloat16), 'rep', scatter_dimension=2...]
    ppermute x0 -> x85, waiting for transfers between devices: none -> 292 us  [the longest x58 154 us: swap(): return lax.ppermute(v, axis, [(i, i ^ mask) for i in range(n)])]
    all_gather x8 -> x0, waiting for transfers between devices: 239 us -> none  [the longest x1 74.6 us: per_device(): lax.all_gather(expert_in, 'fsdp', axis=1, tiled=True)]
    unnamed x28 -> x0, waiting for transfers between devices: 114 us -> none
    ppermute x0 -> x85, starting transfers between devices: none -> 84.6 us  [the longest x58 49.4 us: swap(): return lax.ppermute(v, axis, [(i, i ^ mask) for i in range(n)])]
    all_gather x8 -> x1, blocking collectives: 96.4 us -> 18.1 us  [per_device_tokens(): meta_all = lax.all_gather(meta, 'fsdp', axis=0, tiled=True)]
    dynamic_update_slice x0 -> x30, local copies, waits for them, and re-layouts: none -> 74.9 us  [the longest x16 65.6 us: assemble(): whole = lax.dynamic_update_slice(whole, piece, ((me ^ m) * shard, 0))]
    dot_general x23 -> x17, matrix products: 109 us -> 50.7 us  [the longest x1 10.3 us: per_device_tokens(): jnp.einsum('rqhd,rkhd->rhqk', grad_mixed, values, preferred_element_type=...]
  transfers between devices with their start and end apart: 22 -> 85, of which waited for: 20 -> 34; matrix products, arithmetic and copies ran while one was open for 14% -> 31% of each run, Pallas kernels for 0% -> 0%
where the time goes in v1:
time: 668 us; the launch traced here: 656 us
  waiting for transfers between devices  292 us (44%)
  local copies, waits for them, and re-layouts  131 us (20%)
  starting transfers between devices  84.6 us (13%)
  matrix products  52.6 us (8%)
  Pallas kernels  37.8 us (6%)
  other arithmetic  37.3 us (6%)
  blocking collectives  18.1 us (3%)
    ppermute x58, waiting for transfers between devices, swap(): return lax.ppermute(v, axis, [(i, i ^ mask) for i in range(n)])  154 us
    ppermute x9, waiting for transfers between devices, line_sum(): outward = lax.ppermute(total, 'rep', [(1, 0), (2, 3)])  100 us
    dynamic_update_slice x16, local copies, waits for them, and re-layouts, assemble(): whole = lax.dynamic_update_slice(whole, piece, ((me ^ m) * shard, 0))  65.6 us
    ppermute x58, starting transfers between devices, swap(): return lax.ppermute(v, axis, [(i, i ^ mask) for i in range(n)])  49.4 us
    pallas_call x1, Pallas kernels, moe(): pl.pallas_call(lambda *r: moe_kernel(n, cap, *r), out_shape=(sd((n // 2,...  37.8 us
    ppermute x9, waiting for transfers between devices, line_sum(): inward = lax.ppermute(v, 'rep', [(0, 1), (3, 2)])  37.7 us
    all_gather x1, blocking collectives, per_device_tokens(): meta_all = lax.all_gather(meta, 'fsdp', axis=0, tiled=True)  18.1 us
    ppermute x9, starting transfers between devices, line_sum(): inward = lax.ppermute(v, 'rep', [(0, 1), (3, 2)])  16.8 us
  transfers between devices with their start and end apart: 85, of which 34 were waited for; matrix products, arithmetic and copies ran while one was open for 31% of the time, Pallas kernels for 0%

profile of v1, /device:TPU:0, one launch (start us, length us, event | category | flops | bytes accessed | tf_op | source)
XLA Modules:
  0.0 656.3 jit_solution(5151654871269180740)
XLA Ops:
  8.3 3.0 collective-permute-start.1
  21.2 18.1 %all-gather = s32[8,1,9]{2,1,0:T(1,128)S(1)} all-gather(s32[1,1,9]{2,1,0:T(1,128)S(1)} %reshape.502), channel_id=1, replica_groups=mesh['fsdp'=8,'rep'=4] {'fsdp'}, dimensions={0}, use_global_device_ids=true | all-gather | bytes 324 | tf_op jit(solution)/shard_map/all_gather | solution.py:581
  40.4 2.2 broadcast_in_dim.42
  42.6 6.9 %dynamic_update_slice.96 = bf16[768,2432]{0,1:T(8,128)(2,1)} dynamic-update-slice(bf16[768,2432]{0,1:T(8,128)(2,1)} %broadcast_in_dim.42, bf16[96,2432]{0,1:T(8,128)(2,1)S(1)} %copy.169, s32[]{:T(128)S(6)} %select_n.208, s32[]{:T(128)} %constant.86.clone.1) | dynamic-update-slice | bytes 933892 | tf_op jit(solution)/shard_map/dynamic_update_slice | solution.py:560
  59.2 3.9 collective-permute-done.12
  70.3 7.8 %dynamic_update_slice.97 = bf16[768,2432]{0,1:T(8,128)(2,1)} dynamic-update-slice(bf16[768,2432]{0,1:T(8,128)(2,1)} %dynamic_update_slice.96, bf16[96,2432]{0,1:T(8,128)(2,1)S(1)} %copy.170, s32[]{:T(128)S(6)} %select_n.209, s32[]{:T(128)} %constant.86.clone.1) | dynamic-update-slice | bytes 933892 | tf_op jit(solution)/shard_map/dynamic_update_slice | solution.py:560
  78.4 7.8 %dynamic_update_slice.98 = bf16[768,2432]{0,1:T(8,128)(2,1)} dynamic-update-slice(bf16[768,2432]{0,1:T(8,128)(2,1)} %dynamic_update_slice.97, bf16[96,2432]{0,1:T(8,128)(2,1)S(1)} %copy.171, s32[]{:T(128)S(6)} %select_n.210, s32[]{:T(128)} %constant.86.clone.1) | dynamic-update-slice | bytes 933892 | tf_op jit(solution)/shard_map/dynamic_update_slice | solution.py:560
  91.0 7.8 %dynamic_update_slice.99 = bf16[768,2432]{0,1:T(8,128)(2,1)} dynamic-update-slice(bf16[768,2432]{0,1:T(8,128)(2,1)} %dynamic_update_slice.98, bf16[96,2432]{0,1:T(8,128)(2,1)S(1)} %copy.172, s32[]{:T(128)S(6)} %select_n.211, s32[]{:T(128)} %constant.86.clone.1) | dynamic-update-slice | bytes 933892 | tf_op jit(solution)/shard_map/dynamic_update_slice | solution.py:560
  98.8 6.9 %dynamic_update_slice.100 = bf16[768,2432]{0,1:T(8,128)(2,1)} dynamic-update-slice(bf16[768,2432]{0,1:T(8,128)(2,1)} %dynamic_update_slice.99, bf16[96,2432]{0,1:T(8,128)(2,1)S(1)} %copy.173, s32[]{:T(128)S(6)} %select_n.212, s32[]{:T(128)} %constant.86.clone.1) | dynamic-update-slice | bytes 933892 | tf_op jit(solution)/shard_map/dynamic_update_slice | solution.py:560
  107.0 7.8 %dynamic_update_slice.101 = bf16[768,2432]{0,1:T(8,128)(2,1)} dynamic-update-slice(bf16[768,2432]{0,1:T(8,128)(2,1)} %dynamic_update_slice.100, bf16[96,2432]{0,1:T(8,128)(2,1)S(1)} %copy.174, s32[]{:T(128)S(6)} %select_n.213, s32[]{:T(128)} %constant.86.clone.1) | dynamic-update-slice | bytes 933892 | tf_op jit(solution)/shard_map/dynamic_update_slice | solution.py:560
  114.9 7.8 %dynamic_update_slice.102 = bf16[768,2432]{0,1:T(8,128)(2,1)} dynamic-update-slice(bf16[768,2432]{0,1:T(8,128)(2,1)} %dynamic_update_slice.101, bf16[96,2432]{0,1:T(8,128)(2,1)S(1)} %copy.175, s32[]{:T(128)S(6)} %select_n.214, s32[]{:T(128)} %constant.86.clone.1) | dynamic-update-slice | bytes 933892 | tf_op jit(solution)/shard_map/dynamic_update_slice | solution.py:560
  124.0 7.5 %dynamic_update_slice.103 = bf16[768,2432]{0,1:T(8,128)(2,1)} dynamic-update-slice(bf16[768,2432]{0,1:T(8,128)(2,1)} %dynamic_update_slice.102, bf16[96,2432]{0,1:T(8,128)(2,1)S(1)} %copy.176, s32[]{:T(128)S(6)} %select_n.215, s32[]{:T(128)} %constant.86.clone.1) | dynamic-update-slice | bytes 933892 | tf_op jit(solution)/shard_map/dynamic_update_slice | solution.py:560
  133.5 3.8 fusion.8
  142.0 2.3 copy-done
  144.4 2.1 fusion.18
  146.6 2.5 fusion.89
  149.1 2.8 collective-permute-start.24
  153.5 2.1 collective-permute-start.32
  155.8 31.5 %collective-permute-done.32 = bf16[3,96,384]{2,1,0:T(8,128)(2,1)S(1)} collective-permute-done((bf16[3,96,384]{2,1,0:T(8,128)(2,1)S(1)}, bf16[3,96,384]{2,1,0:T(8,128)(2,1)S(1)}, u32[]{:S(2)}, u32[]{:S(2)}) %collective-permute-start.32) | collective-permute-done | bytes 221216 | tf_op jit(solution)/shard_map/ppermute | solution.py:487
  187.3 8.3 %collective-permute-done.33 = bf16[3,96,384]{2,1,0:T(8,128)(2,1)S(1)} collective-permute-done((bf16[3,96,384]{2,1,0:T(8,128)(2,1)S(1)}, bf16[3,96,384]{2,1,0:T(8,128)(2,1)S(1)}, u32[]{:S(2)}, u32[]{:S(2)}) %collective-permute-start.33) | collective-permute-done | bytes 221216 | tf_op jit(solution)/shard_map/ppermute | solution.py:487
  197.5 6.2 collective-permute-done.34
  213.4 8.7 %collective-permute-done.15.r_3_ = bf16[448,768]{1,0:T(8,128)(2,1)S(1)} collective-permute-done((bf16[448,768]{1,0:T(8,128)(2,1)S(1)}, bf16[448,768]{1,0:T(8,128)(2,1)S(1)}, u32[]{:S(2)}, u32[]{:S(2)}) %collective-permute-start.15) | collective-permute-done | bytes 688160 | tf_op jit(solution)/shard_map/ppermute | solution.py:487
  222.1 12.8 %collective-permute-done.17.r_5_ = bf16[448,768]{1,0:T(8,128)(2,1)S(1)} collective-permute-done((bf16[448,768]{1,0:T(8,128)(2,1)S(1)}, bf16[448,768]{1,0:T(8,128)(2,1)S(1)}, u32[]{:S(2)}, u32[]{:S(2)}) %collective-permute-start.17) | collective-permute-done | bytes 688160 | tf_op jit(solution)/shard_map/ppermute | solution.py:487
  244.4 37.8 %moe.1 = (bf16[4,448,768]{2,1,0:T(8,128)(2,1)}, bf16[4,448,768]{2,1,0:T(8,128)(2,1)}, bf16[4,448,768]{2,1,0:T(8,128)(2,1)}, bf16[4,448,768]{2,1,0:T(8,128)(2,1)}...) custom-call(s32[8,9]{1,0:T(8,128)} %broadcast_select_fusion.r_0_, ...), custom_call_target="tpu_custom_call" | custom-call | tf_op jit(solution)/shard_map/moe/pallas_call | solution.py:469
  283.0 3.7 collective-permute-start.73
  296.3 5.7 collective-permute-done.58
  303.3 2.5 collective-permute-done.59
  308.5 2.0 collective-permute-start.62
  310.6 7.0 %collective-permute-done.61 = bf16[3,96,384]{2,1,0:T(8,128)(2,1)S(1)} collective-permute-done((bf16[3,96,384]{2,1,0:T(8,128)(2,1)S(1)}, bf16[3,96,384]{2,1,0:T(8,128)(2,1)S(1)}, u32[]{:S(2)}, u32[]{:S(2)}) %collective-permute-start.61) | collective-permute-done | bytes 221216 | tf_op jit(solution)/shard_map/ppermute | solution.py:487
  317.5 2.2 collective-permute-start.63
  321.2 4.2 collective-permute-done.63
  325.7 3.3 collective-permute-start.64
  334.0 8.3 %collective-permute-done.64 = bf16[96,3072]{1,0:T(8,128)(2,1)S(1)} collective-permute-done((bf16[96,3072]{1,0:T(8,128)(2,1)S(1)}, bf16[96,3072]{1,0:T(8,128)(2,1)S(1)}, u32[]{:S(2)}, u32[]{:S(2)}) %collective-permute-start.64) | collective-permute-done | bytes 589856 | tf_op jit(solution)/shard_map/ppermute | solution.py:509
  343.0 11.9 %collective-permute-done.67 = bf16[96,3072]{1,0:T(8,128)(2,1)S(1)} collective-permute-done((bf16[96,3072]{1,0:T(8,128)(2,1)S(1)}, bf16[96,3072]{1,0:T(8,128)(2,1)S(1)}, u32[]{:S(2)}, u32[]{:S(2)}) %collective-permute-start.67) | collective-permute-done | bytes 589856 | tf_op jit(solution)/shard_map/ppermute | solution.py:509
  355.6 11.9 %collective-permute-done.70 = bf16[96,3072]{1,0:T(8,128)(2,1)S(1)} collective-permute-done((bf16[96,3072]{1,0:T(8,128)(2,1)S(1)}, bf16[96,3072]{1,0:T(8,128)(2,1)S(1)}, u32[]{:S(2)}, u32[]{:S(2)}) %collective-permute-start.70) | collective-permute-done | bytes 589856 | tf_op jit(solution)/shard_map/ppermute | solution.py:509
  376.8 38.6 %collective-permute-done.78 = bf16[384,768]{1,0:T(8,128)(2,1)S(1)} collective-permute-done((bf16[384,768]{1,0:T(8,128)(2,1)S(1)}, bf16[384,768]{1,0:T(8,128)(2,1)S(1)}, u32[]{:S(2)}, u32[]{:S(2)}) %collective-permute-start.78) | collective-permute-done | bytes 589856 | tf_op jit(solution)/shard_map/ppermute | solution.py:513
  416.8 11.3 %collective-permute-done.81 = bf16[384,768]{1,0:T(8,128)(2,1)S(1)} collective-permute-done((bf16[384,768]{1,0:T(8,128)(2,1)S(1)}, bf16[384,768]{1,0:T(8,128)(2,1)S(1)}, u32[]{:S(2)}, u32[]{:S(2)}) %collective-permute-start.81) | collective-permute-done | bytes 589856 | tf_op jit(solution)/shard_map/ppermute | solution.py:513
  429.4 12.0 %collective-permute-done.84 = bf16[384,768]{1,0:T(8,128)(2,1)S(1)} collective-permute-done((bf16[384,768]{1,0:T(8,128)(2,1)S(1)}, bf16[384,768]{1,0:T(8,128)(2,1)S(1)}, u32[]{:S(2)}, u32[]{:S(2)}) %collective-permute-start.84) | collective-permute-done | bytes 589856 | tf_op jit(solution)/shard_map/ppermute | solution.py:513
  443.2 2.1 maximum_convert_fusion.1
  445.2 8.8 %collective-permute-done.66 = bf16[96,3072]{1,0:T(8,128)(2,1)S(1)} collective-permute-done((bf16[96,3072]{1,0:T(8,128)(2,1)S(1)}, bf16[96,3072]{1,0:T(8,128)(2,1)S(1)}, u32[]{:S(2)}, u32[]{:S(2)}) %collective-permute-start.66) | collective-permute-done | bytes 589856 | tf_op jit(solution)/shard_map/ppermute | solution.py:513
  457.5 9.2 %collective-permute-done.69 = bf16[96,3072]{1,0:T(8,128)(2,1)S(1)} collective-permute-done((bf16[96,3072]{1,0:T(8,128)(2,1)S(1)}, bf16[96,3072]{1,0:T(8,128)(2,1)S(1)}, u32[]{:S(2)}, u32[]{:S(2)}) %collective-permute-start.69) | collective-permute-done | bytes 589856 | tf_op jit(solution)/shard_map/ppermute | solution.py:513
  467.9 6.0 collective-permute-done.40
  474.5 12.0 %collective-permute-done.42 = bf16[448,768]{1,0:T(8,128)(2,1)S(1)} collective-permute-done((bf16[448,768]{1,0:T(8,128)(2,1)S(1)}, bf16[448,768]{1,0:T(8,128)(2,1)S(1)}, u32[]{:S(2)}, u32[]{:S(2)}) %collective-permute-start.42) | collective-permute-done | bytes 688160 | tf_op jit(solution)/shard_map/ppermute | solution.py:487
  488.3 2.8 convolution_convert_fusion.4
  491.1 2.2 copy.182
  493.3 10.3 %multiply_reduce_fusion = (f32[12,416]{1,0:T(8,128)S(1)}, f32[12,416,416]{1,2,0:T(8,128)}) fusion(f32[12,416,416]{1,2,0:T(8,128)} %copy-done, f32[12,416]{1,0:T(8,128)S(1)} %log_add_fusion, bf16[416,12,64]{0,2,1:T(8,128)(2,1)} %bitcast.215, bf16[416,12,64]{0,2,1:T(8,128)(2,1)} %bitcast.220), kind=kOutput, calls=%fused_computation.2 | convolution fusion | flops 272039040 | bytes 17931264 | tf_op jit(solution)/shard_map/rqhd,rkhd->rhqk/dot_general | solution.py:691
  503.6 12.1 %multiply_convert_fusion = bf16[12,416,416]{1,2,0:T(8,128)(2,1)} fusion(f32[12,416,416]{1,2,0:T(8,128)} %get-tuple-element.206, f32[12,416,416]{1,2,0:T(8,128)} %copy-done, f32[12,416]{1,0:T(8,128)S(1)} %get-tuple-element.205, f32[12,416]{1,0:T(8,128)S(1)} %log_add_fusion), kind=kLoop, calls=%fused_computation.1 | loop fusion | flops 8306688 | bytes 20806656 | tf_op jit(solution)/shard_map/convert_element_type | solution.py:692
  515.7 4.0 bitcast_reduce_fusion.1
  521.5 6.1 bitcast_reduce_fusion
  527.6 3.0 fusion.35
  537.0 5.8 convolution_convert_fusion
  543.5 7.3 %concatenate.14 = bf16[768,2432]{1,0:T(8,128)(2,1)} concatenate(bf16[768,2304]{1,0:T(8,128)(2,1)} %convolution_convert_fusion, bf16[768,1]{1,0:T(8,128)(2,1)} %stack.156, bf16[768,1]{1,0:T(8,128)(2,1)} %stack.157, bf16[768,1]{1,0:T(8,128)(2,1)} %stack.158, bf16[768,1]{1,0:T(8,128)(2,1)} %stack.159, bf16[768,1]{1,0:T(8,128)(2,1)} %stack.160, bf16[768,1]{1,0:T(8,128)(2,1)} %stack.161, ...), dimensions={1} | concatenate | bytes 7471104 | tf_op jit(solution)/shard_map/concatenate | solution.py:721
  554.1 2.1 maximum_convert_fusion
  557.1 2.1 fusion.46
  567.0 10.6 %collective-permute-done.36 = bf16[448,768]{1,0:T(8,128)(2,1)S(1)} collective-permute-done((bf16[448,768]{1,0:T(8,128)(2,1)S(1)}, bf16[448,768]{1,0:T(8,128)(2,1)S(1)}, u32[]{:S(2)}, u32[]{:S(2)}) %collective-permute-start.36) | collective-permute-done | bytes 688160 | tf_op jit(solution)/shard_map/ppermute | solution.py:487
  579.0 14.6 %collective-permute-done.37 = bf16[448,768]{1,0:T(8,128)(2,1)S(1)} collective-permute-done((bf16[448,768]{1,0:T(8,128)(2,1)S(1)}, bf16[448,768]{1,0:T(8,128)(2,1)S(1)}, u32[]{:S(2)}, u32[]{:S(2)}) %collective-permute-start.37) | collective-permute-done | bytes 688160 | tf_op jit(solution)/shard_map/ppermute | solution.py:487
  593.5 2.8 fusion.28
  596.5 2.2 collective-permute-start.51
  600.0 2.3 collective-permute-done.44
  604.1 9.4 %collective-permute-done.45 = bf16[96,2432]{1,0:T(8,128)(2,1)S(1)} collective-permute-done((bf16[96,2432]{1,0:T(8,128)(2,1)S(1)}, bf16[96,2432]{1,0:T(8,128)(2,1)S(1)}, u32[]{:S(2)}, u32[]{:S(2)}) %collective-permute-start.45) | collective-permute-done | bytes 466976 | tf_op jit(solution)/shard_map/ppermute | solution.py:487
  615.6 3.9 collective-permute-done.52
  621.0 4.9 collective-permute-done.47
  632.6 16.0 %collective-permute-done.56 = bf16[96,768]{1,0:T(8,128)(2,1)S(1)} collective-permute-done((bf16[96,768]{1,0:T(8,128)(2,1)S(1)}, bf16[96,768]{1,0:T(8,128)(2,1)S(1)}, u32[]{:S(2)}, u32[]{:S(2)}) %collective-permute-start.56) | collective-permute-done | bytes 147488 | tf_op jit(solution)/shard_map/ppermute | solution.py:513
  649.3 4.3 collective-permute-done.49
  (417 shorter events, 154.1 us)
Async XLA Ops:
  8.3 55.3 %collective-permute-start.1 = (bf16[96,2432]{1,0:T(8,128)(2,1)S(1)}, bf16[96,2432]{1,0:T(8,128)(2,1)S(1)}, u32[]{:S(2)}, u32[]{:S(2)}) collective-permute-start(bf16[96,2432]{1,0:T(8,128)(2,1)S(1)} %concatenate.12), channel_id=1, source_target_pairs={{0,8},{4,12},{8,0},{12,4},{16,24},{20,28},{24,16},{28,20},{1,9},{5... | collective-permute-start | bytes 1400840 | tf_op jit(solution)/shard_map/ppermute | solution.py:487
  11.3 52.4 %collective-permute-start.3 = (bf16[96,2432]{1,0:T(8,128)(2,1)S(1)}, bf16[96,2432]{1,0:T(8,128)(2,1)}, u32[]{:S(2)}, u32[]{:S(2)}) collective-permute-start(bf16[96,2432]{1,0:T(8,128)(2,1)S(1)} %concatenate.12), channel_id=1, source_target_pairs={{0,16},{4,20},{8,24},{12,28},{16,0},{20,4},{24,8},{28,12},{1,17},{... | collective-permute-start | bytes 1400840 | tf_op jit(solution)/shard_map/ppermute | solution.py:487
  12.8 51.3 %collective-permute-start.5 = (bf16[96,2432]{1,0:T(8,128)(2,1)S(1)}, bf16[96,2432]{1,0:T(8,128)(2,1)S(1)}, u32[]{:S(2)}, u32[]{:S(2)}) collective-permute-start(bf16[96,2432]{1,0:T(8,128)(2,1)S(1)} %concatenate.12), channel_id=1, source_target_pairs={{0,24},{4,28},{8,16},{12,20},{16,8},{20,12},{24,0},{28,4},{1,25},{... | collective-permute-start | bytes 1400840 | tf_op jit(solution)/shard_map/ppermute | solution.py:487
  12.8 38.5 %collective-permute-start.7 = (bf16[96,768]{1,0:T(8,128)(2,1)}, bf16[96,768]{1,0:T(8,128)(2,1)S(1)}, u32[]{:S(2)}, u32[]{:S(2)}) collective-permute-start(bf16[96,768]{1,0:T(8,128)(2,1)} %param.29), channel_id=1, source_target_pairs={{0,4},{4,0},{8,12},{12,8},{16,20},{20,16},{24,28},{28,24},{1,5},{5... | collective-permute-start | bytes 442376 | tf_op jit(solution)/shard_map/ppermute | solution.py:487
  12.8 42.6 %collective-permute-start.8 = (bf16[96,768]{1,0:T(8,128)(2,1)}, bf16[96,768]{1,0:T(8,128)(2,1)S(1)}, u32[]{:S(2)}, u32[]{:S(2)}) collective-permute-start(bf16[96,768]{1,0:T(8,128)(2,1)} %param.29), channel_id=1, source_target_pairs={{0,8},{4,12},{8,0},{12,4},{16,24},{20,28},{24,16},{28,20},{1,9},{5... | collective-permute-start | bytes 442376 | tf_op jit(solution)/shard_map/ppermute | solution.py:487
  63.6 24.3 %collective-permute-start.2 = (bf16[96,2432]{1,0:T(8,128)(2,1)S(1)}, bf16[96,2432]{1,0:T(8,128)(2,1)}, u32[]{:S(2)}, u32[]{:S(2)}) collective-permute-start(bf16[96,2432]{1,0:T(8,128)(2,1)S(1)} %collective-permute-done.1), channel_id=1, source_target_pairs={{0,4},{4,0},{8,12},{12,8},{16,20},{20,16},{24,28},{28,24},{1,5},{5... | collective-permute-start | bytes 1400840 | tf_op jit(solution)/shard_map/ppermute | solution.py:487
  63.7 42.0 %collective-permute-start.4 = (bf16[96,2432]{1,0:T(8,128)(2,1)}, bf16[96,2432]{1,0:T(8,128)(2,1)}, u32[]{:S(2)}, u32[]{:S(2)}) collective-permute-start(bf16[96,2432]{1,0:T(8,128)(2,1)} %collective-permute-done.3), channel_id=1, source_target_pairs={{0,4},{4,0},{8,12},{12,8},{16,20},{20,16},{24,28},{28,24},{1,5},{5... | collective-permute-start | bytes 1400840 | tf_op jit(solution)/shard_map/ppermute | solution.py:487
  64.1 58.5 %collective-permute-start.6 = (bf16[96,2432]{1,0:T(8,128)(2,1)S(1)}, bf16[96,2432]{1,0:T(8,128)(2,1)}, u32[]{:S(2)}, u32[]{:S(2)}) collective-permute-start(bf16[96,2432]{1,0:T(8,128)(2,1)S(1)} %collective-permute-done.5), channel_id=1, source_target_pairs={{0,4},{4,0},{8,12},{12,8},{16,20},{20,16},{24,28},{28,24},{1,5},{5... | collective-permute-start | bytes 1400840 | tf_op jit(solution)/shard_map/ppermute | solution.py:487
  67.3 81.7 %collective-permute-start.28 = (bf16[3,96,384]{2,1,0:T(8,128)(2,1)}, bf16[3,96,384]{2,1,0:T(8,128)(2,1)}, u32[]{:S(2)}, u32[]{:S(2)}) collective-permute-start(bf16[3,96,384]{2,1,0:T(8,128)(2,1)} %get-tuple-element.187), channel_id=1, source_target_pairs={{0,4},{4,0},{8,12},{12,8},{16,20},{20,16},{24,28},{28,24},{1,5},{5... | collective-permute-start | bytes 663560 | tf_op jit(solution)/shard_map/ppermute | solution.py:487
  68.9 83.0 %collective-permute-start.29 = (bf16[3,96,384]{2,1,0:T(8,128)(2,1)}, bf16[3,96,384]{2,1,0:T(8,128)(2,1)}, u32[]{:S(2)}, u32[]{:S(2)}) collective-permute-start(bf16[3,96,384]{2,1,0:T(8,128)(2,1)} %get-tuple-element.186), channel_id=1, source_target_pairs={{0,8},{4,12},{8,0},{12,4},{16,24},{20,28},{24,16},{28,20},{1,9},{5... | collective-permute-start | bytes 663560 | tf_op jit(solution)/shard_map/ppermute | solution.py:487
  87.9 65.5 %collective-permute-start.30 = (bf16[3,96,384]{2,1,0:T(8,128)(2,1)}, bf16[3,96,384]{2,1,0:T(8,128)(2,1)}, u32[]{:S(2)}, u32[]{:S(2)}) collective-permute-start(bf16[3,96,384]{2,1,0:T(8,128)(2,1)} %get-tuple-element.185), channel_id=1, source_target_pairs={{0,12},{4,8},{8,4},{12,0},{16,28},{20,24},{24,20},{28,16},{1,13},{... | collective-permute-start | bytes 663560 | tf_op jit(solution)/shard_map/ppermute | solution.py:487
  105.7 47.8 %collective-permute-start.31 = (bf16[3,96,384]{2,1,0:T(8,128)(2,1)}, bf16[3,96,384]{2,1,0:T(8,128)(2,1)}, u32[]{:S(2)}, u32[]{:S(2)}) collective-permute-start(bf16[3,96,384]{2,1,0:T(8,128)(2,1)} %get-tuple-element.184), channel_id=1, source_target_pairs={{0,16},{4,20},{8,24},{12,28},{16,0},{20,4},{24,8},{28,12},{1,17},{... | collective-permute-start | bytes 663560 | tf_op jit(solution)/shard_map/ppermute | solution.py:487
  122.6 74.3 %collective-permute-start.22 = (bf16[448,768]{1,0:T(8,128)(2,1)}, bf16[448,768]{1,0:T(8,128)(2,1)}, u32[]{:S(2)}, u32[]{:S(2)}) collective-permute-start(bf16[448,768]{1,0:T(8,128)(2,1)} %convolution_convert_fusion.2.r_9_), channel_id=1, source_target_pairs={{0,8},{4,12},{8,0},{12,4},{16,24},{20,28},{24,16},{28,20},{1,9},{5... | collective-permute-start | bytes 2064392 | tf_op jit(solution)/shard_map/ppermute | solution.py:487
  149.1 48.4 %collective-permute-start.24 = (bf16[448,768]{1,0:T(8,128)(2,1)}, bf16[448,768]{1,0:T(8,128)(2,1)S(1)}, u32[]{:S(2)}, u32[]{:S(2)}) collective-permute-start(bf16[448,768]{1,0:T(8,128)(2,1)} %convolution_convert_fusion.2.r_9_), channel_id=1, source_target_pairs={{0,16},{4,20},{8,24},{12,28},{16,0},{20,4},{24,8},{28,12},{1,17},{... | collective-permute-start | bytes 2064392 | tf_op jit(solution)/shard_map/ppermute | solution.py:487
  151.9 51.9 %collective-permute-start.26 = (bf16[448,768]{1,0:T(8,128)(2,1)}, bf16[448,768]{1,0:T(8,128)(2,1)S(1)}, u32[]{:S(2)}, u32[]{:S(2)}) collective-permute-start(bf16[448,768]{1,0:T(8,128)(2,1)} %convolution_convert_fusion.2.r_9_), channel_id=1, source_target_pairs={{0,24},{4,28},{8,16},{12,20},{16,8},{20,12},{24,0},{28,4},{1,25},{... | collective-permute-start | bytes 2064392 | tf_op jit(solution)/shard_map/ppermute | solution.py:487
  153.4 51.9 %collective-permute-start.21 = (bf16[448,768]{1,0:T(8,128)(2,1)}, bf16[448,768]{1,0:T(8,128)(2,1)S(1)}, u32[]{:S(2)}, u32[]{:S(2)}) collective-permute-start(bf16[448,768]{1,0:T(8,128)(2,1)} %convolution_convert_fusion.2.r_9_), channel_id=1, source_target_pairs={{0,4},{4,0},{8,12},{12,8},{16,20},{20,16},{24,28},{28,24},{1,5},{5... | collective-permute-start | bytes 2064392 | tf_op jit(solution)/shard_map/ppermute | solution.py:487
  153.5 33.8 %collective-permute-start.32 = (bf16[3,96,384]{2,1,0:T(8,128)(2,1)S(1)}, bf16[3,96,384]{2,1,0:T(8,128)(2,1)S(1)}, u32[]{:S(2)}, u32[]{:S(2)}) collective-permute-start(bf16[3,96,384]{2,1,0:T(8,128)(2,1)S(1)} %copy-done.43), channel_id=1, source_target_pairs={{0,20},{4,16},{8,28},{12,24},{16,4},{20,0},{24,12},{28,8},{1,21},{... | collective-permute-start | bytes 663560 | tf_op jit(solution)/shard_map/ppermute | solution.py:487
  187.3 8.3 %collective-permute-start.33 = (bf16[3,96,384]{2,1,0:T(8,128)(2,1)S(1)}, bf16[3,96,384]{2,1,0:T(8,128)(2,1)S(1)}, u32[]{:S(2)}, u32[]{:S(2)}) collective-permute-start(bf16[3,96,384]{2,1,0:T(8,128)(2,1)S(1)} %copy-done.42), channel_id=1, source_target_pairs={{0,24},{4,28},{8,16},{12,20},{16,8},{20,12},{24,0},{28,4},{1,25},{... | collective-permute-start | bytes 663560 | tf_op jit(solution)/shard_map/ppermute | solution.py:487
  196.9 15.9 %collective-permute-start.23 = (bf16[448,768]{1,0:T(8,128)(2,1)}, bf16[448,768]{1,0:T(8,128)(2,1)S(1)}, u32[]{:S(2)}, u32[]{:S(2)}) collective-permute-start(bf16[448,768]{1,0:T(8,128)(2,1)} %collective-permute-done.22.r_11_), channel_id=1, source_target_pairs={{0,4},{4,0},{8,12},{12,8},{16,20},{20,16},{24,28},{28,24},{1,5},{5... | collective-permute-start | bytes 2064392 | tf_op jit(solution)/shard_map/ppermute | solution.py:487
  197.4 15.4 %collective-permute-start.25 = (bf16[448,768]{1,0:T(8,128)(2,1)S(1)}, bf16[448,768]{1,0:T(8,128)(2,1)S(1)}, u32[]{:S(2)}, u32[]{:S(2)}) collective-permute-start(bf16[448,768]{1,0:T(8,128)(2,1)S(1)} %collective-permute-done.24.r_13_), channel_id=1, source_target_pairs={{0,4},{4,0},{8,12},{12,8},{16,20},{20,16},{24,28},{28,24},{1,5},{5... | collective-permute-start | bytes 2064392 | tf_op jit(solution)/shard_map/ppermute | solution.py:487
  203.7 18.4 %collective-permute-start.15 = (bf16[448,768]{1,0:T(8,128)(2,1)S(1)}, bf16[448,768]{1,0:T(8,128)(2,1)S(1)}, u32[]{:S(2)}, u32[]{:S(2)}) collective-permute-start(bf16[448,768]{1,0:T(8,128)(2,1)S(1)} %convolution_convert_fusion.3.r_1_), channel_id=1, source_target_pairs={{0,8},{4,12},{8,0},{12,4},{16,24},{20,28},{24,16},{28,20},{1,9},{5... | collective-permute-start | bytes 2064392 | tf_op jit(solution)/shard_map/ppermute | solution.py:487
  203.8 31.0 %collective-permute-start.17 = (bf16[448,768]{1,0:T(8,128)(2,1)S(1)}, bf16[448,768]{1,0:T(8,128)(2,1)S(1)}, u32[]{:S(2)}, u32[]{:S(2)}) collective-permute-start(bf16[448,768]{1,0:T(8,128)(2,1)S(1)} %convolution_convert_fusion.3.r_1_), channel_id=1, source_target_pairs={{0,16},{4,20},{8,24},{12,28},{16,0},{20,4},{24,8},{28,12},{1,17},{... | collective-permute-start | bytes 2064392 | tf_op jit(solution)/shard_map/ppermute | solution.py:487
  205.4 30.9 %collective-permute-start.19 = (bf16[448,768]{1,0:T(8,128)(2,1)S(1)}, bf16[448,768]{1,0:T(8,128)(2,1)S(1)}, u32[]{:S(2)}, u32[]{:S(2)}) collective-permute-start(bf16[448,768]{1,0:T(8,128)(2,1)S(1)} %convolution_convert_fusion.3.r_1_), channel_id=1, source_target_pairs={{0,24},{4,28},{8,16},{12,20},{16,8},{20,12},{24,0},{28,4},{1,25},{... | collective-permute-start | bytes 2064392 | tf_op jit(solution)/shard_map/ppermute | solution.py:487
  212.8 29.3 %collective-permute-start.27 = (bf16[448,768]{1,0:T(8,128)(2,1)S(1)}, bf16[448,768]{1,0:T(8,128)(2,1)S(1)}, u32[]{:S(2)}, u32[]{:S(2)}) collective-permute-start(bf16[448,768]{1,0:T(8,128)(2,1)S(1)} %collective-permute-done.26.r_15_), channel_id=1, source_target_pairs={{0,4},{4,0},{8,12},{12,8},{16,20},{20,16},{24,28},{28,24},{1,5},{5... | collective-permute-start | bytes 2064392 | tf_op jit(solution)/shard_map/ppermute | solution.py:487
  212.9 29.2 %collective-permute-start.14 = (bf16[448,768]{1,0:T(8,128)(2,1)S(1)}, bf16[448,768]{1,0:T(8,128)(2,1)S(1)}, u32[]{:S(2)}, u32[]{:S(2)}) collective-permute-start(bf16[448,768]{1,0:T(8,128)(2,1)S(1)} %convolution_convert_fusion.3.r_1_), channel_id=1, source_target_pairs={{0,4},{4,0},{8,12},{12,8},{16,20},{20,16},{24,28},{28,24},{1,5},{5... | collective-permute-start | bytes 2064392 | tf_op jit(solution)/shard_map/ppermute | solution.py:487
  222.1 20.1 %collective-permute-start.16 = (bf16[448,768]{1,0:T(8,128)(2,1)S(1)}, bf16[448,768]{1,0:T(8,128)(2,1)S(1)}, u32[]{:S(2)}, u32[]{:S(2)}) collective-permute-start(bf16[448,768]{1,0:T(8,128)(2,1)S(1)} %collective-permute-done.15.r_3_), channel_id=1, source_target_pairs={{0,4},{4,0},{8,12},{12,8},{16,20},{20,16},{24,28},{28,24},{1,5},{5... | collective-permute-start | bytes 2064392 | tf_op jit(solution)/shard_map/ppermute | solution.py:487
  283.0 9.4 %collective-permute-start.73 = (bf16[3,384]{1,0:T(4,128)(2,1)S(1)}, bf16[3,384]{1,0:T(4,128)(2,1)S(1)}, u32[]{:S(2)}, u32[]{:S(2)}) collective-permute-start(bf16[3,384]{1,0:T(4,128)(2,1)S(1)} %bitcast.235), channel_id=1, source_target_pairs={{0,1},{3,2},{4,5},{7,6},{8,9},{11,10},{12,13},{15,14},{16,17},{19,... | collective-permute-start | bytes 6920 | tf_op jit(solution)/shard_map/ppermute | solution.py:509
  288.2 42.1 %collective-permute-start.76 = (bf16[384,768]{1,0:T(8,128)(2,1)S(1)}, bf16[384,768]{1,0:T(8,128)(2,1)S(1)}, u32[]{:S(2)}, u32[]{:S(2)}) collective-permute-start(bf16[384,768]{1,0:T(8,128)(2,1)S(1)} %get-tuple-element.162), channel_id=1, source_target_pairs={{0,1},{3,2},{4,5},{7,6},{8,9},{11,10},{12,13},{15,14},{16,17},{19,... | collective-permute-start | bytes 1769480 | tf_op jit(solution)/shard_map/ppermute | solution.py:509
  289.7 42.6 %collective-permute-start.79 = (bf16[384,768]{1,0:T(8,128)(2,1)S(1)}, bf16[384,768]{1,0:T(8,128)(2,1)S(1)}, u32[]{:S(2)}, u32[]{:S(2)}) collective-permute-start(bf16[384,768]{1,0:T(8,128)(2,1)S(1)} %get-tuple-element.164), channel_id=1, source_target_pairs={{0,1},{3,2},{4,5},{7,6},{8,9},{11,10},{12,13},{15,14},{16,17},{19,... | collective-permute-start | bytes 1769480 | tf_op jit(solution)/shard_map/ppermute | solution.py:509
  291.0 42.4 %collective-permute-start.82 = (bf16[384,768]{1,0:T(8,128)(2,1)S(1)}, bf16[384,768]{1,0:T(8,128)(2,1)S(1)}, u32[]{:S(2)}, u32[]{:S(2)}) collective-permute-start(bf16[384,768]{1,0:T(8,128)(2,1)S(1)} %get-tuple-element.163), channel_id=1, source_target_pairs={{0,1},{3,2},{4,5},{7,6},{8,9},{11,10},{12,13},{15,14},{16,17},{19,... | collective-permute-start | bytes 1769480 | tf_op jit(solution)/shard_map/ppermute | solution.py:509
  295.1 10.7 %collective-permute-start.59 = (bf16[3,96,384]{2,1,0:T(8,128)(2,1)S(1)}, bf16[3,96,384]{2,1,0:T(8,128)(2,1)S(1)}, u32[]{:S(2)}, u32[]{:S(2)}) collective-permute-start(bf16[3,96,384]{2,1,0:T(8,128)(2,1)S(1)} %get-tuple-element.175), channel_id=1, source_target_pairs={{0,12},{4,8},{8,4},{12,0},{16,28},{20,24},{24,20},{28,16},{1,13},{... | collective-permute-start | bytes 663560 | tf_op jit(solution)/shard_map/ppermute | solution.py:487
  305.8 11.7 %collective-permute-start.61 = (bf16[3,96,384]{2,1,0:T(8,128)(2,1)S(1)}, bf16[3,96,384]{2,1,0:T(8,128)(2,1)S(1)}, u32[]{:S(2)}, u32[]{:S(2)}) collective-permute-start(bf16[3,96,384]{2,1,0:T(8,128)(2,1)S(1)} %get-tuple-element.173), channel_id=1, source_target_pairs={{0,20},{4,16},{8,28},{12,24},{16,4},{20,0},{24,12},{28,8},{1,21},{... | collective-permute-start | bytes 663560 | tf_op jit(solution)/shard_map/ppermute | solution.py:487
  308.5 11.3 %collective-permute-start.62 = (bf16[3,96,384]{2,1,0:T(8,128)(2,1)S(1)}, bf16[3,96,384]{2,1,0:T(8,128)(2,1)S(1)}, u32[]{:S(2)}, u32[]{:S(2)}) collective-permute-start(bf16[3,96,384]{2,1,0:T(8,128)(2,1)S(1)} %get-tuple-element.172), channel_id=1, source_target_pairs={{0,24},{4,28},{8,16},{12,20},{16,8},{20,12},{24,0},{28,4},{1,25},{... | collective-permute-start | bytes 663560 | tf_op jit(solution)/shard_map/ppermute | solution.py:487
  319.8 9.3 %collective-permute-start.75 = (bf16[3,384]{1,0:T(4,128)(2,1)S(1)}, bf16[3,384]{1,0:T(4,128)(2,1)S(1)}, u32[]{:S(2)}, u32[]{:S(2)}) collective-permute-start(bf16[3,384]{1,0:T(4,128)(2,1)S(1)} %add_convert_fusion.28), channel_id=1, source_target_pairs={{1,0},{2,3},{5,4},{6,7},{9,8},{10,11},{13,12},{14,15},{17,16},{18,... | collective-permute-start | bytes 6920 | tf_op jit(solution)/shard_map/ppermute | solution.py:513
  325.7 16.6 %collective-permute-start.64 = (bf16[96,3072]{1,0:T(8,128)(2,1)S(1)}, bf16[96,3072]{1,0:T(8,128)(2,1)S(1)}, u32[]{:S(2)}, u32[]{:S(2)}) collective-permute-start(bf16[96,3072]{1,0:T(8,128)(2,1)S(1)} %get-tuple-element.168), channel_id=1, source_target_pairs={{0,1},{3,2},{4,5},{7,6},{8,9},{11,10},{12,13},{15,14},{16,17},{19,... | collective-permute-start | bytes 1769480 | tf_op jit(solution)/shard_map/ppermute | solution.py:509
  329.0 25.9 %collective-permute-start.67 = (bf16[96,3072]{1,0:T(8,128)(2,1)S(1)}, bf16[96,3072]{1,0:T(8,128)(2,1)S(1)}, u32[]{:S(2)}, u32[]{:S(2)}) collective-permute-start(bf16[96,3072]{1,0:T(8,128)(2,1)S(1)} %get-tuple-element.170), channel_id=1, source_target_pairs={{0,1},{3,2},{4,5},{7,6},{8,9},{11,10},{12,13},{15,14},{16,17},{19,... | collective-permute-start | bytes 1769480 | tf_op jit(solution)/shard_map/ppermute | solution.py:509
  330.4 37.2 %collective-permute-start.70 = (bf16[96,3072]{1,0:T(8,128)(2,1)S(1)}, bf16[96,3072]{1,0:T(8,128)(2,1)S(1)}, u32[]{:S(2)}, u32[]{:S(2)}) collective-permute-start(bf16[96,3072]{1,0:T(8,128)(2,1)S(1)} %get-tuple-element.169), channel_id=1, source_target_pairs={{0,1},{3,2},{4,5},{7,6},{8,9},{11,10},{12,13},{15,14},{16,17},{19,... | collective-permute-start | bytes 1769480 | tf_op jit(solution)/shard_map/ppermute | solution.py:509
  332.3 122.6 %collective-permute-start.39 = (bf16[4,448,768]{2,1,0:T(8,128)(2,1)S(1)}, bf16[4,448,768]{2,1,0:T(8,128)(2,1)S(1)}, u32[]{:S(2)}, u32[]{:S(2)}) collective-permute-start(bf16[4,448,768]{2,1,0:T(8,128)(2,1)S(1)} %copy-done.64), channel_id=1, source_target_pairs={{0,4},{4,0},{8,12},{12,8},{16,20},{20,16},{24,28},{28,24},{1,5},{5... | collective-permute-start | bytes 8257544 | tf_op jit(solution)/shard_map/ppermute | solution.py:487
  333.5 222.7 %collective-permute-start.35 = (bf16[4,448,768]{2,1,0:T(8,128)(2,1)}, bf16[4,448,768]{2,1,0:T(8,128)(2,1)}, u32[]{:S(2)}, u32[]{:S(2)}) collective-permute-start(bf16[4,448,768]{2,1,0:T(8,128)(2,1)} %get-tuple-element.25), channel_id=1, source_target_pairs={{0,4},{4,0},{8,12},{12,8},{16,20},{20,16},{24,28},{28,24},{1,5},{5... | collective-permute-start | bytes 8257544 | tf_op jit(solution)/shard_map/ppermute | solution.py:487
  342.3 26.6 %collective-permute-start.77 = (bf16[384,768]{1,0:T(8,128)(2,1)S(1)}, bf16[384,768]{1,0:T(8,128)(2,1)S(1)}, u32[]{:S(2)}, u32[]{:S(2)}) collective-permute-start(bf16[384,768]{1,0:T(8,128)(2,1)S(1)} %get-tuple-element.159), channel_id=1, source_target_pairs={{1,2},{2,1},{5,6},{6,5},{9,10},{10,9},{13,14},{14,13},{17,18},{18,... | collective-permute-start | bytes 1769480 | tf_op jit(solution)/shard_map/ppermute | solution.py:511
  354.9 14.8 %collective-permute-start.80 = (bf16[384,768]{1,0:T(8,128)(2,1)S(1)}, bf16[384,768]{1,0:T(8,128)(2,1)S(1)}, u32[]{:S(2)}, u32[]{:S(2)}) collective-permute-start(bf16[384,768]{1,0:T(8,128)(2,1)S(1)} %get-tuple-element.161), channel_id=1, source_target_pairs={{1,2},{2,1},{5,6},{6,5},{9,10},{10,9},{13,14},{14,13},{17,18},{18,... | collective-permute-start | bytes 1769480 | tf_op jit(solution)/shard_map/ppermute | solution.py:511
  371.5 43.9 %collective-permute-start.78 = (bf16[384,768]{1,0:T(8,128)(2,1)S(1)}, bf16[384,768]{1,0:T(8,128)(2,1)S(1)}, u32[]{:S(2)}, u32[]{:S(2)}) collective-permute-start(bf16[384,768]{1,0:T(8,128)(2,1)S(1)} %add_convert_fusion.13), channel_id=1, source_target_pairs={{1,0},{2,3},{5,4},{6,7},{9,8},{10,11},{13,12},{14,15},{17,16},{18,... | collective-permute-start | bytes 1769480 | tf_op jit(solution)/shard_map/ppermute | solution.py:513
  373.0 55.1 %collective-permute-start.81 = (bf16[384,768]{1,0:T(8,128)(2,1)S(1)}, bf16[384,768]{1,0:T(8,128)(2,1)S(1)}, u32[]{:S(2)}, u32[]{:S(2)}) collective-permute-start(bf16[384,768]{1,0:T(8,128)(2,1)S(1)} %add_convert_fusion.11), channel_id=1, source_target_pairs={{1,0},{2,3},{5,4},{6,7},{9,8},{10,11},{13,12},{14,15},{17,16},{18,... | collective-permute-start | bytes 1769480 | tf_op jit(solution)/shard_map/ppermute | solution.py:513
  374.4 66.9 %collective-permute-start.84 = (bf16[384,768]{1,0:T(8,128)(2,1)S(1)}, bf16[384,768]{1,0:T(8,128)(2,1)S(1)}, u32[]{:S(2)}, u32[]{:S(2)}) collective-permute-start(bf16[384,768]{1,0:T(8,128)(2,1)S(1)} %add_convert_fusion.9), channel_id=1, source_target_pairs={{1,0},{2,3},{5,4},{6,7},{9,8},{10,11},{13,12},{14,15},{17,16},{18,... | collective-permute-start | bytes 1769480 | tf_op jit(solution)/shard_map/ppermute | solution.py:513
  415.4 38.6 %collective-permute-start.66 = (bf16[96,3072]{1,0:T(8,128)(2,1)S(1)}, bf16[96,3072]{1,0:T(8,128)(2,1)S(1)}, u32[]{:S(2)}, u32[]{:S(2)}) collective-permute-start(bf16[96,3072]{1,0:T(8,128)(2,1)S(1)} %add_convert_fusion.19), channel_id=1, source_target_pairs={{1,0},{2,3},{5,4},{6,7},{9,8},{10,11},{13,12},{14,15},{17,16},{18,... | collective-permute-start | bytes 1769480 | tf_op jit(solution)/shard_map/ppermute | solution.py:513
  428.0 38.6 %collective-permute-start.69 = (bf16[96,3072]{1,0:T(8,128)(2,1)S(1)}, bf16[96,3072]{1,0:T(8,128)(2,1)S(1)}, u32[]{:S(2)}, u32[]{:S(2)}) collective-permute-start(bf16[96,3072]{1,0:T(8,128)(2,1)S(1)} %add_convert_fusion.17), channel_id=1, source_target_pairs={{1,0},{2,3},{5,4},{6,7},{9,8},{10,11},{13,12},{14,15},{17,16},{18,... | collective-permute-start | bytes 1769480 | tf_op jit(solution)/shard_map/ppermute | solution.py:513
  441.4 111.4 %collective-permute-start.72 = (bf16[96,3072]{1,0:T(8,128)(2,1)}, bf16[96,3072]{1,0:T(8,128)(2,1)}, u32[]{:S(2)}, u32[]{:S(2)}) collective-permute-start(bf16[96,3072]{1,0:T(8,128)(2,1)} %add_convert_fusion.15), channel_id=1, source_target_pairs={{1,0},{2,3},{5,4},{6,7},{9,8},{10,11},{13,12},{14,15},{17,16},{18,... | collective-permute-start | bytes 1769480 | tf_op jit(solution)/shard_map/ppermute | solution.py:513
  455.5 18.4 %collective-permute-start.40 = (bf16[448,768]{1,0:T(8,128)(2,1)S(1)}, bf16[448,768]{1,0:T(8,128)(2,1)S(1)}, u32[]{:S(2)}, u32[]{:S(2)}) collective-permute-start(bf16[448,768]{1,0:T(8,128)(2,1)S(1)} %get-tuple-element.145), channel_id=1, source_target_pairs={{0,8},{4,12},{8,0},{12,4},{16,24},{20,28},{24,16},{28,20},{1,9},{5... | collective-permute-start | bytes 2064392 | tf_op jit(solution)/shard_map/ppermute | solution.py:487
  457.5 17.0 %collective-permute-start.41 = (bf16[448,768]{1,0:T(8,128)(2,1)S(1)}, bf16[448,768]{1,0:T(8,128)(2,1)S(1)}, u32[]{:S(2)}, u32[]{:S(2)}) collective-permute-start(bf16[448,768]{1,0:T(8,128)(2,1)S(1)} %get-tuple-element.147), channel_id=1, source_target_pairs={{0,16},{4,20},{8,24},{12,28},{16,0},{20,4},{24,8},{28,12},{1,17},{... | collective-permute-start | bytes 2064392 | tf_op jit(solution)/shard_map/ppermute | solution.py:487
  466.7 19.8 %collective-permute-start.42 = (bf16[448,768]{1,0:T(8,128)(2,1)S(1)}, bf16[448,768]{1,0:T(8,128)(2,1)S(1)}, u32[]{:S(2)}, u32[]{:S(2)}) collective-permute-start(bf16[448,768]{1,0:T(8,128)(2,1)S(1)} %get-tuple-element.146), channel_id=1, source_target_pairs={{0,24},{4,28},{8,16},{12,20},{16,8},{20,12},{24,0},{28,4},{1,25},{... | collective-permute-start | bytes 2064392 | tf_op jit(solution)/shard_map/ppermute | solution.py:487
  552.7 11.2 %collective-permute-start.43 = (bf16[4,96,2432]{2,1,0:T(8,128)(2,1)S(1)}, bf16[4,96,2432]{2,1,0:T(8,128)(2,1)S(1)}, u32[]{:S(2)}, u32[]{:S(2)}) collective-permute-start(bf16[4,96,2432]{2,1,0:T(8,128)(2,1)S(1)} %pad_maximum_fusion.1), channel_id=1, source_target_pairs={{0,4},{4,0},{8,12},{12,8},{16,20},{20,16},{24,28},{28,24},{1,5},{5... | collective-permute-start | bytes 5603336 | tf_op jit(solution)/shard_map/ppermute | solution.py:487
  559.3 18.3 %collective-permute-start.36 = (bf16[448,768]{1,0:T(8,128)(2,1)S(1)}, bf16[448,768]{1,0:T(8,128)(2,1)S(1)}, u32[]{:S(2)}, u32[]{:S(2)}) collective-permute-start(bf16[448,768]{1,0:T(8,128)(2,1)S(1)} %get-tuple-element.148), channel_id=1, source_target_pairs={{0,8},{4,12},{8,0},{12,4},{16,24},{20,28},{24,16},{28,20},{1,9},{5... | collective-permute-start | bytes 2064392 | tf_op jit(solution)/shard_map/ppermute | solution.py:487
  561.0 32.5 %collective-permute-start.37 = (bf16[448,768]{1,0:T(8,128)(2,1)S(1)}, bf16[448,768]{1,0:T(8,128)(2,1)S(1)}, u32[]{:S(2)}, u32[]{:S(2)}) collective-permute-start(bf16[448,768]{1,0:T(8,128)(2,1)S(1)} %get-tuple-element.150), channel_id=1, source_target_pairs={{0,16},{4,20},{8,24},{12,28},{16,0},{20,4},{24,8},{28,12},{1,17},{... | collective-permute-start | bytes 2064392 | tf_op jit(solution)/shard_map/ppermute | solution.py:487
  561.7 31.9 %collective-permute-start.38 = (bf16[448,768]{1,0:T(8,128)(2,1)S(1)}, bf16[448,768]{1,0:T(8,128)(2,1)S(1)}, u32[]{:S(2)}, u32[]{:S(2)}) collective-permute-start(bf16[448,768]{1,0:T(8,128)(2,1)S(1)} %get-tuple-element.149), channel_id=1, source_target_pairs={{0,24},{4,28},{8,16},{12,20},{16,8},{20,12},{24,0},{28,4},{1,25},{... | collective-permute-start | bytes 2064392 | tf_op jit(solution)/shard_map/ppermute | solution.py:487
  563.8 32.6 %collective-permute-start.50 = (bf16[4,96,768]{2,1,0:T(8,128)(2,1)S(1)}, bf16[4,96,768]{2,1,0:T(8,128)(2,1)S(1)}, u32[]{:S(2)}, u32[]{:S(2)}) collective-permute-start(bf16[4,96,768]{2,1,0:T(8,128)(2,1)S(1)} %pad_maximum_fusion.4), channel_id=1, source_target_pairs={{0,4},{4,0},{8,12},{12,8},{16,20},{20,16},{24,28},{28,24},{1,5},{5... | collective-permute-start | bytes 1769480 | tf_op jit(solution)/shard_map/ppermute | solution.py:487
  565.2 37.2 %collective-permute-start.44 = (bf16[96,2432]{1,0:T(8,128)(2,1)S(1)}, bf16[96,2432]{1,0:T(8,128)(2,1)S(1)}, u32[]{:S(2)}, u32[]{:S(2)}) collective-permute-start(bf16[96,2432]{1,0:T(8,128)(2,1)S(1)} %get-tuple-element.142), channel_id=1, source_target_pairs={{0,8},{4,12},{8,0},{12,4},{16,24},{20,28},{24,16},{28,20},{1,9},{5... | collective-permute-start | bytes 1400840 | tf_op jit(solution)/shard_map/ppermute | solution.py:487
  577.6 36.0 %collective-permute-start.45 = (bf16[96,2432]{1,0:T(8,128)(2,1)S(1)}, bf16[96,2432]{1,0:T(8,128)(2,1)S(1)}, u32[]{:S(2)}, u32[]{:S(2)}) collective-permute-start(bf16[96,2432]{1,0:T(8,128)(2,1)S(1)} %get-tuple-element.144), channel_id=1, source_target_pairs={{0,16},{4,20},{8,24},{12,28},{16,0},{20,4},{24,8},{28,12},{1,17},{... | collective-permute-start | bytes 1400840 | tf_op jit(solution)/shard_map/ppermute | solution.py:487
  593.5 20.0 %collective-permute-start.46 = (bf16[96,2432]{1,0:T(8,128)(2,1)S(1)}, bf16[96,2432]{1,0:T(8,128)(2,1)S(1)}, u32[]{:S(2)}, u32[]{:S(2)}) collective-permute-start(bf16[96,2432]{1,0:T(8,128)(2,1)S(1)} %get-tuple-element.143), channel_id=1, source_target_pairs={{0,24},{4,28},{8,16},{12,20},{16,8},{20,12},{24,0},{28,4},{1,25},{... | collective-permute-start | bytes 1400840 | tf_op jit(solution)/shard_map/ppermute | solution.py:487
  596.5 19.1 %collective-permute-start.51 = (bf16[96,768]{1,0:T(8,128)(2,1)S(1)}, bf16[96,768]{1,0:T(8,128)(2,1)S(1)}, u32[]{:S(2)}, u32[]{:S(2)}) collective-permute-start(bf16[96,768]{1,0:T(8,128)(2,1)S(1)} %get-tuple-element.179), channel_id=1, source_target_pairs={{0,8},{4,12},{8,0},{12,4},{16,24},{20,28},{24,16},{28,20},{1,9},{5... | collective-permute-start | bytes 442376 | tf_op jit(solution)/shard_map/ppermute | solution.py:487
  598.7 20.8 %collective-permute-start.52 = (bf16[96,768]{1,0:T(8,128)(2,1)S(1)}, bf16[96,768]{1,0:T(8,128)(2,1)S(1)}, u32[]{:S(2)}, u32[]{:S(2)}) collective-permute-start(bf16[96,768]{1,0:T(8,128)(2,1)S(1)} %get-tuple-element.181), channel_id=1, source_target_pairs={{0,16},{4,20},{8,24},{12,28},{16,0},{20,4},{24,8},{28,12},{1,17},{... | collective-permute-start | bytes 442376 | tf_op jit(solution)/shard_map/ppermute | solution.py:487
  602.4 17.1 %collective-permute-start.53 = (bf16[96,768]{1,0:T(8,128)(2,1)S(1)}, bf16[96,768]{1,0:T(8,128)(2,1)S(1)}, u32[]{:S(2)}, u32[]{:S(2)}) collective-permute-start(bf16[96,768]{1,0:T(8,128)(2,1)S(1)} %get-tuple-element.180), channel_id=1, source_target_pairs={{0,24},{4,28},{8,16},{12,20},{16,8},{20,12},{24,0},{28,4},{1,25},{... | collective-permute-start | bytes 442376 | tf_op jit(solution)/shard_map/ppermute | solution.py:487
  613.9 12.1 %collective-permute-start.47 = (bf16[96,2432]{1,0:T(8,128)(2,1)S(1)}, bf16[96,2432]{1,0:T(8,128)(2,1)S(1)}, u32[]{:S(2)}, u32[]{:S(2)}) collective-permute-start(bf16[96,2432]{1,0:T(8,128)(2,1)S(1)} %add_convert_fusion.23), channel_id=1, source_target_pairs={{0,1},{3,2},{4,5},{7,6},{8,9},{11,10},{12,13},{15,14},{16,17},{19,... | collective-permute-start | bytes 1400840 | tf_op jit(solution)/shard_map/ppermute | solution.py:509
  628.3 20.3 %collective-permute-start.56 = (bf16[96,768]{1,0:T(8,128)(2,1)S(1)}, bf16[96,768]{1,0:T(8,128)(2,1)S(1)}, u32[]{:S(2)}, u32[]{:S(2)}) collective-permute-start(bf16[96,768]{1,0:T(8,128)(2,1)S(1)} %add_convert_fusion.25), channel_id=1, source_target_pairs={{1,0},{2,3},{5,4},{6,7},{9,8},{10,11},{13,12},{14,15},{17,16},{18,... | collective-permute-start | bytes 442376 | tf_op jit(solution)/shard_map/ppermute | solution.py:513
  629.7 23.8 %collective-permute-start.49 = (bf16[96,2432]{1,0:T(8,128)(2,1)S(1)}, bf16[96,2432]{1,0:T(8,128)(2,1)S(1)}, u32[]{:S(2)}, u32[]{:S(2)}) collective-permute-start(bf16[96,2432]{1,0:T(8,128)(2,1)S(1)} %add_convert_fusion.21), channel_id=1, source_target_pairs={{1,0},{2,3},{5,4},{6,7},{9,8},{10,11},{13,12},{14,15},{17,16},{18,... | collective-permute-start | bytes 1400840 | tf_op jit(solution)/shard_map/ppermute | solution.py:513
  (88 other events, 1187.9 us)

commit v2 on v0

--- a/solution.py
+++ b/solution.py
@@ -1,6 +1,8 @@
 import jax
 import jax.numpy as jnp
 from jax import lax
+from jax.experimental import pallas as pl
+from jax.experimental.pallas import tpu as pltpu
 from jax.sharding import PartitionSpec as P
 
 HEAD = 64
@@ -44,7 +46,7 @@
     )
 
 
-def per_device(
+def per_device_weights(
     tokens,
     starts,
     routes,
@@ -398,6 +400,790 @@
     )
 
 
+LANES = 128
+BF = jnp.bfloat16
+F32 = jnp.float32
+VMEM_BYTES = 60 * 1024 * 1024
+SMEM = pl.BlockSpec(memory_space=pltpu.SMEM)
+VMEM = pl.BlockSpec(memory_space=pltpu.VMEM)
+ANYWHERE = pl.BlockSpec(memory_space=pl.ANY)
+
+
+def dot_nn(a, b):
+    return lax.dot_general(a, b, (((1,), (0,)), ((), ())), preferred_element_type=F32)
+
+
+def dot_nt(a, b):
+    return lax.dot_general(a, b, (((1,), (1,)), ((), ())), preferred_element_type=F32)
+
+
+def dot_tn(a, b):
+    return lax.dot_general(a, b, (((0,), (0,)), ((), ())), preferred_element_type=F32)
+
+
+def kernel_call(body, name, out_shape, in_specs, out_specs, scratch, flops, args):
+    return pl.pallas_call(
+        body,
+        out_shape=out_shape,
+        in_specs=in_specs,
+        out_specs=out_specs,
+        scratch_shapes=scratch,
+        compiler_params=pltpu.CompilerParams(vmem_limit_bytes=VMEM_BYTES),
+        cost_estimate=pl.CostEstimate(
+            flops=int(flops), bytes_accessed=8 << 20, transcendentals=0
+        ),
+        name=name,
+    )(*args)
+
+
+def sds(shape, dtype=BF):
+    return jax.ShapeDtypeStruct(shape, dtype)
+
+
+def center(v):
+    mean = jnp.mean(v, -1, keepdims=True)
+    centred = v - mean
+    inverse = lax.rsqrt(jnp.mean(centred * centred, -1, keepdims=True) + EPSILON)
+    return centred * inverse, inverse
+
+
+def norm_grad(normed, inverse, gain, gradient):
+    dn = gradient * gain
+    return inverse * (
+        dn - jnp.mean(dn, -1, keepdims=True) - normed * jnp.mean(dn * normed, -1, keepdims=True)
+    )
+
+
+def exact_rows(place, v):
+    high = v.astype(BF)
+    rest = (v - high.astype(F32)).astype(BF)
+    return dot_nn(place, high) + dot_nn(place, rest)
+
+
+def segment_bias(starts, length, segs):
+    col = lax.broadcasted_iota(jnp.int32, (length, 1), 0)
+    row = lax.broadcasted_iota(jnp.int32, (1, length), 1)
+    col_seg = jnp.zeros((length, 1), jnp.int32)
+    row_seg = jnp.zeros((1, length), jnp.int32)
+    for k in range(segs):
+        col_seg = col_seg + jnp.where(col >= starts[0, k], 1, 0)
+        row_seg = row_seg + jnp.where(row >= starts[0, k], 1, 0)
+    return jnp.where(col_seg == row_seg, 0.0, MASKED)
+
+
+def load_pieces(me, refs, layout, dst, sems, part=None):
+    copies = []
+    for i, (ref, (mask, offset, rows, shard)) in enumerate(zip(refs, layout, strict=True)):
+        at = pl.multiple_of((me ^ mask) * shard + offset, 16)
+        src = ref if part is None else ref.at[part]
+        copy = pltpu.make_async_copy(src, dst.at[pl.ds(at, rows)], sems.at[i])
+        copy.start()
+        copies.append(copy)
+    return copies
+
+
+def attention_forward(layout, segs, *refs):
+    count = len(layout)
+    me_ref, starts, tokens, vec = refs[:4]
+    pieces = refs[4 : 4 + count]
+    qkv, mixed, lse, n1_out, weights, v_t, mixed_t, bias, sems = refs[4 + count :]
+    tok, width = tokens.shape
+    copies = load_pieces(me_ref[0], pieces, layout, weights, sems)
+    bias[...] = segment_bias(starts, tok, segs)
+    normed, _ = center(tokens[...].astype(F32))
+    n1_out[...] = (normed * vec[0:1, :] + vec[1:2, :]).astype(BF)
+    for copy in copies:
+        copy.wait()
+    for i in range(3):
+        part = dot_nn(n1_out[...], weights[:, i * width : (i + 1) * width])
+        if i != 1:
+            part = part + (vec[2:3, :] if i == 0 else vec[3:4, :])
+        part = part.astype(BF)
+        if i == 0:
+            part = part * jnp.asarray(HEAD**-0.5, BF)
+        qkv[:, i * width : (i + 1) * width] = part
+    v_t[...] = qkv[:, 2 * width :].T
+    half = lax.broadcasted_iota(jnp.int32, (1, LANES), 1) < HEAD
+
+    def pair(p, carry):
+        at = pl.multiple_of(p * LANES, LANES)
+        q_pair = qkv[:, pl.ds(at, LANES)]
+        k_pair = qkv[:, pl.ds(pl.multiple_of(width + p * LANES, LANES), LANES)]
+        for s in range(2):
+            q_one = jnp.where(half if s == 0 else ~half, q_pair, jnp.zeros_like(q_pair))
+            scores = dot_nt(k_pair, q_one) + bias[...]
+            top = jnp.max(scores, 0, keepdims=True)
+            e = jnp.exp(scores - top)
+            total = jnp.sum(e, 0, keepdims=True)
+            probs = (e * (1.0 / total)).astype(BF)
+            rows = pl.ds(pl.multiple_of(p * LANES + s * HEAD, HEAD), HEAD)
+            mixed_t[rows, :] = dot_nn(v_t[rows, :], probs)
+            lse[pl.ds(2 * p + s, 1), :] = top + jnp.log(total)
+        return carry
+
+    lax.fori_loop(0, width // LANES, pair, 0)
+    mixed[...] = mixed_t[...].T.astype(BF)
+
+
+def call_attention_forward(me, starts, tokens, vec, pieces, layout):
+    tok, width = tokens.shape
+    heads16 = (width // HEAD + 7) // 8 * 8
+    return kernel_call(
+        lambda *refs: attention_forward(layout, starts.shape[1], *refs),
+        "attention_forward",
+        (sds((tok, 3 * width)), sds((tok, width)), sds((heads16, tok), F32), sds((tok, width))),
+        [SMEM, SMEM, VMEM, VMEM] + [ANYWHERE] * len(pieces),
+        (VMEM,) * 4,
+        [
+            pltpu.VMEM((width, 3 * width), BF),
+            pltpu.VMEM((width, tok), BF),
+            pltpu.VMEM((width, tok), F32),
+            pltpu.VMEM((tok, tok), F32),
+            pltpu.SemaphoreType.DMA((len(pieces),)),
+        ],
+        2 * tok * width * 3 * width * 3,
+        (me, starts, tokens, vec, *pieces),
+    )
+
+
+def attention_backward(n, layout, segs, n_vec, *refs):
+    count = len(layout)
+    me_ref, starts, tokens, vec, vec_grads, qkv, lse, n1, g_mixed, g_hidden = refs[:10]
+    pieces = refs[10 : 10 + count]
+    input_grad, keep, send = refs[10 + count : 13 + count]
+    weights, k_t, gq_t, bias, g_qkv, g_w, v_rows, sems, out_sems = refs[13 + count :]
+    tok, width = tokens.shape
+    shard = width // n
+    me = me_ref[0]
+    copies = load_pieces(me, pieces, layout, weights, sems)
+    bias[...] = segment_bias(starts, tok, segs)
+    k_t[...] = qkv[:, width : 2 * width].T
+    half = lax.broadcasted_iota(jnp.int32, (1, LANES), 1) < HEAD
+
+    def pair(p, carry):
+        at = pl.ds(pl.multiple_of(p * LANES, LANES), LANES)
+        at_k = pl.ds(pl.multiple_of(width + p * LANES, LANES), LANES)
+        at_v = pl.ds(pl.multiple_of(2 * width + p * LANES, LANES), LANES)
+        q_pair, k_pair, v_pair, gm_pair = qkv[:, at], qkv[:, at_k], qkv[:, at_v], g_mixed[:, at]
+        gv, gk = [], []
+        for s in range(2):
+            own = half if s == 0 else ~half
+            q_one = jnp.where(own, q_pair, jnp.zeros_like(q_pair))
+            gm_one = jnp.where(own, gm_pair, jnp.zeros_like(gm_pair))
+            scores = dot_nt(k_pair, q_one) + bias[...]
+            probs = jnp.exp(scores - lse[pl.ds(2 * p + s, 1), :])
+            g_probs = dot_nt(v_pair, gm_one)
+            delta = jnp.sum(probs * g_probs, 0, keepdims=True)
+            g_scores = (probs * (g_probs - delta)).astype(BF)
+            gv.append(dot_nn(probs.astype(BF), gm_pair))
+            gk.append(dot_nn(g_scores, q_pair))
+            rows = pl.ds(pl.multiple_of(p * LANES + s * HEAD, HEAD), HEAD)
+            gq_t[rows, :] = dot_nn(k_t[rows, :], g_scores)
+        g_qkv[:, at_v] = jnp.where(half, gv[0], gv[1]).astype(BF)
+        g_qkv[:, at_k] = jnp.where(half, gk[0], gk[1]).astype(BF)
+        return carry
+
+    lax.fori_loop(0, width // LANES, pair, 0)
+    g_qkv[:, :width] = (gq_t[...].T * (HEAD**-0.5)).astype(BF)
+    for i in range(3):
+        cols = slice(i * width, (i + 1) * width)
+        g_w[:, cols] = dot_tn(n1[...], g_qkv[:, cols]).astype(BF)
+    for copy in copies:
+        copy.wait()
+    g_n1 = jnp.zeros((tok, width), F32)
+    for i in range(3):
+        cols = slice(i * width, (i + 1) * width)
+        g_n1 = g_n1 + dot_nt(g_qkv[:, cols], weights[:, cols])
+    normed, inverse = center(tokens[...].astype(F32))
+    input_grad[...] = g_hidden[...] + norm_grad(normed, inverse, vec[0:1, :], g_n1)
+    v_rows[...] = jnp.zeros_like(v_rows)
+    v_rows[0:1, :] = jnp.sum(g_n1 * normed, 0, keepdims=True)
+    v_rows[1:2, :] = jnp.sum(g_n1, 0, keepdims=True)
+    v_rows[2:3, :] = jnp.sum(g_qkv[:, :width].astype(F32), 0, keepdims=True)
+    v_rows[3:4, :] = jnp.sum(g_qkv[:, 2 * width :].astype(F32), 0, keepdims=True)
+    v_rows[4 : n_vec, :] = vec_grads[4 : n_vec, :]
+    g_w[:, 3 * width :] = v_rows[...].T.astype(BF)
+    outs = []
+    for m in range(n):
+        src = g_w.at[pl.ds(pl.multiple_of((me ^ m) * shard, 16), shard)]
+        copy = pltpu.make_async_copy(src, (send if m % 2 else keep).at[m // 2], out_sems.at[m])
+        copy.start()
+        outs.append(copy)
+    for copy in outs:
+        copy.wait()
+
+
+def call_attention_backward(
+    n, me, starts, tokens, vec, vec_grads, qkv, lse, n1, g_mixed, g_hidden, pieces, layout, n_vec
+):
+    tok, width = tokens.shape
+    shard = width // n
+    return kernel_call(
+        lambda *refs: attention_backward(n, layout, starts.shape[1], n_vec, *refs),
+        "attention_backward",
+        (sds((tok, width), F32),) + (sds((n // 2, shard, 3 * width + LANES)),) * 2,
+        [SMEM, SMEM] + [VMEM] * 8 + [ANYWHERE] * len(pieces),
+        (VMEM, ANYWHERE, ANYWHERE),
+        [
+            pltpu.VMEM((width, 3 * width), BF),
+            pltpu.VMEM((width, tok), BF),
+            pltpu.VMEM((width, tok), F32),
+            pltpu.VMEM((tok, tok), F32),
+            pltpu.VMEM((tok, 3 * width), BF),
+            pltpu.VMEM((width, 3 * width + LANES), BF),
+            pltpu.VMEM((LANES, width), F32),
+            pltpu.SemaphoreType.DMA((len(pieces),)),
+            pltpu.SemaphoreType.DMA((n,)),
+        ],
+        2 * tok * width * 3 * width * 5,
+        (me, starts, tokens, vec, vec_grads, qkv, lse, n1, g_mixed, g_hidden, *pieces),
+    )
+
+
+def mix_out(layout, *refs):
+    count = len(layout)
+    me_ref, mixed, tokens, vec, place = refs[:5]
+    pieces = refs[5 : 5 + count]
+    hidden, sorted_two, weights, sems = refs[5 + count :]
+    copies = load_pieces(me_ref[0], pieces, layout, weights, sems, EXPERTS)
+    for copy in copies:
+        copy.wait()
+    value = tokens[...].astype(F32) + dot_nn(mixed[...], weights[...]) + vec[4:5, :]
+    hidden[...] = value
+    normed, _ = center(value)
+    sorted_two[...] = dot_nn(place[...], (normed * vec[5:6, :] + vec[6:7, :]).astype(BF)).astype(BF)
+
+
+def call_mix_out(me, mixed, tokens, vec, place, pieces, layout):
+    tok, width = tokens.shape
+    return kernel_call(
+        lambda *refs: mix_out(layout, *refs),
+        "mix_out",
+        (sds((tok, width), F32), sds((place.shape[0], width))),
+        [SMEM] + [VMEM] * 4 + [ANYWHERE] * len(pieces),
+        (VMEM, VMEM),
+        [pltpu.VMEM((width, width), BF), pltpu.SemaphoreType.DMA((len(pieces),))],
+        2 * tok * width * width * 3,
+        (me, mixed, tokens, vec, place, *pieces),
+    )
+
+
+def load_blocks(refs, layout, dst, sems):
+    copies = []
+    for i, (ref, (block, offset, rows)) in enumerate(zip(refs, layout, strict=True)):
+        copy = pltpu.make_async_copy(ref, dst.at[block, pl.ds(offset, rows)], sems.at[i])
+        copy.start()
+        copies.append(copy)
+    return copies
+
+
+def load_expert_weights(me, refs, layout, dst, sems):
+    copies = []
+    for i, (ref, (mask, offset, rows, shard)) in enumerate(zip(refs, layout, strict=True)):
+        at = pl.multiple_of((me ^ mask) * shard + offset, 16)
+        copy = pltpu.make_async_copy(ref.at[pl.ds(0, EXPERTS)], dst.at[:, pl.ds(at, rows)], sems.at[i])
+        copy.start()
+        copies.append(copy)
+    return copies
+
+
+def window(meta, block, e):
+    begin = pl.multiple_of(meta[block, 3 * e], 16)
+    row = lax.broadcasted_iota(jnp.int32, (CAP, 1), 0)
+    return pl.ds(begin, CAP), (row >= meta[block, 3 * e + 1]) & (row < meta[block, 3 * e + 2])
+
+
+def experts(nb, lay_x, lay_g, lay_w, *refs):
+    cx, cg, cw = len(lay_x), len(lay_g), len(lay_w)
+    me_ref, meta, b_in = refs[:3]
+    at = 3
+    x_refs, at = refs[at : at + cx], at + cx
+    g_refs, at = refs[at : at + cg], at + cg
+    w_refs, at = refs[at : at + cw], at + cw
+    down_mine, down_other = refs[at : at + 2]
+    res, dsl, act_out, dp_out = refs[at + 2 : at + 6]
+    x_all, g_all, w_in, w_down, res_s, dsl_s, xs, gs, sx, sg, sw, sd, so = refs[at + 6 :]
+    me = me_ref[0]
+    shard_ff = down_mine.shape[1]
+    core = me % 2
+    copies = load_expert_weights(me, w_refs, lay_w, w_in, sw)
+    for i, ref in enumerate((down_mine, down_other)):
+        rows = pl.ds(pl.multiple_of((core if i == 0 else 1 - core) * shard_ff, 16), shard_ff)
+        copy = pltpu.make_async_copy(ref, w_down.at[:, rows], sd.at[i])
+        copy.start()
+        copies.append(copy)
+    copies += load_blocks(x_refs, lay_x, x_all, sx) + load_blocks(g_refs, lay_g, g_all, sg)
+    res_s[...] = jnp.zeros_like(res_s)
+    dsl_s[...] = jnp.zeros_like(dsl_s)
+    for copy in copies:
+        copy.wait()
+
+    def expert(e, carry):
+        spans = []
+        for b in range(nb):
+            span, inside = window(meta, b, e)
+            spans.append((span, inside))
+            g = g_all[b, span, :]
+            xs[b * CAP : (b + 1) * CAP, :] = x_all[b, span, :]
+            gs[b * CAP : (b + 1) * CAP, :] = jnp.where(inside, g, jnp.zeros_like(g))
+        pre = dot_nn(xs[...], w_in[e]) + b_in[e]
+        cdf = 0.5 * (1.0 + lax.erf(pre * 0.7071067811865476))
+        act = (pre * cdf).astype(BF)
+        slope = cdf + pre * jnp.exp(-0.5 * pre * pre) * 0.3989422804014327
+        dp = (dot_nt(gs[...], w_down[e]) * slope).astype(BF)
+        act_out[e] = act
+        dp_out[e] = dp
+        for dst, value in ((dsl_s, dot_nt(dp, w_in[e])), (res_s, dot_nn(act, w_down[e]))):
+            value = value.astype(BF)
+            for b, (span, inside) in enumerate(spans):
+                dst[b, span, :] = jnp.where(inside, value[b * CAP : (b + 1) * CAP], dst[b, span, :])
+        return carry
+
+    lax.fori_loop(0, EXPERTS, expert, 0)
+    outs = []
+    for i, (src, dst) in enumerate(((dsl_s, dsl), (res_s, res))):
+        copy = pltpu.make_async_copy(src, dst, so.at[i])
+        copy.start()
+        outs.append(copy)
+    for copy in outs:
+        copy.wait()
+
+
+def call_experts(nb, me, meta, b_in, xp, lay_x, gp, lay_g, wp, lay_w, down_mine, down_other):
+    rows, width = max(o + r for _, o, r in lay_x), xp[0].shape[1]
+    ff = 2 * down_mine.shape[1]
+    dma = pltpu.SemaphoreType.DMA
+    return kernel_call(
+        lambda *refs: experts(nb, lay_x, lay_g, lay_w, *refs),
+        "experts",
+        (sds((nb, rows, width)),) * 2 + (sds((EXPERTS, nb * CAP, ff)),) * 2,
+        [SMEM, SMEM, VMEM] + [ANYWHERE] * (len(xp) + len(gp) + len(wp) + 2),
+        (ANYWHERE, ANYWHERE, VMEM, VMEM),
+        [pltpu.VMEM((nb, rows, width), BF)] * 2
+        + [pltpu.VMEM((EXPERTS, width, ff), BF), pltpu.VMEM((EXPERTS, ff, width), BF)]
+        + [pltpu.VMEM((nb, rows, width), BF)] * 2
+        + [pltpu.VMEM((nb * CAP, width), BF)] * 2
+        + [dma((len(xp),)), dma((len(gp),)), dma((len(wp),)), dma((2,)), dma((2,))],
+        2 * nb * CAP * EXPERTS * width * ff * 4,
+        (me, meta, b_in, *xp, *gp, *wp, down_mine, down_other),
+    )
+
+
+def expert_grads(n, calls, lay_x, lay_g, *refs):
+    cx, cg, cc = len(lay_x), len(lay_g), len(calls)
+    me_ref, meta = refs[:2]
+    at = 2
+    x_refs, at = refs[at : at + cx], at + cx
+    g_refs, at = refs[at : at + cg], at + cg
+    acts, at = refs[at : at + cc], at + cc
+    dps, at = refs[at : at + cc], at + cc
+    down_keep, down_send, in_keep, in_send = refs[at : at + 4]
+    x_all, g_all, act_s, dp_s, xs, gs, g_down, g_in, sx, sg, sa, sp, so = refs[at + 4 :]
+    me = me_ref[0]
+    core = me % 2
+    blocks = sum(calls)
+    _, width, ff = g_in.shape
+    shard = width // n
+    copies = load_blocks(x_refs, lay_x, x_all, sx) + load_blocks(g_refs, lay_g, g_all, sg)
+    first = 0
+    for i, nb in enumerate(calls):
+        for src, dst, sem in ((acts[i], act_s, sa), (dps[i], dp_s, sp)):
+            copy = pltpu.make_async_copy(src, dst.at[:, pl.ds(first * CAP, nb * CAP)], sem.at[i])
+            copy.start()
+            copies.append(copy)
+        first += nb
+    for copy in copies:
+        copy.wait()
+    down_rows = EXPERTS * (ff // 2)
+
+    def expert(e, carry):
+        for b in range(blocks):
+            span, inside = window(meta, b, e)
+            g = g_all[b, span, :]
+            xs[b * CAP : (b + 1) * CAP, :] = x_all[b, span, :]
+            gs[b * CAP : (b + 1) * CAP, :] = jnp.where(inside, g, jnp.zeros_like(g))
+        g_down[e] = dot_tn(act_s[e], gs[...]).astype(BF)
+        g_in[e] = dot_tn(xs[...], dp_s[e]).astype(BF)
+        return carry
+
+    lax.fori_loop(0, EXPERTS, expert, 0)
+    lane = jnp.zeros((16, width - ff // 2), F32)
+    row = lax.broadcasted_iota(jnp.int32, (16, 1), 0)
+    low = jnp.zeros((16, ff // 2), F32)
+    high = jnp.zeros((16, ff // 2), F32)
+    for e in range(EXPERTS):
+        total = jnp.sum(dp_s[e].astype(F32), 0, keepdims=True)
+        low = low + jnp.where(row == e, total[:, : ff // 2], 0.0)
+        high = high + jnp.where(row == e, total[:, ff // 2 :], 0.0)
+    first_core = core == 0
+    tail = pl.ds(down_rows, 16)
+    down_keep[tail, :] = jnp.concatenate([jnp.where(first_core, low, high), lane], 1).astype(BF)
+    down_send[tail, :] = jnp.concatenate([jnp.where(first_core, high, low), lane], 1).astype(BF)
+    half = ff // 2
+    outs = []
+    for e in range(EXPERTS):
+        for i, dst in enumerate((down_keep, down_send)):
+            src = g_down.at[e, pl.ds(pl.multiple_of((core if i == 0 else 1 - core) * half, 16), half)]
+            outs.append(
+                pltpu.make_async_copy(src, dst.at[pl.ds(e * half, half)], so.at[2 * e + i])
+            )
+    for m in range(n):
+        src = g_in.at[:, pl.ds(pl.multiple_of((me ^ m) * shard, 16), shard)]
+        dst = (in_send if m % 2 else in_keep).at[m // 2]
+        outs.append(pltpu.make_async_copy(src, dst, so.at[2 * EXPERTS + m]))
+    for copy in outs:
+        copy.start()
+    for copy in outs:
+        copy.wait()
+
+
+def call_expert_grads(n, me, meta, xp, lay_x, gp, lay_g, acts, dps, calls):
+    rows, width = max(o + r for _, o, r in lay_x), xp[0].shape[1]
+    ff = acts[0].shape[2]
+    blocks = sum(calls)
+    dma = pltpu.SemaphoreType.DMA
+    shard = width // n
+    down = EXPERTS * (ff // 2) + 16
+    return kernel_call(
+        lambda *refs: expert_grads(n, calls, lay_x, lay_g, *refs),
+        "expert_grads",
+        (sds((down, width)),) * 2 + (sds((n // 2, EXPERTS, shard, ff)),) * 2,
+        [SMEM, SMEM] + [ANYWHERE] * (len(xp) + len(gp) + 2 * len(calls)),
+        (VMEM, VMEM, ANYWHERE, ANYWHERE),
+        [pltpu.VMEM((blocks, rows, width), BF)] * 2
+        + [pltpu.VMEM((EXPERTS, blocks * CAP, ff), BF)] * 2
+        + [pltpu.VMEM((blocks * CAP, width), BF)] * 2
+        + [pltpu.VMEM((EXPERTS, ff, width), BF), pltpu.VMEM((EXPERTS, width, ff), BF)]
+        + [dma((len(xp),)), dma((len(gp),)), dma((len(calls),)), dma((len(calls),))]
+        + [dma((2 * EXPERTS + n,))],
+        2 * blocks * CAP * EXPERTS * width * ff * 2,
+        (me, meta, *xp, *gp, *acts, *dps),
+    )
+
+
+def mix_out_backward(n, layout, terms, *refs):
+    count = len(layout)
+    me_ref, place_t, hidden, cot, vec, mixed, down_bias = refs[:7]
+    got = refs[7 : 7 + terms]
+    pieces = refs[7 + terms : 7 + terms + count]
+    g_hidden, g_mixed, vec_grads, keep, send = refs[7 + terms + count : 12 + terms + count]
+    weights, g_w, sems, out_sems = refs[12 + terms + count :]
+    me = me_ref[0]
+    tok, width = hidden.shape
+    shard = width // n
+    copies = load_pieces(me, pieces, layout, weights, sems, EXPERTS)
+    total = got[0][...].astype(F32)
+    for ref in got[1:]:
+        total = total + ref[...].astype(F32)
+    gradient = exact_rows(place_t[...], total)
+    normed, inverse = center(hidden[...])
+    value = cot[...].astype(F32) + norm_grad(normed, inverse, vec[5:6, :], gradient)
+    g_hidden[...] = value
+    branch = value.astype(BF)
+    vec_grads[...] = jnp.zeros_like(vec_grads)
+    vec_grads[4:5, :] = jnp.sum(branch.astype(F32), 0, keepdims=True)
+    vec_grads[5:6, :] = jnp.sum(gradient * normed, 0, keepdims=True)
+    vec_grads[6:7, :] = jnp.sum(gradient, 0, keepdims=True)
+    vec_grads[7 : 7 + EXPERTS, :] = down_bias[...]
+    for copy in copies:
+        copy.wait()
+    g_mixed[...] = dot_nt(branch, weights[...]).astype(BF)
+    g_w[...] = dot_tn(mixed[...], branch).astype(BF)
+    outs = []
+    for m in range(n):
+        src = g_w.at[pl.ds(pl.multiple_of((me ^ m) * shard, 16), shard)]
+        copy = pltpu.make_async_copy(src, (send if m % 2 else keep).at[m // 2], out_sems.at[m])
+        copy.start()
+        outs.append(copy)
+    for copy in outs:
+        copy.wait()
+
+
+def call_mix_out_backward(n, me, place_t, hidden, cot, vec, mixed, down_bias, got, pieces, layout):
+    tok, width = hidden.shape
+    shard = width // n
+    return kernel_call(
+        lambda *refs: mix_out_backward(n, layout, len(got), *refs),
+        "mix_out_backward",
+        (sds((tok, width), F32), sds((tok, width)), sds((16, width), F32))
+        + (sds((n // 2, shard, width)),) * 2,
+        [SMEM] + [VMEM] * (6 + len(got)) + [ANYWHERE] * len(pieces),
+        (VMEM, VMEM, VMEM, ANYWHERE, ANYWHERE),
+        [pltpu.VMEM((width, width), BF)] * 2
+        + [pltpu.SemaphoreType.DMA((len(pieces),)), pltpu.SemaphoreType.DMA((n,))],
+        2 * tok * width * width * 3,
+        (me, place_t, hidden, cot, vec, mixed, down_bias, *got, *pieces),
+    )
+
+
+def finish_output(terms, *refs):
+    place_t, hidden, route, vec = refs[:4]
+    got = refs[4 : 4 + terms]
+    out = refs[4 + terms]
+    total = got[0][...].astype(F32)
+    for ref in got[1:]:
+        total = total + ref[...].astype(F32)
+    value = hidden[...] + exact_rows(place_t[...], total)
+    for e in range(EXPERTS):
+        value = value + jnp.where(route[...] == e, vec[7 + e : 8 + e, :], 0.0)
+    out[...] = value.astype(BF)
+
+
+def call_finish_output(place_t, hidden, route, vec, got):
+    return kernel_call(
+        lambda *refs: finish_output(len(got), *refs),
+        "finish_output",
+        sds(hidden.shape),
+        [VMEM] * (4 + len(got)),
+        VMEM,
+        [],
+        4 * place_t.size * hidden.shape[1],
+        (place_t, hidden, route, vec, *got),
+    )
+
+
+def swap(v, n, mask):
+    return lax.ppermute(v, "fsdp", [(i, i ^ mask) for i in range(n)])
+
+
+def gather_chips(v, n):
+    rows = v.shape[0]
+    half = rows // 32 * 16
+    along, across = swap(v, n, 2), swap(v, n, 4)
+    return [
+        (v, 0, 0),
+        (along, 2, 0),
+        (across, 4, 0),
+        (swap(along[:half], n, 4), 6, 0),
+        (swap(across[half:], n, 2), 6, half),
+    ]
+
+
+def gather_all(v, n):
+    pieces = gather_chips(v, n)
+    return pieces + [(swap(p, n, 1), mask ^ 1, offset) for p, mask, offset in pieces]
+
+
+def layout_of(pieces, shard):
+    return [(mask, offset, p.shape[0], shard) for p, mask, offset in pieces]
+
+
+def blocks_of(pieces, masks):
+    return [(masks.index(mask), offset, p.shape[0]) for p, mask, offset in pieces]
+
+
+def scatter_chips(terms, n):
+    return [terms[0]] + [swap(terms[i], n, 2 * i) for i in range(1, n // 2)]
+
+
+def add_low(*terms):
+    total = terms[0].astype(F32)
+    for term in terms[1:]:
+        total = total + term.astype(F32)
+    return total.astype(BF)
+
+
+def scatter_all(keep, send, n):
+    other = swap(send, n, 1)
+    return add_low(*scatter_chips([add_low(keep[i], other[i]) for i in range(n // 2)], n))
+
+
+def line_in(v):
+    return add_low(v, lax.ppermute(v, "rep", [(0, 1), (3, 2)]))
+
+
+def line_across(v):
+    return add_low(v, lax.ppermute(v, "rep", [(1, 2), (2, 1)]))
+
+
+def line_out(v):
+    at = lax.axis_index("rep")
+    return jnp.where((at == 0) | (at == 3), lax.ppermute(v, "rep", [(1, 0), (2, 3)]), v)
+
+
+def line_sum(v):
+    return line_out(line_across(line_in(v)))
+
+
+def per_device_tokens(
+    n,
+    tokens,
+    starts,
+    routes,
+    norm1_gain,
+    norm1_bias,
+    query_weight,
+    query_bias,
+    key_weight,
+    value_weight,
+    value_bias,
+    out_weight,
+    out_bias,
+    norm2_gain,
+    norm2_bias,
+    expert_in,
+    expert_in_bias,
+    expert_out,
+    expert_out_bias,
+    cotangent,
+):
+    index = lax.axis_index("fsdp")
+    me = index.astype(jnp.int32).reshape(1)
+    tok_count, width = tokens.shape
+    shard = width // n
+    ff_shard = expert_out.shape[1]
+    ff_pair = 2 * ff_shard
+    masks = list(range(0, n, 2))
+    order = index ^ jnp.arange(n, dtype=jnp.int32)
+
+    w_qkv = gather_all(jnp.concatenate([query_weight, key_weight, value_weight], 1), n)
+
+    route_ids = routes[:, 0]
+    member = (route_ids[:, None] == jnp.arange(EXPERTS, dtype=jnp.int32)[None, :]).astype(jnp.int32)
+    rank = jnp.sum(jnp.cumsum(member, 0) * member, 1) - 1
+    counts = jnp.sum(member, 0)
+    padded = (counts + 15) // 16
+    base = jnp.cumsum(padded) - padded
+    slots = tok_count + 16 * (EXPERTS - 1)
+    position = jnp.sum(member * base[None, :], 1) * 16 + rank
+    slot = jnp.arange(slots, dtype=jnp.int32)
+    place = (slot[:, None] == position[None, :]).astype(BF)
+    place_t = (position[:, None] == slot[None, :]).astype(BF)
+    begin = jnp.minimum(base, (slots - CAP) // 16)
+    meta = jnp.stack([begin, base - begin, base - begin + padded], 1).reshape(3 * EXPERTS)
+
+    vectors = [norm1_gain, norm1_bias, query_bias, value_bias, out_bias, norm2_gain, norm2_bias]
+    n_vec = len(vectors) + EXPERTS
+    small = jnp.concatenate([jnp.stack(vectors), expert_out_bias], 0)
+    small = jnp.pad(small, ((0, 0), (0, LANES - shard)))
+    meta_row = jnp.pad(meta.astype(BF), (0, LANES - meta.shape[0]))[None]
+    bias_rows = expert_in_bias.reshape(-1, LANES)
+    small = jnp.concatenate([small, meta_row, bias_rows], 0)
+    small = jnp.pad(small, ((0, 32 - small.shape[0]), (0, 0)))
+    small_all = lax.all_gather(small, "fsdp", axis=0, tiled=False)
+    vec = small_all[:, :n_vec, :shard].transpose(1, 0, 2).reshape(n_vec, width).astype(F32)
+    vec = jnp.pad(vec, ((0, 16 - n_vec), (0, 0)))
+    by_mask = jnp.take(small_all, order, axis=0)
+    meta_rel = by_mask[:, n_vec, : 3 * EXPERTS].astype(jnp.int32)[0::2] * 16
+    pair_bias = lax.dynamic_slice(small_all, (index // 2 * 2, n_vec + 1, 0), (2,) + bias_rows.shape)
+    b_in = pair_bias.reshape(2, EXPERTS, ff_shard).transpose(1, 0, 2).reshape(EXPERTS, 1, ff_pair).astype(F32)
+
+    def in_piece(mask):
+        cols = (index ^ mask) // 2 * ff_pair
+        part = lax.dynamic_slice(expert_in, (0, 0, cols), (EXPERTS, shard, ff_pair))
+        return jnp.concatenate([part, out_weight[None]], 0)
+
+    w_two = [(swap(in_piece(m), n, m) if m else in_piece(m), m, 0) for m in masks]
+    w_two = w_two + [(swap(p, n, 1), m ^ 1, 0) for p, m, _ in w_two]
+    lay_two = [(m, 0, shard, shard) for _, m, _ in w_two]
+    w_two = [p for p, _, _ in w_two]
+    down_other = swap(expert_out, n, 1)
+
+    def sort(v):
+        return dot_nn(place, v).astype(BF)
+
+    grad_pieces = gather_chips(sort(cotangent), n)
+    down_bias = dot_tn(member.astype(BF), cotangent)
+
+    lay_qkv = layout_of(w_qkv, shard)
+    w_qkv = [p for p, _, _ in w_qkv]
+    qkv, mixed, lse, n1 = call_attention_forward(me, starts, tokens, vec, w_qkv, lay_qkv)
+    hidden, sorted_two = call_mix_out(me, mixed, tokens, vec, place, w_two, lay_two)
+    token_pieces = gather_chips(sorted_two, n)
+
+    calls = ((0,), (1, 2), (3,))
+    res, dsl, acts, dps = [], [], [], []
+    for call in calls:
+        here = [masks[i] for i in call]
+        xp = [p for p in token_pieces if p[1] in here]
+        gp = [p for p in grad_pieces if p[1] in here]
+        r, d, a, p = call_experts(
+            len(call),
+            me,
+            meta_rel[call[0] : call[-1] + 1],
+            b_in,
+            [v for v, _, _ in xp],
+            blocks_of(xp, here),
+            [v for v, _, _ in gp],
+            blocks_of(gp, here),
+            w_two,
+            lay_two,
+            expert_out,
+            down_other,
+        )
+        res += [r[i] for i in range(len(call))]
+        dsl += [d[i] for i in range(len(call))]
+        acts.append(a)
+        dps.append(p)
+    got_dsl = scatter_chips(dsl, n)
+    down_keep, down_send, in_keep, in_send = call_expert_grads(
+        n,
+        me,
+        meta_rel,
+        [v for v, _, _ in token_pieces],
+        blocks_of(token_pieces, masks),
+        [v for v, _, _ in grad_pieces],
+        blocks_of(grad_pieces, masks),
+        acts,
+        dps,
+        tuple(len(call) for call in calls),
+    )
+    got_res = scatter_chips(res, n)
+    route = routes
+    output = call_finish_output(place_t, hidden, route, vec, got_res)
+
+    g_hidden, g_mixed, vec_grads, out_keep, out_send = call_mix_out_backward(
+        n, me, place_t, hidden, cotangent, vec, mixed, down_bias, got_dsl, w_two, lay_two
+    )
+    sum_out = line_sum(scatter_all(out_keep, out_send, n)).astype(F32)
+
+    down = add_low(down_keep, swap(down_send, n, 1))
+    cut = down.shape[0] // 32 * 16
+    sum_down = jnp.concatenate([line_sum(down[:cut]), line_sum(down[cut:])], 0)
+    sum_in_bias = sum_down[EXPERTS * ff_shard : EXPERTS * ff_shard + EXPERTS, :ff_shard].astype(F32)
+    sum_down = sum_down[: EXPERTS * ff_shard].reshape(EXPERTS, ff_shard, width).astype(F32)
+    in_other = swap(in_send, n, 1)
+    in_got = scatter_chips([add_low(in_keep[i], in_other[i]) for i in range(n // 2)], n)
+    chip_order = index // 2 ^ jnp.arange(n // 2, dtype=jnp.int32)
+    lines = [
+        line_sum(jnp.stack(in_got[: n // 4])),
+        line_sum(jnp.stack(in_got[n // 4 :])),
+    ]
+    sum_in = jnp.take(jnp.concatenate(lines, 0), chip_order, axis=0)
+    sum_in = sum_in.transpose(1, 2, 0, 3).reshape(EXPERTS, shard, n * ff_shard).astype(F32)
+
+    input_grad, keep, send = call_attention_backward(
+        n, me, starts, tokens, vec, vec_grads, qkv, lse, n1, g_mixed, g_hidden, w_qkv, lay_qkv, n_vec
+    )
+    sum_last = line_sum(scatter_all(keep, send, n)).astype(F32)
+    sum_vec = sum_last[:, 3 * width : 3 * width + n_vec].T
+    return (
+        output,
+        input_grad,
+        sum_vec[0],
+        sum_vec[1],
+        sum_last[:, :width],
+        sum_vec[2],
+        sum_last[:, width : 2 * width],
+        sum_last[:, 2 * width : 3 * width],
+        sum_vec[3],
+        sum_out,
+        sum_vec[4],
+        sum_vec[5],
+        sum_vec[6],
+        sum_in,
+        sum_in_bias,
+        sum_down,
+        sum_vec[7:],
+    )
+
+
+def plan_of(n, replicas):
+    if n == 8 and replicas == 4:
+        return lambda *args: per_device_tokens(n, *args)
+    return per_device_weights
+
+
 def solution(mesh):
     in_specs = (
         P(("fsdp", "rep"), None),
@@ -439,6 +1225,7 @@
         P(None, "fsdp", None),
         P(None, "fsdp"),
     )
+    per_device = plan_of(mesh.shape["fsdp"], mesh.shape["rep"])
     return jax.shard_map(
         per_device, mesh=mesh, in_specs=in_specs, out_specs=out_specs, check_vma=False
     )

time: 1310 us -> 439 us (0.34)
  waiting for transfers between devices: 937 us -> 172 us
  blocking collectives: 153 us -> 21.6 us
  matrix products: 112 us -> 2.21 us
  Pallas kernels: 0 us -> 107 us
  starting transfers between devices: 1.26 us -> 79.2 us
  local copies, waits for them, and re-layouts: 50.5 us -> 24.6 us
  between operations: 17.2 us -> 1.89 us
    reduce_scatter x8 -> x0, waiting for transfers between devices: 585 us -> none  [the longest x1 241 us: per_device(): lax.psum_scatter(grad_in.astype(jnp.bfloat16), 'rep', scatter_dimension=2...]
    all_gather x8 -> x0, waiting for transfers between devices: 239 us -> none  [the longest x1 74.6 us: per_device(): lax.all_gather(expert_in, 'fsdp', axis=1, tiled=True)]
    ppermute x0 -> x62, waiting for transfers between devices: none -> 172 us  [the longest x6 72.8 us: line_out(): lax.ppermute(v, 'rep', [(1, 0), (2, 3)])]
    unnamed x28 -> x0, waiting for transfers between devices: 114 us -> none
    dot_general x24 -> x2, matrix products: 112 us -> 2.21 us  [the longest x1 1.41 us: dot_nn(): lax.dot_general(a, b, (((1,), (0,)), ((), ())), preferred_element_type=F32)]
    pallas_call x0 -> x9, Pallas kernels: none -> 107 us  [kernel_call(): pl.pallas_call(body, out_shape=out_shape, in_specs=in_specs, out_specs=ou...]
    ppermute x0 -> x62, starting transfers between devices: none -> 79.2 us  [the longest x44 36.5 us: swap(): return lax.ppermute(v, 'fsdp', [(i, i ^ mask) for i in range(n)])]
    all_gather x8 -> x1, blocking collectives: 96.4 us -> 21.6 us  [per_device_tokens(): small_all = lax.all_gather(small, 'fsdp', axis=0, tiled=False)]
  transfers between devices with their start and end apart: 22 -> 62, of which waited for: 20 -> 19; matrix products, arithmetic and copies ran while one was open for 14% -> 9% of each run, Pallas kernels for 0% -> 23%
where the time goes in v2:
time: 439 us; the launch traced here: 433 us
  waiting for transfers between devices  172 us (39%)
  Pallas kernels  107 us (24%)
  starting transfers between devices  79.2 us (18%)
  local copies, waits for them, and re-layouts  24.6 us (6%)
  other arithmetic  24.6 us (6%)
  blocking collectives  21.6 us (5%)
    pallas_call x9, Pallas kernels, kernel_call(): pl.pallas_call(body, out_shape=out_shape, in_specs=in_specs, out_specs=ou...  107 us
    ppermute x6, waiting for transfers between devices, line_out(): lax.ppermute(v, 'rep', [(1, 0), (2, 3)])  72.8 us
    ppermute x44, waiting for transfers between devices, swap(): return lax.ppermute(v, 'fsdp', [(i, i ^ mask) for i in range(n)])  50 us
    ppermute x6, waiting for transfers between devices, line_in(): return add_low(v, lax.ppermute(v, 'rep', [(0, 1), (3, 2)]))  49.1 us
    ppermute x44, starting transfers between devices, swap(): return lax.ppermute(v, 'fsdp', [(i, i ^ mask) for i in range(n)])  36.5 us
    ppermute x6, starting transfers between devices, line_in(): return add_low(v, lax.ppermute(v, 'rep', [(0, 1), (3, 2)]))  30.5 us
    all_gather x1, blocking collectives, per_device_tokens(): small_all = lax.all_gather(small, 'fsdp', axis=0, tiled=False)  21.6 us
    convert_element_type x18, other arithmetic, add_low(): return total.astype(BF)  9.16 us
  transfers between devices with their start and end apart: 62, of which 19 were waited for; matrix products, arithmetic and copies ran while one was open for 9% of the time, Pallas kernels for 23%

profile of v2, /device:TPU:0, one launch (start us, length us, event | category | flops | bytes accessed | tf_op | source)
XLA Modules:
  0.0 433.1 jit_solution(10580521063340171258)
XLA Ops:
  0.7 1.6 constant_dynamic-update-slice_fusion.2
  2.2 1.6 constant_dynamic-update-slice_fusion.1
  3.8 1.6 constant_dynamic-update-slice_fusion.refs_4_.refs_10_
  5.4 2.9 collective-permute-start
  8.4 1.5 collective-permute-start.1
  9.9 1.6 constant_dynamic-slice_fusion
  15.6 21.6 %all-gather = bf16[256,128]{1,0:T(8,128)(2,1)S(1)} all-gather(bf16[32,128]{1,0:T(8,128)(2,1)S(1)} %pad.25), channel_id=2, replica_groups=mesh['fsdp'=8,'rep'=4] {'fsdp'}, dimensions={0}, use_global_device_ids=true | all-gather | bytes 73728 | tf_op jit(solution)/shard_map/all_gather | solution.py:1063
  38.0 1.5 collective-permute-start.11
  42.4 1.6 collective-permute-start.3
  44.5 10.9 %collective-permute-done.11.refs_8_.refs_10_.refs_14_ = bf16[4,96,768]{2,1,0:T(8,128)(2,1)S(1)} collective-permute-done((bf16[4,96,768]{2,1,0:T(8,128)(2,1)}, bf16[4,96,768]{2,1,0:T(8,128)(2,1)S(1)}, u32[]{:S(2)}, u32[]{:S(2)}) %collective-permute-start.11) | collective-permute-done | bytes 589856 | tf_op jit(solution)/shard_map/ppermute | solution.py:946
  55.3 4.1 collective-permute-done.2.refs_7_.refs_13_
  60.0 1.4 convolution_convert_fusion.refs_4_.refs_7_
  63.7 13.3 %attention_forward.1 = (bf16[416,2304]{1,0:T(8,128)(2,1)}, bf16[416,768]{1,0:T(8,128)(2,1)}, f32[16,416]{1,0:T(8,128)}, bf16[416,768]{1,0:T(8,128)(2,1)}) custom-call(s32[1]{0:T(128)} %bitcast.4.refs_0_, s32[1,4]{1,0:T(1,128)} %refs_1_.3, bf16[416,768]{1,0:T(8,128)(2,1)} %refs_2_.6, f32[16,768]{1,0:T(8,128)} %pad_convert_fusion.refs_3_.refs_4_, ...), custom_call_target="tpu_custom_call" | custom-call | flops 4416602112 | bytes 8388608 | tf_op jit(solution)/shard_map/attention_forward/pallas_call | solution.py:425
  77.6 1.5 collective-permute-start.20
  79.1 5.4 %mix_out.1 = (f32[416,768]{1,0:T(8,128)}, bf16[448,768]{1,0:T(8,128)(2,1)}) custom-call(s32[1]{0:T(128)} %bitcast.4.refs_0_, bf16[416,768]{1,0:T(8,128)(2,1)} %get-tuple-element.47.refs_1_.refs_5_, bf16[416,768]{1,0:T(8,128)(2,1)} %refs_2_.6, f32[16,768]{1,0:T(8,128)} %pad_convert_fusion.refs_3_.refs_4_, bf16[448,416]{1,0:T(8,128)(2,1)} %fusion.3.refs_4_, ...), custom_call_target="tpu_custom_call" | custom-call | flops 1472200704 | bytes 8388608 | tf_op jit(solution)/shard_map/mix_out/pallas_call | solution.py:425
  85.1 1.5 collective-permute-start.18
  89.1 6.5 %collective-permute-done.19.refs_5_.refs_8_ = bf16[448,768]{1,0:T(8,128)(2,1)} collective-permute-done((bf16[448,768]{1,0:T(8,128)(2,1)}, bf16[448,768]{1,0:T(8,128)(2,1)}, u32[]{:S(2)}, u32[]{:S(2)}) %collective-permute-start.19) | collective-permute-done | bytes 688160 | tf_op jit(solution)/shard_map/ppermute | solution.py:946
  97.3 1.5 collective-permute-start.26
  98.8 11.4 %collective-permute-done.17.refs_3_ = bf16[448,768]{1,0:T(8,128)(2,1)S(1)} collective-permute-done((bf16[448,768]{1,0:T(8,128)(2,1)}, bf16[448,768]{1,0:T(8,128)(2,1)S(1)}, u32[]{:S(2)}, u32[]{:S(2)}) %collective-permute-start.17) | collective-permute-done | bytes 688160 | tf_op jit(solution)/shard_map/ppermute | solution.py:946
  112.5 1.5 collective-permute-start.24
  114.0 15.1 %experts.4 = (bf16[2,448,768]{2,1,0:T(8,128)(2,1)}, bf16[2,448,768]{2,1,0:T(8,128)(2,1)}, bf16[3,416,768]{2,1,0:T(8,128)(2,1)}, bf16[3,416,768]{2,1,0:T(8,128)(2,1)}) custom-call(s32[1]{0:T(128)} %bitcast.4.refs_0_, s32[2,9]{1,0:T(2,128)} %slice.190.refs_1_, f32[3,1,768]{2,1,0:T(1,128)} %reshape.300.refs_2_, bf16[448,768]{1,0:T(8,128)(2,1)} %copy-done.14, ...), custom_call_target="tpu_custom_call" | custom-call | flops 5888802816 | bytes 8388608 | tf_op jit(solution)/shard_map/experts/pallas_call | solution.py:425
  129.1 1.4 slice_bitcast_fusion
  131.8 1.5 collective-permute-start.29
  133.3 10.6 %experts.5 = (bf16[1,448,768]{2,1,0:T(8,128)(2,1)}, bf16[1,448,768]{2,1,0:T(8,128)(2,1)}, bf16[3,208,768]{2,1,0:T(8,128)(2,1)}, bf16[3,208,768]{2,1,0:T(8,128)(2,1)}) custom-call(s32[1]{0:T(128)} %bitcast.4.refs_0_, s32[1,9]{1,0:T(1,128)} %get-tuple-element.162.refs_1_, f32[3,1,768]{2,1,0:T(1,128)} %reshape.300.refs_2_, ...), custom_call_target="tpu_custom_call" | custom-call | flops 2944401408 | bytes 8388608 | tf_op jit(solution)/shard_map/experts/pallas_call | solution.py:425
  143.9 1.5 collective-permute-start.30
  147.2 10.6 %experts.3 = (bf16[1,448,768]{2,1,0:T(8,128)(2,1)}, bf16[1,448,768]{2,1,0:T(8,128)(2,1)}, bf16[3,208,768]{2,1,0:T(8,128)(2,1)}, bf16[3,208,768]{2,1,0:T(8,128)(2,1)}) custom-call(s32[1]{0:T(128)} %bitcast.4.refs_0_, s32[1,9]{1,0:T(1,128)} %get-tuple-element.163.refs_1_, f32[3,1,768]{2,1,0:T(1,128)} %reshape.300.refs_2_, ...), custom_call_target="tpu_custom_call" | custom-call | flops 2944401408 | bytes 8388608 | tf_op jit(solution)/shard_map/experts/pallas_call | solution.py:425
  157.8 3.7 collective-permute-done.29.refs_9_
  162.4 8.5 %mix_out_backward.1 = (f32[416,768]{1,0:T(8,128)}, bf16[416,768]{1,0:T(8,128)(2,1)}, f32[16,768]{1,0:T(8,128)}, bf16[4,96,768]{2,1,0:T(8,128)(2,1)}, bf16[4,96,768]{2,1,0:T(8,128)(2,1)}) custom-call(s32[1]{0:T(128)} %bitcast.4.refs_0_, bf16[416,448]{1,0:T(8,128)(2,1)} %fusion.4.refs_0_.refs_1_, f32[416,768]{1,0:T(8,128)} %get-tuple-element.48.refs_1_.refs_2_, ...), custom_call_target="tpu_custom_call" | custom-call | flops 1472200704 | bytes 8388608 | tf_op jit(solution)/shard_map/mix_out_backward/pallas_call | solution.py:425
  172.3 1.6 collective-permute-start.21
  173.8 18.7 %expert_grads.1 = (bf16[1168,768]{1,0:T(8,128)(2,1)}, bf16[1168,768]{1,0:T(8,128)(2,1)}, bf16[4,3,96,768]{3,2,1,0:T(8,128)(2,1)}, bf16[4,3,96,768]{3,2,1,0:T(8,128)(2,1)}) custom-call(s32[1]{0:T(128)} %bitcast.4.refs_0_, s32[4,9]{1,0:T(4,128)} %copy-done.19, bf16[448,768]{1,0:T(8,128)(2,1)} %get-tuple-element.49.refs_3_.refs_2_, ...), custom_call_target="tpu_custom_call" | custom-call | flops 5888802816 | bytes 8388608 | tf_op jit(solution)/shard_map/expert_grads/pallas_call | solution.py:425
  192.9 1.5 collective-permute-start.41
  194.9 1.6 collective-permute-start.39
  197.3 3.3 collective-permute-done.41
  201.1 2.1 collective-permute-done.40
  203.2 1.4 collective-permute-start.27
  205.7 3.5 collective-permute-start.42
  209.2 20.4 %attention_backward.1 = (f32[416,768]{1,0:T(8,128)}, bf16[4,96,2432]{2,1,0:T(8,128)(2,1)}, bf16[4,96,2432]{2,1,0:T(8,128)(2,1)}) custom-call(s32[1]{0:T(128)} %bitcast.4.refs_0_, s32[1,4]{1,0:T(1,128)} %refs_1_.3, bf16[416,768]{1,0:T(8,128)(2,1)} %refs_2_.6, f32[16,768]{1,0:T(8,128)} %pad_convert_fusion.refs_3_.refs_4_, ...), custom_call_target="tpu_custom_call" | custom-call | flops 7361003520 | bytes 8388608 | tf_op jit(solution)/shard_map/attention_backward/pallas_call | solution.py:425
  230.0 2.7 collective-permute-done.22.refs_6_
  233.4 4.4 %finish_output.1 = bf16[416,768]{1,0:T(8,128)(2,1)} custom-call(bf16[416,448]{1,0:T(8,128)(2,1)} %fusion.4.refs_0_.refs_1_, f32[416,768]{1,0:T(8,128)} %get-tuple-element.48.refs_1_.refs_2_, s32[416,1]{1,0:T(8,128)} %copy.49.refs_2_, f32[16,768]{1,0:T(8,128)} %pad_convert_fusion.refs_3_.refs_4_, bf16[448,768]{1,0:T(8,128)(2,1)} %bitcast.112, ...), custom_call_target="tpu_custom_call" | custom-call | flops 572522496 | bytes 8388608 | tf_op jit(solution)/shard_map/finish_output/pallas_call | solution.py:425
  237.8 1.3 collective-permute-start.44
  239.1 2.5 add_convert_fusion.18
  241.7 1.5 collective-permute-start.51
  243.6 1.6 collective-permute-start.46
  246.6 5.7 %collective-permute-start.56 = (bf16[592,768]{1,0:T(8,128)(2,1)S(1)}, bf16[592,768]{1,0:T(8,128)(2,1)S(1)}, u32[]{:S(2)}, u32[]{:S(2)}) collective-permute-start(bf16[592,768]{1,0:T(8,128)(2,1)S(1)} %slice.277), channel_id=1, source_target_pairs={{0,1},{3,2},{4,5},{7,6},{8,9},{11,10},{12,13},{15,14},{16,17},{19,... | collective-permute-start | bytes 2727944 | tf_op jit(solution)/shard_map/ppermute | solution.py:992
  253.0 2.7 collective-permute-done.51
  255.7 6.3 %collective-permute-start.59 = (bf16[576,768]{1,0:T(8,128)(2,1)S(1)}, bf16[576,768]{1,0:T(8,128)(2,1)S(1)}, u32[]{:S(2)}, u32[]{:S(2)}) collective-permute-start(bf16[576,768]{1,0:T(8,128)(2,1)S(1)} %slice.279), channel_id=1, source_target_pairs={{0,1},{3,2},{4,5},{7,6},{8,9},{11,10},{12,13},{15,14},{16,17},{19,... | collective-permute-start | bytes 2654216 | tf_op jit(solution)/shard_map/ppermute | solution.py:992
  263.0 6.2 %collective-permute-start.52 = (bf16[2,3,96,768]{3,2,1,0:T(8,128)(2,1)S(1)}, bf16[2,3,96,768]{3,2,1,0:T(8,128)(2,1)S(1)}, u32[]{:S(2)}, u32[]{:S(2)}) collective-permute-start(bf16[2,3,96,768]{3,2,1,0:T(8,128)(2,1)S(1)} %pad_maximum_fusion.7), channel_id=1, source_target_pairs={{0,1},{3,2},{4,5},{7,6},{8,9},{11,10},{12,13},{15,14},{16,17},{19,... | collective-permute-start | bytes 2654216 | tf_op jit(solution)/shard_map/ppermute | solution.py:992
  269.7 1.5 collective-permute-start.34
  271.8 20.0 %collective-permute-done.59 = bf16[576,768]{1,0:T(8,128)(2,1)S(1)} collective-permute-done((bf16[576,768]{1,0:T(8,128)(2,1)S(1)}, bf16[576,768]{1,0:T(8,128)(2,1)S(1)}, u32[]{:S(2)}, u32[]{:S(2)}) %collective-permute-start.59) | collective-permute-done | bytes 884768 | tf_op jit(solution)/shard_map/ppermute | solution.py:992
  292.6 4.4 %collective-permute-start.47 = (bf16[2,3,96,768]{3,2,1,0:T(8,128)(2,1)S(1)}, bf16[2,3,96,768]{3,2,1,0:T(8,128)(2,1)S(1)}, u32[]{:S(2)}, u32[]{:S(2)}) collective-permute-start(bf16[2,3,96,768]{3,2,1,0:T(8,128)(2,1)S(1)} %pad_maximum_fusion.6), channel_id=1, source_target_pairs={{0,1},{3,2},{4,5},{7,6},{8,9},{11,10},{12,13},{15,14},{16,17},{19,... | collective-permute-start | bytes 2654216 | tf_op jit(solution)/shard_map/ppermute | solution.py:992
  298.7 1.6 collective-permute-done.32
  300.6 4.4 %collective-permute-start.35 = (bf16[96,2432]{1,0:T(8,128)(2,1)S(1)}, bf16[96,2432]{1,0:T(8,128)(2,1)S(1)}, u32[]{:S(2)}, u32[]{:S(2)}) collective-permute-start(bf16[96,2432]{1,0:T(8,128)(2,1)S(1)} %fusion.2), channel_id=1, source_target_pairs={{0,1},{3,2},{4,5},{7,6},{8,9},{11,10},{12,13},{15,14},{16,17},{19,... | collective-permute-start | bytes 1400840 | tf_op jit(solution)/shard_map/ppermute | solution.py:992
  305.1 5.7 %collective-permute-done.52 = bf16[2,3,96,768]{3,2,1,0:T(8,128)(2,1)S(1)} collective-permute-done((bf16[2,3,96,768]{3,2,1,0:T(8,128)(2,1)S(1)}, bf16[2,3,96,768]{3,2,1,0:T(8,128)(2,1)S(1)}, u32[]{:S(2)}, u32[]{:S(2)}) %collective-permute-start.52) | collective-permute-done | bytes 884768 | tf_op jit(solution)/shard_map/ppermute | solution.py:992
  311.7 18.0 %collective-permute-done.47 = bf16[2,3,96,768]{3,2,1,0:T(8,128)(2,1)S(1)} collective-permute-done((bf16[2,3,96,768]{3,2,1,0:T(8,128)(2,1)S(1)}, bf16[2,3,96,768]{3,2,1,0:T(8,128)(2,1)S(1)}, u32[]{:S(2)}, u32[]{:S(2)}) %collective-permute-start.47) | collective-permute-done | bytes 884768 | tf_op jit(solution)/shard_map/ppermute | solution.py:992
  330.9 5.4 %collective-permute-done.35 = bf16[96,2432]{1,0:T(8,128)(2,1)S(1)} collective-permute-done((bf16[96,2432]{1,0:T(8,128)(2,1)S(1)}, bf16[96,2432]{1,0:T(8,128)(2,1)S(1)}, u32[]{:S(2)}, u32[]{:S(2)}) %collective-permute-start.35) | collective-permute-done | bytes 466976 | tf_op jit(solution)/shard_map/ppermute | solution.py:992
  339.8 1.3 collective-permute-start.58
  341.3 1.3 collective-permute-start.37
  342.9 1.3 collective-permute-start.54
  346.8 47.7 %collective-permute-done.37 = bf16[96,2432]{1,0:T(8,128)(2,1)S(1)} collective-permute-done((bf16[96,2432]{1,0:T(8,128)(2,1)S(1)}, bf16[96,2432]{1,0:T(8,128)(2,1)S(1)}, u32[]{:S(2)}, u32[]{:S(2)}) %collective-permute-start.37) | collective-permute-done | bytes 466976 | tf_op jit(solution)/shard_map/ppermute | solution.py:1001
  399.8 2.1 convert.35
  402.5 11.1 %collective-permute-done.54 = bf16[2,3,96,768]{3,2,1,0:T(8,128)(2,1)} collective-permute-done((bf16[2,3,96,768]{3,2,1,0:T(8,128)(2,1)S(1)}, bf16[2,3,96,768]{3,2,1,0:T(8,128)(2,1)}, u32[]{:S(2)}, u32[]{:S(2)}) %collective-permute-start.54) | collective-permute-done | bytes 884768 | tf_op jit(solution)/shard_map/ppermute | solution.py:1001
  413.6 1.3 broadcast_select_fusion.2
  414.8 13.4 %collective-permute-done.49 = bf16[2,3,96,768]{3,2,1,0:T(8,128)(2,1)} collective-permute-done((bf16[2,3,96,768]{3,2,1,0:T(8,128)(2,1)}, bf16[2,3,96,768]{3,2,1,0:T(8,128)(2,1)}, u32[]{:S(2)}, u32[]{:S(2)}) %collective-permute-start.49) | collective-permute-done | bytes 884768 | tf_op jit(solution)/shard_map/ppermute | solution.py:1001
  430.6 2.2 copy.53
  (244 shorter events, 52.3 us)
Async XLA Ops:
  5.4 32.6 %collective-permute-start = (bf16[96,2304]{1,0:T(8,128)(2,1)}, bf16[96,2304]{1,0:T(8,128)(2,1)S(1)}, u32[]{:S(2)}, u32[]{:S(2)}) collective-permute-start(bf16[96,2304]{1,0:T(8,128)(2,1)} %constant_dynamic-update-slice_fusion.refs_4_.refs_10_), channel_id=1, source_target_pairs={{0,8},{4,12},{8,0},{12,4},{16,24},{20,28},{24,16},{28,20},{1,9},{5... | collective-permute-start | bytes 1327112 | tf_op jit(solution)/shard_map/ppermute | solution.py:946
  8.4 32.5 %collective-permute-start.1 = (bf16[96,2304]{1,0:T(8,128)(2,1)}, bf16[96,2304]{1,0:T(8,128)(2,1)}, u32[]{:S(2)}, u32[]{:S(2)}) collective-permute-start(bf16[96,2304]{1,0:T(8,128)(2,1)} %constant_dynamic-update-slice_fusion.refs_4_.refs_10_), channel_id=1, source_target_pairs={{0,16},{4,20},{8,24},{12,28},{16,0},{20,4},{24,8},{28,12},{1,17},{... | collective-permute-start | bytes 1327112 | tf_op jit(solution)/shard_map/ppermute | solution.py:946
  9.9 32.5 %collective-permute-start.4 = (bf16[96,2304]{1,0:T(8,128)(2,1)}, bf16[96,2304]{1,0:T(8,128)(2,1)}, u32[]{:S(2)}, u32[]{:S(2)}) collective-permute-start(bf16[96,2304]{1,0:T(8,128)(2,1)} %constant_dynamic-update-slice_fusion.refs_4_.refs_10_), channel_id=1, source_target_pairs={{0,4},{4,0},{8,12},{12,8},{16,20},{20,16},{24,28},{28,24},{1,5},{5... | collective-permute-start | bytes 1327112 | tf_op jit(solution)/shard_map/ppermute | solution.py:946
  11.6 48.4 %copy-start.1 = (bf16[416,768]{1,0:T(8,128)(2,1)S(1)}, bf16[416,768]{1,0:T(8,128)(2,1)}, u32[]{:S(2)}) copy-start(bf16[416,768]{1,0:T(8,128)(2,1)} %refs_3_.1) | copy-start | bytes 1916932
  12.9 50.8 %copy-start = (bf16[4,96,768]{2,1,0:T(8,128)(2,1)}, bf16[4,96,768]{2,1,0:T(8,128)(2,1)S(1)}, u32[]{:S(2)}) copy-start(bf16[4,96,768]{2,1,0:T(8,128)(2,1)S(1)} %get-tuple-element.161.refs_5_.refs_7_.refs_11_) | copy-start | bytes 1769476
  12.9 31.1 %collective-permute-start.9 = (bf16[4,96,768]{2,1,0:T(8,128)(2,1)}, bf16[4,96,768]{2,1,0:T(8,128)(2,1)S(1)}, u32[]{:S(2)}, u32[]{:S(2)}) collective-permute-start(bf16[4,96,768]{2,1,0:T(8,128)(2,1)} %get-tuple-element.159), channel_id=1, source_target_pairs={{0,8},{4,12},{8,0},{12,4},{16,24},{20,28},{24,16},{28,20},{1,9},{5... | collective-permute-start | bytes 1769480 | tf_op jit(solution)/shard_map/ppermute | solution.py:946
  13.4 30.5 %collective-permute-start.10 = (bf16[4,96,768]{2,1,0:T(8,128)(2,1)}, bf16[4,96,768]{2,1,0:T(8,128)(2,1)S(1)}, u32[]{:S(2)}, u32[]{:S(2)}) collective-permute-start(bf16[4,96,768]{2,1,0:T(8,128)(2,1)} %get-tuple-element.160), channel_id=1, source_target_pairs={{0,16},{4,20},{8,24},{12,28},{16,0},{20,4},{24,8},{28,12},{1,17},{... | collective-permute-start | bytes 1769480 | tf_op jit(solution)/shard_map/ppermute | solution.py:946
  38.0 17.3 %collective-permute-start.11 = (bf16[4,96,768]{2,1,0:T(8,128)(2,1)}, bf16[4,96,768]{2,1,0:T(8,128)(2,1)S(1)}, u32[]{:S(2)}, u32[]{:S(2)}) collective-permute-start(bf16[4,96,768]{2,1,0:T(8,128)(2,1)} %get-tuple-element.158), channel_id=1, source_target_pairs={{0,24},{4,28},{8,16},{12,20},{16,8},{20,12},{24,0},{28,4},{1,25},{... | collective-permute-start | bytes 1769480 | tf_op jit(solution)/shard_map/ppermute | solution.py:946
  40.8 18.6 %collective-permute-start.2 = (bf16[48,2304]{1,0:T(8,128)(2,1)S(1)}, bf16[48,2304]{1,0:T(8,128)(2,1)S(1)}, u32[]{:S(2)}, u32[]{:S(2)}) collective-permute-start(bf16[48,2304]{1,0:T(8,128)(2,1)S(1)} %slice.247), channel_id=1, source_target_pairs={{0,16},{4,20},{8,24},{12,28},{16,0},{20,4},{24,8},{28,12},{1,17},{... | collective-permute-start | bytes 663560 | tf_op jit(solution)/shard_map/ppermute | solution.py:946
  42.4 17.1 %collective-permute-start.3 = (bf16[48,2304]{1,0:T(8,128)(2,1)S(1)}, bf16[48,2304]{1,0:T(8,128)(2,1)S(1)}, u32[]{:S(2)}, u32[]{:S(2)}) collective-permute-start(bf16[48,2304]{1,0:T(8,128)(2,1)S(1)} %slice.248), channel_id=1, source_target_pairs={{0,8},{4,12},{8,0},{12,4},{16,24},{20,28},{24,16},{28,20},{1,9},{5... | collective-permute-start | bytes 663560 | tf_op jit(solution)/shard_map/ppermute | solution.py:946
  44.0 17.4 %collective-permute-start.5 = (bf16[96,2304]{1,0:T(8,128)(2,1)S(1)}, bf16[96,2304]{1,0:T(8,128)(2,1)S(1)}, u32[]{:S(2)}, u32[]{:S(2)}) collective-permute-start(bf16[96,2304]{1,0:T(8,128)(2,1)S(1)} %collective-permute-done.refs_5_.refs_11_), channel_id=1, source_target_pairs={{0,4},{4,0},{8,12},{12,8},{16,20},{20,16},{24,28},{28,24},{1,5},{5... | collective-permute-start | bytes 1327112 | tf_op jit(solution)/shard_map/ppermute | solution.py:946
  44.0 17.5 %collective-permute-start.6 = (bf16[96,2304]{1,0:T(8,128)(2,1)}, bf16[96,2304]{1,0:T(8,128)(2,1)S(1)}, u32[]{:S(2)}, u32[]{:S(2)}) collective-permute-start(bf16[96,2304]{1,0:T(8,128)(2,1)} %collective-permute-done.1.refs_6_.refs_12_), channel_id=1, source_target_pairs={{0,4},{4,0},{8,12},{12,8},{16,20},{20,16},{24,28},{28,24},{1,5},{5... | collective-permute-start | bytes 1327112 | tf_op jit(solution)/shard_map/ppermute | solution.py:946
  55.3 58.6 %collective-permute-start.16 = (bf16[3,384,768]{2,1,0:T(8,128)(2,1)}, bf16[3,384,768]{2,1,0:T(8,128)(2,1)}, u32[]{:S(2)}, u32[]{:S(2)}) collective-permute-start(bf16[3,384,768]{2,1,0:T(8,128)(2,1)} %refs_15_.3), channel_id=1, source_target_pairs={{0,4},{4,0},{8,12},{12,8},{16,20},{20,16},{24,28},{28,24},{1,5},{5... | collective-permute-start | bytes 5308424 | tf_op jit(solution)/shard_map/ppermute | solution.py:946
  59.4 2.5 collective-permute-start.7
  59.5 2.8 collective-permute-start.8
  61.4 15.6 %collective-permute-start.12 = (bf16[4,96,768]{2,1,0:T(8,128)(2,1)S(1)}, bf16[4,96,768]{2,1,0:T(8,128)(2,1)}, u32[]{:S(2)}, u32[]{:S(2)}) collective-permute-start(bf16[4,96,768]{2,1,0:T(8,128)(2,1)S(1)} %get-tuple-element.161.refs_5_.refs_7_.refs_11_), channel_id=1, source_target_pairs={{0,4},{4,0},{8,12},{12,8},{16,20},{20,16},{24,28},{28,24},{1,5},{5... | collective-permute-start | bytes 1769480 | tf_op jit(solution)/shard_map/ppermute | solution.py:946
  61.5 16.1 %collective-permute-start.13 = (bf16[4,96,768]{2,1,0:T(8,128)(2,1)S(1)}, bf16[4,96,768]{2,1,0:T(8,128)(2,1)}, u32[]{:S(2)}, u32[]{:S(2)}) collective-permute-start(bf16[4,96,768]{2,1,0:T(8,128)(2,1)S(1)} %collective-permute-done.9.refs_6_.refs_8_.refs_12_), channel_id=1, source_target_pairs={{0,4},{4,0},{8,12},{12,8},{16,20},{20,16},{24,28},{28,24},{1,5},{5... | collective-permute-start | bytes 1769480 | tf_op jit(solution)/shard_map/ppermute | solution.py:946
  61.9 17.2 %collective-permute-start.14 = (bf16[4,96,768]{2,1,0:T(8,128)(2,1)S(1)}, bf16[4,96,768]{2,1,0:T(8,128)(2,1)}, u32[]{:S(2)}, u32[]{:S(2)}) collective-permute-start(bf16[4,96,768]{2,1,0:T(8,128)(2,1)S(1)} %collective-permute-done.10.refs_7_.refs_9_.refs_13_), channel_id=1, source_target_pairs={{0,4},{4,0},{8,12},{12,8},{16,20},{20,16},{24,28},{28,24},{1,5},{5... | collective-permute-start | bytes 1769480 | tf_op jit(solution)/shard_map/ppermute | solution.py:946
  62.3 16.8 %collective-permute-start.15 = (bf16[4,96,768]{2,1,0:T(8,128)(2,1)S(1)}, bf16[4,96,768]{2,1,0:T(8,128)(2,1)}, u32[]{:S(2)}, u32[]{:S(2)}) collective-permute-start(bf16[4,96,768]{2,1,0:T(8,128)(2,1)S(1)} %collective-permute-done.11.refs_8_.refs_10_.refs_14_), channel_id=1, source_target_pairs={{0,4},{4,0},{8,12},{12,8},{16,20},{20,16},{24,28},{28,24},{1,5},{5... | collective-permute-start | bytes 1769480 | tf_op jit(solution)/shard_map/ppermute | solution.py:946
  77.0 18.7 %collective-permute-start.19 = (bf16[448,768]{1,0:T(8,128)(2,1)}, bf16[448,768]{1,0:T(8,128)(2,1)}, u32[]{:S(2)}, u32[]{:S(2)}) collective-permute-start(bf16[448,768]{1,0:T(8,128)(2,1)} %convolution_convert_fusion.refs_4_.refs_7_), channel_id=1, source_target_pairs={{0,8},{4,12},{8,0},{12,4},{16,24},{20,28},{24,16},{28,20},{1,9},{5... | collective-permute-start | bytes 2064392 | tf_op jit(solution)/shard_map/ppermute | solution.py:946
  77.6 19.7 %collective-permute-start.20 = (bf16[448,768]{1,0:T(8,128)(2,1)}, bf16[448,768]{1,0:T(8,128)(2,1)S(1)}, u32[]{:S(2)}, u32[]{:S(2)}) collective-permute-start(bf16[448,768]{1,0:T(8,128)(2,1)} %convolution_convert_fusion.refs_4_.refs_7_), channel_id=1, source_target_pairs={{0,16},{4,20},{8,24},{12,28},{16,0},{20,4},{24,8},{28,12},{1,17},{... | collective-permute-start | bytes 2064392 | tf_op jit(solution)/shard_map/ppermute | solution.py:946
  84.5 25.8 %collective-permute-start.17 = (bf16[448,768]{1,0:T(8,128)(2,1)}, bf16[448,768]{1,0:T(8,128)(2,1)S(1)}, u32[]{:S(2)}, u32[]{:S(2)}) collective-permute-start(bf16[448,768]{1,0:T(8,128)(2,1)} %get-tuple-element.49.refs_3_.refs_2_), channel_id=1, source_target_pairs={{0,8},{4,12},{8,0},{12,4},{16,24},{20,28},{24,16},{28,20},{1,9},{5... | collective-permute-start | bytes 2064392 | tf_op jit(solution)/shard_map/ppermute | solution.py:946
  85.1 26.6 %collective-permute-start.18 = (bf16[448,768]{1,0:T(8,128)(2,1)}, bf16[448,768]{1,0:T(8,128)(2,1)S(1)}, u32[]{:S(2)}, u32[]{:S(2)}) collective-permute-start(bf16[448,768]{1,0:T(8,128)(2,1)} %get-tuple-element.49.refs_3_.refs_2_), channel_id=1, source_target_pairs={{0,16},{4,20},{8,24},{12,28},{16,0},{20,4},{24,8},{28,12},{1,17},{... | collective-permute-start | bytes 2064392 | tf_op jit(solution)/shard_map/ppermute | solution.py:946
  96.6 34.5 %collective-permute-start.25 = (bf16[224,768]{1,0:T(8,128)(2,1)S(1)}, bf16[224,768]{1,0:T(8,128)(2,1)S(1)}, u32[]{:S(2)}, u32[]{:S(2)}) collective-permute-start(bf16[224,768]{1,0:T(8,128)(2,1)S(1)} %slice.252), channel_id=1, source_target_pairs={{0,16},{4,20},{8,24},{12,28},{16,0},{20,4},{24,8},{28,12},{1,17},{... | collective-permute-start | bytes 1032200 | tf_op jit(solution)/shard_map/ppermute | solution.py:946
  97.3 36.0 %collective-permute-start.26 = (bf16[224,768]{1,0:T(8,128)(2,1)S(1)}, bf16[224,768]{1,0:T(8,128)(2,1)}, u32[]{:S(2)}, u32[]{:S(2)}) collective-permute-start(bf16[224,768]{1,0:T(8,128)(2,1)S(1)} %slice.253), channel_id=1, source_target_pairs={{0,8},{4,12},{8,0},{12,4},{16,24},{20,28},{24,16},{28,20},{1,9},{5... | collective-permute-start | bytes 1032200 | tf_op jit(solution)/shard_map/ppermute | solution.py:946
  111.1 22.2 %collective-permute-start.23 = (bf16[224,768]{1,0:T(8,128)(2,1)}, bf16[224,768]{1,0:T(8,128)(2,1)}, u32[]{:S(2)}, u32[]{:S(2)}) collective-permute-start(bf16[224,768]{1,0:T(8,128)(2,1)} %slice.250), channel_id=1, source_target_pairs={{0,16},{4,20},{8,24},{12,28},{16,0},{20,4},{24,8},{28,12},{1,17},{... | collective-permute-start | bytes 1032200 | tf_op jit(solution)/shard_map/ppermute | solution.py:946
  112.5 20.8 %collective-permute-start.24 = (bf16[224,768]{1,0:T(8,128)(2,1)}, bf16[224,768]{1,0:T(8,128)(2,1)}, u32[]{:S(2)}, u32[]{:S(2)}) collective-permute-start(bf16[224,768]{1,0:T(8,128)(2,1)} %slice.251), channel_id=1, source_target_pairs={{0,8},{4,12},{8,0},{12,4},{16,24},{20,28},{24,16},{28,20},{1,9},{5... | collective-permute-start | bytes 1032200 | tf_op jit(solution)/shard_map/ppermute | solution.py:946
  130.5 27.3 %collective-permute-start.28 = (bf16[448,768]{1,0:T(8,128)(2,1)S(1)}, bf16[448,768]{1,0:T(8,128)(2,1)S(1)}, u32[]{:S(2)}, u32[]{:S(2)}) collective-permute-start(bf16[448,768]{1,0:T(8,128)(2,1)S(1)} %get-tuple-element.149), channel_id=1, source_target_pairs={{0,8},{4,12},{8,0},{12,4},{16,24},{20,28},{24,16},{28,20},{1,9},{5... | collective-permute-start | bytes 2064392 | tf_op jit(solution)/shard_map/ppermute | solution.py:946
  131.8 29.7 %collective-permute-start.29 = (bf16[448,768]{1,0:T(8,128)(2,1)S(1)}, bf16[448,768]{1,0:T(8,128)(2,1)S(1)}, u32[]{:S(2)}, u32[]{:S(2)}) collective-permute-start(bf16[448,768]{1,0:T(8,128)(2,1)S(1)} %get-tuple-element.148), channel_id=1, source_target_pairs={{0,16},{4,20},{8,24},{12,28},{16,0},{20,4},{24,8},{28,12},{1,17},{... | collective-permute-start | bytes 2064392 | tf_op jit(solution)/shard_map/ppermute | solution.py:946
  143.9 17.6 %collective-permute-start.30 = (bf16[448,768]{1,0:T(8,128)(2,1)}, bf16[448,768]{1,0:T(8,128)(2,1)}, u32[]{:S(2)}, u32[]{:S(2)}) collective-permute-start(bf16[448,768]{1,0:T(8,128)(2,1)} %bitcast.133), channel_id=1, source_target_pairs={{0,24},{4,28},{8,16},{12,20},{16,8},{20,12},{24,0},{28,4},{1,25},{... | collective-permute-start | bytes 2064392 | tf_op jit(solution)/shard_map/ppermute | solution.py:946
  171.0 21.8 %collective-permute-start.38 = (bf16[4,96,768]{2,1,0:T(8,128)(2,1)}, bf16[4,96,768]{2,1,0:T(8,128)(2,1)S(1)}, u32[]{:S(2)}, u32[]{:S(2)}) collective-permute-start(bf16[4,96,768]{2,1,0:T(8,128)(2,1)} %get-tuple-element.66), channel_id=1, source_target_pairs={{0,4},{4,0},{8,12},{12,8},{16,20},{20,16},{24,28},{28,24},{1,5},{5... | collective-permute-start | bytes 1769480 | tf_op jit(solution)/shard_map/ppermute | solution.py:946
  172.3 33.4 %collective-permute-start.21 = (bf16[448,768]{1,0:T(8,128)(2,1)}, bf16[448,768]{1,0:T(8,128)(2,1)S(1)}, u32[]{:S(2)}, u32[]{:S(2)}) collective-permute-start(bf16[448,768]{1,0:T(8,128)(2,1)} %get-tuple-element.151), channel_id=1, source_target_pairs={{0,8},{4,12},{8,0},{12,4},{16,24},{20,28},{24,16},{28,20},{1,9},{5... | collective-permute-start | bytes 2064392 | tf_op jit(solution)/shard_map/ppermute | solution.py:946
  192.5 46.6 %collective-permute-start.45 = (bf16[4,3,96,768]{3,2,1,0:T(8,128)(2,1)}, bf16[4,3,96,768]{3,2,1,0:T(8,128)(2,1)}, u32[]{:S(2)}, u32[]{:S(2)}) collective-permute-start(bf16[4,3,96,768]{3,2,1,0:T(8,128)(2,1)} %get-tuple-element.74), channel_id=1, source_target_pairs={{0,4},{4,0},{8,12},{12,8},{16,20},{20,16},{24,28},{28,24},{1,5},{5... | collective-permute-start | bytes 5308424 | tf_op jit(solution)/shard_map/ppermute | solution.py:946
  192.9 7.7 %collective-permute-start.41 = (bf16[96,768]{1,0:T(8,128)(2,1)S(1)}, bf16[96,768]{1,0:T(8,128)(2,1)S(1)}, u32[]{:S(2)}, u32[]{:S(2)}) collective-permute-start(bf16[96,768]{1,0:T(8,128)(2,1)S(1)} %get-tuple-element.153), channel_id=1, source_target_pairs={{0,24},{4,28},{8,16},{12,20},{16,8},{20,12},{24,0},{28,4},{1,25},{... | collective-permute-start | bytes 442376 | tf_op jit(solution)/shard_map/ppermute | solution.py:946
  194.4 8.8 %collective-permute-start.40 = (bf16[96,768]{1,0:T(8,128)(2,1)S(1)}, bf16[96,768]{1,0:T(8,128)(2,1)S(1)}, u32[]{:S(2)}, u32[]{:S(2)}) collective-permute-start(bf16[96,768]{1,0:T(8,128)(2,1)S(1)} %get-tuple-element.154), channel_id=1, source_target_pairs={{0,16},{4,20},{8,24},{12,28},{16,0},{20,4},{24,8},{28,12},{1,17},{... | collective-permute-start | bytes 442376 | tf_op jit(solution)/shard_map/ppermute | solution.py:946
  194.9 9.7 %collective-permute-start.39 = (bf16[96,768]{1,0:T(8,128)(2,1)S(1)}, bf16[96,768]{1,0:T(8,128)(2,1)}, u32[]{:S(2)}, u32[]{:S(2)}) collective-permute-start(bf16[96,768]{1,0:T(8,128)(2,1)S(1)} %get-tuple-element.152), channel_id=1, source_target_pairs={{0,8},{4,12},{8,0},{12,4},{16,24},{20,28},{24,16},{28,20},{1,9},{5... | collective-permute-start | bytes 442376 | tf_op jit(solution)/shard_map/ppermute | solution.py:946
  200.6 32.1 %collective-permute-start.22 = (bf16[448,768]{1,0:T(8,128)(2,1)}, bf16[448,768]{1,0:T(8,128)(2,1)}, u32[]{:S(2)}, u32[]{:S(2)}) collective-permute-start(bf16[448,768]{1,0:T(8,128)(2,1)} %get-tuple-element.150), channel_id=1, source_target_pairs={{0,16},{4,20},{8,24},{12,28},{16,0},{20,4},{24,8},{28,12},{1,17},{... | collective-permute-start | bytes 2064392 | tf_op jit(solution)/shard_map/ppermute | solution.py:946
  203.2 30.2 %collective-permute-start.27 = (bf16[448,768]{1,0:T(8,128)(2,1)}, bf16[448,768]{1,0:T(8,128)(2,1)}, u32[]{:S(2)}, u32[]{:S(2)}) collective-permute-start(bf16[448,768]{1,0:T(8,128)(2,1)} %bitcast.21), channel_id=1, source_target_pairs={{0,24},{4,28},{8,16},{12,20},{16,8},{20,12},{24,0},{28,4},{1,25},{... | collective-permute-start | bytes 2064392 | tf_op jit(solution)/shard_map/ppermute | solution.py:946
  204.6 39.0 %collective-permute-start.55 = (bf16[1168,768]{1,0:T(8,128)(2,1)}, bf16[1168,768]{1,0:T(8,128)(2,1)S(1)}, u32[]{:S(2)}, u32[]{:S(2)}) collective-permute-start(bf16[1168,768]{1,0:T(8,128)(2,1)} %get-tuple-element.76), channel_id=1, source_target_pairs={{0,4},{4,0},{8,12},{12,8},{16,20},{20,16},{24,28},{28,24},{1,5},{5... | collective-permute-start | bytes 5382152 | tf_op jit(solution)/shard_map/ppermute | solution.py:946
  205.7 23.9 %collective-permute-start.42 = (bf16[96,768]{1,0:T(8,128)(2,1)S(1)}, bf16[96,768]{1,0:T(8,128)(2,1)S(1)}, u32[]{:S(2)}, u32[]{:S(2)}) collective-permute-start(bf16[96,768]{1,0:T(8,128)(2,1)S(1)} %fusion.15), channel_id=1, source_target_pairs={{0,1},{3,2},{4,5},{7,6},{8,9},{11,10},{12,13},{15,14},{16,17},{19,... | collective-permute-start | bytes 442376 | tf_op jit(solution)/shard_map/ppermute | solution.py:992
  229.7 39.6 %collective-permute-start.31 = (bf16[4,96,2432]{2,1,0:T(8,128)(2,1)}, bf16[4,96,2432]{2,1,0:T(8,128)(2,1)S(1)}, u32[]{:S(2)}, u32[]{:S(2)}) collective-permute-start(bf16[4,96,2432]{2,1,0:T(8,128)(2,1)} %get-tuple-element.64), channel_id=1, source_target_pairs={{0,4},{4,0},{8,12},{12,8},{16,20},{20,16},{24,28},{28,24},{1,5},{5... | collective-permute-start | bytes 5603336 | tf_op jit(solution)/shard_map/ppermute | solution.py:946
  232.7 5.1 %collective-permute-start.43 = (bf16[96,768]{1,0:T(8,128)(2,1)S(1)}, bf16[96,768]{1,0:T(8,128)(2,1)S(1)}, u32[]{:S(2)}, u32[]{:S(2)}) collective-permute-start(bf16[96,768]{1,0:T(8,128)(2,1)S(1)} %add_convert_fusion.20), channel_id=1, source_target_pairs={{1,2},{2,1},{5,6},{6,5},{9,10},{10,9},{13,14},{14,13},{17,18},{18,... | collective-permute-start | bytes 442376 | tf_op jit(solution)/shard_map/ppermute | solution.py:996
  237.8 8.8 %collective-permute-start.44 = (bf16[96,768]{1,0:T(8,128)(2,1)S(1)}, bf16[96,768]{1,0:T(8,128)(2,1)S(1)}, u32[]{:S(2)}, u32[]{:S(2)}) collective-permute-start(bf16[96,768]{1,0:T(8,128)(2,1)S(1)} %add_convert_fusion.19), channel_id=1, source_target_pairs={{1,0},{2,3},{5,4},{6,7},{9,8},{10,11},{13,12},{14,15},{17,16},{18,... | collective-permute-start | bytes 442376 | tf_op jit(solution)/shard_map/ppermute | solution.py:1001
  241.7 14.1 %collective-permute-start.51 = (bf16[3,96,768]{2,1,0:T(8,128)(2,1)S(1)}, bf16[3,96,768]{2,1,0:T(8,128)(2,1)S(1)}, u32[]{:S(2)}, u32[]{:S(2)}) collective-permute-start(bf16[3,96,768]{2,1,0:T(8,128)(2,1)S(1)} %get-tuple-element.141), channel_id=1, source_target_pairs={{0,24},{4,28},{8,16},{12,20},{16,8},{20,12},{24,0},{28,4},{1,25},{... | collective-permute-start | bytes 1327112 | tf_op jit(solution)/shard_map/ppermute | solution.py:946
  243.1 19.8 %collective-permute-start.50 = (bf16[3,96,768]{2,1,0:T(8,128)(2,1)S(1)}, bf16[3,96,768]{2,1,0:T(8,128)(2,1)S(1)}, u32[]{:S(2)}, u32[]{:S(2)}) collective-permute-start(bf16[3,96,768]{2,1,0:T(8,128)(2,1)S(1)} %get-tuple-element.142), channel_id=1, source_target_pairs={{0,16},{4,20},{8,24},{12,28},{16,0},{20,4},{24,8},{28,12},{1,17},{... | collective-permute-start | bytes 1327112 | tf_op jit(solution)/shard_map/ppermute | solution.py:946
  243.6 25.6 %collective-permute-start.46 = (bf16[3,96,768]{2,1,0:T(8,128)(2,1)S(1)}, bf16[3,96,768]{2,1,0:T(8,128)(2,1)S(1)}, u32[]{:S(2)}, u32[]{:S(2)}) collective-permute-start(bf16[3,96,768]{2,1,0:T(8,128)(2,1)S(1)} %get-tuple-element.143), channel_id=1, source_target_pairs={{0,8},{4,12},{8,0},{12,4},{16,24},{20,28},{24,16},{28,20},{1,9},{5... | collective-permute-start | bytes 1327112 | tf_op jit(solution)/shard_map/ppermute | solution.py:946
  246.6 46.0 %collective-permute-start.56 = (bf16[592,768]{1,0:T(8,128)(2,1)S(1)}, bf16[592,768]{1,0:T(8,128)(2,1)S(1)}, u32[]{:S(2)}, u32[]{:S(2)}) collective-permute-start(bf16[592,768]{1,0:T(8,128)(2,1)S(1)} %slice.277), channel_id=1, source_target_pairs={{0,1},{3,2},{4,5},{7,6},{8,9},{11,10},{12,13},{15,14},{16,17},{19,... | collective-permute-start | bytes 2727944 | tf_op jit(solution)/shard_map/ppermute | solution.py:992
  255.7 36.0 %collective-permute-start.59 = (bf16[576,768]{1,0:T(8,128)(2,1)S(1)}, bf16[576,768]{1,0:T(8,128)(2,1)S(1)}, u32[]{:S(2)}, u32[]{:S(2)}) collective-permute-start(bf16[576,768]{1,0:T(8,128)(2,1)S(1)} %slice.279), channel_id=1, source_target_pairs={{0,1},{3,2},{4,5},{7,6},{8,9},{11,10},{12,13},{15,14},{16,17},{19,... | collective-permute-start | bytes 2654216 | tf_op jit(solution)/shard_map/ppermute | solution.py:992
  263.0 47.7 %collective-permute-start.52 = (bf16[2,3,96,768]{3,2,1,0:T(8,128)(2,1)S(1)}, bf16[2,3,96,768]{3,2,1,0:T(8,128)(2,1)S(1)}, u32[]{:S(2)}, u32[]{:S(2)}) collective-permute-start(bf16[2,3,96,768]{3,2,1,0:T(8,128)(2,1)S(1)} %pad_maximum_fusion.7), channel_id=1, source_target_pairs={{0,1},{3,2},{4,5},{7,6},{8,9},{11,10},{12,13},{15,14},{16,17},{19,... | collective-permute-start | bytes 2654216 | tf_op jit(solution)/shard_map/ppermute | solution.py:992
  269.7 27.5 %collective-permute-start.34 = (bf16[96,2432]{1,0:T(8,128)(2,1)S(1)}, bf16[96,2432]{1,0:T(8,128)(2,1)S(1)}, u32[]{:S(2)}, u32[]{:S(2)}) collective-permute-start(bf16[96,2432]{1,0:T(8,128)(2,1)S(1)} %get-tuple-element.138), channel_id=1, source_target_pairs={{0,24},{4,28},{8,16},{12,20},{16,8},{20,12},{24,0},{28,4},{1,25},{... | collective-permute-start | bytes 1400840 | tf_op jit(solution)/shard_map/ppermute | solution.py:946
  271.3 26.7 %collective-permute-start.33 = (bf16[96,2432]{1,0:T(8,128)(2,1)S(1)}, bf16[96,2432]{1,0:T(8,128)(2,1)S(1)}, u32[]{:S(2)}, u32[]{:S(2)}) collective-permute-start(bf16[96,2432]{1,0:T(8,128)(2,1)S(1)} %get-tuple-element.139), channel_id=1, source_target_pairs={{0,16},{4,20},{8,24},{12,28},{16,0},{20,4},{24,8},{28,12},{1,17},{... | collective-permute-start | bytes 1400840 | tf_op jit(solution)/shard_map/ppermute | solution.py:946
  291.8 8.6 %collective-permute-start.32 = (bf16[96,2432]{1,0:T(8,128)(2,1)S(1)}, bf16[96,2432]{1,0:T(8,128)(2,1)S(1)}, u32[]{:S(2)}, u32[]{:S(2)}) collective-permute-start(bf16[96,2432]{1,0:T(8,128)(2,1)S(1)} %get-tuple-element.137), channel_id=1, source_target_pairs={{0,8},{4,12},{8,0},{12,4},{16,24},{20,28},{24,16},{28,20},{1,9},{5... | collective-permute-start | bytes 1400840 | tf_op jit(solution)/shard_map/ppermute | solution.py:946
  292.6 37.1 %collective-permute-start.47 = (bf16[2,3,96,768]{3,2,1,0:T(8,128)(2,1)S(1)}, bf16[2,3,96,768]{3,2,1,0:T(8,128)(2,1)S(1)}, u32[]{:S(2)}, u32[]{:S(2)}) collective-permute-start(bf16[2,3,96,768]{3,2,1,0:T(8,128)(2,1)S(1)} %pad_maximum_fusion.6), channel_id=1, source_target_pairs={{0,1},{3,2},{4,5},{7,6},{8,9},{11,10},{12,13},{15,14},{16,17},{19,... | collective-permute-start | bytes 2654216 | tf_op jit(solution)/shard_map/ppermute | solution.py:992
  297.3 39.9 %collective-permute-start.60 = (bf16[576,768]{1,0:T(8,128)(2,1)S(1)}, bf16[576,768]{1,0:T(8,128)(2,1)S(1)}, u32[]{:S(2)}, u32[]{:S(2)}) collective-permute-start(bf16[576,768]{1,0:T(8,128)(2,1)S(1)} %add_convert_fusion.4), channel_id=1, source_target_pairs={{1,2},{2,1},{5,6},{6,5},{9,10},{10,9},{13,14},{14,13},{17,18},{18,... | collective-permute-start | bytes 2654216 | tf_op jit(solution)/shard_map/ppermute | solution.py:996
  298.0 41.6 %collective-permute-start.57 = (bf16[592,768]{1,0:T(8,128)(2,1)S(1)}, bf16[592,768]{1,0:T(8,128)(2,1)S(1)}, u32[]{:S(2)}, u32[]{:S(2)}) collective-permute-start(bf16[592,768]{1,0:T(8,128)(2,1)S(1)} %add_convert_fusion.2), channel_id=1, source_target_pairs={{1,2},{2,1},{5,6},{6,5},{9,10},{10,9},{13,14},{14,13},{17,18},{18,... | collective-permute-start | bytes 2727944 | tf_op jit(solution)/shard_map/ppermute | solution.py:996
  300.6 35.7 %collective-permute-start.35 = (bf16[96,2432]{1,0:T(8,128)(2,1)S(1)}, bf16[96,2432]{1,0:T(8,128)(2,1)S(1)}, u32[]{:S(2)}, u32[]{:S(2)}) collective-permute-start(bf16[96,2432]{1,0:T(8,128)(2,1)S(1)} %fusion.2), channel_id=1, source_target_pairs={{0,1},{3,2},{4,5},{7,6},{8,9},{11,10},{12,13},{15,14},{16,17},{19,... | collective-permute-start | bytes 1400840 | tf_op jit(solution)/shard_map/ppermute | solution.py:992
  311.0 31.6 %collective-permute-start.53 = (bf16[2,3,96,768]{3,2,1,0:T(8,128)(2,1)S(1)}, bf16[2,3,96,768]{3,2,1,0:T(8,128)(2,1)S(1)}, u32[]{:S(2)}, u32[]{:S(2)}) collective-permute-start(bf16[2,3,96,768]{3,2,1,0:T(8,128)(2,1)S(1)} %add_convert_fusion.6), channel_id=1, source_target_pairs={{1,2},{2,1},{5,6},{6,5},{9,10},{10,9},{13,14},{14,13},{17,18},{18,... | collective-permute-start | bytes 2654216 | tf_op jit(solution)/shard_map/ppermute | solution.py:996
  329.9 14.3 %collective-permute-start.48 = (bf16[2,3,96,768]{3,2,1,0:T(8,128)(2,1)S(1)}, bf16[2,3,96,768]{3,2,1,0:T(8,128)(2,1)S(1)}, u32[]{:S(2)}, u32[]{:S(2)}) collective-permute-start(bf16[2,3,96,768]{3,2,1,0:T(8,128)(2,1)S(1)} %add_convert_fusion.8), channel_id=1, source_target_pairs={{1,2},{2,1},{5,6},{6,5},{9,10},{10,9},{13,14},{14,13},{17,18},{18,... | collective-permute-start | bytes 2654216 | tf_op jit(solution)/shard_map/ppermute | solution.py:996
  336.4 4.7 %collective-permute-start.36 = (bf16[96,2432]{1,0:T(8,128)(2,1)S(1)}, bf16[96,2432]{1,0:T(8,128)(2,1)S(1)}, u32[]{:S(2)}, u32[]{:S(2)}) collective-permute-start(bf16[96,2432]{1,0:T(8,128)(2,1)S(1)} %add_convert_fusion.10), channel_id=1, source_target_pairs={{1,2},{2,1},{5,6},{6,5},{9,10},{10,9},{13,14},{14,13},{17,18},{18,... | collective-permute-start | bytes 1400840 | tf_op jit(solution)/shard_map/ppermute | solution.py:996
  338.3 58.8 %collective-permute-start.61 = (bf16[576,768]{1,0:T(8,128)(2,1)}, bf16[576,768]{1,0:T(8,128)(2,1)}, u32[]{:S(2)}, u32[]{:S(2)}) collective-permute-start(bf16[576,768]{1,0:T(8,128)(2,1)} %add_convert_fusion.3), channel_id=1, source_target_pairs={{1,0},{2,3},{5,4},{6,7},{9,8},{10,11},{13,12},{14,15},{17,16},{18,... | collective-permute-start | bytes 2654216 | tf_op jit(solution)/shard_map/ppermute | solution.py:1001
  339.8 58.5 %collective-permute-start.58 = (bf16[592,768]{1,0:T(8,128)(2,1)S(1)}, bf16[592,768]{1,0:T(8,128)(2,1)}, u32[]{:S(2)}, u32[]{:S(2)}) collective-permute-start(bf16[592,768]{1,0:T(8,128)(2,1)S(1)} %add_convert_fusion.1), channel_id=1, source_target_pairs={{1,0},{2,3},{5,4},{6,7},{9,8},{10,11},{13,12},{14,15},{17,16},{18,... | collective-permute-start | bytes 2727944 | tf_op jit(solution)/shard_map/ppermute | solution.py:1001
  341.3 53.2 %collective-permute-start.37 = (bf16[96,2432]{1,0:T(8,128)(2,1)S(1)}, bf16[96,2432]{1,0:T(8,128)(2,1)S(1)}, u32[]{:S(2)}, u32[]{:S(2)}) collective-permute-start(bf16[96,2432]{1,0:T(8,128)(2,1)S(1)} %add_convert_fusion.9), channel_id=1, source_target_pairs={{1,0},{2,3},{5,4},{6,7},{9,8},{10,11},{13,12},{14,15},{17,16},{18,... | collective-permute-start | bytes 1400840 | tf_op jit(solution)/shard_map/ppermute | solution.py:1001
  342.9 70.6 %collective-permute-start.54 = (bf16[2,3,96,768]{3,2,1,0:T(8,128)(2,1)S(1)}, bf16[2,3,96,768]{3,2,1,0:T(8,128)(2,1)}, u32[]{:S(2)}, u32[]{:S(2)}) collective-permute-start(bf16[2,3,96,768]{3,2,1,0:T(8,128)(2,1)S(1)} %add_convert_fusion.5), channel_id=1, source_target_pairs={{1,0},{2,3},{5,4},{6,7},{9,8},{10,11},{13,12},{14,15},{17,16},{18,... | collective-permute-start | bytes 2654216 | tf_op jit(solution)/shard_map/ppermute | solution.py:1001
  345.5 82.7 %collective-permute-start.49 = (bf16[2,3,96,768]{3,2,1,0:T(8,128)(2,1)}, bf16[2,3,96,768]{3,2,1,0:T(8,128)(2,1)}, u32[]{:S(2)}, u32[]{:S(2)}) collective-permute-start(bf16[2,3,96,768]{3,2,1,0:T(8,128)(2,1)} %add_convert_fusion.7), channel_id=1, source_target_pairs={{1,0},{2,3},{5,4},{6,7},{9,8},{10,11},{13,12},{14,15},{17,16},{18,... | collective-permute-start | bytes 2654216 | tf_op jit(solution)/shard_map/ppermute | solution.py:1001
  (34 other events, 308.6 us)

commit v3 on v0

--- a/solution.py
+++ b/solution.py
@@ -1,8 +1,12 @@
 import jax
 import jax.numpy as jnp
 from jax import lax
+from jax.experimental import pallas as pl
+from jax.experimental.pallas import tpu as pltpu
 from jax.sharding import PartitionSpec as P
 
+FSDP = "fsdp"
+REP = "rep"
 HEAD = 64
 EXPERTS = 3
 CAP = 208
@@ -44,7 +48,7 @@
     )
 
 
-def per_device(
+def per_device_weights(
     tokens,
     starts,
     routes,
@@ -73,15 +77,15 @@
     head_shape = (seq_rows, seq_len, head_count, HEAD)
     scale_factor = HEAD ** (-0.5)
     gain_one, shift_one, w_query, b_query, w_key, w_value, b_value, w_out, b_out = (
-        lax.all_gather(norm1_gain, "fsdp", axis=0, tiled=True),
-        lax.all_gather(norm1_bias, "fsdp", axis=0, tiled=True),
-        lax.all_gather(query_weight, "fsdp", axis=0, tiled=True),
-        lax.all_gather(query_bias, "fsdp", axis=0, tiled=True),
-        lax.all_gather(key_weight, "fsdp", axis=0, tiled=True),
-        lax.all_gather(value_weight, "fsdp", axis=0, tiled=True),
-        lax.all_gather(value_bias, "fsdp", axis=0, tiled=True),
-        lax.all_gather(out_weight, "fsdp", axis=0, tiled=True),
-        lax.all_gather(out_bias, "fsdp", axis=0, tiled=True),
+        lax.all_gather(norm1_gain, FSDP, axis=0, tiled=True),
+        lax.all_gather(norm1_bias, FSDP, axis=0, tiled=True),
+        lax.all_gather(query_weight, FSDP, axis=0, tiled=True),
+        lax.all_gather(query_bias, FSDP, axis=0, tiled=True),
+        lax.all_gather(key_weight, FSDP, axis=0, tiled=True),
+        lax.all_gather(value_weight, FSDP, axis=0, tiled=True),
+        lax.all_gather(value_bias, FSDP, axis=0, tiled=True),
+        lax.all_gather(out_weight, FSDP, axis=0, tiled=True),
+        lax.all_gather(out_bias, FSDP, axis=0, tiled=True),
     )
     resid_in = tokens.astype(jnp.float32)
     normed_one = normalize(
@@ -133,12 +137,12 @@
         + b_out.astype(jnp.float32)
     )
     gain_two, shift_two, w_in, b_in, w_down, b_down = (
-        lax.all_gather(norm2_gain, "fsdp", axis=0, tiled=True),
-        lax.all_gather(norm2_bias, "fsdp", axis=0, tiled=True),
-        lax.all_gather(expert_in, "fsdp", axis=1, tiled=True),
-        lax.all_gather(expert_in_bias, "fsdp", axis=1, tiled=True),
-        lax.all_gather(expert_out, "fsdp", axis=1, tiled=True),
-        lax.all_gather(expert_out_bias, "fsdp", axis=1, tiled=True),
+        lax.all_gather(norm2_gain, FSDP, axis=0, tiled=True),
+        lax.all_gather(norm2_bias, FSDP, axis=0, tiled=True),
+        lax.all_gather(expert_in, FSDP, axis=1, tiled=True),
+        lax.all_gather(expert_in_bias, FSDP, axis=1, tiled=True),
+        lax.all_gather(expert_out, FSDP, axis=1, tiled=True),
+        lax.all_gather(expert_out_bias, FSDP, axis=1, tiled=True),
     )
     normed_two = normalize(
         hidden, gain_two.astype(jnp.float32), shift_two.astype(jnp.float32)
@@ -165,9 +169,9 @@
     routed = result.reshape(EXPERTS * CAP, model_width)[slot_ids]
     output = (hidden + routed).astype(jnp.bfloat16)
     gain_two_back, w_in_back, w_down_back = (
-        lax.all_gather(norm2_gain, "fsdp", axis=0, tiled=True),
-        lax.all_gather(expert_in, "fsdp", axis=1, tiled=True),
-        lax.all_gather(expert_out, "fsdp", axis=1, tiled=True),
+        lax.all_gather(norm2_gain, FSDP, axis=0, tiled=True),
+        lax.all_gather(expert_in, FSDP, axis=1, tiled=True),
+        lax.all_gather(expert_out, FSDP, axis=1, tiled=True),
     )
     grad_output = cotangent.astype(jnp.float32)
     grad_packed = (
@@ -194,37 +198,37 @@
     grad_hidden = grad_output + grad_from_norm
     column_in, column_down = (
         lax.psum_scatter(
-            grad_in.astype(jnp.bfloat16), "rep", scatter_dimension=2, tiled=True
+            grad_in.astype(jnp.bfloat16), REP, scatter_dimension=2, tiled=True
         ).astype(jnp.float32),
         lax.psum_scatter(
-            grad_down.astype(jnp.bfloat16), "rep", scatter_dimension=2, tiled=True
+            grad_down.astype(jnp.bfloat16), REP, scatter_dimension=2, tiled=True
         ).astype(jnp.float32),
     )
     share_in, share_down, part_gain_two, part_shift_two, part_in_bias, part_down_bias = (
-        lax.psum_scatter(column_in, "fsdp", scatter_dimension=1, tiled=True),
-        lax.psum_scatter(column_down, "fsdp", scatter_dimension=1, tiled=True),
-        lax.psum_scatter(grad_gain_two, "fsdp", scatter_dimension=0, tiled=True),
-        lax.psum_scatter(grad_shift_two, "fsdp", scatter_dimension=0, tiled=True),
-        lax.psum_scatter(grad_in_bias, "fsdp", scatter_dimension=1, tiled=True),
-        lax.psum_scatter(grad_down_bias, "fsdp", scatter_dimension=1, tiled=True),
+        lax.psum_scatter(column_in, FSDP, scatter_dimension=1, tiled=True),
+        lax.psum_scatter(column_down, FSDP, scatter_dimension=1, tiled=True),
+        lax.psum_scatter(grad_gain_two, FSDP, scatter_dimension=0, tiled=True),
+        lax.psum_scatter(grad_shift_two, FSDP, scatter_dimension=0, tiled=True),
+        lax.psum_scatter(grad_in_bias, FSDP, scatter_dimension=1, tiled=True),
+        lax.psum_scatter(grad_down_bias, FSDP, scatter_dimension=1, tiled=True),
     )
     sum_in, sum_down, stack_gain_two, stack_shift_two, stack_in_bias, stack_down_bias = (
-        lax.all_gather(share_in.astype(jnp.bfloat16), "rep", axis=2, tiled=True).astype(
+        lax.all_gather(share_in.astype(jnp.bfloat16), REP, axis=2, tiled=True).astype(
             share_in.dtype
         ),
-        lax.all_gather(share_down.astype(jnp.bfloat16), "rep", axis=2, tiled=True).astype(
+        lax.all_gather(share_down.astype(jnp.bfloat16), REP, axis=2, tiled=True).astype(
             share_down.dtype
         ),
-        lax.all_gather(part_gain_two[None].astype(jnp.bfloat16), "rep", axis=0, tiled=True).astype(
+        lax.all_gather(part_gain_two[None].astype(jnp.bfloat16), REP, axis=0, tiled=True).astype(
             jnp.float32
         ),
-        lax.all_gather(part_shift_two[None].astype(jnp.bfloat16), "rep", axis=0, tiled=True).astype(
+        lax.all_gather(part_shift_two[None].astype(jnp.bfloat16), REP, axis=0, tiled=True).astype(
             jnp.float32
         ),
-        lax.all_gather(part_in_bias[None].astype(jnp.bfloat16), "rep", axis=0, tiled=True).astype(
+        lax.all_gather(part_in_bias[None].astype(jnp.bfloat16), REP, axis=0, tiled=True).astype(
             jnp.float32
         ),
-        lax.all_gather(part_down_bias[None].astype(jnp.bfloat16), "rep", axis=0, tiled=True).astype(
+        lax.all_gather(part_down_bias[None].astype(jnp.bfloat16), REP, axis=0, tiled=True).astype(
             jnp.float32
         ),
     )
@@ -233,11 +237,11 @@
     sum_in_bias = jnp.sum(stack_in_bias, 0)
     sum_down_bias = jnp.sum(stack_down_bias, 0)
     gain_one_back, w_query_back, w_key_back, w_value_back, w_out_back = (
-        lax.all_gather(norm1_gain, "fsdp", axis=0, tiled=True),
-        lax.all_gather(query_weight, "fsdp", axis=0, tiled=True),
-        lax.all_gather(key_weight, "fsdp", axis=0, tiled=True),
-        lax.all_gather(value_weight, "fsdp", axis=0, tiled=True),
-        lax.all_gather(out_weight, "fsdp", axis=0, tiled=True),
+        lax.all_gather(norm1_gain, FSDP, axis=0, tiled=True),
+        lax.all_gather(query_weight, FSDP, axis=0, tiled=True),
+        lax.all_gather(key_weight, FSDP, axis=0, tiled=True),
+        lax.all_gather(value_weight, FSDP, axis=0, tiled=True),
+        lax.all_gather(out_weight, FSDP, axis=0, tiled=True),
     )
     grad_branch = grad_hidden.astype(jnp.bfloat16)
     grad_out_bias = jnp.sum(grad_branch.astype(jnp.float32), 0)
@@ -300,16 +304,16 @@
     input_grad = grad_hidden + grad_from_first
     column_query, column_key, column_value, column_out = (
         lax.psum_scatter(
-            grad_query_weight.astype(jnp.bfloat16), "rep", scatter_dimension=1, tiled=True
+            grad_query_weight.astype(jnp.bfloat16), REP, scatter_dimension=1, tiled=True
         ).astype(jnp.float32),
         lax.psum_scatter(
-            grad_key_weight.astype(jnp.bfloat16), "rep", scatter_dimension=1, tiled=True
+            grad_key_weight.astype(jnp.bfloat16), REP, scatter_dimension=1, tiled=True
         ).astype(jnp.float32),
         lax.psum_scatter(
-            grad_value_weight.astype(jnp.bfloat16), "rep", scatter_dimension=1, tiled=True
+            grad_value_weight.astype(jnp.bfloat16), REP, scatter_dimension=1, tiled=True
         ).astype(jnp.float32),
         lax.psum_scatter(
-            grad_out_weight.astype(jnp.bfloat16), "rep", scatter_dimension=1, tiled=True
+            grad_out_weight.astype(jnp.bfloat16), REP, scatter_dimension=1, tiled=True
         ).astype(jnp.float32),
     )
     (
@@ -323,15 +327,15 @@
         part_value_bias,
         part_out_bias,
     ) = (
-        lax.psum_scatter(column_query, "fsdp", scatter_dimension=0, tiled=True),
-        lax.psum_scatter(column_key, "fsdp", scatter_dimension=0, tiled=True),
-        lax.psum_scatter(column_value, "fsdp", scatter_dimension=0, tiled=True),
-        lax.psum_scatter(column_out, "fsdp", scatter_dimension=0, tiled=True),
-        lax.psum_scatter(grad_gain_one, "fsdp", scatter_dimension=0, tiled=True),
-        lax.psum_scatter(grad_shift_one, "fsdp", scatter_dimension=0, tiled=True),
-        lax.psum_scatter(grad_query_bias, "fsdp", scatter_dimension=0, tiled=True),
-        lax.psum_scatter(grad_value_bias, "fsdp", scatter_dimension=0, tiled=True),
-        lax.psum_scatter(grad_out_bias, "fsdp", scatter_dimension=0, tiled=True),
+        lax.psum_scatter(column_query, FSDP, scatter_dimension=0, tiled=True),
+        lax.psum_scatter(column_key, FSDP, scatter_dimension=0, tiled=True),
+        lax.psum_scatter(column_value, FSDP, scatter_dimension=0, tiled=True),
+        lax.psum_scatter(column_out, FSDP, scatter_dimension=0, tiled=True),
+        lax.psum_scatter(grad_gain_one, FSDP, scatter_dimension=0, tiled=True),
+        lax.psum_scatter(grad_shift_one, FSDP, scatter_dimension=0, tiled=True),
+        lax.psum_scatter(grad_query_bias, FSDP, scatter_dimension=0, tiled=True),
+        lax.psum_scatter(grad_value_bias, FSDP, scatter_dimension=0, tiled=True),
+        lax.psum_scatter(grad_out_bias, FSDP, scatter_dimension=0, tiled=True),
     )
     (
         sum_query,
@@ -344,31 +348,31 @@
         stack_value_bias,
         stack_out_bias,
     ) = (
-        lax.all_gather(share_query.astype(jnp.bfloat16), "rep", axis=1, tiled=True).astype(
+        lax.all_gather(share_query.astype(jnp.bfloat16), REP, axis=1, tiled=True).astype(
             share_query.dtype
         ),
-        lax.all_gather(share_key.astype(jnp.bfloat16), "rep", axis=1, tiled=True).astype(
+        lax.all_gather(share_key.astype(jnp.bfloat16), REP, axis=1, tiled=True).astype(
             share_key.dtype
         ),
-        lax.all_gather(share_value.astype(jnp.bfloat16), "rep", axis=1, tiled=True).astype(
+        lax.all_gather(share_value.astype(jnp.bfloat16), REP, axis=1, tiled=True).astype(
             share_value.dtype
         ),
-        lax.all_gather(share_out.astype(jnp.bfloat16), "rep", axis=1, tiled=True).astype(
+        lax.all_gather(share_out.astype(jnp.bfloat16), REP, axis=1, tiled=True).astype(
             share_out.dtype
         ),
-        lax.all_gather(part_gain_one[None].astype(jnp.bfloat16), "rep", axis=0, tiled=True).astype(
+        lax.all_gather(part_gain_one[None].astype(jnp.bfloat16), REP, axis=0, tiled=True).astype(
             jnp.float32
         ),
-        lax.all_gather(part_shift_one[None].astype(jnp.bfloat16), "rep", axis=0, tiled=True).astype(
+        lax.all_gather(part_shift_one[None].astype(jnp.bfloat16), REP, axis=0, tiled=True).astype(
             jnp.float32
         ),
         lax.all_gather(
-            part_query_bias[None].astype(jnp.bfloat16), "rep", axis=0, tiled=True
+            part_query_bias[None].astype(jnp.bfloat16), REP, axis=0, tiled=True
         ).astype(jnp.float32),
         lax.all_gather(
-            part_value_bias[None].astype(jnp.bfloat16), "rep", axis=0, tiled=True
+            part_value_bias[None].astype(jnp.bfloat16), REP, axis=0, tiled=True
         ).astype(jnp.float32),
-        lax.all_gather(part_out_bias[None].astype(jnp.bfloat16), "rep", axis=0, tiled=True).astype(
+        lax.all_gather(part_out_bias[None].astype(jnp.bfloat16), REP, axis=0, tiled=True).astype(
             jnp.float32
         ),
     )
@@ -398,47 +402,1332 @@
     )
 
 
+LANES = 128
+BF = jnp.bfloat16
+F32 = jnp.float32
+VMEM_BYTES = 60 * 1024 * 1024
+SMEM = pl.BlockSpec(memory_space=pltpu.SMEM)
+VMEM = pl.BlockSpec(memory_space=pltpu.VMEM)
+ANYWHERE = pl.BlockSpec(memory_space=pl.ANY)
+
+
+def dot_nn(a, b):
+    return lax.dot_general(a, b, (((1,), (0,)), ((), ())), preferred_element_type=F32)
+
+
+def dot_nt(a, b):
+    return lax.dot_general(a, b, (((1,), (1,)), ((), ())), preferred_element_type=F32)
+
+
+def dot_tn(a, b):
+    return lax.dot_general(a, b, (((0,), (0,)), ((), ())), preferred_element_type=F32)
+
+
+def kernel_call(body, named, out_shape, in_specs, out_specs, scratch, args, alias=None):
+    return pl.pallas_call(
+        body,
+        out_shape=out_shape,
+        in_specs=in_specs,
+        out_specs=out_specs,
+        scratch_shapes=scratch,
+        input_output_aliases=alias or {},
+        compiler_params=pltpu.CompilerParams(vmem_limit_bytes=VMEM_BYTES),
+        name=named.__name__,
+    )(*args)
+
+
+def hold(values, done):
+    shapes = tuple(jax.ShapeDtypeStruct(v.shape, v.dtype) for v in values)
+    return kernel_call(
+        lambda *refs: None,
+        hold,
+        shapes,
+        [ANYWHERE] * (len(values) + len(done)),
+        (ANYWHERE,) * len(values),
+        [],
+        (*values, *done),
+        {i: i for i in range(len(values))},
+    )
+
+
+def sds(shape, dtype=BF):
+    return jax.ShapeDtypeStruct(shape, dtype)
+
+
+def center(v):
+    mean = jnp.mean(v, -1, keepdims=True)
+    centred = v - mean
+    inverse = lax.rsqrt(jnp.mean(centred * centred, -1, keepdims=True) + EPSILON)
+    return centred * inverse, inverse
+
+
+def norm_grad(normed, inverse, gain, gradient):
+    dn = gradient * gain
+    return inverse * (
+        dn - jnp.mean(dn, -1, keepdims=True) - normed * jnp.mean(dn * normed, -1, keepdims=True)
+    )
+
+
+def exact_rows(place, v):
+    high = v.astype(BF)
+    rest = (v - high.astype(F32)).astype(BF)
+    return dot_nn(place, high) + dot_nn(place, rest)
+
+
+def segment_bias(starts, length, segs):
+    col = lax.broadcasted_iota(jnp.int32, (length, 1), 0)
+    row = lax.broadcasted_iota(jnp.int32, (1, length), 1)
+    col_seg = jnp.zeros((length, 1), jnp.int32)
+    row_seg = jnp.zeros((1, length), jnp.int32)
+    for k in range(segs):
+        col_seg = col_seg + jnp.where(col >= starts[0, k], 1, 0)
+        row_seg = row_seg + jnp.where(row >= starts[0, k], 1, 0)
+    return jnp.where(col_seg == row_seg, 0.0, MASKED)
+
+
+def cuts(layout, start, count):
+    found = []
+    for i, part, mask, offset, rows in layout:
+        low, high = max(offset, start), min(offset + rows, start + count)
+        if low < high:
+            found.append((i, part, mask, low - offset, low - start, high - low))
+    return found
+
+
+def rows_of(ref, part, row, rows):
+    return ref.at[pl.ds(row, rows)] if part is None else ref.at[part, pl.ds(row, rows)]
+
+
+def load_weight(me, refs, layout, segment, shard, dst, sems):
+    copies = []
+    for k, (i, part, mask, row, at, rows) in enumerate(cuts(layout, segment * shard, shard)):
+        to = pl.multiple_of((me ^ mask) * shard + at, 16)
+        src = rows_of(refs[i], part, row, rows)
+        copy = pltpu.make_async_copy(src, dst.at[pl.ds(to, rows)], sems.at[k])
+        copy.start()
+        copies.append(copy)
+    return copies
+
+
+def attention_forward(n, layout, segs, n_vec, *refs):
+    count = 1 + max(i for i, *_ in layout)
+    me_ref, starts, tokens = refs[:3]
+    pieces = refs[3 : 3 + count]
+    qkv, mixed, lse, n1_out, vec, b_in = refs[3 + count : 9 + count]
+    weights, smalls, v_t, mixed_t, bias, sems, small_sems = refs[9 + count :]
+    tok, width = tokens.shape
+    shard = width // n
+    me = me_ref[0]
+    small_copies = []
+    for k, (i, part, mask, row, at, rows) in enumerate(cuts(layout, 4 * shard, 16)):
+        copy = pltpu.make_async_copy(
+            rows_of(pieces[i], part, row, rows),
+            smalls.at[mask, pl.ds(at, rows)],
+            small_sems.at[k],
+        )
+        copy.start()
+        small_copies.append(copy)
+    copies = []
+    for i in range(3):
+        cols = weights.at[:, pl.ds(i * width, width)]
+        copies.append(load_weight(me, pieces, layout, i, shard, cols, sems.at[i]))
+    bias[...] = segment_bias(starts, tok, segs)
+    normed, _ = center(tokens[...].astype(F32))
+    for copy in small_copies:
+        copy.wait()
+    lane = lax.broadcasted_iota(jnp.int32, (LANES, width), 0)
+    col = lax.broadcasted_iota(jnp.int32, (LANES, width), 1)
+    total = jnp.zeros((16, width), F32)
+    for m in range(n):
+        spread = ((col - (me ^ m) * shard == lane) & (lane < shard)).astype(F32).astype(BF)
+        total = total + dot_nn(smalls[m, :, :LANES], spread)
+    vec[...] = total
+    half_ff = width // 2
+    mine, other = smalls[0].astype(F32)[:, :half_ff], smalls[1].astype(F32)[:, :half_ff]
+    first = me % 2 == 0
+    b_in[:, :half_ff] = jnp.where(first, mine, other)
+    b_in[:, half_ff:] = jnp.where(first, other, mine)
+    n1_out[...] = (normed * vec[0:1, :] + vec[1:2, :]).astype(BF)
+    for i in range(3):
+        for copy in copies[i]:
+            copy.wait()
+        part = dot_nn(n1_out[...], weights[:, i * width : (i + 1) * width])
+        if i != 1:
+            part = part + (vec[2:3, :] if i == 0 else vec[3:4, :])
+        part = part.astype(BF)
+        if i == 0:
+            part = part * jnp.asarray(HEAD**-0.5, BF)
+        qkv[:, i * width : (i + 1) * width] = part
+    v_t[...] = qkv[:, 2 * width :].T
+    half = lax.broadcasted_iota(jnp.int32, (1, LANES), 1) < HEAD
+
+    def pair(p, carry):
+        at = pl.multiple_of(p * LANES, LANES)
+        q_pair = qkv[:, pl.ds(at, LANES)]
+        k_pair = qkv[:, pl.ds(pl.multiple_of(width + p * LANES, LANES), LANES)]
+        for s in range(2):
+            q_one = jnp.where(half if s == 0 else ~half, q_pair, jnp.zeros_like(q_pair))
+            scores = dot_nt(k_pair, q_one) + bias[...]
+            top = jnp.max(scores, 0, keepdims=True)
+            e = jnp.exp(scores - top)
+            total = jnp.sum(e, 0, keepdims=True)
+            probs = (e * (1.0 / total)).astype(BF)
+            rows = pl.ds(pl.multiple_of(p * LANES + s * HEAD, HEAD), HEAD)
+            mixed_t[rows, :] = dot_nn(v_t[rows, :], probs)
+            lse[pl.ds(2 * p + s, 1), :] = top + jnp.log(total)
+        return carry
+
+    lax.fori_loop(0, width // LANES, pair, 0)
+    mixed[...] = mixed_t[...].T.astype(BF)
+
+
+def call_attention_forward(n, me, starts, tokens, pieces, layout, n_vec):
+    tok, width = tokens.shape
+    heads16 = (width // HEAD + 7) // 8 * 8
+    f32_row = sds((16, width), F32)
+    return kernel_call(
+        lambda *refs: attention_forward(n, layout, starts.shape[1], n_vec, *refs),
+        attention_forward,
+        (sds((tok, 3 * width)), sds((tok, width)), sds((heads16, tok), F32), sds((tok, width)))
+        + (f32_row, f32_row),
+        [SMEM, SMEM, VMEM] + [ANYWHERE] * len(pieces),
+        (VMEM,) * 6,
+        [
+            pltpu.VMEM((width, 3 * width), BF),
+            pltpu.VMEM((n, 16, width), BF),
+            pltpu.VMEM((width, tok), BF),
+            pltpu.VMEM((width, tok), F32),
+            pltpu.VMEM((tok, tok), F32),
+            pltpu.SemaphoreType.DMA((3, len(layout))),
+            pltpu.SemaphoreType.DMA((len(layout),)),
+        ],
+        (me, starts, tokens, *pieces),
+    )
+
+
+def head_grads(first, pairs, width, qkv, lse, g_mixed, bias, k_t, gq_t, g_qkv):
+    half = lax.broadcasted_iota(jnp.int32, (1, LANES), 1) < HEAD
+    span = pairs * LANES
+
+    def pair(p, carry):
+        def cols(part):
+            return pl.ds(pl.multiple_of(part * width + (first + p) * LANES, LANES), LANES)
+
+        def put(part):
+            return pl.ds(pl.multiple_of(part * span + p * LANES, LANES), LANES)
+
+        q_pair, k_pair, v_pair = qkv[:, cols(0)], qkv[:, cols(1)], qkv[:, cols(2)]
+        gm_pair = g_mixed[:, cols(0)]
+        gv, gk = [], []
+        for s in range(2):
+            own = half if s == 0 else ~half
+            q_one = jnp.where(own, q_pair, jnp.zeros_like(q_pair))
+            gm_one = jnp.where(own, gm_pair, jnp.zeros_like(gm_pair))
+            scores = dot_nt(k_pair, q_one) + bias[...]
+            probs = jnp.exp(scores - lse[pl.ds(2 * (first + p) + s, 1), :])
+            g_probs = dot_nt(v_pair, gm_one)
+            delta = jnp.sum(probs * g_probs, 0, keepdims=True)
+            g_scores = (probs * (g_probs - delta)).astype(BF)
+            gv.append(dot_nn(probs.astype(BF), gm_pair))
+            gk.append(dot_nn(g_scores, q_pair))
+            rows = pl.ds(pl.multiple_of(p * LANES + s * HEAD, HEAD), HEAD)
+            gq_t[rows, :] = dot_nn(k_t[rows, :], g_scores)
+        g_qkv[:, put(2)] = jnp.where(half, gv[0], gv[1]).astype(BF)
+        g_qkv[:, put(1)] = jnp.where(half, gk[0], gk[1]).astype(BF)
+        return carry
+
+    at = slice(width + first * LANES, width + first * LANES + span)
+    k_t[...] = qkv[:, at].T
+    lax.fori_loop(0, pairs, pair, 0)
+    g_qkv[:, :span] = (gq_t[...].T * (HEAD**-0.5)).astype(BF)
+
+
+def share_rows(n, me, shard, whole, keep, send, sems):
+    outs = []
+    core = me % 2
+    for k in range(n // 2):
+        for i, dst in enumerate((keep, send)):
+            owner = 2 * k + (core if i == 0 else 1 - core)
+            src = whole.at[pl.ds(pl.multiple_of(owner * shard, 16), shard)]
+            copy = pltpu.make_async_copy(src, dst.at[k], sems.at[2 * k + i])
+            copy.start()
+            outs.append(copy)
+    return outs
+
+
+def attention_backward_one(n, segs, pairs, deps, *refs):
+    me_ref, starts, qkv, lse, n1, g_mixed, g_out = refs[:7]
+    g_qkv, keep, send = refs[7 + deps : 10 + deps]
+    k_t, gq_t, bias, g_w, out_sems = refs[10 + deps :]
+    tok, width = n1.shape
+    span = pairs * LANES
+    bias[...] = segment_bias(starts, tok, segs)
+    head_grads(0, pairs, width, qkv, lse, g_mixed, bias, k_t, gq_t, g_qkv)
+    g_w[:, :width] = g_out[...]
+    for i in range(3):
+        part = dot_tn(n1[...], g_qkv[:, i * span : (i + 1) * span])
+        g_w[:, width + i * span : width + (i + 1) * span] = part.astype(BF)
+    for copy in share_rows(n, me_ref[0], width // n, g_w, keep, send, out_sems):
+        copy.wait()
+
+
+def call_attention_backward_one(n, me, starts, qkv, lse, n1, g_mixed, g_out, pairs, deps=()):
+    tok, width = n1.shape
+    shard, span = width // n, pairs * LANES
+    cols = width + 3 * span
+    return kernel_call(
+        lambda *refs: attention_backward_one(n, starts.shape[1], pairs, len(deps), *refs),
+        attention_backward_one,
+        (sds((tok, 3 * span)),) + (sds((n // 2, shard, cols)),) * 2,
+        [SMEM, SMEM] + [VMEM] * 5 + [ANYWHERE] * len(deps),
+        (VMEM, ANYWHERE, ANYWHERE),
+        [
+            pltpu.VMEM((span, tok), BF),
+            pltpu.VMEM((span, tok), F32),
+            pltpu.VMEM((tok, tok), F32),
+            pltpu.VMEM((width, cols), BF),
+            pltpu.SemaphoreType.DMA((n,)),
+        ],
+        (me, starts, qkv, lse, n1, g_mixed, g_out, *deps),
+    )
+
+
+def attention_backward_two(n, layout, segs, n_vec, first, deps, *refs):
+    count = 1 + max(i for i, *_ in layout)
+    me_ref, starts, tokens, vec, vec_grads, qkv, lse, n1, g_mixed, g_hidden, g_first = refs[:11]
+    pieces = refs[11 : 11 + count]
+    at = 11 + count + deps
+    input_grad, keep, send = refs[at : at + 3]
+    weights, k_t, gq_t, bias, g_qkv, g_w, v_rows, sems, out_sems = refs[at + 3 :]
+    tok, width = tokens.shape
+    shard = width // n
+    span_one = first * LANES
+    span = width - span_one
+    me = me_ref[0]
+    copies = []
+    for i in range(3):
+        cols = weights.at[:, pl.ds(i * width, width)]
+        copies += load_weight(me, pieces, layout, i, shard, cols, sems.at[i])
+    bias[...] = segment_bias(starts, tok, segs)
+    head_grads(first, span // LANES, width, qkv, lse, g_mixed, bias, k_t, gq_t, g_qkv)
+    for i in range(3):
+        cols = slice(i * span, (i + 1) * span)
+        g_w[:, cols] = dot_tn(n1[...], g_qkv[:, cols]).astype(BF)
+    for copy in copies:
+        copy.wait()
+    g_n1 = jnp.zeros((tok, width), F32)
+    for i in range(3):
+        one = slice(i * width, i * width + span_one)
+        two = slice(i * width + span_one, (i + 1) * width)
+        g_n1 = g_n1 + dot_nt(g_first[:, i * span_one : (i + 1) * span_one], weights[:, one])
+        g_n1 = g_n1 + dot_nt(g_qkv[:, i * span : (i + 1) * span], weights[:, two])
+    normed, inverse = center(tokens[...].astype(F32))
+    input_grad[...] = g_hidden[...] + norm_grad(normed, inverse, vec[0:1, :], g_n1)
+    v_rows[...] = jnp.zeros_like(v_rows)
+    v_rows[0:1, :] = jnp.sum(g_n1 * normed, 0, keepdims=True)
+    v_rows[1:2, :] = jnp.sum(g_n1, 0, keepdims=True)
+    for row, i in ((2, 0), (3, 2)):
+        one = g_first[:, i * span_one : (i + 1) * span_one].astype(F32)
+        two = g_qkv[:, i * span : (i + 1) * span].astype(F32)
+        v_rows[row : row + 1, :span_one] = jnp.sum(one, 0, keepdims=True)
+        v_rows[row : row + 1, span_one:] = jnp.sum(two, 0, keepdims=True)
+    v_rows[4:n_vec, :] = vec_grads[4:n_vec, :]
+    g_w[:, 3 * span :] = v_rows[...].T.astype(BF)
+    for copy in share_rows(n, me, shard, g_w, keep, send, out_sems):
+        copy.wait()
+
+
+def call_attention_backward_two(
+    n,
+    me,
+    starts,
+    tokens,
+    vec,
+    vec_grads,
+    qkv,
+    lse,
+    n1,
+    g_mixed,
+    g_hidden,
+    g_first,
+    pieces,
+    layout,
+    n_vec,
+    first,
+    deps=(),
+):
+    tok, width = tokens.shape
+    shard, span = width // n, width - first * LANES
+    cols = 3 * span + LANES
+    return kernel_call(
+        lambda *refs: attention_backward_two(
+            n, layout, starts.shape[1], n_vec, first, len(deps), *refs
+        ),
+        attention_backward_two,
+        (sds((tok, width), F32),) + (sds((n // 2, shard, cols)),) * 2,
+        [SMEM, SMEM] + [VMEM] * 9 + [ANYWHERE] * (len(pieces) + len(deps)),
+        (VMEM, ANYWHERE, ANYWHERE),
+        [
+            pltpu.VMEM((width, 3 * width), BF),
+            pltpu.VMEM((span, tok), BF),
+            pltpu.VMEM((span, tok), F32),
+            pltpu.VMEM((tok, tok), F32),
+            pltpu.VMEM((tok, 3 * span), BF),
+            pltpu.VMEM((width, cols), BF),
+            pltpu.VMEM((LANES, width), F32),
+            pltpu.SemaphoreType.DMA((3, len(layout))),
+            pltpu.SemaphoreType.DMA((n,)),
+        ],
+        (
+            me,
+            starts,
+            tokens,
+            vec,
+            vec_grads,
+            qkv,
+            lse,
+            n1,
+            g_mixed,
+            g_hidden,
+            g_first,
+            *pieces,
+            *deps,
+        ),
+    )
+
+
+def place_rows(position, slots):
+    row = lax.broadcasted_iota(jnp.int32, (slots, position.shape[1]), 0)
+    return (row == position[...]).astype(F32).astype(BF)
+
+
+def take_rows(position, slots):
+    row = lax.broadcasted_iota(jnp.int32, (position.shape[0], slots), 1)
+    return (row == position[...]).astype(F32).astype(BF)
+
+
+def mix_out(n, layout, slots, deps, *refs):
+    count = 1 + max(i for i, *_ in layout)
+    me_ref, mixed, tokens, vec, position = refs[:5]
+    pieces = refs[5 : 5 + count]
+    hidden, sorted_two, weights, sems = refs[5 + count + deps :]
+    width = tokens.shape[1]
+    copies = load_weight(me_ref[0], pieces, layout, 3, width // n, weights, sems)
+    place = place_rows(position, slots)
+    for copy in copies:
+        copy.wait()
+    value = tokens[...].astype(F32) + dot_nn(mixed[...], weights[...]) + vec[4:5, :]
+    hidden[...] = value
+    normed, _ = center(value)
+    sorted_two[...] = dot_nn(place, (normed * vec[5:6, :] + vec[6:7, :]).astype(BF)).astype(BF)
+
+
+def call_mix_out(n, me, mixed, tokens, vec, position, slots, pieces, layout, deps=()):
+    tok, width = tokens.shape
+    return kernel_call(
+        lambda *refs: mix_out(n, layout, slots, len(deps), *refs),
+        mix_out,
+        (sds((tok, width), F32), sds((slots, width))),
+        [SMEM] + [VMEM] * 4 + [ANYWHERE] * (len(pieces) + len(deps)),
+        (VMEM, VMEM),
+        [pltpu.VMEM((width, width), BF), pltpu.SemaphoreType.DMA((len(layout),))],
+        (me, mixed, tokens, vec, position, *pieces, *deps),
+    )
+
+
+def pack(count, *refs):
+    weights = refs[:count]
+    vectors, down_bias, in_bias, out, small = refs[count:]
+    rows = weights[0].shape[0]
+    for i, ref in enumerate(weights):
+        out[i * rows : (i + 1) * rows, :] = ref[...]
+    small[...] = jnp.zeros_like(small)
+    n_vec = vectors.shape[0]
+    small[:n_vec, :rows] = vectors[...].astype(F32)
+    small[n_vec : n_vec + EXPERTS, :rows] = down_bias[...].astype(F32)
+    small[n_vec + EXPERTS : n_vec + 2 * EXPERTS, : in_bias.shape[1]] = in_bias[...].astype(F32)
+    out[count * rows :, :] = small[...].astype(BF)
+
+
+def call_pack(weights, vectors, down_bias, in_bias):
+    rows, width = weights[0].shape
+    return kernel_call(
+        lambda *refs: pack(len(weights), *refs),
+        pack,
+        sds((len(weights) * rows + 16, width)),
+        [VMEM] * (len(weights) + 3),
+        VMEM,
+        [pltpu.VMEM((16, width), F32)],
+        (*weights, vectors, down_bias, in_bias),
+    )
+
+
+def load_blocks(refs, layout, dst, sems):
+    copies = []
+    for i, (ref, (block, offset, rows, row)) in enumerate(zip(refs, layout, strict=True)):
+        copy = pltpu.make_async_copy(
+            ref.at[pl.ds(row, rows)], dst.at[block, pl.ds(offset, rows)], sems.at[i]
+        )
+        copy.start()
+        copies.append(copy)
+    return copies
+
+
+def start_all(copies):
+    for copy in copies:
+        copy.start()
+    return copies
+
+
+def wait_all(copies):
+    for copy in copies:
+        copy.wait()
+
+
+def window(meta, block, e):
+    begin = pl.multiple_of(meta[block, 3 * e], 16)
+    row = lax.broadcasted_iota(jnp.int32, (CAP, 1), 0)
+    return pl.ds(begin, CAP), (row >= meta[block, 3 * e + 1]) & (row < meta[block, 3 * e + 2])
+
+
+def experts(chips, bias_row, lay_x, lay_g, deps, *refs):
+    nb, cx, cg, cw = len(chips), len(lay_x), len(lay_g), 2
+    me_ref, meta, b_in = refs[:3]
+    at = 3
+    x_refs, at = refs[at : at + cx], at + cx
+    g_refs, at = refs[at : at + cg], at + cg
+    w_refs, at = refs[at : at + cw], at + cw
+    down = refs[at : at + 2]
+    at += 2 + deps
+    dsl, (res, act_out, dp_out) = refs[at : at + nb], refs[at + nb : at + nb + 3]
+    at += nb + 3
+    x_all, g_all, w_in, w_down, res_s, dsl_s, xs, gs, act_s, dp_s = refs[at : at + 10]
+    sx, sg, sw, sd, so, sa = refs[at + 10 :]
+    rows = w_refs[0].shape[2]
+    me = me_ref[0]
+    half = w_down.shape[1] // 2
+    core = me % 2
+    loads = load_blocks(x_refs, lay_x, x_all, sx) + load_blocks(g_refs, lay_g, g_all, sg)
+    weights = []
+    for e in range(EXPERTS):
+        copies = []
+        for i, ref in enumerate(w_refs):
+            for k in range(ref.shape[0]):
+                owner = 2 * k + (core if i == 0 else 1 - core)
+                to = pl.ds(pl.multiple_of(owner * rows, 16), rows)
+                copies.append(pltpu.make_async_copy(ref.at[k, e], w_in.at[e, to], sw.at[e, i, k]))
+        for i, ref in enumerate(down):
+            to = pl.multiple_of((core if i == 0 else 1 - core) * half, 16)
+            copies.append(pltpu.make_async_copy(ref.at[e], w_down.at[e, pl.ds(to, half)], sd.at[e, i]))
+        weights.append(start_all(copies))
+    res_s[...] = jnp.zeros_like(res_s)
+    dsl_s[...] = jnp.zeros_like(dsl_s)
+    wait_all(loads)
+    outs = []
+    for e in range(EXPERTS):
+        spans = []
+        for b in range(nb):
+            span, inside = window(meta, b, e)
+            spans.append((span, inside))
+            g = g_all[b, span, :]
+            xs[b * CAP : (b + 1) * CAP, :] = x_all[b, span, :]
+            gs[b * CAP : (b + 1) * CAP, :] = jnp.where(inside, g, jnp.zeros_like(g))
+        wait_all(weights[e])
+        pre = dot_nn(xs[...], w_in[e]) + b_in[bias_row + e : bias_row + e + 1, :]
+        cdf = 0.5 * (1.0 + lax.erf(pre * 0.7071067811865476))
+        act = (pre * cdf).astype(BF)
+        slope = cdf + pre * jnp.exp(-0.5 * pre * pre) * 0.3989422804014327
+        dp = (dot_nt(gs[...], w_down[e]) * slope).astype(BF)
+        act_s[e] = act
+        dp_s[e] = dp
+        outs += start_all(
+            [
+                pltpu.make_async_copy(act_s.at[e], act_out.at[e], sa.at[0, e]),
+                pltpu.make_async_copy(dp_s.at[e], dp_out.at[e], sa.at[1, e]),
+            ]
+        )
+        for dst, value in ((dsl_s, dot_nt(dp, w_in[e])), (res_s, dot_nn(act, w_down[e]))):
+            value = value.astype(BF)
+            for b, (span, inside) in enumerate(spans):
+                dst[b, span, :] = jnp.where(inside, value[b * CAP : (b + 1) * CAP], dst[b, span, :])
+    for b in range(nb):
+        outs += start_all(
+            [
+                pltpu.make_async_copy(dsl_s.at[b], dsl[b], so.at[0, b]),
+                pltpu.make_async_copy(res_s.at[b], res.at[(me // 2) ^ chips[b]], so.at[1, b]),
+            ]
+        )
+    wait_all(outs)
+
+
+def call_experts(chips, bias_row, me, meta, b_in, xp, lay_x, gp, lay_g, wp, down, res, blocks):
+    nb, rows, width = len(chips), max(o + r for _, o, r, _ in lay_x), xp[0].shape[1]
+    ff = 2 * down[0].shape[1]
+    dma = pltpu.SemaphoreType.DMA
+    deps = () if res is None else (res,)
+    alias = {} if res is None else {5 + len(xp) + len(gp) + len(wp): nb}
+    out = kernel_call(
+        lambda *refs: experts(chips, bias_row, lay_x, lay_g, len(deps), *refs),
+        experts,
+        (sds((rows, width)),) * nb
+        + (sds((blocks, rows, width)),)
+        + (sds((EXPERTS, nb * CAP, ff)),) * 2,
+        [SMEM, SMEM, VMEM] + [ANYWHERE] * (len(xp) + len(gp) + len(wp) + 2 + len(deps)),
+        (ANYWHERE,) * (nb + 3),
+        [pltpu.VMEM((nb, rows, width), BF)] * 2
+        + [pltpu.VMEM((EXPERTS, width, ff), BF), pltpu.VMEM((EXPERTS, ff, width), BF)]
+        + [pltpu.VMEM((nb, rows, width), BF)] * 2
+        + [pltpu.VMEM((nb * CAP, width), BF)] * 2
+        + [pltpu.VMEM((EXPERTS, nb * CAP, ff), BF)] * 2
+        + [dma((len(xp),)), dma((len(gp),)), dma((EXPERTS, 2, blocks)), dma((EXPERTS, 2))]
+        + [dma((2, nb)), dma((2, EXPERTS))],
+        (me, meta, b_in, *xp, *gp, *wp, *down, *deps),
+        alias,
+    )
+    return list(out[:nb]), out[nb], out[nb + 1], out[nb + 2]
+
+
+def down_grads(calls, lay_g, deps, *refs):
+    cg, cc = len(lay_g), len(calls)
+    me_ref, meta = refs[:2]
+    g_refs, acts = refs[2 : 2 + cg], refs[2 + cg : 2 + cg + cc]
+    at = 2 + cg + cc + deps
+    keep, send = refs[at], refs[at + 1 : at + 1 + EXPERTS]
+    g_all, act_s, gs, g_down, sg, sa, so = refs[at + 1 + EXPERTS :]
+    core = me_ref[0] % 2
+    half = g_down.shape[1] // 2
+    loads = load_blocks(g_refs, lay_g, g_all, sg)
+    hidden = load_hidden(acts, calls, act_s, sa)
+    wait_all(loads)
+    outs = []
+    for e in range(EXPERTS):
+        for b in range(sum(calls)):
+            span, inside = window(meta, b, e)
+            g = g_all[b, span, :]
+            gs[b * CAP : (b + 1) * CAP, :] = jnp.where(inside, g, jnp.zeros_like(g))
+        wait_all(hidden[e])
+        g_down[e] = dot_tn(act_s[e], gs[...]).astype(BF)
+        for i, dst in enumerate((keep.at[e], send[e])):
+            src = g_down.at[e, pl.ds(pl.multiple_of((core if i == 0 else 1 - core) * half, 16), half)]
+            outs.append(pltpu.make_async_copy(src, dst, so.at[e, i]))
+            outs[-1].start()
+    wait_all(outs)
+
+
+def load_hidden(parts, calls, dst, sems):
+    hidden = []
+    for e in range(EXPERTS):
+        copies, first = [], 0
+        for i, nb in enumerate(calls):
+            rows = pl.ds(first * CAP, nb * CAP)
+            copies.append(pltpu.make_async_copy(parts[i].at[e], dst.at[e, rows], sems.at[e, i]))
+            first += nb
+        hidden.append(start_all(copies))
+    return hidden
+
+
+def call_down_grads(me, meta, gp, lay_g, acts, calls, deps=()):
+    rows, width = max(o + r for _, o, r, _ in lay_g), gp[0].shape[1]
+    ff, blocks = acts[0].shape[2], sum(calls)
+    dma = pltpu.SemaphoreType.DMA
+    return kernel_call(
+        lambda *refs: down_grads(calls, lay_g, len(deps), *refs),
+        down_grads,
+        (sds((EXPERTS, ff // 2, width)),) + (sds((ff // 2, width)),) * EXPERTS,
+        [SMEM, SMEM] + [ANYWHERE] * (len(gp) + len(acts) + len(deps)),
+        (ANYWHERE,) * (1 + EXPERTS),
+        [
+            pltpu.VMEM((blocks, rows, width), BF),
+            pltpu.VMEM((EXPERTS, blocks * CAP, ff), BF),
+            pltpu.VMEM((blocks * CAP, width), BF),
+            pltpu.VMEM((EXPERTS, ff, width), BF),
+            dma((len(gp),)),
+            dma((EXPERTS, len(calls))),
+            dma((EXPERTS, 2)),
+        ],
+        (me, meta, *gp, *acts, *deps),
+    )
+
+
+def in_grads(n, calls, lay_x, deps, *refs):
+    cx, cc = len(lay_x), len(calls)
+    me_ref, meta = refs[:2]
+    x_refs, dps = refs[2 : 2 + cx], refs[2 + cx : 2 + cx + cc]
+    at = 2 + cx + cc + deps
+    keep, bias_keep, bias_send = refs[at : at + 3]
+    send = refs[at + 3 : at + 3 + EXPERTS]
+    x_all, dp_s, xs, g_in, sx, sp, so = refs[at + 3 + EXPERTS :]
+    me = me_ref[0]
+    _, width, ff = g_in.shape
+    shard, half = width // n, ff // 2
+    loads = load_blocks(x_refs, lay_x, x_all, sx)
+    hidden = load_hidden(dps, calls, dp_s, sp)
+    wait_all(loads)
+    outs = []
+    row = lax.broadcasted_iota(jnp.int32, (16, 1), 0)
+    low = jnp.zeros((16, half), F32)
+    high = jnp.zeros((16, half), F32)
+    for e in range(EXPERTS):
+        for b in range(sum(calls)):
+            span, _ = window(meta, b, e)
+            xs[b * CAP : (b + 1) * CAP, :] = x_all[b, span, :]
+        wait_all(hidden[e])
+        g_in[e] = dot_tn(xs[...], dp_s[e]).astype(BF)
+        outs += share_rows(n, me, shard, g_in.at[e], keep.at[:, e], send[e], so.at[e])
+        total = jnp.sum(dp_s[e].astype(F32), 0, keepdims=True)
+        low = low + jnp.where(row == e, total[:, :half], 0.0)
+        high = high + jnp.where(row == e, total[:, half:], 0.0)
+    first_core = me % 2 == 0
+    bias_keep[...] = jnp.where(first_core, low, high).astype(BF)
+    bias_send[...] = jnp.where(first_core, high, low).astype(BF)
+    wait_all(outs)
+
+
+def call_in_grads(n, me, meta, xp, lay_x, dps, calls, deps=()):
+    rows, width = max(o + r for _, o, r, _ in lay_x), xp[0].shape[1]
+    ff, blocks = dps[0].shape[2], sum(calls)
+    dma = pltpu.SemaphoreType.DMA
+    return kernel_call(
+        lambda *refs: in_grads(n, calls, lay_x, len(deps), *refs),
+        in_grads,
+        (sds((n // 2, EXPERTS, width // n, ff)),)
+        + (sds((16, ff // 2)),) * 2
+        + (sds((n // 2, width // n, ff)),) * EXPERTS,
+        [SMEM, SMEM] + [ANYWHERE] * (len(xp) + len(dps) + len(deps)),
+        (ANYWHERE, VMEM, VMEM) + (ANYWHERE,) * EXPERTS,
+        [
+            pltpu.VMEM((blocks, rows, width), BF),
+            pltpu.VMEM((EXPERTS, blocks * CAP, ff), BF),
+            pltpu.VMEM((blocks * CAP, width), BF),
+            pltpu.VMEM((EXPERTS, width, ff), BF),
+            dma((len(xp),)),
+            dma((EXPERTS, len(calls))),
+            dma((EXPERTS, n)),
+        ],
+        (me, meta, *xp, *dps, *deps),
+    )
+
+
+def mix_out_backward(n, layout, terms, deps, *refs):
+    count = 1 + max(i for i, *_ in layout)
+    me_ref, position, route, hidden, cot, vec, mixed = refs[:7]
+    got = refs[7 : 7 + terms]
+    pieces = refs[7 + terms : 7 + terms + count]
+    at = 7 + terms + count + deps
+    g_hidden, g_mixed, vec_grads, g_w = refs[at : at + 4]
+    weights, sems = refs[at + 4 :]
+    me = me_ref[0]
+    tok, width = hidden.shape
+    shard = width // n
+    copies = load_weight(me, pieces, layout, 3, shard, weights, sems)
+    total = got[0][...].astype(F32)
+    for ref in got[1:]:
+        total = total + ref[...].astype(F32)
+    gradient = exact_rows(take_rows(position, total.shape[0]), total)
+    normed, inverse = center(hidden[...])
+    value = cot[...].astype(F32) + norm_grad(normed, inverse, vec[5:6, :], gradient)
+    g_hidden[...] = value
+    branch = value.astype(BF)
+    vec_grads[...] = jnp.zeros_like(vec_grads)
+    vec_grads[4:5, :] = jnp.sum(branch.astype(F32), 0, keepdims=True)
+    vec_grads[5:6, :] = jnp.sum(gradient * normed, 0, keepdims=True)
+    vec_grads[6:7, :] = jnp.sum(gradient, 0, keepdims=True)
+    lane = lax.broadcasted_iota(jnp.int32, (tok, 16), 1)
+    member = (lane == route[...] + 7).astype(F32).astype(BF)
+    vec_grads[...] += dot_tn(member, cot[...])
+    for copy in copies:
+        copy.wait()
+    g_mixed[...] = dot_nt(branch, weights[...]).astype(BF)
+    g_w[...] = dot_tn(mixed[...], branch).astype(BF)
+
+
+def call_mix_out_backward(
+    n, me, position, route, hidden, cot, vec, mixed, got, pieces, layout, deps=()
+):
+    tok, width = hidden.shape
+    return kernel_call(
+        lambda *refs: mix_out_backward(n, layout, len(got), len(deps), *refs),
+        mix_out_backward,
+        (sds((tok, width), F32), sds((tok, width)), sds((16, width), F32), sds((width, width))),
+        [SMEM] + [VMEM] * (6 + len(got)) + [ANYWHERE] * (len(pieces) + len(deps)),
+        (VMEM,) * 4,
+        [pltpu.VMEM((width, width), BF), pltpu.SemaphoreType.DMA((len(layout),))],
+        (me, position, route, hidden, cot, vec, mixed, *got, *pieces, *deps),
+    )
+
+
+def finish_output(deps, *refs):
+    position, hidden, route, vec = refs[:4]
+    got = refs[4]
+    out = refs[5 + deps]
+    value = hidden[...] + dot_nn(take_rows(position, got.shape[0]), got[...])
+    for e in range(EXPERTS):
+        value = value + jnp.where(route[...] == e, vec[7 + e : 8 + e, :], 0.0)
+    out[...] = value.astype(BF)
+
+
+def call_finish_output(position, hidden, route, vec, got, deps=()):
+    return kernel_call(
+        lambda *refs: finish_output(len(deps), *refs),
+        finish_output,
+        sds(hidden.shape),
+        [VMEM] * 5 + [ANYWHERE] * len(deps),
+        VMEM,
+        [],
+        (position, hidden, route, vec, got, *deps),
+    )
+
+
+def join(body, named, outs, scalars, arrays, deps=()):
+    n_s, n_a, n_d, n_o = len(scalars), len(arrays), len(deps), len(outs)
+
+    def kernel(*refs):
+        at = n_s + n_a + n_d
+        body(refs[:n_s], refs[n_s : n_s + n_a], refs[at : at + n_o])
+
+    return kernel_call(
+        kernel,
+        named,
+        tuple(outs),
+        [SMEM] * n_s + [VMEM] * n_a + [ANYWHERE] * n_d,
+        (VMEM,) * n_o,
+        [],
+        (*scalars, *arrays, *deps),
+    )
+
+
+def plus(*values):
+    total = values[0].astype(F32)
+    for value in values[1:]:
+        total = total + value.astype(F32)
+    return total
+
+
+def call_halves(own, along, across, deps=()):
+    rows, width = along.shape
+    half = rows // 32 * 16
+
+    def body(_, ins, outs):
+        outs[0][...] = ins[1][:half]
+        outs[1][...] = ins[2][half:]
+        for i in range(3):
+            outs[2][i] = ins[i][...]
+
+    shapes = (sds((half, width)), sds((rows - half, width)), sds((3, rows, width)))
+    return join(body, call_halves, shapes, (), (own, along, across), deps)
+
+
+def call_two_halves(first, second, deps=()):
+    cuts_at = [pair[0].shape[0] // 32 * 16 for pair in (first, second)]
+    width = first[0].shape[1]
+    split = cuts_at[0]
+
+    def body(_, ins, outs):
+        outs[0][:split] = ins[0][:split]
+        outs[0][split:] = ins[2][: cuts_at[1]]
+        rest = ins[0].shape[0] - split
+        outs[1][:rest] = ins[1][split:]
+        outs[1][rest:] = ins[3][cuts_at[1] :]
+
+    rows = first[0].shape[0] + second[0].shape[0]
+    shapes = (sds((sum(cuts_at), width)), sds((rows - sum(cuts_at), width)))
+    return join(body, call_two_halves, shapes, (), (*first, *second), deps)
+
+
+def call_columns_and_sort(n, whole, position, slots, value, meta, deps):
+    experts_, rows, cols = whole.shape
+    pair = cols // (n // 2)
+
+    def body(_, ins, outs):
+        for k in range(n // 2):
+            outs[0][k] = ins[0][:, :, k * pair : (k + 1) * pair]
+        outs[1][:slots, :] = dot_nn(place_rows(ins[1], slots), ins[2][...]).astype(BF)
+        outs[1][slots:, :] = jnp.zeros((16, value.shape[1]), BF)
+        outs[1][slots:, :LANES] = jnp.broadcast_to(ins[3][...], (16, LANES)).astype(BF)
+
+    shapes = (sds((n // 2, experts_, rows, pair)), sds((slots + 16, value.shape[1])))
+    return join(body, call_columns_and_sort, shapes, (), (whole, position, value, meta), deps)
+
+
+def call_pair_down(kept, keep, got, deps=()):
+    experts_, rows, width = keep.shape
+    half = rows // 2
+
+    def body(scalars, ins, outs):
+        mine = pl.multiple_of(scalars[0][0] * half, 16)
+        other = pl.multiple_of((1 - scalars[0][0]) * half, 16)
+        for out, at in zip(outs, (mine, other), strict=True):
+            for e in range(experts_):
+                part = plus(ins[0][e, pl.ds(at, half)], ins[1 + e][pl.ds(at, half)])
+                out[e] = part.astype(BF)
+
+    shapes = (sds((experts_, half, width)),) * 2
+    return join(body, call_pair_down, shapes, (kept,), (keep, *got), deps)
+
+
+def call_pair_in(keep, got, bias_keep, bias_got, d_keep, d_got, cut, deps=()):
+    count = len(got)
+
+    def body(_, ins, outs):
+        for e in range(count):
+            outs[0][:, e] = plus(ins[0][:, e], ins[5 + e][...]).astype(BF)
+        outs[1][...] = plus(ins[1][...], ins[2][...]).astype(BF)
+        outs[2][...] = plus(ins[3][:cut], ins[4][:cut]).astype(BF)
+        outs[3][...] = plus(ins[3][cut:], ins[4][cut:]).astype(BF)
+
+    shapes = (sds(keep.shape), sds(bias_keep.shape))
+    shapes += (sds((cut, *d_keep.shape[1:])), sds((d_keep.shape[0] - cut, *d_keep.shape[1:])))
+    arrays = (keep, bias_keep, bias_got, d_keep, d_got, *got)
+    return join(body, call_pair_in, shapes, (), arrays, deps)
+
+
+def call_split_rows(kept, whole, deps=()):
+    chips, experts_, rows, ff = whole.shape
+    half = rows // 2
+    two = chips // 2
+
+    def body(scalars, ins, outs):
+        outs[0][...] = ins[0][:, :, pl.ds(pl.multiple_of(scalars[0][0] * half, 16), half)]
+        other = pl.ds(pl.multiple_of((1 - scalars[0][0]) * half, 16), half)
+        for i in range(2):
+            outs[1 + i][...] = ins[0][i * two : (i + 1) * two, :, other]
+
+    shapes = (sds((chips, experts_, half, ff)),) + (sds((two, experts_, half, ff)),) * 2
+    return join(body, call_split_rows, shapes, (kept,), (whole,), deps)
+
+
+def call_pair_shares(one, two, deps=()):
+    chips, rows, cols_one = one[0].shape
+    cols = cols_one + two[0].shape[2]
+
+    def body(_, ins, outs):
+        outs[0][:, :, :cols_one] = plus(ins[0][...], ins[1][...]).astype(BF)
+        outs[0][:, :, cols_one:] = plus(ins[2][...], ins[3][...]).astype(BF)
+
+    return join(body, call_pair_shares, (sds((chips, rows, cols)),), (), (*one, *two), deps)[0]
+
+
+def call_line_sums(parts, across, i_keep, i_got, deps=()):
+    cut = parts[0].shape[0]
+    rest = parts[1].shape[0]
+    two = i_got[0].shape[0]
+
+    def body(_, ins, outs):
+        outs[0][:cut] = plus(ins[0][...], ins[2][...]).astype(BF)
+        outs[0][cut:] = plus(ins[1][...], ins[3][...]).astype(BF)
+        for i in range(2):
+            at = slice(i * two, (i + 1) * two)
+            outs[1][at] = plus(ins[4][at], ins[5 + i][...]).astype(BF)
+
+    shapes = (sds((cut + rest, *parts[0].shape[1:])), sds(i_keep.shape))
+    return join(body, call_line_sums, shapes, (), (*parts, *across, i_keep, *i_got), deps)
+
+
+def call_sums(jobs, deps=()):
+    flat = [v for job in jobs for v in job]
+
+    def body(_, ins, outs):
+        at = 0
+        for job, out in zip(jobs, outs, strict=True):
+            out[...] = plus(*[ref[...] for ref in ins[at : at + len(job)]]).astype(BF)
+            at += len(job)
+
+    return join(body, call_sums, [sds(job[0].shape) for job in jobs], (), flat, deps)
+
+
+def call_attention_shares(kept, got, bias, deps=()):
+    chips, rows, cols = got.shape
+    half = rows // 2
+
+    def body(scalars, ins, outs):
+        mine = pl.multiple_of(scalars[0][0] * half, 16)
+        other = pl.multiple_of((1 - scalars[0][0]) * half, 16)
+        for out, at in zip(outs, (mine, other), strict=True):
+            out[:half, :] = plus(*[ins[0][k, pl.ds(at, half)] for k in range(chips)]).astype(BF)
+            out[half:, :] = jnp.zeros((16, cols), BF)
+            out[half:, : bias.shape[1]] = ins[1][...]
+
+    shapes = (sds((half + 16, cols)),) * 2
+    return join(body, call_attention_shares, shapes, (kept,), (got, bias), deps)
+
+
+def call_down_result(kept, mine, got, deps=()):
+    experts_, half, width = mine.shape
+
+    def body(scalars, ins, outs):
+        outs[0][:, pl.ds(pl.multiple_of(scalars[0][0] * half, 16), half)] = ins[0][...].astype(F32)
+        at = pl.multiple_of((1 - scalars[0][0]) * half, 16)
+        outs[0][:, pl.ds(at, half)] = ins[1][...].astype(F32)
+
+    shape = (sds((experts_, 2 * half, width), F32),)
+    return join(body, call_down_result, shape, (kept,), (mine, got), deps)[0]
+
+
+def call_in_result(kept, mine, got, deps=()):
+    chips, experts_, half, ff = mine.shape
+
+    def body(scalars, ins, outs):
+        for ref, which in ((ins[0], scalars[0][0]), (ins[1], 1 - scalars[0][0])):
+            rows = pl.ds(pl.multiple_of(which * half, 16), half)
+            for k in range(chips):
+                outs[0][:, rows, k * ff : (k + 1) * ff] = ref[k].astype(F32)
+
+    shape = (sds((experts_, 2 * half, chips * ff), F32),)
+    return join(body, call_in_result, shape, (kept,), (mine, got), deps)[0]
+
+
+def call_attention_result(kept, mine, got, width, span, n_vec, ff_shard, deps=()):
+    half = mine.shape[0] - 16
+    last = width - span
+    cols_one = width + 3 * span
+
+    def body(scalars, ins, outs):
+        for ref, which in ((ins[0], scalars[0][0]), (ins[1], 1 - scalars[0][0])):
+            rows = pl.ds(pl.multiple_of(which * half, 16), half)
+            outs[0][rows, :] = ref[:half, :width].astype(F32)
+            for i in range(3):
+                one = ref[:half, width + i * span : width + (i + 1) * span]
+                two = ref[:half, cols_one + i * last : cols_one + (i + 1) * last]
+                outs[1 + i][rows, :span] = one.astype(F32)
+                outs[1 + i][rows, span:] = two.astype(F32)
+            outs[6][rows, :] = ref[:half, cols_one + 3 * last :].astype(F32)
+        outs[4][...] = outs[6][...].T[:16]
+        outs[5][...] = ins[0][half:, :ff_shard].astype(F32)
+
+    shapes = (sds((2 * half, width), F32),) * 4 + (sds((16, 2 * half), F32),)
+    shapes += (sds((16, ff_shard), F32), sds((2 * half, LANES), F32))
+    return join(body, call_attention_result, shapes, (kept,), (mine, got), deps)
+
+
+def swap(v, n, mask):
+    return lax.ppermute(v, FSDP, [(i, i ^ mask) for i in range(n)])
+
+
+def blocks_of(pieces, here):
+    mine = [p for p in pieces if p[1] in here]
+    return [p[0] for p in mine], [(here.index(c), at, rows, row) for _, c, at, rows, row in mine]
+
+
+def scatter_chips(terms, n):
+    return [terms[0]] + [swap(terms[i], n, 2 * i) for i in range(1, n // 2)]
+
+
+def exchange(v, n):
+    groups = [list(range(core, n, 2)) for core in range(2)]
+    return lax.all_to_all(v, FSDP, 0, 0, axis_index_groups=groups)
+
+
+def plane_sum(v, n):
+    groups = [list(range(core, n, 2)) for core in range(2)]
+    return lax.psum_scatter(v, FSDP, scatter_dimension=0, axis_index_groups=groups)
+
+
+def line(v, step):
+    pairs = [(0, 3), (3, 0), (1, 2), (2, 1)] if step == 1 else [(0, 1), (1, 0), (2, 3), (3, 2)]
+    return lax.ppermute(v, REP, pairs)
+
+
+def per_device_tokens(
+    n,
+    tokens,
+    starts,
+    routes,
+    norm1_gain,
+    norm1_bias,
+    query_weight,
+    query_bias,
+    key_weight,
+    value_weight,
+    value_bias,
+    out_weight,
+    out_bias,
+    norm2_gain,
+    norm2_bias,
+    expert_in,
+    expert_in_bias,
+    expert_out,
+    expert_out_bias,
+    cotangent,
+):
+    index = lax.axis_index(FSDP)
+    me = index.astype(jnp.int32).reshape(1)
+    tok_count, width = tokens.shape
+    shard = width // n
+    ff_shard = expert_out.shape[1]
+    ff_pair = 2 * ff_shard
+
+    vectors = [norm1_gain, norm1_bias, query_bias, value_bias, out_bias, norm2_gain, norm2_bias]
+    n_vec = len(vectors) + EXPERTS
+    payload = call_pack(
+        (query_weight, key_weight, value_weight, out_weight),
+        jnp.stack(vectors),
+        expert_out_bias,
+        expert_in_bias,
+    )
+    along, across = swap(payload, n, 2), swap(payload, n, 4)
+    top, bottom, three = call_halves(payload, along, across)
+    top_got, bottom_got = swap(top, n, 4), swap(bottom, n, 2)
+    rows, half = payload.shape[0], top.shape[0]
+    w_attn = [payload, along, across, top_got, bottom_got]
+    w_attn += [swap(three, n, 1), swap(top_got, n, 1), swap(bottom_got, n, 1)]
+    lay_attn = [(i, None, m, 0, rows) for i, m in enumerate((0, 2, 4))]
+    lay_attn += [(5, i, m, 0, rows) for i, m in enumerate((1, 3, 5))]
+    lay_attn += [(3, None, 6, 0, half), (4, None, 6, half, rows - half)]
+    lay_attn += [(6, None, 7, 0, half), (7, None, 7, half, rows - half)]
+
+    route_ids = routes[:, 0]
+    member = (route_ids[:, None] == jnp.arange(EXPERTS, dtype=jnp.int32)[None, :]).astype(jnp.int32)
+    rank = jnp.sum(jnp.cumsum(member, 0) * member, 1) - 1
+    padded = (jnp.sum(member, 0) + 15) // 16
+    base = jnp.cumsum(padded) - padded
+    slots = tok_count + 16 * (EXPERTS - 1)
+    position = (jnp.sum(member * base[None, :], 1) * 16 + rank).astype(jnp.int32)
+    position_row, position_col = position[None, :], position[:, None]
+    begin = jnp.minimum(base, (slots - CAP) // 16)
+    meta = jnp.stack([begin, base - begin, base - begin + padded], 1).reshape(1, 3 * EXPERTS) * 16
+    meta = meta.astype(jnp.int32)
+    down_other = swap(expert_out, n, 1)
+
+    meta_row = jnp.pad((meta // 16).astype(F32), ((0, 0), (0, LANES - meta.shape[1])))
+    columns, sorted_grad = call_columns_and_sort(
+        n, expert_in, position_row, slots, cotangent, meta_row, (top,)
+    )
+    w_mine = exchange(hold((columns,), (w_attn[6], w_attn[7]))[0], n)
+    grad_along, grad_across = swap(sorted_grad, n, 2), swap(sorted_grad, n, 4)
+
+    qkv, mixed, lse, n1, vec, in_bias = call_attention_forward(
+        n, me, starts, tokens, w_attn, lay_attn, n_vec
+    )
+    hidden, sorted_two = call_mix_out(
+        n,
+        me,
+        mixed,
+        tokens,
+        vec,
+        position_row,
+        slots,
+        w_attn,
+        lay_attn,
+    )
+    tok_along, tok_across = swap(sorted_two, n, 2), swap(sorted_two, n, 4)
+    (w_mine,) = hold((w_mine,), (sorted_two,))
+    w_pair = (w_mine, swap(w_mine, n, 1))
+
+    calls = ((0,), (1, 2), (3,))
+    sizes = tuple(len(call) for call in calls)
+    dsl, acts, dps = [], [], []
+
+    def run(call, metas, token_pieces, grad_pieces, res):
+        d, res, a, p = call_experts(
+            call,
+            n_vec,
+            me,
+            metas,
+            in_bias,
+            *blocks_of(token_pieces, call),
+            *blocks_of(grad_pieces, call),
+            w_pair,
+            (expert_out, down_other),
+            res,
+            n // 2,
+        )
+        dsl.extend(d)
+        acts.append(a)
+        dps.append(p)
+        return res
+
+    def meta_of(rows):
+        return rows[:, : 3 * EXPERTS].astype(jnp.int32) * 16
+
+    token_pieces = [(sorted_two, 0, 0, slots, 0)]
+    grad_pieces = [(sorted_grad, 0, 0, slots, 0)]
+    res = run(calls[0], meta, token_pieces, grad_pieces, None)
+    tops, bottoms = call_two_halves((tok_along, tok_across), (grad_along, grad_across), (dps[0],))
+    tops, bottoms = swap(tops, n, 4), swap(bottoms, n, 2)
+    half, low = slots // 32 * 16, sorted_grad.shape[0] // 32 * 16
+    rest = slots - half
+    token_pieces += [(tok_along, 1, 0, slots, 0), (tok_across, 2, 0, slots, 0)]
+    token_pieces += [(tops, 3, 0, half, 0), (bottoms, 3, half, rest, 0)]
+    grad_pieces += [(grad_along, 1, 0, slots, 0), (grad_across, 2, 0, slots, 0)]
+    grad_pieces += [(tops, 3, 0, low, half), (bottoms, 3, low, slots - low, rest)]
+    meta_xy = meta_of(
+        jnp.concatenate([grad_along[slots : slots + 1], grad_across[slots : slots + 1]], 0)
+    )
+    meta_d = meta_of(bottoms[-16:-15])
+    meta_rel = jnp.concatenate([meta, meta_xy, meta_d], 0)
+    res = run(calls[1], meta_xy, token_pieces, grad_pieces, res)
+    res = run(calls[2], meta_d, token_pieces, grad_pieces, res)
+    got_dsl = scatter_chips(dsl, n)
+
+    at = lax.axis_index(REP)
+    kept = jnp.where((at == 0) | (at == 3), 1, 0).astype(jnp.int32).reshape(1)
+    down_keep, *down_send = call_down_grads(
+        me,
+        meta_rel,
+        *blocks_of(grad_pieces, range(n // 2)),
+        acts,
+        sizes,
+        (got_dsl[1],),
+    )
+    down_got = [swap(v, n, 1) for v in down_send]
+
+    g_hidden, g_mixed, vec_grads, g_out = call_mix_out_backward(
+        n,
+        me,
+        position_col,
+        routes,
+        hidden,
+        cotangent,
+        vec,
+        mixed,
+        got_dsl,
+        w_attn,
+        lay_attn,
+        (down_keep,),
+    )
+    (res,) = hold((res,), (g_out,))
+    got_res = plane_sum(res, n)
+    d_keep, d_send = call_pair_down(kept, down_keep, down_got, (g_out,))
+    d_got = line(d_send, 0)
+    in_keep, in_bias_keep, in_bias_send, *in_send = call_in_grads(
+        n,
+        me,
+        meta_rel,
+        *blocks_of(token_pieces, range(n // 2)),
+        dps,
+        sizes,
+        (d_send,),
+    )
+    *in_send, in_bias_send = hold((*in_send, in_bias_send), (in_keep,))
+    in_other, in_bias_other = [swap(v, n, 1) for v in in_send], swap(in_bias_send, n, 1)
+
+    first = width // LANES // 2
+    span = first * LANES
+    g_first, keep_one, send_one = call_attention_backward_one(
+        n, me, starts, qkv, lse, n1, g_mixed, g_out, first, (in_keep,)
+    )
+    i_terms, bias_term, *d_parts = call_pair_in(
+        in_keep, in_other, in_bias_keep, in_bias_other, d_keep, d_got, 1, (g_first,)
+    )
+    d_first = line(d_parts[0], 1)
+    i_plane = exchange(i_terms, n)
+    (send_one,) = hold((send_one,), (i_terms,))
+    other_one = swap(send_one, n, 1)
+    input_grad, keep_two, send_two = call_attention_backward_two(
+        n,
+        me,
+        starts,
+        tokens,
+        vec,
+        vec_grads,
+        qkv,
+        lse,
+        n1,
+        g_mixed,
+        g_hidden,
+        g_first,
+        w_attn,
+        lay_attn,
+        n_vec,
+        first,
+        (i_terms,),
+    )
+    send_two, d_second = hold((send_two, d_parts[1]), (keep_two, d_first))
+    other_two = swap(send_two, n, 1)
+    d_across = (d_first, line(d_second, 1))
+    i_keep, *i_send = call_split_rows(kept, i_plane, (keep_two,))
+    i_got = [line(v, 0) for v in i_send]
+    p_terms = call_pair_shares((keep_one, other_one), (keep_two, other_two), (keep_two,))
+    d_total, i_part = call_line_sums(
+        (d_parts[0], d_second), d_across, i_keep, i_got, (p_terms,)
+    )
+    d_rest, i_across = line(d_total, 2), line(i_part, 1)
+    (p_terms,) = hold((p_terms,), (d_total,))
+    p_plane = exchange(p_terms, n)
+    sum_down = call_down_result(kept, d_total, d_rest)
+    p_keep, p_send = call_attention_shares(kept, p_plane, bias_term, (sum_down,))
+    p_got = line(p_send, 0)
+    (i_total,) = call_sums([(i_part, i_across)], (p_send,))
+    i_rest = line(i_total, 2)
+    (p_part,) = call_sums([(p_keep, p_got)], (i_total,))
+    p_across = line(p_part, 1)
+    (p_total,) = call_sums([(p_part, p_across)])
+    p_rest = line(p_total, 2)
+    output = call_finish_output(position_col, hidden, routes, vec, got_res, (p_total,))
+    sum_in = call_in_result(kept, i_total, i_rest, (output,))
+    sum_out, sum_query, sum_key, sum_value, sum_vec, bias_rows, _ = call_attention_result(
+        kept, p_total, p_rest, width, span, n_vec, ff_shard, (output,)
+    )
+    sum_in_bias = bias_rows[:EXPERTS]
+    return (
+        output,
+        input_grad,
+        sum_vec[0],
+        sum_vec[1],
+        sum_query,
+        sum_vec[2],
+        sum_key,
+        sum_value,
+        sum_vec[3],
+        sum_out,
+        sum_vec[4],
+        sum_vec[5],
+        sum_vec[6],
+        sum_in,
+        sum_in_bias,
+        sum_down,
+        sum_vec[7:n_vec],
+    )
+
+
+def plan_of(n, replicas):
+    if n == 8 and replicas == 4:
+        return lambda *args: per_device_tokens(n, *args)
+    return per_device_weights
+
+
 def solution(mesh):
     in_specs = (
-        P(("fsdp", "rep"), None),
-        P(("fsdp", "rep"), None),
-        P(("fsdp", "rep"), None),
-        P("fsdp"),
-        P("fsdp"),
-        P("fsdp", None),
-        P("fsdp"),
-        P("fsdp", None),
-        P("fsdp", None),
-        P("fsdp"),
-        P("fsdp", None),
-        P("fsdp"),
-        P("fsdp"),
-        P("fsdp"),
-        P(None, "fsdp", None),
-        P(None, "fsdp"),
-        P(None, "fsdp", None),
-        P(None, "fsdp"),
-        P(("fsdp", "rep"), None),
+        P((FSDP, REP), None),
+        P((FSDP, REP), None),
+        P((FSDP, REP), None),
+        P(FSDP),
+        P(FSDP),
+        P(FSDP, None),
+        P(FSDP),
+        P(FSDP, None),
+        P(FSDP, None),
+        P(FSDP),
+        P(FSDP, None),
+        P(FSDP),
+        P(FSDP),
+        P(FSDP),
+        P(None, FSDP, None),
+        P(None, FSDP),
+        P(None, FSDP, None),
+        P(None, FSDP),
+        P((FSDP, REP), None),
     )
     out_specs = (
-        P(("fsdp", "rep"), None),
-        P(("fsdp", "rep"), None),
-        P("fsdp"),
-        P("fsdp"),
-        P("fsdp", None),
-        P("fsdp"),
-        P("fsdp", None),
-        P("fsdp", None),
-        P("fsdp"),
-        P("fsdp", None),
-        P("fsdp"),
-        P("fsdp"),
-        P("fsdp"),
-        P(None, "fsdp", None),
-        P(None, "fsdp"),
-        P(None, "fsdp", None),
-        P(None, "fsdp"),
-    )
+        P((FSDP, REP), None),
+        P((FSDP, REP), None),
+        P(FSDP),
+        P(FSDP),
+        P(FSDP, None),
+        P(FSDP),
+        P(FSDP, None),
+        P(FSDP, None),
+        P(FSDP),
+        P(FSDP, None),
+        P(FSDP),
+        P(FSDP),
+        P(FSDP),
+        P(None, FSDP, None),
+        P(None, FSDP),
+        P(None, FSDP, None),
+        P(None, FSDP),
+    )
+    per_device = plan_of(mesh.shape[FSDP], mesh.shape[REP])
     return jax.shard_map(
         per_device, mesh=mesh, in_specs=in_specs, out_specs=out_specs, check_vma=False
     )

time: 1310 us -> 386 us (0.29)
  waiting for transfers between devices: 937 us -> 125 us
  Pallas kernels: 0 us -> 161 us
  blocking collectives: 153 us -> 0 us
  matrix products: 112 us -> 0 us
  starting transfers between devices: 1.26 us -> 45.1 us
  other arithmetic: 36.1 us -> 5.28 us
  local copies, waits for them, and re-layouts: 50.5 us -> 28.9 us
    reduce_scatter x8 -> x0, waiting for transfers between devices: 585 us -> none  [the longest x1 241 us: per_device(): lax.psum_scatter(grad_in.astype(jnp.bfloat16), 'rep', scatter_dimension=2...]
    all_gather x8 -> x0, waiting for transfers between devices: 239 us -> none  [the longest x1 74.6 us: per_device(): lax.all_gather(expert_in, 'fsdp', axis=1, tiled=True)]
    pallas_call x0 -> x34, Pallas kernels: none -> 161 us  [kernel_call(): pl.pallas_call(body, out_shape=out_shape, in_specs=in_specs, out_specs=ou...]
    ppermute x0 -> x38, waiting for transfers between devices: none -> 120 us  [the longest x11 80.2 us: line(): return lax.ppermute(v, REP, pairs)]
    unnamed x28 -> x2, waiting for transfers between devices: 114 us -> 0.02 us
    dot_general x24 -> x0, matrix products: 112 us -> none  [the longest x1 11.3 us: per_device(): jnp.einsum('ecd,efd->ecf', grad_packed, w_down_back, preferred_element_ty...]
    all_gather x8 -> x0, blocking collectives: 96.4 us -> none  [the longest x1 14.4 us: per_device(): lax.all_gather(share_key.astype(jnp.bfloat16), 'rep', axis=1, tiled=True)]
    unnamed x3 -> x0, blocking collectives: 57 us -> none
  transfers between devices with their start and end apart: 22 -> 42, of which waited for: 20 -> 16; matrix products, arithmetic and copies ran while one was open for 14% -> 2% of each run, Pallas kernels for 0% -> 39%
where the time goes in v3:
time: 386 us; the launch traced here: 380 us
  Pallas kernels  161 us (42%)
  waiting for transfers between devices  125 us (32%)
  starting transfers between devices  45.1 us (12%)
  local copies, waits for them, and re-layouts  28.9 us (7%)
  between operations  15 us (4%)
  other arithmetic  5.28 us (1%)
    pallas_call x34, Pallas kernels, kernel_call(): pl.pallas_call(body, out_shape=out_shape, in_specs=in_specs, out_specs=ou...  161 us
    ppermute x11, waiting for transfers between devices, line(): return lax.ppermute(v, REP, pairs)  80.2 us
    ppermute x27, waiting for transfers between devices, swap(): return lax.ppermute(v, FSDP, [(i, i ^ mask) for i in range(n)])  39.8 us
    unnamed x84, local copies, waits for them, and re-layouts  20.3 us
    ppermute x27, starting transfers between devices, swap(): return lax.ppermute(v, FSDP, [(i, i ^ mask) for i in range(n)])  19.2 us
    ppermute x11, starting transfers between devices, line(): return lax.ppermute(v, REP, pairs)  13.9 us
    all_to_all x3, starting transfers between devices, exchange(): return lax.all_to_all(v, FSDP, 0, 0, axis_index_groups=groups)  11.9 us
  transfers between devices with their start and end apart: 42, of which 16 were waited for; matrix products, arithmetic and copies ran while one was open for 2% of the time, Pallas kernels for 39%

profile of v3, /device:TPU:0, one launch (start us, length us, event | category | flops | bytes accessed | tf_op | source)
XLA Modules:
  0.0 380.1 jit_solution(3758264200128944611)
XLA Ops:
  7.2 1.4 stack.37.refs_4_
  8.6 2.1 pack.1.refs_0_.refs_3_.refs_5_.refs_11_
  10.7 2.9 collective-permute-start
  13.6 1.5 collective-permute-start.1
  18.4 9.2 %collective-permute-done.refs_1_.refs_4_.refs_6_.refs_12_ = bf16[400,768]{1,0:T(8,128)(2,1)S(1)} collective-permute-done((bf16[400,768]{1,0:T(8,128)(2,1)}, bf16[400,768]{1,0:T(8,128)(2,1)S(1)}, u32[]{:S(2)}, u32[]{:S(2)}) %collective-permute-start) | collective-permute-done | bytes 614432 | tf_op jit(solution)/shard_map/ppermute | solution.py:1403
  27.7 1.5 collective-permute-done.1.refs_2_.refs_5_.refs_7_.refs_13_
  30.0 2.9 call_halves.1
  32.9 1.5 collective-permute-start.2
  36.0 4.6 %collective-permute-done.2.refs_6_.refs_8_.refs_14_ = bf16[192,768]{1,0:T(8,128)(2,1)S(1)} collective-permute-done((bf16[192,768]{1,0:T(8,128)(2,1)}, bf16[192,768]{1,0:T(8,128)(2,1)S(1)}, u32[]{:S(2)}, u32[]{:S(2)}) %collective-permute-start.2) | collective-permute-done | bytes 294944 | tf_op jit(solution)/shard_map/ppermute | solution.py:1403
  40.6 1.8 collective-permute-done.3.refs_7_.refs_9_.refs_15_
  43.1 3.7 call_columns_and_sort.1
  47.6 3.7 all-to-all-start
  51.9 14.7 %attention_forward.1 = (bf16[416,2304]{1,0:T(8,128)(2,1)}, bf16[416,768]{1,0:T(8,128)(2,1)}, f32[16,416]{1,0:T(8,128)}, bf16[416,768]{1,0:T(8,128)(2,1)}, f32[16,768]{1,0:T(8,128)}, /*index=5*/f32[16,768]{1,0:T(8,128)}) custom-call(s32[1]{0:T(128)} %bitcast.5.refs_0_, s32[1,4]{1,0:T(1,128)} %refs_1_.7, bf16[416,768]{1,0:T(8,128)(2,1)} %refs_2_.11, ...), custom_call_target="tpu_custom_call" | custom-call | tf_op jit(solution)/shard_map/attention_forward/pallas_call | solution.py:427
  66.6 5.2 %mix_out.1 = (f32[416,768]{1,0:T(8,128)}, bf16[448,768]{1,0:T(8,128)(2,1)}) custom-call(s32[1]{0:T(128)} %bitcast.5.refs_0_, bf16[416,768]{1,0:T(8,128)(2,1)} %get-tuple-element.93.refs_1_.refs_6_, bf16[416,768]{1,0:T(8,128)(2,1)} %refs_2_.11, f32[16,768]{1,0:T(8,128)} %get-tuple-element.94.refs_3_.refs_5_, s32[1,416]{1,0:T(1,128)} %bitcast.55, ...), custom_call_target="tpu_custom_call" | custom-call | tf_op jit(solution)/shard_map/mix_out/pallas_call | solution.py:427
  71.8 1.8 all-to-all-done.refs_0_
  74.8 1.5 collective-permute-start.10
  76.8 1.5 collective-permute-start.7
  80.1 9.8 %experts.3 = (bf16[448,768]{1,0:T(8,128)(2,1)}, bf16[4,448,768]{2,1,0:T(8,128)(2,1)}, bf16[3,208,768]{2,1,0:T(8,128)(2,1)}, bf16[3,208,768]{2,1,0:T(8,128)(2,1)}) custom-call(s32[1]{0:T(128)} %bitcast.5.refs_0_, s32[1,9]{1,0:T(1,128)} %copy-done.38, f32[16,768]{1,0:T(8,128)} %get-tuple-element.98.refs_2_, ...), custom_call_target="tpu_custom_call" | custom-call | tf_op jit(solution)/shard_map/experts/pallas_call | solution.py:427
  89.9 4.0 %collective-permute-done.10.refs_3_.refs_6_.refs_4_ = bf16[464,768]{1,0:T(8,128)(2,1)} collective-permute-done((bf16[464,768]{1,0:T(8,128)(2,1)}, bf16[464,768]{1,0:T(8,128)(2,1)}, u32[]{:S(2)}, u32[]{:S(2)}) %collective-permute-start.10) | collective-permute-done | bytes 712736 | tf_op jit(solution)/shard_map/ppermute | solution.py:1403
  93.9 1.5 collective-permute-done.9.refs_2_.refs_5_.refs_3_
  95.4 14.0 %collective-permute-done.7.refs_0_.refs_3_ = bf16[448,768]{1,0:T(8,128)(2,1)} collective-permute-done((bf16[448,768]{1,0:T(8,128)(2,1)}, bf16[448,768]{1,0:T(8,128)(2,1)}, u32[]{:S(2)}, u32[]{:S(2)}) %collective-permute-start.7) | collective-permute-done | bytes 688160 | tf_op jit(solution)/shard_map/ppermute | solution.py:1403
  110.3 2.9 call_two_halves.1
  113.7 1.5 collective-permute-start.14
  117.1 14.1 %experts.4 = (bf16[448,768]{1,0:T(8,128)(2,1)}, bf16[448,768]{1,0:T(8,128)(2,1)}, bf16[4,448,768]{2,1,0:T(8,128)(2,1)}, bf16[3,416,768]{2,1,0:T(8,128)(2,1)}, bf16[3,416,768]{2,1,0:T(8,128)(2,1)}) custom-call(s32[1]{0:T(128)} %bitcast.5.refs_0_, s32[2,9]{1,0:T(2,128)} %convert_multiply_fusion.refs_1_, ...), custom_call_target="tpu_custom_call", output_to_operand_aliasing={{2}: (11, {})} | custom-call | tf_op jit(solution)/shard_map/experts/pallas_call | solution.py:427
  131.9 1.5 collective-permute-start.16
  134.8 9.6 %experts.5 = (bf16[448,768]{1,0:T(8,128)(2,1)}, bf16[4,448,768]{2,1,0:T(8,128)(2,1)}, bf16[3,208,768]{2,1,0:T(8,128)(2,1)}, bf16[3,208,768]{2,1,0:T(8,128)(2,1)}) custom-call(s32[1]{0:T(128)} %bitcast.5.refs_0_, s32[1,9]{1,0:T(1,128)} %fusion.1.refs_1_, f32[16,768]{1,0:T(8,128)} %get-tuple-element.98.refs_2_, ...), custom_call_target="tpu_custom_call", output_to_operand_aliasing={{1}: (11, {})} | custom-call | tf_op jit(solution)/shard_map/experts/pallas_call | solution.py:427
  144.4 1.5 collective-permute-start.17
  146.5 3.2 collective-permute-done.15.refs_10_.refs_8_
  150.5 10.5 %down_grads.1 = (bf16[3,384,768]{2,1,0:T(8,128)(2,1)}, bf16[384,768]{1,0:T(8,128)(2,1)}, bf16[384,768]{1,0:T(8,128)(2,1)}, bf16[384,768]{1,0:T(8,128)(2,1)}) custom-call(s32[1]{0:T(128)} %bitcast.5.refs_0_, s32[4,9]{1,0:T(4,128)} %pad_add_fusion.refs_1_, bf16[464,768]{1,0:T(8,128)(2,1)} %get-tuple-element.97.refs_4_.refs_2_, ...), custom_call_target="tpu_custom_call" | custom-call | tf_op jit(solution)/shard_map/down_grads/pallas_call | solution.py:427
  164.5 7.3 %mix_out_backward.1 = (f32[416,768]{1,0:T(8,128)}, bf16[416,768]{1,0:T(8,128)(2,1)}, f32[16,768]{1,0:T(8,128)}, bf16[768,768]{1,0:T(8,128)(2,1)}) custom-call(s32[1]{0:T(128)} %bitcast.5.refs_0_, s32[416,1]{1,0:T(8,128)} %copy.60.refs_1_.refs_0_, s32[416,1]{1,0:T(8,128)} %copy.61.refs_2_, f32[416,768]{1,0:T(8,128)} %get-tuple-element.95.refs_3_.refs_1_, ...), custom_call_target="tpu_custom_call" | custom-call | tf_op jit(solution)/shard_map/mix_out_backward/pallas_call | solution.py:427
  172.9 3.5 call_pair_down.1
  176.4 1.6 collective-permute-start.22
  178.0 10.8 %in_grads.1 = (bf16[4,3,96,768]{3,2,1,0:T(8,128)(2,1)}, bf16[16,384]{1,0:T(8,128)(2,1)}, bf16[16,384]{1,0:T(8,128)(2,1)}, bf16[4,96,768]{2,1,0:T(8,128)(2,1)}, b...) custom-call(s32[1]{0:T(128)} %bitcast.5.refs_0_, s32[4,9]{1,0:T(4,128)} %pad_add_fusion.refs_1_, ...), custom_call_target="tpu_custom_call" | custom-call | tf_op jit(solution)/shard_map/in_grads/pallas_call | solution.py:427
  189.9 11.4 %attention_backward_one.1 = (bf16[416,1152]{1,0:T(8,128)(2,1)}, bf16[4,96,1920]{2,1,0:T(8,128)(2,1)}, bf16[4,96,1920]{2,1,0:T(8,128)(2,1)}) custom-call(s32[1]{0:T(128)} %bitcast.5.refs_0_, s32[1,4]{1,0:T(1,128)} %refs_1_.7, bf16[416,2304]{1,0:T(8,128)(2,1)} %get-tuple-element.115.refs_2_.refs_5_, f32[16,416]{1,0:T(8,128)} %get-tuple-element.116.refs_3_.refs_6_, ...), custom_call_target="tpu_custom_call" | custom-call | tf_op jit(solution)/shard_map/attention_backward_one/pallas_call | solution.py:427
  202.8 4.4 %call_pair_in.1 = (bf16[4,3,96,768]{3,2,1,0:T(8,128)(2,1)}, bf16[16,384]{1,0:T(8,128)(2,1)}, bf16[1,192,768]{2,1,0:T(8,128)(2,1)}, bf16[2,192,768]{2,1,0:T(8,128)(2,1)}) custom-call(bf16[4,3,96,768]{3,2,1,0:T(8,128)(2,1)} %get-tuple-element.125.refs_7_.refs_4_.refs_0_, bf16[16,384]{1,0:T(8,128)(2,1)} %get-tuple-element.128.refs_1_, ...), custom_call_target="tpu_custom_call" | custom-call | tf_op jit(solution)/shard_map/call_pair_in/pallas_call | solution.py:427
  207.3 3.8 %all-to-all-start.1 = ((bf16[4,3,96,768]{3,2,1,0:T(8,128)(2,1)}), bf16[4,3,96,768]{3,2,1,0:T(8,128)(2,1)S(1)}, u32[]{:S(2)}, u32[]{:S(2)}) async-start(bf16[4,3,96,768]{3,2,1,0:T(8,128)(2,1)} %get-tuple-element.139.refs_1_.refs_19_), calls=%async_computation.1 | async-start | bytes 3538944 | tf_op jit(solution)/shard_map/all_to_all | solution.py:1417
  212.1 2.4 collective-permute-start.27
  214.4 15.8 %attention_backward_two.1 = (f32[416,768]{1,0:T(8,128)}, bf16[4,96,1280]{2,1,0:T(8,128)(2,1)}, bf16[4,96,1280]{2,1,0:T(8,128)(2,1)}) custom-call(s32[1]{0:T(128)} %bitcast.5.refs_0_, s32[1,4]{1,0:T(1,128)} %refs_1_.7, bf16[416,768]{1,0:T(8,128)(2,1)} %refs_2_.11, f32[16,768]{1,0:T(8,128)} %get-tuple-element.94.refs_3_.refs_5_, ...), custom_call_target="tpu_custom_call" | custom-call | tf_op jit(solution)/shard_map/attention_backward_two/pallas_call | solution.py:427
  231.0 1.5 collective-permute-start.29
  232.5 3.3 all-to-all-done.1.refs_1_
  237.1 2.8 call_split_rows.1
  239.8 1.5 collective-permute-start.30
  243.0 4.4 %call_pair_shares.1.refs_7_.refs_0_ = bf16[4,96,3200]{2,1,0:T(8,128)(2,1)} custom-call(bf16[4,96,1920]{2,1,0:T(8,128)(2,1)} %get-tuple-element.126.refs_0_, bf16[4,96,1920]{2,1,0:T(8,128)(2,1)} %copy-done.16, bf16[4,96,1280]{2,1,0:T(8,128)(2,1)} %get-tuple-element.142.refs_2_.refs_4_, bf16[4,96,1280]{2,1,0:T(8,128)(2,1)} %collective-permute-done.28.refs_3_, ...), custom_call_target="tpu_custom_call" | custom-call | tf_op jit(solution)/shard_map/call_pair_shares/pallas_call | solution.py:427
  247.4 2.0 collective-permute-done.29.refs_3_
  249.3 9.1 %collective-permute-done.30.refs_5_ = bf16[2,3,48,768]{3,2,1,0:T(8,128)(2,1)S(1)} collective-permute-done((bf16[2,3,48,768]{3,2,1,0:T(8,128)(2,1)}, bf16[2,3,48,768]{3,2,1,0:T(8,128)(2,1)S(1)}, u32[]{:S(2)}, u32[]{:S(2)}) %collective-permute-start.30) | collective-permute-done | bytes 442400 | tf_op jit(solution)/shard_map/ppermute | solution.py:1427
  258.4 9.4 %collective-permute-done.31.refs_6_ = bf16[2,3,48,768]{3,2,1,0:T(8,128)(2,1)S(1)} collective-permute-done((bf16[2,3,48,768]{3,2,1,0:T(8,128)(2,1)}, bf16[2,3,48,768]{3,2,1,0:T(8,128)(2,1)S(1)}, u32[]{:S(2)}, u32[]{:S(2)}) %collective-permute-start.31) | collective-permute-done | bytes 442400 | tf_op jit(solution)/shard_map/ppermute | solution.py:1427
  268.6 3.4 call_line_sums.1
  272.0 4.3 %all-to-all-start.2 = ((bf16[4,96,3200]{2,1,0:T(8,128)(2,1)}), bf16[4,96,3200]{2,1,0:T(8,128)(2,1)S(1)}, u32[]{:S(2)}, u32[]{:S(2)}) async-start(bf16[4,96,3200]{2,1,0:T(8,128)(2,1)} %hold.13), calls=%async_computation.2 | async-start | bytes 4915200 | tf_op jit(solution)/shard_map/all_to_all | solution.py:1417
  276.3 2.0 collective-permute-start.34
  278.3 37.1 %collective-permute-done.32.refs_2_ = bf16[3,192,768]{2,1,0:T(8,128)(2,1)} collective-permute-done((bf16[3,192,768]{2,1,0:T(8,128)(2,1)S(1)}, bf16[3,192,768]{2,1,0:T(8,128)(2,1)}, u32[]{:S(2)}, u32[]{:S(2)}) %collective-permute-start.32) | collective-permute-done | bytes 884768 | tf_op jit(solution)/shard_map/ppermute | solution.py:1427
  315.5 3.5 call_down_result.1.refs_3_
  318.9 1.4 copy-done.7
  320.4 2.7 call_attention_shares.1
  323.1 2.6 call_sums.3.refs_2_.refs_1_
  325.7 2.0 collective-permute-start.37
  327.7 7.1 %collective-permute-done.33.refs_1_ = bf16[64,3200]{1,0:T(8,128)(2,1)S(1)} collective-permute-done((bf16[64,3200]{1,0:T(8,128)(2,1)}, bf16[64,3200]{1,0:T(8,128)(2,1)S(1)}, u32[]{:S(2)}, u32[]{:S(2)}) %collective-permute-start.33) | collective-permute-done | bytes 409632 | tf_op jit(solution)/shard_map/ppermute | solution.py:1427
  335.6 2.0 call_sums.4.refs_0_
  337.5 15.5 %collective-permute-done.35.refs_1_ = bf16[64,3200]{1,0:T(8,128)(2,1)S(1)} collective-permute-done((bf16[64,3200]{1,0:T(8,128)(2,1)}, bf16[64,3200]{1,0:T(8,128)(2,1)S(1)}, u32[]{:S(2)}, u32[]{:S(2)}) %collective-permute-start.35) | collective-permute-done | bytes 409632 | tf_op jit(solution)/shard_map/ppermute | solution.py:1427
  353.7 2.0 call_sums.5.refs_5_.refs_1_
  355.7 2.4 collective-permute-start.36
  358.1 3.3 finish_output.1.refs_3_
  362.3 3.5 call_in_result.1
  366.5 2.2 call_attention_result.1
  368.7 1.5 slice_bitcast_fusion
  (168 shorter events, 36.5 us)
Async XLA Ops:
  7.2 35.2 %copy-start.35 = (s32[416,1]{0,1:T(1,128)S(1)}, s32[416,1]{0,1:T(1,128)}, u32[]{:S(2)}) copy-start(s32[416,1]{0,1:T(1,128)} %param.21) | copy-start | bytes 4996
  10.7 17.0 %collective-permute-start = (bf16[400,768]{1,0:T(8,128)(2,1)}, bf16[400,768]{1,0:T(8,128)(2,1)S(1)}, u32[]{:S(2)}, u32[]{:S(2)}) collective-permute-start(bf16[400,768]{1,0:T(8,128)(2,1)} %pack.1.refs_0_.refs_3_.refs_5_.refs_11_), channel_id=1, source_target_pairs={{0,8},{4,12},{8,0},{12,4},{16,24},{20,28},{24,16},{28,20},{1,9},{5... | collective-permute-start | bytes 1843208 | tf_op jit(solution)/shard_map/ppermute | solution.py:1403
  13.6 15.5 %collective-permute-start.1 = (bf16[400,768]{1,0:T(8,128)(2,1)}, bf16[400,768]{1,0:T(8,128)(2,1)S(1)}, u32[]{:S(2)}, u32[]{:S(2)}) collective-permute-start(bf16[400,768]{1,0:T(8,128)(2,1)} %pack.1.refs_0_.refs_3_.refs_5_.refs_11_), channel_id=1, source_target_pairs={{0,16},{4,20},{8,24},{12,28},{16,0},{20,4},{24,8},{28,12},{1,17},{... | collective-permute-start | bytes 1843208 | tf_op jit(solution)/shard_map/ppermute | solution.py:1403
  18.4 28.4 %copy-start.38 = (s32[1,9]{1,0:T(1,128)}, s32[1,9]{1,0:T(1,128)S(1)}, u32[]{:S(2)}) copy-start(s32[1,9]{1,0:T(1,128)S(1)} %mul.50.refs_1_) | copy-start | bytes 112
  27.7 1.5 copy-start.3
  32.9 7.8 %collective-permute-start.2 = (bf16[192,768]{1,0:T(8,128)(2,1)}, bf16[192,768]{1,0:T(8,128)(2,1)S(1)}, u32[]{:S(2)}, u32[]{:S(2)}) collective-permute-start(bf16[192,768]{1,0:T(8,128)(2,1)} %get-tuple-element.90.refs_4_), channel_id=1, source_target_pairs={{0,16},{4,20},{8,24},{12,28},{16,0},{20,4},{24,8},{28,12},{1,17},{... | collective-permute-start | bytes 884744 | tf_op jit(solution)/shard_map/ppermute | solution.py:1403
  34.4 8.0 %collective-permute-start.3 = (bf16[208,768]{1,0:T(8,128)(2,1)}, bf16[208,768]{1,0:T(8,128)(2,1)S(1)}, u32[]{:S(2)}, u32[]{:S(2)}) collective-permute-start(bf16[208,768]{1,0:T(8,128)(2,1)} %get-tuple-element.91), channel_id=1, source_target_pairs={{0,8},{4,12},{8,0},{12,4},{16,24},{20,28},{24,16},{28,20},{1,9},{5... | collective-permute-start | bytes 958472 | tf_op jit(solution)/shard_map/ppermute | solution.py:1403
  36.0 15.9 %collective-permute-start.4 = (bf16[3,400,768]{2,1,0:T(8,128)(2,1)}, bf16[3,400,768]{2,1,0:T(8,128)(2,1)}, u32[]{:S(2)}, u32[]{:S(2)}) collective-permute-start(bf16[3,400,768]{2,1,0:T(8,128)(2,1)} %get-tuple-element.92), channel_id=1, source_target_pairs={{0,4},{4,0},{8,12},{12,8},{16,20},{20,16},{24,28},{28,24},{1,5},{5... | collective-permute-start | bytes 5529608 | tf_op jit(solution)/shard_map/ppermute | solution.py:1403
  40.6 6.2 %copy-start.13 = (bf16[192,768]{1,0:T(8,128)(2,1)}, bf16[192,768]{1,0:T(8,128)(2,1)S(1)}, u32[]{:S(2)}) copy-start(bf16[192,768]{1,0:T(8,128)(2,1)S(1)} %collective-permute-done.2.refs_6_.refs_8_.refs_14_) | copy-start | bytes 884740
  40.6 6.1 %collective-permute-start.5 = (bf16[192,768]{1,0:T(8,128)(2,1)S(1)}, bf16[192,768]{1,0:T(8,128)(2,1)S(1)}, u32[]{:S(2)}, u32[]{:S(2)}) collective-permute-start(bf16[192,768]{1,0:T(8,128)(2,1)S(1)} %collective-permute-done.2.refs_6_.refs_8_.refs_14_), channel_id=1, source_target_pairs={{0,4},{4,0},{8,12},{12,8},{16,20},{20,16},{24,28},{28,24},{1,5},{5... | collective-permute-start | bytes 884744 | tf_op jit(solution)/shard_map/ppermute | solution.py:1403
  42.4 4.4 %copy-start.12 = (bf16[208,768]{1,0:T(8,128)(2,1)}, bf16[208,768]{1,0:T(8,128)(2,1)S(1)}, u32[]{:S(2)}) copy-start(bf16[208,768]{1,0:T(8,128)(2,1)S(1)} %collective-permute-done.3.refs_7_.refs_9_.refs_15_) | copy-start | bytes 958468
  42.4 4.4 %collective-permute-start.6 = (bf16[208,768]{1,0:T(8,128)(2,1)S(1)}, bf16[208,768]{1,0:T(8,128)(2,1)S(1)}, u32[]{:S(2)}, u32[]{:S(2)}) collective-permute-start(bf16[208,768]{1,0:T(8,128)(2,1)S(1)} %collective-permute-done.3.refs_7_.refs_9_.refs_15_), channel_id=1, source_target_pairs={{0,4},{4,0},{8,12},{12,8},{16,20},{20,16},{24,28},{28,24},{1,5},{5... | collective-permute-start | bytes 958472 | tf_op jit(solution)/shard_map/ppermute | solution.py:1403
  47.6 3.8 copy-start.1
  47.6 26.0 %all-to-all-start = ((bf16[4,3,96,768]{3,2,1,0:T(8,128)(2,1)}), bf16[4,3,96,768]{3,2,1,0:T(8,128)(2,1)S(1)}, u32[]{:S(2)}, u32[]{:S(2)}) async-start(bf16[4,3,96,768]{3,2,1,0:T(8,128)(2,1)} %hold.7), calls=%async_computation | async-start | bytes 3538944 | tf_op jit(solution)/shard_map/all_to_all | solution.py:1417
  51.3 306.8 %reduce-scatter.4.cloned.1.call-start = ((), (), s32[]{:S(2)}) async-start(), calls=%async_computation.4 | async-start | bytes 3440640
  51.4 26.9 %collective-permute-start.12 = (bf16[3,384,768]{2,1,0:T(8,128)(2,1)S(1)}, bf16[3,384,768]{2,1,0:T(8,128)(2,1)}, u32[]{:S(2)}, u32[]{:S(2)}) collective-permute-start(bf16[3,384,768]{2,1,0:T(8,128)(2,1)S(1)} %copy-done.1), channel_id=1, source_target_pairs={{0,4},{4,0},{8,12},{12,8},{16,20},{20,16},{24,28},{28,24},{1,5},{5... | collective-permute-start | bytes 5308424 | tf_op jit(solution)/shard_map/ppermute | solution.py:1403
  73.6 1.2 copy-start
  74.8 4.1 %collective-permute-start.11 = (bf16[4,3,96,768]{3,2,1,0:T(8,128)(2,1)}, bf16[4,3,96,768]{3,2,1,0:T(8,128)(2,1)S(1)}, u32[]{:S(2)}, u32[]{:S(2)}) collective-permute-start(bf16[4,3,96,768]{3,2,1,0:T(8,128)(2,1)} %hold.8.refs_5_.refs_7_), channel_id=1, source_target_pairs={{0,4},{4,0},{8,12},{12,8},{16,20},{20,16},{24,28},{28,24},{1,5},{5... | collective-permute-start | bytes 5308424 | tf_op jit(solution)/shard_map/ppermute | solution.py:1403
  74.8 19.1 %collective-permute-start.10 = (bf16[464,768]{1,0:T(8,128)(2,1)}, bf16[464,768]{1,0:T(8,128)(2,1)}, u32[]{:S(2)}, u32[]{:S(2)}) collective-permute-start(bf16[464,768]{1,0:T(8,128)(2,1)} %get-tuple-element.97.refs_4_.refs_2_), channel_id=1, source_target_pairs={{0,16},{4,20},{8,24},{12,28},{16,0},{20,4},{24,8},{28,12},{1,17},{... | collective-permute-start | bytes 2138120 | tf_op jit(solution)/shard_map/ppermute | solution.py:1403
  76.3 19.1 %collective-permute-start.9 = (bf16[464,768]{1,0:T(8,128)(2,1)}, bf16[464,768]{1,0:T(8,128)(2,1)}, u32[]{:S(2)}, u32[]{:S(2)}) collective-permute-start(bf16[464,768]{1,0:T(8,128)(2,1)} %get-tuple-element.97.refs_4_.refs_2_), channel_id=1, source_target_pairs={{0,8},{4,12},{8,0},{12,4},{16,24},{20,28},{24,16},{28,20},{1,9},{5... | collective-permute-start | bytes 2138120 | tf_op jit(solution)/shard_map/ppermute | solution.py:1403
  76.8 32.6 %collective-permute-start.7 = (bf16[448,768]{1,0:T(8,128)(2,1)}, bf16[448,768]{1,0:T(8,128)(2,1)}, u32[]{:S(2)}, u32[]{:S(2)}) collective-permute-start(bf16[448,768]{1,0:T(8,128)(2,1)} %get-tuple-element.96.refs_1_.refs_3_.refs_2_), channel_id=1, source_target_pairs={{0,8},{4,12},{8,0},{12,4},{16,24},{20,28},{24,16},{28,20},{1,9},{5... | collective-permute-start | bytes 2064392 | tf_op jit(solution)/shard_map/ppermute | solution.py:1403
  78.3 31.1 %collective-permute-start.8 = (bf16[448,768]{1,0:T(8,128)(2,1)}, bf16[448,768]{1,0:T(8,128)(2,1)S(1)}, u32[]{:S(2)}, u32[]{:S(2)}) collective-permute-start(bf16[448,768]{1,0:T(8,128)(2,1)} %get-tuple-element.96.refs_1_.refs_3_.refs_2_), channel_id=1, source_target_pairs={{0,16},{4,20},{8,24},{12,28},{16,0},{20,4},{24,8},{28,12},{1,17},{... | collective-permute-start | bytes 2064392 | tf_op jit(solution)/shard_map/ppermute | solution.py:1403
  78.8 1.2 copy-start.2
  113.1 20.2 %collective-permute-start.13 = (bf16[464,768]{1,0:T(8,128)(2,1)}, bf16[464,768]{1,0:T(8,128)(2,1)S(1)}, u32[]{:S(2)}, u32[]{:S(2)}) collective-permute-start(bf16[464,768]{1,0:T(8,128)(2,1)} %get-tuple-element.101), channel_id=1, source_target_pairs={{0,8},{4,12},{8,0},{12,4},{16,24},{20,28},{24,16},{28,20},{1,9},{5... | collective-permute-start | bytes 2138120 | tf_op jit(solution)/shard_map/ppermute | solution.py:1403
  113.7 20.2 %collective-permute-start.14 = (bf16[448,768]{1,0:T(8,128)(2,1)}, bf16[448,768]{1,0:T(8,128)(2,1)S(1)}, u32[]{:S(2)}, u32[]{:S(2)}) collective-permute-start(bf16[448,768]{1,0:T(8,128)(2,1)} %get-tuple-element.102), channel_id=1, source_target_pairs={{0,16},{4,20},{8,24},{12,28},{16,0},{20,4},{24,8},{28,12},{1,17},{... | collective-permute-start | bytes 2064392 | tf_op jit(solution)/shard_map/ppermute | solution.py:1403
  131.2 18.5 %collective-permute-start.15 = (bf16[448,768]{1,0:T(8,128)(2,1)}, bf16[448,768]{1,0:T(8,128)(2,1)S(1)}, u32[]{:S(2)}, u32[]{:S(2)}) collective-permute-start(bf16[448,768]{1,0:T(8,128)(2,1)} %get-tuple-element.107), channel_id=1, source_target_pairs={{0,8},{4,12},{8,0},{12,4},{16,24},{20,28},{24,16},{28,20},{1,9},{5... | collective-permute-start | bytes 2064392 | tf_op jit(solution)/shard_map/ppermute | solution.py:1403
  131.9 31.5 %collective-permute-start.16 = (bf16[448,768]{1,0:T(8,128)(2,1)}, bf16[448,768]{1,0:T(8,128)(2,1)S(1)}, u32[]{:S(2)}, u32[]{:S(2)}) collective-permute-start(bf16[448,768]{1,0:T(8,128)(2,1)} %get-tuple-element.108), channel_id=1, source_target_pairs={{0,16},{4,20},{8,24},{12,28},{16,0},{20,4},{24,8},{28,12},{1,17},{... | collective-permute-start | bytes 2064392 | tf_op jit(solution)/shard_map/ppermute | solution.py:1403
  134.8 11.1 %copy-start.37 = (s32[2,9]{1,0:T(2,128)S(1)}, s32[2,9]{1,0:T(2,128)}, u32[]{:S(2)}) copy-start(s32[2,9]{1,0:T(2,128)} %convert_multiply_fusion.refs_1_) | copy-start | bytes 220
  134.8 11.1 %copy-start.39 = (s32[1,9]{1,0:T(1,128)S(1)}, s32[1,9]{1,0:T(1,128)}, u32[]{:S(2)}) copy-start(s32[1,9]{1,0:T(1,128)} %copy-done.38) | copy-start | bytes 112
  134.8 11.1 %copy-start.40 = (s32[1,9]{1,0:T(1,128)S(1)}, s32[1,9]{1,0:T(1,128)}, u32[]{:S(2)}) copy-start(s32[1,9]{1,0:T(1,128)} %fusion.1.refs_1_) | copy-start | bytes 112
  144.4 19.0 %collective-permute-start.17 = (bf16[448,768]{1,0:T(8,128)(2,1)}, bf16[448,768]{1,0:T(8,128)(2,1)S(1)}, u32[]{:S(2)}, u32[]{:S(2)}) collective-permute-start(bf16[448,768]{1,0:T(8,128)(2,1)} %get-tuple-element.109), channel_id=1, source_target_pairs={{0,24},{4,28},{8,16},{12,20},{16,8},{20,12},{24,0},{28,4},{1,25},{... | collective-permute-start | bytes 2064392 | tf_op jit(solution)/shard_map/ppermute | solution.py:1403
  150.5 12.0 %copy-start.34 = (s32[416]{0:T(512)S(1)}, s32[416]{0:T(512)}, u32[]{:S(2)}) copy-start(s32[416]{0:T(512)} %add_add_fusion) | copy-start | bytes 4996
  161.1 10.7 %collective-permute-start.18 = (bf16[384,768]{1,0:T(8,128)(2,1)}, bf16[384,768]{1,0:T(8,128)(2,1)S(1)}, u32[]{:S(2)}, u32[]{:S(2)}) collective-permute-start(bf16[384,768]{1,0:T(8,128)(2,1)} %get-tuple-element.121), channel_id=1, source_target_pairs={{0,4},{4,0},{8,12},{12,8},{16,20},{20,16},{24,28},{28,24},{1,5},{5... | collective-permute-start | bytes 1769480 | tf_op jit(solution)/shard_map/ppermute | solution.py:1403
  161.1 10.6 %collective-permute-start.19 = (bf16[384,768]{1,0:T(8,128)(2,1)}, bf16[384,768]{1,0:T(8,128)(2,1)S(1)}, u32[]{:S(2)}, u32[]{:S(2)}) collective-permute-start(bf16[384,768]{1,0:T(8,128)(2,1)} %get-tuple-element.122), channel_id=1, source_target_pairs={{0,4},{4,0},{8,12},{12,8},{16,20},{20,16},{24,28},{28,24},{1,5},{5... | collective-permute-start | bytes 1769480 | tf_op jit(solution)/shard_map/ppermute | solution.py:1403
  161.6 10.1 %collective-permute-start.20 = (bf16[384,768]{1,0:T(8,128)(2,1)}, bf16[384,768]{1,0:T(8,128)(2,1)S(1)}, u32[]{:S(2)}, u32[]{:S(2)}) collective-permute-start(bf16[384,768]{1,0:T(8,128)(2,1)} %get-tuple-element.123), channel_id=1, source_target_pairs={{0,4},{4,0},{8,12},{12,8},{16,20},{20,16},{24,28},{28,24},{1,5},{5... | collective-permute-start | bytes 1769480 | tf_op jit(solution)/shard_map/ppermute | solution.py:1403
  163.4 1.1 copy-start.21
  171.8 1.1 copy-start.23
  171.8 1.2 copy-start.24
  176.4 25.0 %collective-permute-start.22 = (bf16[3,192,768]{2,1,0:T(8,128)(2,1)}, bf16[3,192,768]{2,1,0:T(8,128)(2,1)S(1)}, u32[]{:S(2)}, u32[]{:S(2)}) collective-permute-start(bf16[3,192,768]{2,1,0:T(8,128)(2,1)} %get-tuple-element.124.refs_10_), channel_id=1, source_target_pairs={{0,1},{1,0},{2,3},{3,2},{4,5},{5,4},{6,7},{7,6},{8,9},{9,8},{10,11... | collective-permute-start | bytes 2654216 | tf_op jit(solution)/shard_map/ppermute | solution.py:1427
  188.9 12.5 %collective-permute-start.23 = (bf16[4,96,768]{2,1,0:T(8,128)(2,1)}, bf16[4,96,768]{2,1,0:T(8,128)(2,1)S(1)}, u32[]{:S(2)}, u32[]{:S(2)}) collective-permute-start(bf16[4,96,768]{2,1,0:T(8,128)(2,1)} %get-tuple-element.135), channel_id=1, source_target_pairs={{0,4},{4,0},{8,12},{12,8},{16,20},{20,16},{24,28},{28,24},{1,5},{5... | collective-permute-start | bytes 1769480 | tf_op jit(solution)/shard_map/ppermute | solution.py:1403
  189.1 12.3 %collective-permute-start.24 = (bf16[4,96,768]{2,1,0:T(8,128)(2,1)}, bf16[4,96,768]{2,1,0:T(8,128)(2,1)S(1)}, u32[]{:S(2)}, u32[]{:S(2)}) collective-permute-start(bf16[4,96,768]{2,1,0:T(8,128)(2,1)} %get-tuple-element.136), channel_id=1, source_target_pairs={{0,4},{4,0},{8,12},{12,8},{16,20},{20,16},{24,28},{28,24},{1,5},{5... | collective-permute-start | bytes 1769480 | tf_op jit(solution)/shard_map/ppermute | solution.py:1403
  189.4 12.0 %collective-permute-start.25 = (bf16[4,96,768]{2,1,0:T(8,128)(2,1)}, bf16[4,96,768]{2,1,0:T(8,128)(2,1)S(1)}, u32[]{:S(2)}, u32[]{:S(2)}) collective-permute-start(bf16[4,96,768]{2,1,0:T(8,128)(2,1)} %get-tuple-element.137), channel_id=1, source_target_pairs={{0,4},{4,0},{8,12},{12,8},{16,20},{20,16},{24,28},{28,24},{1,5},{5... | collective-permute-start | bytes 1769480 | tf_op jit(solution)/shard_map/ppermute | solution.py:1403
  189.6 11.7 %collective-permute-start.21 = (bf16[16,384]{1,0:T(8,128)(2,1)}, bf16[16,384]{1,0:T(8,128)(2,1)S(1)}, u32[]{:S(2)}, u32[]{:S(2)}) collective-permute-start(bf16[16,384]{1,0:T(8,128)(2,1)} %get-tuple-element.133), channel_id=1, source_target_pairs={{0,4},{4,0},{8,12},{12,8},{16,20},{20,16},{24,28},{28,24},{1,5},{5... | collective-permute-start | bytes 36872 | tf_op jit(solution)/shard_map/ppermute | solution.py:1403
  201.4 1.2 copy-start.27
  201.4 1.4 copy-start.18
  207.3 28.6 %all-to-all-start.1 = ((bf16[4,3,96,768]{3,2,1,0:T(8,128)(2,1)}), bf16[4,3,96,768]{3,2,1,0:T(8,128)(2,1)S(1)}, u32[]{:S(2)}, u32[]{:S(2)}) async-start(bf16[4,3,96,768]{3,2,1,0:T(8,128)(2,1)} %get-tuple-element.139.refs_1_.refs_19_), calls=%async_computation.1 | async-start | bytes 3538944 | tf_op jit(solution)/shard_map/all_to_all | solution.py:1417
  211.1 30.8 %collective-permute-start.26 = (bf16[4,96,1920]{2,1,0:T(8,128)(2,1)}, bf16[4,96,1920]{2,1,0:T(8,128)(2,1)S(1)}, u32[]{:S(2)}, u32[]{:S(2)}) collective-permute-start(bf16[4,96,1920]{2,1,0:T(8,128)(2,1)} %hold.11), channel_id=1, source_target_pairs={{0,4},{4,0},{8,12},{12,8},{16,20},{20,16},{24,28},{28,24},{1,5},{5... | collective-permute-start | bytes 4423688 | tf_op jit(solution)/shard_map/ppermute | solution.py:1403
  212.1 18.2 %collective-permute-start.27 = (bf16[1,192,768]{2,1,0:T(8,128)(2,1)S(1)}, bf16[1,192,768]{2,1,0:T(8,128)(2,1)S(1)}, u32[]{:S(2)}, u32[]{:S(2)}) collective-permute-start(bf16[1,192,768]{2,1,0:T(8,128)(2,1)S(1)} %copy-done.33), channel_id=1, source_target_pairs={{0,3},{3,0},{1,2},{2,1},{4,7},{7,4},{5,6},{6,5},{8,11},{11,8},{9,1... | collective-permute-start | bytes 884744 | tf_op jit(solution)/shard_map/ppermute | solution.py:1427
  231.0 10.9 %collective-permute-start.28 = (bf16[4,96,1280]{2,1,0:T(8,128)(2,1)}, bf16[4,96,1280]{2,1,0:T(8,128)(2,1)}, u32[]{:S(2)}, u32[]{:S(2)}) collective-permute-start(bf16[4,96,1280]{2,1,0:T(8,128)(2,1)} %get-tuple-element.146), channel_id=1, source_target_pairs={{0,4},{4,0},{8,12},{12,8},{16,20},{20,16},{24,28},{28,24},{1,5},{5... | collective-permute-start | bytes 2949128 | tf_op jit(solution)/shard_map/ppermute | solution.py:1403
  231.0 18.3 %collective-permute-start.29 = (bf16[2,192,768]{2,1,0:T(8,128)(2,1)}, bf16[2,192,768]{2,1,0:T(8,128)(2,1)}, u32[]{:S(2)}, u32[]{:S(2)}) collective-permute-start(bf16[2,192,768]{2,1,0:T(8,128)(2,1)} %get-tuple-element.147.refs_1_), channel_id=1, source_target_pairs={{0,3},{3,0},{1,2},{2,1},{4,7},{7,4},{5,6},{6,5},{8,11},{11,8},{9,1... | collective-permute-start | bytes 1769480 | tf_op jit(solution)/shard_map/ppermute | solution.py:1427
  235.8 1.2 copy-start.10
  239.8 18.6 %collective-permute-start.30 = (bf16[2,3,48,768]{3,2,1,0:T(8,128)(2,1)}, bf16[2,3,48,768]{3,2,1,0:T(8,128)(2,1)S(1)}, u32[]{:S(2)}, u32[]{:S(2)}) collective-permute-start(bf16[2,3,48,768]{3,2,1,0:T(8,128)(2,1)} %get-tuple-element.149), channel_id=1, source_target_pairs={{0,1},{1,0},{2,3},{3,2},{4,5},{5,4},{6,7},{7,6},{8,9},{9,8},{10,11... | collective-permute-start | bytes 1327112 | tf_op jit(solution)/shard_map/ppermute | solution.py:1427
  241.3 26.5 %collective-permute-start.31 = (bf16[2,3,48,768]{3,2,1,0:T(8,128)(2,1)}, bf16[2,3,48,768]{3,2,1,0:T(8,128)(2,1)S(1)}, u32[]{:S(2)}, u32[]{:S(2)}) collective-permute-start(bf16[2,3,48,768]{3,2,1,0:T(8,128)(2,1)} %get-tuple-element.150), channel_id=1, source_target_pairs={{0,1},{1,0},{2,3},{3,2},{4,5},{5,4},{6,7},{7,6},{8,9},{9,8},{10,11... | collective-permute-start | bytes 1327112 | tf_op jit(solution)/shard_map/ppermute | solution.py:1427
  241.9 1.1 copy-start.16
  258.4 9.4 %copy-start.28 = (bf16[2,3,48,768]{3,2,1,0:T(8,128)(2,1)}, bf16[2,3,48,768]{3,2,1,0:T(8,128)(2,1)S(1)}, u32[]{:S(2)}) copy-start(bf16[2,3,48,768]{3,2,1,0:T(8,128)(2,1)S(1)} %collective-permute-done.30.refs_5_) | copy-start | bytes 1327108
  272.0 4.4 %copy-start.14 = (bf16[3,192,768]{2,1,0:T(8,128)(2,1)S(1)}, bf16[3,192,768]{2,1,0:T(8,128)(2,1)}, u32[]{:S(2)}) copy-start(bf16[3,192,768]{2,1,0:T(8,128)(2,1)} %get-tuple-element.151.refs_1_) | copy-start | bytes 2654212
  272.0 47.0 %all-to-all-start.2 = ((bf16[4,96,3200]{2,1,0:T(8,128)(2,1)}), bf16[4,96,3200]{2,1,0:T(8,128)(2,1)S(1)}, u32[]{:S(2)}, u32[]{:S(2)}) async-start(bf16[4,96,3200]{2,1,0:T(8,128)(2,1)} %hold.13), calls=%async_computation.2 | async-start | bytes 4915200 | tf_op jit(solution)/shard_map/all_to_all | solution.py:1417
  276.3 39.2 %collective-permute-start.32 = (bf16[3,192,768]{2,1,0:T(8,128)(2,1)S(1)}, bf16[3,192,768]{2,1,0:T(8,128)(2,1)}, u32[]{:S(2)}, u32[]{:S(2)}) collective-permute-start(bf16[3,192,768]{2,1,0:T(8,128)(2,1)S(1)} %copy-done.14), channel_id=1, source_target_pairs={{0,1},{1,0},{2,3},{3,2},{4,5},{5,4},{6,7},{7,6},{8,9},{9,8},{10,11... | collective-permute-start | bytes 2654216 | tf_op jit(solution)/shard_map/ppermute | solution.py:1427
  276.3 46.8 %collective-permute-start.34 = (bf16[4,3,48,768]{3,2,1,0:T(8,128)(2,1)}, bf16[4,3,48,768]{3,2,1,0:T(8,128)(2,1)}, u32[]{:S(2)}, u32[]{:S(2)}) collective-permute-start(bf16[4,3,48,768]{3,2,1,0:T(8,128)(2,1)} %get-tuple-element.155.refs_0_), channel_id=1, source_target_pairs={{0,3},{3,0},{1,2},{2,1},{4,7},{7,4},{5,6},{6,5},{8,11},{11,8},{9,1... | collective-permute-start | bytes 2654216 | tf_op jit(solution)/shard_map/ppermute | solution.py:1427
  318.9 1.4 copy-start.7
  323.1 11.7 %collective-permute-start.33 = (bf16[64,3200]{1,0:T(8,128)(2,1)}, bf16[64,3200]{1,0:T(8,128)(2,1)S(1)}, u32[]{:S(2)}, u32[]{:S(2)}) collective-permute-start(bf16[64,3200]{1,0:T(8,128)(2,1)} %get-tuple-element.154.refs_2_), channel_id=1, source_target_pairs={{0,1},{1,0},{2,3},{3,2},{4,5},{5,4},{6,7},{7,6},{8,9},{9,8},{10,11... | collective-permute-start | bytes 1228808 | tf_op jit(solution)/shard_map/ppermute | solution.py:1427
  325.7 35.7 %collective-permute-start.37 = (bf16[4,3,48,768]{3,2,1,0:T(8,128)(2,1)}, bf16[4,3,48,768]{3,2,1,0:T(8,128)(2,1)S(1)}, u32[]{:S(2)}, u32[]{:S(2)}) collective-permute-start(bf16[4,3,48,768]{3,2,1,0:T(8,128)(2,1)} %call_sums.3.refs_2_.refs_1_), channel_id=1, source_target_pairs={{0,1},{1,0},{2,3},{3,2},{4,5},{5,4},{6,7},{7,6},{8,9},{9,8},{10,11... | collective-permute-start | bytes 2654216 | tf_op jit(solution)/shard_map/ppermute | solution.py:1427
  337.5 15.5 %collective-permute-start.35 = (bf16[64,3200]{1,0:T(8,128)(2,1)}, bf16[64,3200]{1,0:T(8,128)(2,1)S(1)}, u32[]{:S(2)}, u32[]{:S(2)}) collective-permute-start(bf16[64,3200]{1,0:T(8,128)(2,1)} %call_sums.4.refs_0_), channel_id=1, source_target_pairs={{0,3},{3,0},{1,2},{2,1},{4,7},{7,4},{5,6},{6,5},{8,11},{11,8},{9,1... | collective-permute-start | bytes 1228808 | tf_op jit(solution)/shard_map/ppermute | solution.py:1427
  355.7 10.1 %collective-permute-start.36 = (bf16[64,3200]{1,0:T(8,128)(2,1)}, bf16[64,3200]{1,0:T(8,128)(2,1)S(1)}, u32[]{:S(2)}, u32[]{:S(2)}) collective-permute-start(bf16[64,3200]{1,0:T(8,128)(2,1)} %call_sums.5.refs_5_.refs_1_), channel_id=1, source_target_pairs={{0,1},{1,0},{2,3},{3,2},{4,5},{5,4},{6,7},{7,6},{8,9},{9,8},{10,11... | collective-permute-start | bytes 1228808 | tf_op jit(solution)/shard_map/ppermute | solution.py:1427
  (19 other events, 15.5 us)
Sparse Core Ops, SparseCore 0:
  178.2 52.2 reduce-scatter.3

commit v4 on v3

--- a/solution.py
+++ b/solution.py
@@ -471,7 +471,7 @@
 def exact_rows(place, v):
     high = v.astype(BF)
     rest = (v - high.astype(F32)).astype(BF)
-    return dot_nn(place, high) + dot_nn(place, rest)
+    return dot_tn(place, high) + dot_tn(place, rest)
 
 
 def segment_bias(starts, length, segs):
@@ -801,9 +801,9 @@
     return (row == position[...]).astype(F32).astype(BF)
 
 
-def take_rows(position, slots):
-    row = lax.broadcasted_iota(jnp.int32, (position.shape[0], slots), 1)
-    return (row == position[...]).astype(F32).astype(BF)
+def member_rows(route, first):
+    row = lax.broadcasted_iota(jnp.int32, (16, route.shape[1]), 0)
+    return (row == route[...] + first).astype(F32).astype(BF)
 
 
 def mix_out(n, layout, slots, deps, *refs):
@@ -1123,7 +1123,7 @@
     total = got[0][...].astype(F32)
     for ref in got[1:]:
         total = total + ref[...].astype(F32)
-    gradient = exact_rows(take_rows(position, total.shape[0]), total)
+    gradient = exact_rows(place_rows(position, total.shape[0]), total)
     normed, inverse = center(hidden[...])
     value = cot[...].astype(F32) + norm_grad(normed, inverse, vec[5:6, :], gradient)
     g_hidden[...] = value
@@ -1132,9 +1132,7 @@
     vec_grads[4:5, :] = jnp.sum(branch.astype(F32), 0, keepdims=True)
     vec_grads[5:6, :] = jnp.sum(gradient * normed, 0, keepdims=True)
     vec_grads[6:7, :] = jnp.sum(gradient, 0, keepdims=True)
-    lane = lax.broadcasted_iota(jnp.int32, (tok, 16), 1)
-    member = (lane == route[...] + 7).astype(F32).astype(BF)
-    vec_grads[...] += dot_tn(member, cot[...])
+    vec_grads[...] += dot_nn(member_rows(route, 7), cot[...])
     for copy in copies:
         copy.wait()
     g_mixed[...] = dot_nt(branch, weights[...]).astype(BF)
@@ -1160,9 +1158,8 @@
     position, hidden, route, vec = refs[:4]
     got = refs[4]
     out = refs[5 + deps]
-    value = hidden[...] + dot_nn(take_rows(position, got.shape[0]), got[...])
-    for e in range(EXPERTS):
-        value = value + jnp.where(route[...] == e, vec[7 + e : 8 + e, :], 0.0)
+    value = hidden[...] + dot_tn(place_rows(position, got.shape[0]), got[...])
+    value = value + dot_tn(member_rows(route, 7), vec[...].astype(BF))
     out[...] = value.astype(BF)
 
 
@@ -1390,12 +1387,16 @@
                 two = ref[:half, cols_one + i * last : cols_one + (i + 1) * last]
                 outs[1 + i][rows, :span] = one.astype(F32)
                 outs[1 + i][rows, span:] = two.astype(F32)
-            outs[6][rows, :] = ref[:half, cols_one + 3 * last :].astype(F32)
-        outs[4][...] = outs[6][...].T[:16]
-        outs[5][...] = ins[0][half:, :ff_shard].astype(F32)
-
-    shapes = (sds((2 * half, width), F32),) * 4 + (sds((16, 2 * half), F32),)
-    shapes += (sds((16, ff_shard), F32), sds((2 * half, LANES), F32))
+            outs[4][rows, :] = ref[:half, cols_one + 3 * last :].astype(F32)
+        rows = outs[4][...].T
+        outs[5][...] = ins[0][half : half + EXPERTS, :ff_shard].astype(F32)
+        outs[6][...] = rows[n_vec - EXPERTS : n_vec]
+        for i, out in enumerate(outs[7:]):
+            out[...] = rows[i : i + 1]
+
+    shapes = (sds((2 * half, width), F32),) * 4 + (sds((2 * half, LANES), F32),)
+    shapes += (sds((EXPERTS, ff_shard), F32), sds((EXPERTS, 2 * half), F32))
+    shapes += (sds((1, 2 * half), F32),) * (n_vec - EXPERTS)
     return join(body, call_attention_result, shapes, (kept,), (mine, got), deps)
 
 
@@ -1482,7 +1483,7 @@
     base = jnp.cumsum(padded) - padded
     slots = tok_count + 16 * (EXPERTS - 1)
     position = (jnp.sum(member * base[None, :], 1) * 16 + rank).astype(jnp.int32)
-    position_row, position_col = position[None, :], position[:, None]
+    position_row, route_row = position[None, :], route_ids[None, :]
     begin = jnp.minimum(base, (slots - CAP) // 16)
     meta = jnp.stack([begin, base - begin, base - begin + padded], 1).reshape(1, 3 * EXPERTS) * 16
     meta = meta.astype(jnp.int32)
@@ -1574,8 +1575,8 @@
     g_hidden, g_mixed, vec_grads, g_out = call_mix_out_backward(
         n,
         me,
-        position_col,
-        routes,
+        position_row,
+        route_row,
         hidden,
         cotangent,
         vec,
@@ -1644,21 +1645,23 @@
     d_rest, i_across = line(d_total, 2), line(i_part, 1)
     (p_terms,) = hold((p_terms,), (d_total,))
     p_plane = exchange(p_terms, n)
-    sum_down = call_down_result(kept, d_total, d_rest)
-    p_keep, p_send = call_attention_shares(kept, p_plane, bias_term, (sum_down,))
+    p_keep, p_send = call_attention_shares(kept, p_plane, bias_term)
+    sum_down = call_down_result(kept, d_total, d_rest, (p_send,))
     p_got = line(p_send, 0)
-    (i_total,) = call_sums([(i_part, i_across)], (p_send,))
+    (i_total,) = call_sums([(i_part, i_across)], (sum_down,))
     i_rest = line(i_total, 2)
     (p_part,) = call_sums([(p_keep, p_got)], (i_total,))
     p_across = line(p_part, 1)
     (p_total,) = call_sums([(p_part, p_across)])
     p_rest = line(p_total, 2)
-    output = call_finish_output(position_col, hidden, routes, vec, got_res, (p_total,))
+    output = call_finish_output(position_row, hidden, route_row, vec, got_res, (p_total,))
     sum_in = call_in_result(kept, i_total, i_rest, (output,))
-    sum_out, sum_query, sum_key, sum_value, sum_vec, bias_rows, _ = call_attention_result(
-        kept, p_total, p_rest, width, span, n_vec, ff_shard, (output,)
-    )
-    sum_in_bias = bias_rows[:EXPERTS]
+    sum_out, sum_query, sum_key, sum_value, _, sum_in_bias, sum_down_bias, *sum_vec = (
+        call_attention_result(
+            kept, p_total, p_rest, width, span, n_vec, ff_shard, (output,)
+        )
+    )
+    sum_vec = [v.reshape(shard) for v in sum_vec]
     return (
         output,
         input_grad,
@@ -1676,7 +1679,7 @@
         sum_in,
         sum_in_bias,
         sum_down,
-        sum_vec[7:n_vec],
+        sum_down_bias,
     )
 
 

time: 386 us -> 381 us (0.987)
  local copies, waits for them, and re-layouts: 28.9 us -> 23.3 us
    all_to_all x3, waiting for transfers between devices: 5.1 us -> 31.8 us  [exchange(): return lax.all_to_all(v, FSDP, 0, 0, axis_index_groups=groups)]
    ppermute x11, waiting for transfers between devices: 80.2 us -> 55.6 us  [line(): return lax.ppermute(v, REP, pairs)]
    unnamed x84 -> x81, local copies, waits for them, and re-layouts: 20.3 us -> 19.6 us
  transfers between devices with their start and end apart: 42 -> 42, of which waited for: 16 -> 20; matrix products, arithmetic and copies ran while one was open for 2% -> 2% of each run, Pallas kernels for 39% -> 39%
where the time goes in v4:
time: 381 us; the launch traced here: 375 us
  Pallas kernels  160 us (42%)
  waiting for transfers between devices  128 us (34%)
  starting transfers between devices  42.9 us (11%)
  local copies, waits for them, and re-layouts  23.3 us (6%)
  between operations  15 us (4%)
  other arithmetic  5.28 us (1%)
    pallas_call x34, Pallas kernels, kernel_call(): pl.pallas_call(body, out_shape=out_shape, in_specs=in_specs, out_specs=ou...  160 us
    ppermute x11, waiting for transfers between devices, line(): return lax.ppermute(v, REP, pairs)  55.6 us
    ppermute x27, waiting for transfers between devices, swap(): return lax.ppermute(v, FSDP, [(i, i ^ mask) for i in range(n)])  40.9 us
    all_to_all x3, waiting for transfers between devices, exchange(): return lax.all_to_all(v, FSDP, 0, 0, axis_index_groups=groups)  31.8 us
    unnamed x81, local copies, waits for them, and re-layouts  19.6 us
    ppermute x27, starting transfers between devices, swap(): return lax.ppermute(v, FSDP, [(i, i ^ mask) for i in range(n)])  19.3 us
    all_to_all x3, starting transfers between devices, exchange(): return lax.all_to_all(v, FSDP, 0, 0, axis_index_groups=groups)  11.9 us
    ppermute x11, starting transfers between devices, line(): return lax.ppermute(v, REP, pairs)  11.7 us
  transfers between devices with their start and end apart: 42, of which 20 were waited for; matrix products, arithmetic and copies ran while one was open for 2% of the time, Pallas kernels for 39%

profile of v4, /device:TPU:0, one launch (start us, length us, event | category | flops | bytes accessed | tf_op | source)
XLA Modules:
  0.0 375.2 jit_solution(15383568883158859071)
XLA Ops:
  7.2 1.4 stack.37.refs_4_
  8.6 2.1 pack.1.refs_0_.refs_3_.refs_5_.refs_11_
  10.7 2.9 collective-permute-start
  13.6 1.5 collective-permute-start.1
  18.4 9.2 %collective-permute-done.refs_1_.refs_4_.refs_6_.refs_12_ = bf16[400,768]{1,0:T(8,128)(2,1)S(1)} collective-permute-done((bf16[400,768]{1,0:T(8,128)(2,1)}, bf16[400,768]{1,0:T(8,128)(2,1)S(1)}, u32[]{:S(2)}, u32[]{:S(2)}) %collective-permute-start) | collective-permute-done | bytes 614432 | tf_op jit(solution)/shard_map/ppermute | solution.py:1404
  27.7 1.5 collective-permute-done.1.refs_2_.refs_5_.refs_7_.refs_13_
  30.0 2.9 call_halves.1
  32.9 1.5 collective-permute-start.2
  36.0 4.6 %collective-permute-done.2.refs_6_.refs_8_.refs_14_ = bf16[192,768]{1,0:T(8,128)(2,1)S(1)} collective-permute-done((bf16[192,768]{1,0:T(8,128)(2,1)}, bf16[192,768]{1,0:T(8,128)(2,1)S(1)}, u32[]{:S(2)}, u32[]{:S(2)}) %collective-permute-start.2) | collective-permute-done | bytes 294944 | tf_op jit(solution)/shard_map/ppermute | solution.py:1404
  40.6 1.8 collective-permute-done.3.refs_7_.refs_9_.refs_15_
  43.1 3.7 call_columns_and_sort.1
  47.6 3.7 all-to-all-start
  51.9 14.7 %attention_forward.1 = (bf16[416,2304]{1,0:T(8,128)(2,1)}, bf16[416,768]{1,0:T(8,128)(2,1)}, f32[16,416]{1,0:T(8,128)}, bf16[416,768]{1,0:T(8,128)(2,1)}, f32[16,768]{1,0:T(8,128)}, /*index=5*/f32[16,768]{1,0:T(8,128)}) custom-call(s32[1]{0:T(128)} %bitcast.5.refs_0_, s32[1,4]{1,0:T(1,128)} %refs_1_.7, bf16[416,768]{1,0:T(8,128)(2,1)} %refs_2_.9, ...), custom_call_target="tpu_custom_call" | custom-call | tf_op jit(solution)/shard_map/attention_forward/pallas_call | solution.py:427
  66.7 5.2 %mix_out.1 = (f32[416,768]{1,0:T(8,128)}, bf16[448,768]{1,0:T(8,128)(2,1)}) custom-call(s32[1]{0:T(128)} %bitcast.5.refs_0_, bf16[416,768]{1,0:T(8,128)(2,1)} %get-tuple-element.100.refs_1_.refs_6_, bf16[416,768]{1,0:T(8,128)(2,1)} %refs_2_.9, f32[16,768]{1,0:T(8,128)} %get-tuple-element.101.refs_3_.refs_5_, s32[1,416]{1,0:T(1,128)} %bitcast.48, ...), custom_call_target="tpu_custom_call" | custom-call | tf_op jit(solution)/shard_map/mix_out/pallas_call | solution.py:427
  71.9 1.7 all-to-all-done.refs_0_
  74.8 1.4 collective-permute-start.9
  76.8 1.5 collective-permute-start.7
  80.1 9.8 %experts.3 = (bf16[448,768]{1,0:T(8,128)(2,1)}, bf16[4,448,768]{2,1,0:T(8,128)(2,1)}, bf16[3,208,768]{2,1,0:T(8,128)(2,1)}, bf16[3,208,768]{2,1,0:T(8,128)(2,1)}) custom-call(s32[1]{0:T(128)} %bitcast.5.refs_0_, s32[1,9]{1,0:T(1,128)} %copy-done.37, f32[16,768]{1,0:T(8,128)} %get-tuple-element.105.refs_2_, ...), custom_call_target="tpu_custom_call" | custom-call | tf_op jit(solution)/shard_map/experts/pallas_call | solution.py:427
  89.9 4.0 %collective-permute-done.9.refs_2_.refs_5_.refs_3_ = bf16[464,768]{1,0:T(8,128)(2,1)} collective-permute-done((bf16[464,768]{1,0:T(8,128)(2,1)}, bf16[464,768]{1,0:T(8,128)(2,1)}, u32[]{:S(2)}, u32[]{:S(2)}) %collective-permute-start.9) | collective-permute-done | bytes 712736 | tf_op jit(solution)/shard_map/ppermute | solution.py:1404
  93.9 1.5 collective-permute-done.10.refs_3_.refs_6_.refs_4_
  95.3 12.9 %collective-permute-done.7.refs_0_.refs_3_ = bf16[448,768]{1,0:T(8,128)(2,1)} collective-permute-done((bf16[448,768]{1,0:T(8,128)(2,1)}, bf16[448,768]{1,0:T(8,128)(2,1)}, u32[]{:S(2)}, u32[]{:S(2)}) %collective-permute-start.7) | collective-permute-done | bytes 688160 | tf_op jit(solution)/shard_map/ppermute | solution.py:1404
  110.1 2.9 call_two_halves.1
  113.6 1.5 collective-permute-start.14
  117.0 14.1 %experts.4 = (bf16[448,768]{1,0:T(8,128)(2,1)}, bf16[448,768]{1,0:T(8,128)(2,1)}, bf16[4,448,768]{2,1,0:T(8,128)(2,1)}, bf16[3,416,768]{2,1,0:T(8,128)(2,1)}, bf16[3,416,768]{2,1,0:T(8,128)(2,1)}) custom-call(s32[1]{0:T(128)} %bitcast.5.refs_0_, s32[2,9]{1,0:T(2,128)} %convert_multiply_fusion.refs_1_, ...), custom_call_target="tpu_custom_call", output_to_operand_aliasing={{2}: (11, {})} | custom-call | tf_op jit(solution)/shard_map/experts/pallas_call | solution.py:427
  131.7 1.5 collective-permute-start.16
  134.6 9.6 %experts.5 = (bf16[448,768]{1,0:T(8,128)(2,1)}, bf16[4,448,768]{2,1,0:T(8,128)(2,1)}, bf16[3,208,768]{2,1,0:T(8,128)(2,1)}, bf16[3,208,768]{2,1,0:T(8,128)(2,1)}) custom-call(s32[1]{0:T(128)} %bitcast.5.refs_0_, s32[1,9]{1,0:T(1,128)} %fusion.1.refs_1_, f32[16,768]{1,0:T(8,128)} %get-tuple-element.105.refs_2_, ...), custom_call_target="tpu_custom_call", output_to_operand_aliasing={{1}: (11, {})} | custom-call | tf_op jit(solution)/shard_map/experts/pallas_call | solution.py:427
  144.2 1.6 collective-permute-start.17
  146.4 3.1 collective-permute-done.15.refs_10_.refs_8_
  150.4 10.4 %down_grads.1 = (bf16[3,384,768]{2,1,0:T(8,128)(2,1)}, bf16[384,768]{1,0:T(8,128)(2,1)}, bf16[384,768]{1,0:T(8,128)(2,1)}, bf16[384,768]{1,0:T(8,128)(2,1)}) custom-call(s32[1]{0:T(128)} %bitcast.5.refs_0_, s32[4,9]{1,0:T(4,128)} %pad_add_fusion.refs_1_, bf16[464,768]{1,0:T(8,128)(2,1)} %get-tuple-element.104.refs_4_.refs_2_, ...), custom_call_target="tpu_custom_call" | custom-call | tf_op jit(solution)/shard_map/down_grads/pallas_call | solution.py:427
  163.9 7.1 %mix_out_backward.1 = (f32[416,768]{1,0:T(8,128)}, bf16[416,768]{1,0:T(8,128)(2,1)}, f32[16,768]{1,0:T(8,128)}, bf16[768,768]{1,0:T(8,128)(2,1)}) custom-call(s32[1]{0:T(128)} %bitcast.5.refs_0_, s32[1,416]{1,0:T(1,128)} %bitcast.49, s32[1,416]{1,0:T(1,128)} %bitcast.53, f32[416,768]{1,0:T(8,128)} %get-tuple-element.102.refs_3_.refs_1_, ...), custom_call_target="tpu_custom_call" | custom-call | tf_op jit(solution)/shard_map/mix_out_backward/pallas_call | solution.py:427
  172.2 3.5 call_pair_down.1
  175.7 1.6 collective-permute-start.22
  177.3 10.8 %in_grads.1 = (bf16[4,3,96,768]{3,2,1,0:T(8,128)(2,1)}, bf16[16,384]{1,0:T(8,128)(2,1)}, bf16[16,384]{1,0:T(8,128)(2,1)}, bf16[4,96,768]{2,1,0:T(8,128)(2,1)}, b...) custom-call(s32[1]{0:T(128)} %bitcast.5.refs_0_, s32[4,9]{1,0:T(4,128)} %pad_add_fusion.refs_1_, ...), custom_call_target="tpu_custom_call" | custom-call | tf_op jit(solution)/shard_map/in_grads/pallas_call | solution.py:427
  189.2 11.4 %attention_backward_one.1 = (bf16[416,1152]{1,0:T(8,128)(2,1)}, bf16[4,96,1920]{2,1,0:T(8,128)(2,1)}, bf16[4,96,1920]{2,1,0:T(8,128)(2,1)}) custom-call(s32[1]{0:T(128)} %bitcast.5.refs_0_, s32[1,4]{1,0:T(1,128)} %refs_1_.7, bf16[416,2304]{1,0:T(8,128)(2,1)} %get-tuple-element.122.refs_2_.refs_5_, f32[16,416]{1,0:T(8,128)} %get-tuple-element.123.refs_3_.refs_6_, ...), custom_call_target="tpu_custom_call" | custom-call | tf_op jit(solution)/shard_map/attention_backward_one/pallas_call | solution.py:427
  202.1 4.4 %call_pair_in.1 = (bf16[4,3,96,768]{3,2,1,0:T(8,128)(2,1)}, bf16[16,384]{1,0:T(8,128)(2,1)}, bf16[1,192,768]{2,1,0:T(8,128)(2,1)}, bf16[2,192,768]{2,1,0:T(8,128)(2,1)}) custom-call(bf16[4,3,96,768]{3,2,1,0:T(8,128)(2,1)} %get-tuple-element.132.refs_7_.refs_4_.refs_0_, bf16[16,384]{1,0:T(8,128)(2,1)} %get-tuple-element.135.refs_1_, ...), custom_call_target="tpu_custom_call" | custom-call | tf_op jit(solution)/shard_map/call_pair_in/pallas_call | solution.py:427
  206.5 3.8 %all-to-all-start.1 = ((bf16[4,3,96,768]{3,2,1,0:T(8,128)(2,1)}), bf16[4,3,96,768]{3,2,1,0:T(8,128)(2,1)S(1)}, u32[]{:S(2)}, u32[]{:S(2)}) async-start(bf16[4,3,96,768]{3,2,1,0:T(8,128)(2,1)} %get-tuple-element.146.refs_1_.refs_19_), calls=%async_computation.1 | async-start | bytes 3538944 | tf_op jit(solution)/shard_map/all_to_all | solution.py:1418
  211.3 2.4 collective-permute-start.27
  213.7 15.8 %attention_backward_two.1 = (f32[416,768]{1,0:T(8,128)}, bf16[4,96,1280]{2,1,0:T(8,128)(2,1)}, bf16[4,96,1280]{2,1,0:T(8,128)(2,1)}) custom-call(s32[1]{0:T(128)} %bitcast.5.refs_0_, s32[1,4]{1,0:T(1,128)} %refs_1_.7, bf16[416,768]{1,0:T(8,128)(2,1)} %refs_2_.9, f32[16,768]{1,0:T(8,128)} %get-tuple-element.101.refs_3_.refs_5_, ...), custom_call_target="tpu_custom_call" | custom-call | tf_op jit(solution)/shard_map/attention_backward_two/pallas_call | solution.py:427
  230.2 1.5 collective-permute-start.29
  231.8 3.2 all-to-all-done.1.refs_1_
  236.2 2.8 call_split_rows.1
  239.0 1.5 collective-permute-start.30
  242.2 4.4 %call_pair_shares.1.refs_7_.refs_0_ = bf16[4,96,3200]{2,1,0:T(8,128)(2,1)} custom-call(bf16[4,96,1920]{2,1,0:T(8,128)(2,1)} %get-tuple-element.133.refs_0_, bf16[4,96,1920]{2,1,0:T(8,128)(2,1)} %copy-done.16, bf16[4,96,1280]{2,1,0:T(8,128)(2,1)} %get-tuple-element.149.refs_2_.refs_4_, bf16[4,96,1280]{2,1,0:T(8,128)(2,1)} %collective-permute-done.28.refs_3_, ...), custom_call_target="tpu_custom_call" | custom-call | tf_op jit(solution)/shard_map/call_pair_shares/pallas_call | solution.py:427
  246.6 2.0 collective-permute-done.29.refs_3_
  248.6 9.1 %collective-permute-done.30.refs_5_ = bf16[2,3,48,768]{3,2,1,0:T(8,128)(2,1)S(1)} collective-permute-done((bf16[2,3,48,768]{3,2,1,0:T(8,128)(2,1)}, bf16[2,3,48,768]{3,2,1,0:T(8,128)(2,1)S(1)}, u32[]{:S(2)}, u32[]{:S(2)}) %collective-permute-start.30) | collective-permute-done | bytes 442400 | tf_op jit(solution)/shard_map/ppermute | solution.py:1428
  257.7 9.4 %collective-permute-done.31.refs_6_ = bf16[2,3,48,768]{3,2,1,0:T(8,128)(2,1)S(1)} collective-permute-done((bf16[2,3,48,768]{3,2,1,0:T(8,128)(2,1)}, bf16[2,3,48,768]{3,2,1,0:T(8,128)(2,1)S(1)}, u32[]{:S(2)}, u32[]{:S(2)}) %collective-permute-start.31) | collective-permute-done | bytes 442400 | tf_op jit(solution)/shard_map/ppermute | solution.py:1428
  267.8 3.4 call_line_sums.1
  271.2 4.4 %all-to-all-start.2 = ((bf16[4,96,3200]{2,1,0:T(8,128)(2,1)}), bf16[4,96,3200]{2,1,0:T(8,128)(2,1)S(1)}, u32[]{:S(2)}, u32[]{:S(2)}) async-start(bf16[4,96,3200]{2,1,0:T(8,128)(2,1)} %hold.13), calls=%async_computation.2 | async-start | bytes 4915200 | tf_op jit(solution)/shard_map/all_to_all | solution.py:1418
  275.6 2.0 collective-permute-start.33
  277.6 26.9 %all-to-all-done.2.refs_1_ = bf16[4,96,3200]{2,1,0:T(8,128)(2,1)S(1)} async-done(((bf16[4,96,3200]{2,1,0:T(8,128)(2,1)}), bf16[4,96,3200]{2,1,0:T(8,128)(2,1)S(1)}, u32[]{:S(2)}, u32[]{:S(2)}) %all-to-all-start.2) | async-done | bytes 2457632 | tf_op jit(solution)/shard_map/all_to_all | solution.py:1418
  304.5 1.4 copy-done.7
  305.9 2.7 call_attention_shares.1
  308.7 6.1 %collective-permute-done.34.refs_2_ = bf16[3,192,768]{2,1,0:T(8,128)(2,1)} collective-permute-done((bf16[3,192,768]{2,1,0:T(8,128)(2,1)S(1)}, bf16[3,192,768]{2,1,0:T(8,128)(2,1)}, u32[]{:S(2)}, u32[]{:S(2)}) %collective-permute-start.34) | collective-permute-done | bytes 884768 | tf_op jit(solution)/shard_map/ppermute | solution.py:1428
  314.7 3.5 call_down_result.1.refs_2_
  318.2 2.6 call_sums.3.refs_2_.refs_1_
  320.8 3.9 %collective-permute-done.32.refs_1_ = bf16[64,3200]{1,0:T(8,128)(2,1)S(1)} collective-permute-done((bf16[64,3200]{1,0:T(8,128)(2,1)}, bf16[64,3200]{1,0:T(8,128)(2,1)S(1)}, u32[]{:S(2)}, u32[]{:S(2)}) %collective-permute-start.32) | collective-permute-done | bytes 409632 | tf_op jit(solution)/shard_map/ppermute | solution.py:1428
  325.4 2.0 call_sums.4.refs_0_
  327.4 2.2 collective-permute-start.35
  329.6 22.6 %collective-permute-done.35.refs_1_ = bf16[64,3200]{1,0:T(8,128)(2,1)S(1)} collective-permute-done((bf16[64,3200]{1,0:T(8,128)(2,1)}, bf16[64,3200]{1,0:T(8,128)(2,1)S(1)}, u32[]{:S(2)}, u32[]{:S(2)}) %collective-permute-start.35) | collective-permute-done | bytes 409632 | tf_op jit(solution)/shard_map/ppermute | solution.py:1428
  353.0 2.0 call_sums.5.refs_5_.refs_1_
  354.9 3.1 finish_output.1.refs_3_
  358.9 3.5 call_in_result.1
  362.4 2.6 collective-permute-done.36.refs_2_
  365.7 2.2 call_attention_result.1
  (161 shorter events, 34.6 us)
Async XLA Ops:
  7.2 35.2 %copy-start.34 = (s32[416,1]{0,1:T(1,128)S(1)}, s32[416,1]{0,1:T(1,128)}, u32[]{:S(2)}) copy-start(s32[416,1]{0,1:T(1,128)} %param.21) | copy-start | bytes 4996
  10.7 17.0 %collective-permute-start = (bf16[400,768]{1,0:T(8,128)(2,1)}, bf16[400,768]{1,0:T(8,128)(2,1)S(1)}, u32[]{:S(2)}, u32[]{:S(2)}) collective-permute-start(bf16[400,768]{1,0:T(8,128)(2,1)} %pack.1.refs_0_.refs_3_.refs_5_.refs_11_), channel_id=1, source_target_pairs={{0,8},{4,12},{8,0},{12,4},{16,24},{20,28},{24,16},{28,20},{1,9},{5... | collective-permute-start | bytes 1843208 | tf_op jit(solution)/shard_map/ppermute | solution.py:1404
  13.6 15.5 %collective-permute-start.1 = (bf16[400,768]{1,0:T(8,128)(2,1)}, bf16[400,768]{1,0:T(8,128)(2,1)S(1)}, u32[]{:S(2)}, u32[]{:S(2)}) collective-permute-start(bf16[400,768]{1,0:T(8,128)(2,1)} %pack.1.refs_0_.refs_3_.refs_5_.refs_11_), channel_id=1, source_target_pairs={{0,16},{4,20},{8,24},{12,28},{16,0},{20,4},{24,8},{28,12},{1,17},{... | collective-permute-start | bytes 1843208 | tf_op jit(solution)/shard_map/ppermute | solution.py:1404
  18.4 28.4 %copy-start.37 = (s32[1,9]{1,0:T(1,128)}, s32[1,9]{1,0:T(1,128)S(1)}, u32[]{:S(2)}) copy-start(s32[1,9]{1,0:T(1,128)S(1)} %mul.42.refs_1_) | copy-start | bytes 112
  27.7 1.5 copy-start.3
  32.9 7.8 %collective-permute-start.2 = (bf16[192,768]{1,0:T(8,128)(2,1)}, bf16[192,768]{1,0:T(8,128)(2,1)S(1)}, u32[]{:S(2)}, u32[]{:S(2)}) collective-permute-start(bf16[192,768]{1,0:T(8,128)(2,1)} %get-tuple-element.97.refs_4_), channel_id=1, source_target_pairs={{0,16},{4,20},{8,24},{12,28},{16,0},{20,4},{24,8},{28,12},{1,17},{... | collective-permute-start | bytes 884744 | tf_op jit(solution)/shard_map/ppermute | solution.py:1404
  34.4 8.0 %collective-permute-start.3 = (bf16[208,768]{1,0:T(8,128)(2,1)}, bf16[208,768]{1,0:T(8,128)(2,1)S(1)}, u32[]{:S(2)}, u32[]{:S(2)}) collective-permute-start(bf16[208,768]{1,0:T(8,128)(2,1)} %get-tuple-element.98), channel_id=1, source_target_pairs={{0,8},{4,12},{8,0},{12,4},{16,24},{20,28},{24,16},{28,20},{1,9},{5... | collective-permute-start | bytes 958472 | tf_op jit(solution)/shard_map/ppermute | solution.py:1404
  36.0 15.9 %collective-permute-start.4 = (bf16[3,400,768]{2,1,0:T(8,128)(2,1)}, bf16[3,400,768]{2,1,0:T(8,128)(2,1)}, u32[]{:S(2)}, u32[]{:S(2)}) collective-permute-start(bf16[3,400,768]{2,1,0:T(8,128)(2,1)} %get-tuple-element.99), channel_id=1, source_target_pairs={{0,4},{4,0},{8,12},{12,8},{16,20},{20,16},{24,28},{28,24},{1,5},{5... | collective-permute-start | bytes 5529608 | tf_op jit(solution)/shard_map/ppermute | solution.py:1404
  40.6 6.2 %copy-start.13 = (bf16[192,768]{1,0:T(8,128)(2,1)}, bf16[192,768]{1,0:T(8,128)(2,1)S(1)}, u32[]{:S(2)}) copy-start(bf16[192,768]{1,0:T(8,128)(2,1)S(1)} %collective-permute-done.2.refs_6_.refs_8_.refs_14_) | copy-start | bytes 884740
  40.6 6.1 %collective-permute-start.5 = (bf16[192,768]{1,0:T(8,128)(2,1)S(1)}, bf16[192,768]{1,0:T(8,128)(2,1)S(1)}, u32[]{:S(2)}, u32[]{:S(2)}) collective-permute-start(bf16[192,768]{1,0:T(8,128)(2,1)S(1)} %collective-permute-done.2.refs_6_.refs_8_.refs_14_), channel_id=1, source_target_pairs={{0,4},{4,0},{8,12},{12,8},{16,20},{20,16},{24,28},{28,24},{1,5},{5... | collective-permute-start | bytes 884744 | tf_op jit(solution)/shard_map/ppermute | solution.py:1404
  42.4 4.4 %copy-start.12 = (bf16[208,768]{1,0:T(8,128)(2,1)}, bf16[208,768]{1,0:T(8,128)(2,1)S(1)}, u32[]{:S(2)}) copy-start(bf16[208,768]{1,0:T(8,128)(2,1)S(1)} %collective-permute-done.3.refs_7_.refs_9_.refs_15_) | copy-start | bytes 958468
  42.4 4.4 %collective-permute-start.6 = (bf16[208,768]{1,0:T(8,128)(2,1)S(1)}, bf16[208,768]{1,0:T(8,128)(2,1)S(1)}, u32[]{:S(2)}, u32[]{:S(2)}) collective-permute-start(bf16[208,768]{1,0:T(8,128)(2,1)S(1)} %collective-permute-done.3.refs_7_.refs_9_.refs_15_), channel_id=1, source_target_pairs={{0,4},{4,0},{8,12},{12,8},{16,20},{20,16},{24,28},{28,24},{1,5},{5... | collective-permute-start | bytes 958472 | tf_op jit(solution)/shard_map/ppermute | solution.py:1404
  47.6 3.8 %copy-start.1 = (bf16[3,384,768]{2,1,0:T(8,128)(2,1)S(1)}, bf16[3,384,768]{2,1,0:T(8,128)(2,1)}, u32[]{:S(2)}) copy-start(bf16[3,384,768]{2,1,0:T(8,128)(2,1)} %refs_9_.3) | copy-start | bytes 5308420
  47.6 26.0 %all-to-all-start = ((bf16[4,3,96,768]{3,2,1,0:T(8,128)(2,1)}), bf16[4,3,96,768]{3,2,1,0:T(8,128)(2,1)S(1)}, u32[]{:S(2)}, u32[]{:S(2)}) async-start(bf16[4,3,96,768]{3,2,1,0:T(8,128)(2,1)} %hold.7), calls=%async_computation | async-start | bytes 3538944 | tf_op jit(solution)/shard_map/all_to_all | solution.py:1418
  51.3 303.6 %reduce-scatter.4.cloned.1.call-start = ((), (), s32[]{:S(2)}) async-start(), calls=%async_computation.4 | async-start | bytes 3440640
  51.4 26.9 %collective-permute-start.12 = (bf16[3,384,768]{2,1,0:T(8,128)(2,1)S(1)}, bf16[3,384,768]{2,1,0:T(8,128)(2,1)}, u32[]{:S(2)}, u32[]{:S(2)}) collective-permute-start(bf16[3,384,768]{2,1,0:T(8,128)(2,1)S(1)} %copy-done.1), channel_id=1, source_target_pairs={{0,4},{4,0},{8,12},{12,8},{16,20},{20,16},{24,28},{28,24},{1,5},{5... | collective-permute-start | bytes 5308424 | tf_op jit(solution)/shard_map/ppermute | solution.py:1404
  73.6 1.2 copy-start
  74.8 4.1 %collective-permute-start.11 = (bf16[4,3,96,768]{3,2,1,0:T(8,128)(2,1)}, bf16[4,3,96,768]{3,2,1,0:T(8,128)(2,1)S(1)}, u32[]{:S(2)}, u32[]{:S(2)}) collective-permute-start(bf16[4,3,96,768]{3,2,1,0:T(8,128)(2,1)} %hold.8.refs_5_.refs_7_), channel_id=1, source_target_pairs={{0,4},{4,0},{8,12},{12,8},{16,20},{20,16},{24,28},{28,24},{1,5},{5... | collective-permute-start | bytes 5308424 | tf_op jit(solution)/shard_map/ppermute | solution.py:1404
  74.8 19.1 %collective-permute-start.9 = (bf16[464,768]{1,0:T(8,128)(2,1)}, bf16[464,768]{1,0:T(8,128)(2,1)}, u32[]{:S(2)}, u32[]{:S(2)}) collective-permute-start(bf16[464,768]{1,0:T(8,128)(2,1)} %get-tuple-element.104.refs_4_.refs_2_), channel_id=1, source_target_pairs={{0,8},{4,12},{8,0},{12,4},{16,24},{20,28},{24,16},{28,20},{1,9},{5... | collective-permute-start | bytes 2138120 | tf_op jit(solution)/shard_map/ppermute | solution.py:1404
  76.2 19.1 %collective-permute-start.10 = (bf16[464,768]{1,0:T(8,128)(2,1)}, bf16[464,768]{1,0:T(8,128)(2,1)}, u32[]{:S(2)}, u32[]{:S(2)}) collective-permute-start(bf16[464,768]{1,0:T(8,128)(2,1)} %get-tuple-element.104.refs_4_.refs_2_), channel_id=1, source_target_pairs={{0,16},{4,20},{8,24},{12,28},{16,0},{20,4},{24,8},{28,12},{1,17},{... | collective-permute-start | bytes 2138120 | tf_op jit(solution)/shard_map/ppermute | solution.py:1404
  76.8 31.5 %collective-permute-start.7 = (bf16[448,768]{1,0:T(8,128)(2,1)}, bf16[448,768]{1,0:T(8,128)(2,1)}, u32[]{:S(2)}, u32[]{:S(2)}) collective-permute-start(bf16[448,768]{1,0:T(8,128)(2,1)} %get-tuple-element.103.refs_1_.refs_3_.refs_2_), channel_id=1, source_target_pairs={{0,8},{4,12},{8,0},{12,4},{16,24},{20,28},{24,16},{28,20},{1,9},{5... | collective-permute-start | bytes 2064392 | tf_op jit(solution)/shard_map/ppermute | solution.py:1404
  78.3 31.0 %collective-permute-start.8 = (bf16[448,768]{1,0:T(8,128)(2,1)}, bf16[448,768]{1,0:T(8,128)(2,1)S(1)}, u32[]{:S(2)}, u32[]{:S(2)}) collective-permute-start(bf16[448,768]{1,0:T(8,128)(2,1)} %get-tuple-element.103.refs_1_.refs_3_.refs_2_), channel_id=1, source_target_pairs={{0,16},{4,20},{8,24},{12,28},{16,0},{20,4},{24,8},{28,12},{1,17},{... | collective-permute-start | bytes 2064392 | tf_op jit(solution)/shard_map/ppermute | solution.py:1404
  78.8 1.2 copy-start.2
  113.0 20.2 %collective-permute-start.13 = (bf16[464,768]{1,0:T(8,128)(2,1)}, bf16[464,768]{1,0:T(8,128)(2,1)S(1)}, u32[]{:S(2)}, u32[]{:S(2)}) collective-permute-start(bf16[464,768]{1,0:T(8,128)(2,1)} %get-tuple-element.108), channel_id=1, source_target_pairs={{0,8},{4,12},{8,0},{12,4},{16,24},{20,28},{24,16},{28,20},{1,9},{5... | collective-permute-start | bytes 2138120 | tf_op jit(solution)/shard_map/ppermute | solution.py:1404
  113.6 20.2 %collective-permute-start.14 = (bf16[448,768]{1,0:T(8,128)(2,1)}, bf16[448,768]{1,0:T(8,128)(2,1)S(1)}, u32[]{:S(2)}, u32[]{:S(2)}) collective-permute-start(bf16[448,768]{1,0:T(8,128)(2,1)} %get-tuple-element.109), channel_id=1, source_target_pairs={{0,16},{4,20},{8,24},{12,28},{16,0},{20,4},{24,8},{28,12},{1,17},{... | collective-permute-start | bytes 2064392 | tf_op jit(solution)/shard_map/ppermute | solution.py:1404
  131.1 18.4 %collective-permute-start.15 = (bf16[448,768]{1,0:T(8,128)(2,1)}, bf16[448,768]{1,0:T(8,128)(2,1)S(1)}, u32[]{:S(2)}, u32[]{:S(2)}) collective-permute-start(bf16[448,768]{1,0:T(8,128)(2,1)} %get-tuple-element.114), channel_id=1, source_target_pairs={{0,8},{4,12},{8,0},{12,4},{16,24},{20,28},{24,16},{28,20},{1,9},{5... | collective-permute-start | bytes 2064392 | tf_op jit(solution)/shard_map/ppermute | solution.py:1404
  131.7 31.1 %collective-permute-start.16 = (bf16[448,768]{1,0:T(8,128)(2,1)}, bf16[448,768]{1,0:T(8,128)(2,1)S(1)}, u32[]{:S(2)}, u32[]{:S(2)}) collective-permute-start(bf16[448,768]{1,0:T(8,128)(2,1)} %get-tuple-element.115), channel_id=1, source_target_pairs={{0,16},{4,20},{8,24},{12,28},{16,0},{20,4},{24,8},{28,12},{1,17},{... | collective-permute-start | bytes 2064392 | tf_op jit(solution)/shard_map/ppermute | solution.py:1404
  134.6 11.2 %copy-start.36 = (s32[2,9]{1,0:T(2,128)S(1)}, s32[2,9]{1,0:T(2,128)}, u32[]{:S(2)}) copy-start(s32[2,9]{1,0:T(2,128)} %convert_multiply_fusion.refs_1_) | copy-start | bytes 220
  134.6 11.2 %copy-start.38 = (s32[1,9]{1,0:T(1,128)S(1)}, s32[1,9]{1,0:T(1,128)}, u32[]{:S(2)}) copy-start(s32[1,9]{1,0:T(1,128)} %copy-done.37) | copy-start | bytes 112
  134.6 11.2 %copy-start.39 = (s32[1,9]{1,0:T(1,128)S(1)}, s32[1,9]{1,0:T(1,128)}, u32[]{:S(2)}) copy-start(s32[1,9]{1,0:T(1,128)} %fusion.1.refs_1_) | copy-start | bytes 112
  144.2 18.5 %collective-permute-start.17 = (bf16[448,768]{1,0:T(8,128)(2,1)}, bf16[448,768]{1,0:T(8,128)(2,1)S(1)}, u32[]{:S(2)}, u32[]{:S(2)}) collective-permute-start(bf16[448,768]{1,0:T(8,128)(2,1)} %get-tuple-element.116), channel_id=1, source_target_pairs={{0,24},{4,28},{8,16},{12,20},{16,8},{20,12},{24,0},{28,4},{1,25},{... | collective-permute-start | bytes 2064392 | tf_op jit(solution)/shard_map/ppermute | solution.py:1404
  160.8 10.2 %collective-permute-start.18 = (bf16[384,768]{1,0:T(8,128)(2,1)}, bf16[384,768]{1,0:T(8,128)(2,1)S(1)}, u32[]{:S(2)}, u32[]{:S(2)}) collective-permute-start(bf16[384,768]{1,0:T(8,128)(2,1)} %get-tuple-element.128), channel_id=1, source_target_pairs={{0,4},{4,0},{8,12},{12,8},{16,20},{20,16},{24,28},{28,24},{1,5},{5... | collective-permute-start | bytes 1769480 | tf_op jit(solution)/shard_map/ppermute | solution.py:1404
  160.9 10.1 %collective-permute-start.19 = (bf16[384,768]{1,0:T(8,128)(2,1)}, bf16[384,768]{1,0:T(8,128)(2,1)S(1)}, u32[]{:S(2)}, u32[]{:S(2)}) collective-permute-start(bf16[384,768]{1,0:T(8,128)(2,1)} %get-tuple-element.129), channel_id=1, source_target_pairs={{0,4},{4,0},{8,12},{12,8},{16,20},{20,16},{24,28},{28,24},{1,5},{5... | collective-permute-start | bytes 1769480 | tf_op jit(solution)/shard_map/ppermute | solution.py:1404
  161.4 9.7 %collective-permute-start.20 = (bf16[384,768]{1,0:T(8,128)(2,1)}, bf16[384,768]{1,0:T(8,128)(2,1)S(1)}, u32[]{:S(2)}, u32[]{:S(2)}) collective-permute-start(bf16[384,768]{1,0:T(8,128)(2,1)} %get-tuple-element.130), channel_id=1, source_target_pairs={{0,4},{4,0},{8,12},{12,8},{16,20},{20,16},{24,28},{28,24},{1,5},{5... | collective-permute-start | bytes 1769480 | tf_op jit(solution)/shard_map/ppermute | solution.py:1404
  162.8 1.1 copy-start.21
  171.0 1.1 copy-start.23
  171.1 1.1 copy-start.24
  175.7 25.0 %collective-permute-start.22 = (bf16[3,192,768]{2,1,0:T(8,128)(2,1)}, bf16[3,192,768]{2,1,0:T(8,128)(2,1)S(1)}, u32[]{:S(2)}, u32[]{:S(2)}) collective-permute-start(bf16[3,192,768]{2,1,0:T(8,128)(2,1)} %get-tuple-element.131.refs_10_), channel_id=1, source_target_pairs={{0,1},{1,0},{2,3},{3,2},{4,5},{5,4},{6,7},{7,6},{8,9},{9,8},{10,11... | collective-permute-start | bytes 2654216 | tf_op jit(solution)/shard_map/ppermute | solution.py:1428
  188.1 12.5 %collective-permute-start.23 = (bf16[4,96,768]{2,1,0:T(8,128)(2,1)}, bf16[4,96,768]{2,1,0:T(8,128)(2,1)S(1)}, u32[]{:S(2)}, u32[]{:S(2)}) collective-permute-start(bf16[4,96,768]{2,1,0:T(8,128)(2,1)} %get-tuple-element.142), channel_id=1, source_target_pairs={{0,4},{4,0},{8,12},{12,8},{16,20},{20,16},{24,28},{28,24},{1,5},{5... | collective-permute-start | bytes 1769480 | tf_op jit(solution)/shard_map/ppermute | solution.py:1404
  188.2 12.4 %collective-permute-start.24 = (bf16[4,96,768]{2,1,0:T(8,128)(2,1)}, bf16[4,96,768]{2,1,0:T(8,128)(2,1)S(1)}, u32[]{:S(2)}, u32[]{:S(2)}) collective-permute-start(bf16[4,96,768]{2,1,0:T(8,128)(2,1)} %get-tuple-element.143), channel_id=1, source_target_pairs={{0,4},{4,0},{8,12},{12,8},{16,20},{20,16},{24,28},{28,24},{1,5},{5... | collective-permute-start | bytes 1769480 | tf_op jit(solution)/shard_map/ppermute | solution.py:1404
  188.7 12.0 %collective-permute-start.25 = (bf16[4,96,768]{2,1,0:T(8,128)(2,1)}, bf16[4,96,768]{2,1,0:T(8,128)(2,1)S(1)}, u32[]{:S(2)}, u32[]{:S(2)}) collective-permute-start(bf16[4,96,768]{2,1,0:T(8,128)(2,1)} %get-tuple-element.144), channel_id=1, source_target_pairs={{0,4},{4,0},{8,12},{12,8},{16,20},{20,16},{24,28},{28,24},{1,5},{5... | collective-permute-start | bytes 1769480 | tf_op jit(solution)/shard_map/ppermute | solution.py:1404
  188.8 11.8 %collective-permute-start.21 = (bf16[16,384]{1,0:T(8,128)(2,1)}, bf16[16,384]{1,0:T(8,128)(2,1)S(1)}, u32[]{:S(2)}, u32[]{:S(2)}) collective-permute-start(bf16[16,384]{1,0:T(8,128)(2,1)} %get-tuple-element.140), channel_id=1, source_target_pairs={{0,4},{4,0},{8,12},{12,8},{16,20},{20,16},{24,28},{28,24},{1,5},{5... | collective-permute-start | bytes 36872 | tf_op jit(solution)/shard_map/ppermute | solution.py:1404
  200.6 1.0 copy-start.26
  200.7 1.2 copy-start.27
  200.7 1.4 copy-start.18
  206.5 28.5 %all-to-all-start.1 = ((bf16[4,3,96,768]{3,2,1,0:T(8,128)(2,1)}), bf16[4,3,96,768]{3,2,1,0:T(8,128)(2,1)S(1)}, u32[]{:S(2)}, u32[]{:S(2)}) async-start(bf16[4,3,96,768]{3,2,1,0:T(8,128)(2,1)} %get-tuple-element.146.refs_1_.refs_19_), calls=%async_computation.1 | async-start | bytes 3538944 | tf_op jit(solution)/shard_map/all_to_all | solution.py:1418
  210.4 30.7 %collective-permute-start.26 = (bf16[4,96,1920]{2,1,0:T(8,128)(2,1)}, bf16[4,96,1920]{2,1,0:T(8,128)(2,1)S(1)}, u32[]{:S(2)}, u32[]{:S(2)}) collective-permute-start(bf16[4,96,1920]{2,1,0:T(8,128)(2,1)} %hold.11), channel_id=1, source_target_pairs={{0,4},{4,0},{8,12},{12,8},{16,20},{20,16},{24,28},{28,24},{1,5},{5... | collective-permute-start | bytes 4423688 | tf_op jit(solution)/shard_map/ppermute | solution.py:1404
  211.3 18.2 %collective-permute-start.27 = (bf16[1,192,768]{2,1,0:T(8,128)(2,1)S(1)}, bf16[1,192,768]{2,1,0:T(8,128)(2,1)S(1)}, u32[]{:S(2)}, u32[]{:S(2)}) collective-permute-start(bf16[1,192,768]{2,1,0:T(8,128)(2,1)S(1)} %copy-done.33), channel_id=1, source_target_pairs={{0,3},{3,0},{1,2},{2,1},{4,7},{7,4},{5,6},{6,5},{8,11},{11,8},{9,1... | collective-permute-start | bytes 884744 | tf_op jit(solution)/shard_map/ppermute | solution.py:1428
  230.2 10.8 %collective-permute-start.28 = (bf16[4,96,1280]{2,1,0:T(8,128)(2,1)}, bf16[4,96,1280]{2,1,0:T(8,128)(2,1)}, u32[]{:S(2)}, u32[]{:S(2)}) collective-permute-start(bf16[4,96,1280]{2,1,0:T(8,128)(2,1)} %get-tuple-element.153), channel_id=1, source_target_pairs={{0,4},{4,0},{8,12},{12,8},{16,20},{20,16},{24,28},{28,24},{1,5},{5... | collective-permute-start | bytes 2949128 | tf_op jit(solution)/shard_map/ppermute | solution.py:1404
  230.2 18.3 %collective-permute-start.29 = (bf16[2,192,768]{2,1,0:T(8,128)(2,1)}, bf16[2,192,768]{2,1,0:T(8,128)(2,1)}, u32[]{:S(2)}, u32[]{:S(2)}) collective-permute-start(bf16[2,192,768]{2,1,0:T(8,128)(2,1)} %get-tuple-element.154.refs_1_), channel_id=1, source_target_pairs={{0,3},{3,0},{1,2},{2,1},{4,7},{7,4},{5,6},{6,5},{8,11},{11,8},{9,1... | collective-permute-start | bytes 1769480 | tf_op jit(solution)/shard_map/ppermute | solution.py:1428
  235.0 1.2 copy-start.10
  239.0 18.7 %collective-permute-start.30 = (bf16[2,3,48,768]{3,2,1,0:T(8,128)(2,1)}, bf16[2,3,48,768]{3,2,1,0:T(8,128)(2,1)S(1)}, u32[]{:S(2)}, u32[]{:S(2)}) collective-permute-start(bf16[2,3,48,768]{3,2,1,0:T(8,128)(2,1)} %get-tuple-element.156), channel_id=1, source_target_pairs={{0,1},{1,0},{2,3},{3,2},{4,5},{5,4},{6,7},{7,6},{8,9},{9,8},{10,11... | collective-permute-start | bytes 1327112 | tf_op jit(solution)/shard_map/ppermute | solution.py:1428
  240.5 26.6 %collective-permute-start.31 = (bf16[2,3,48,768]{3,2,1,0:T(8,128)(2,1)}, bf16[2,3,48,768]{3,2,1,0:T(8,128)(2,1)S(1)}, u32[]{:S(2)}, u32[]{:S(2)}) collective-permute-start(bf16[2,3,48,768]{3,2,1,0:T(8,128)(2,1)} %get-tuple-element.157), channel_id=1, source_target_pairs={{0,1},{1,0},{2,3},{3,2},{4,5},{5,4},{6,7},{7,6},{8,9},{9,8},{10,11... | collective-permute-start | bytes 1327112 | tf_op jit(solution)/shard_map/ppermute | solution.py:1428
  241.0 1.1 copy-start.16
  257.7 9.4 %copy-start.28 = (bf16[2,3,48,768]{3,2,1,0:T(8,128)(2,1)}, bf16[2,3,48,768]{3,2,1,0:T(8,128)(2,1)S(1)}, u32[]{:S(2)}) copy-start(bf16[2,3,48,768]{3,2,1,0:T(8,128)(2,1)S(1)} %collective-permute-done.30.refs_5_) | copy-start | bytes 1327108
  271.2 4.4 %copy-start.14 = (bf16[3,192,768]{2,1,0:T(8,128)(2,1)S(1)}, bf16[3,192,768]{2,1,0:T(8,128)(2,1)}, u32[]{:S(2)}) copy-start(bf16[3,192,768]{2,1,0:T(8,128)(2,1)} %get-tuple-element.158.refs_1_) | copy-start | bytes 2654212
  271.2 33.3 %all-to-all-start.2 = ((bf16[4,96,3200]{2,1,0:T(8,128)(2,1)}), bf16[4,96,3200]{2,1,0:T(8,128)(2,1)S(1)}, u32[]{:S(2)}, u32[]{:S(2)}) async-start(bf16[4,96,3200]{2,1,0:T(8,128)(2,1)} %hold.13), calls=%async_computation.2 | async-start | bytes 4915200 | tf_op jit(solution)/shard_map/all_to_all | solution.py:1418
  275.6 39.2 %collective-permute-start.34 = (bf16[3,192,768]{2,1,0:T(8,128)(2,1)S(1)}, bf16[3,192,768]{2,1,0:T(8,128)(2,1)}, u32[]{:S(2)}, u32[]{:S(2)}) collective-permute-start(bf16[3,192,768]{2,1,0:T(8,128)(2,1)S(1)} %copy-done.14), channel_id=1, source_target_pairs={{0,1},{1,0},{2,3},{3,2},{4,5},{5,4},{6,7},{7,6},{8,9},{9,8},{10,11... | collective-permute-start | bytes 2654216 | tf_op jit(solution)/shard_map/ppermute | solution.py:1428
  275.6 42.6 %collective-permute-start.33 = (bf16[4,3,48,768]{3,2,1,0:T(8,128)(2,1)}, bf16[4,3,48,768]{3,2,1,0:T(8,128)(2,1)}, u32[]{:S(2)}, u32[]{:S(2)}) collective-permute-start(bf16[4,3,48,768]{3,2,1,0:T(8,128)(2,1)} %get-tuple-element.162.refs_0_), channel_id=1, source_target_pairs={{0,3},{3,0},{1,2},{2,1},{4,7},{7,4},{5,6},{6,5},{8,11},{11,8},{9,1... | collective-permute-start | bytes 2654216 | tf_op jit(solution)/shard_map/ppermute | solution.py:1428
  304.5 1.4 copy-start.7
  308.7 16.0 %collective-permute-start.32 = (bf16[64,3200]{1,0:T(8,128)(2,1)}, bf16[64,3200]{1,0:T(8,128)(2,1)S(1)}, u32[]{:S(2)}, u32[]{:S(2)}) collective-permute-start(bf16[64,3200]{1,0:T(8,128)(2,1)} %get-tuple-element.161.refs_3_), channel_id=1, source_target_pairs={{0,1},{1,0},{2,3},{3,2},{4,5},{5,4},{6,7},{7,6},{8,9},{9,8},{10,11... | collective-permute-start | bytes 1228808 | tf_op jit(solution)/shard_map/ppermute | solution.py:1428
  320.8 37.2 %collective-permute-start.37 = (bf16[4,3,48,768]{3,2,1,0:T(8,128)(2,1)}, bf16[4,3,48,768]{3,2,1,0:T(8,128)(2,1)S(1)}, u32[]{:S(2)}, u32[]{:S(2)}) collective-permute-start(bf16[4,3,48,768]{3,2,1,0:T(8,128)(2,1)} %call_sums.3.refs_2_.refs_1_), channel_id=1, source_target_pairs={{0,1},{1,0},{2,3},{3,2},{4,5},{5,4},{6,7},{7,6},{8,9},{9,8},{10,11... | collective-permute-start | bytes 2654216 | tf_op jit(solution)/shard_map/ppermute | solution.py:1428
  327.4 24.8 %collective-permute-start.35 = (bf16[64,3200]{1,0:T(8,128)(2,1)}, bf16[64,3200]{1,0:T(8,128)(2,1)S(1)}, u32[]{:S(2)}, u32[]{:S(2)}) collective-permute-start(bf16[64,3200]{1,0:T(8,128)(2,1)} %call_sums.4.refs_0_), channel_id=1, source_target_pairs={{0,3},{3,0},{1,2},{2,1},{4,7},{7,4},{5,6},{6,5},{8,11},{11,8},{9,1... | collective-permute-start | bytes 1228808 | tf_op jit(solution)/shard_map/ppermute | solution.py:1428
  354.9 10.0 %collective-permute-start.36 = (bf16[64,3200]{1,0:T(8,128)(2,1)}, bf16[64,3200]{1,0:T(8,128)(2,1)S(1)}, u32[]{:S(2)}, u32[]{:S(2)}) collective-permute-start(bf16[64,3200]{1,0:T(8,128)(2,1)} %call_sums.5.refs_5_.refs_1_), channel_id=1, source_target_pairs={{0,1},{1,0},{2,3},{3,2},{4,5},{5,4},{6,7},{7,6},{8,9},{9,8},{10,11... | collective-permute-start | bytes 1228808 | tf_op jit(solution)/shard_map/ppermute | solution.py:1428
  (18 other events, 14.5 us)
Sparse Core Ops, SparseCore 0:
  177.4 52.0 reduce-scatter.3

commit v5 on v4

--- a/solution.py
+++ b/solution.py
@@ -1602,7 +1602,7 @@
     *in_send, in_bias_send = hold((*in_send, in_bias_send), (in_keep,))
     in_other, in_bias_other = [swap(v, n, 1) for v in in_send], swap(in_bias_send, n, 1)
 
-    first = width // LANES // 2
+    first = width // LANES // 3
     span = first * LANES
     g_first, keep_one, send_one = call_attention_backward_one(
         n, me, starts, qkv, lse, n1, g_mixed, g_out, first, (in_keep,)

time: 381 us -> 380 us (level)
    unnamed x81 -> x83, local copies, waits for them, and re-layouts: 19.6 us -> 19.3 us
where the time goes in v5:
time: 380 us; the launch traced here: 374 us
  Pallas kernels  159 us (42%)
  waiting for transfers between devices  128 us (34%)
  starting transfers between devices  44 us (12%)
  local copies, waits for them, and re-layouts  23 us (6%)
  between operations  14.9 us (4%)
  other arithmetic  5.29 us (1%)
    pallas_call x34, Pallas kernels, kernel_call(): pl.pallas_call(body, out_shape=out_shape, in_specs=in_specs, out_specs=ou...  159 us
    ppermute x11, waiting for transfers between devices, line(): return lax.ppermute(v, REP, pairs)  53.9 us
    ppermute x27, waiting for transfers between devices, swap(): return lax.ppermute(v, FSDP, [(i, i ^ mask) for i in range(n)])  40.8 us
    all_to_all x3, waiting for transfers between devices, exchange(): return lax.all_to_all(v, FSDP, 0, 0, axis_index_groups=groups)  33.2 us
    ppermute x27, starting transfers between devices, swap(): return lax.ppermute(v, FSDP, [(i, i ^ mask) for i in range(n)])  19.7 us
    unnamed x83, local copies, waits for them, and re-layouts  19.3 us
    ppermute x11, starting transfers between devices, line(): return lax.ppermute(v, REP, pairs)  12.3 us
    all_to_all x3, starting transfers between devices, exchange(): return lax.all_to_all(v, FSDP, 0, 0, axis_index_groups=groups)  12 us
  transfers between devices with their start and end apart: 42, of which 20 were waited for; matrix products, arithmetic and copies ran while one was open for 2% of the time, Pallas kernels for 39%

profile of v5, /device:TPU:0, one launch (start us, length us, event | category | flops | bytes accessed | tf_op | source)
XLA Modules:
  0.0 374.0 jit_solution(14074299522584192891)
XLA Ops:
  7.2 1.4 stack.37.refs_4_
  8.6 2.1 pack.1.refs_0_.refs_3_.refs_5_.refs_11_
  10.7 2.9 collective-permute-start
  13.6 1.5 collective-permute-start.1
  18.4 9.2 %collective-permute-done.refs_1_.refs_4_.refs_6_.refs_12_ = bf16[400,768]{1,0:T(8,128)(2,1)S(1)} collective-permute-done((bf16[400,768]{1,0:T(8,128)(2,1)}, bf16[400,768]{1,0:T(8,128)(2,1)S(1)}, u32[]{:S(2)}, u32[]{:S(2)}) %collective-permute-start) | collective-permute-done | bytes 614432 | tf_op jit(solution)/shard_map/ppermute | solution.py:1404
  27.7 1.5 collective-permute-done.1.refs_2_.refs_5_.refs_7_.refs_13_
  30.0 2.9 call_halves.1
  32.9 1.5 collective-permute-start.2
  36.0 4.6 %collective-permute-done.2.refs_6_.refs_8_.refs_14_ = bf16[192,768]{1,0:T(8,128)(2,1)S(1)} collective-permute-done((bf16[192,768]{1,0:T(8,128)(2,1)}, bf16[192,768]{1,0:T(8,128)(2,1)S(1)}, u32[]{:S(2)}, u32[]{:S(2)}) %collective-permute-start.2) | collective-permute-done | bytes 294944 | tf_op jit(solution)/shard_map/ppermute | solution.py:1404
  40.6 1.8 collective-permute-done.3.refs_7_.refs_9_.refs_15_
  43.1 3.7 call_columns_and_sort.1
  47.6 3.7 all-to-all-start
  52.0 14.7 %attention_forward.1 = (bf16[416,2304]{1,0:T(8,128)(2,1)}, bf16[416,768]{1,0:T(8,128)(2,1)}, f32[16,416]{1,0:T(8,128)}, bf16[416,768]{1,0:T(8,128)(2,1)}, f32[16,768]{1,0:T(8,128)}, /*index=5*/f32[16,768]{1,0:T(8,128)}) custom-call(s32[1]{0:T(128)} %bitcast.5.refs_0_, s32[1,4]{1,0:T(1,128)} %refs_1_.7, bf16[416,768]{1,0:T(8,128)(2,1)} %refs_2_.9, ...), custom_call_target="tpu_custom_call" | custom-call | tf_op jit(solution)/shard_map/attention_forward/pallas_call | solution.py:427
  66.7 5.2 %mix_out.1 = (f32[416,768]{1,0:T(8,128)}, bf16[448,768]{1,0:T(8,128)(2,1)}) custom-call(s32[1]{0:T(128)} %bitcast.5.refs_0_, bf16[416,768]{1,0:T(8,128)(2,1)} %get-tuple-element.100.refs_1_.refs_6_, bf16[416,768]{1,0:T(8,128)(2,1)} %refs_2_.9, f32[16,768]{1,0:T(8,128)} %get-tuple-element.101.refs_3_.refs_5_, s32[1,416]{1,0:T(1,128)} %bitcast.48, ...), custom_call_target="tpu_custom_call" | custom-call | tf_op jit(solution)/shard_map/mix_out/pallas_call | solution.py:427
  71.9 1.7 all-to-all-done.refs_0_
  74.8 1.4 collective-permute-start.9
  76.8 1.5 collective-permute-start.7
  80.1 9.8 %experts.3 = (bf16[448,768]{1,0:T(8,128)(2,1)}, bf16[4,448,768]{2,1,0:T(8,128)(2,1)}, bf16[3,208,768]{2,1,0:T(8,128)(2,1)}, bf16[3,208,768]{2,1,0:T(8,128)(2,1)}) custom-call(s32[1]{0:T(128)} %bitcast.5.refs_0_, s32[1,9]{1,0:T(1,128)} %copy-done.38, f32[16,768]{1,0:T(8,128)} %get-tuple-element.105.refs_2_, ...), custom_call_target="tpu_custom_call" | custom-call | tf_op jit(solution)/shard_map/experts/pallas_call | solution.py:427
  89.9 3.9 %collective-permute-done.9.refs_2_.refs_5_.refs_3_ = bf16[464,768]{1,0:T(8,128)(2,1)} collective-permute-done((bf16[464,768]{1,0:T(8,128)(2,1)}, bf16[464,768]{1,0:T(8,128)(2,1)}, u32[]{:S(2)}, u32[]{:S(2)}) %collective-permute-start.9) | collective-permute-done | bytes 712736 | tf_op jit(solution)/shard_map/ppermute | solution.py:1404
  93.9 1.5 collective-permute-done.10.refs_3_.refs_6_.refs_4_
  95.3 12.9 %collective-permute-done.7.refs_0_.refs_3_ = bf16[448,768]{1,0:T(8,128)(2,1)} collective-permute-done((bf16[448,768]{1,0:T(8,128)(2,1)}, bf16[448,768]{1,0:T(8,128)(2,1)}, u32[]{:S(2)}, u32[]{:S(2)}) %collective-permute-start.7) | collective-permute-done | bytes 688160 | tf_op jit(solution)/shard_map/ppermute | solution.py:1404
  110.1 2.9 call_two_halves.1
  113.6 1.5 collective-permute-start.14
  117.1 14.1 %experts.4 = (bf16[448,768]{1,0:T(8,128)(2,1)}, bf16[448,768]{1,0:T(8,128)(2,1)}, bf16[4,448,768]{2,1,0:T(8,128)(2,1)}, bf16[3,416,768]{2,1,0:T(8,128)(2,1)}, bf16[3,416,768]{2,1,0:T(8,128)(2,1)}) custom-call(s32[1]{0:T(128)} %bitcast.5.refs_0_, s32[2,9]{1,0:T(2,128)} %convert_multiply_fusion.refs_1_, ...), custom_call_target="tpu_custom_call", output_to_operand_aliasing={{2}: (11, {})} | custom-call | tf_op jit(solution)/shard_map/experts/pallas_call | solution.py:427
  131.7 1.5 collective-permute-start.16
  134.6 9.6 %experts.5 = (bf16[448,768]{1,0:T(8,128)(2,1)}, bf16[4,448,768]{2,1,0:T(8,128)(2,1)}, bf16[3,208,768]{2,1,0:T(8,128)(2,1)}, bf16[3,208,768]{2,1,0:T(8,128)(2,1)}) custom-call(s32[1]{0:T(128)} %bitcast.5.refs_0_, s32[1,9]{1,0:T(1,128)} %fusion.1.refs_1_, f32[16,768]{1,0:T(8,128)} %get-tuple-element.105.refs_2_, ...), custom_call_target="tpu_custom_call", output_to_operand_aliasing={{1}: (11, {})} | custom-call | tf_op jit(solution)/shard_map/experts/pallas_call | solution.py:427
  144.2 1.6 collective-permute-start.17
  146.4 3.1 collective-permute-done.15.refs_10_.refs_8_
  150.4 10.4 %down_grads.1 = (bf16[3,384,768]{2,1,0:T(8,128)(2,1)}, bf16[384,768]{1,0:T(8,128)(2,1)}, bf16[384,768]{1,0:T(8,128)(2,1)}, bf16[384,768]{1,0:T(8,128)(2,1)}) custom-call(s32[1]{0:T(128)} %bitcast.5.refs_0_, s32[4,9]{1,0:T(4,128)} %pad_add_fusion.refs_1_, bf16[464,768]{1,0:T(8,128)(2,1)} %get-tuple-element.104.refs_4_.refs_2_, ...), custom_call_target="tpu_custom_call" | custom-call | tf_op jit(solution)/shard_map/down_grads/pallas_call | solution.py:427
  161.5 1.3 collective-permute-done.16.refs_9_
  163.9 7.2 %mix_out_backward.1 = (f32[416,768]{1,0:T(8,128)}, bf16[416,768]{1,0:T(8,128)(2,1)}, f32[16,768]{1,0:T(8,128)}, bf16[768,768]{1,0:T(8,128)(2,1)}) custom-call(s32[1]{0:T(128)} %bitcast.5.refs_0_, s32[1,416]{1,0:T(1,128)} %bitcast.49, s32[1,416]{1,0:T(1,128)} %bitcast.53, f32[416,768]{1,0:T(8,128)} %get-tuple-element.102.refs_3_.refs_1_, ...), custom_call_target="tpu_custom_call" | custom-call | tf_op jit(solution)/shard_map/mix_out_backward/pallas_call | solution.py:427
  172.3 3.5 call_pair_down.1
  175.7 1.6 collective-permute-start.22
  177.3 10.8 %in_grads.1 = (bf16[4,3,96,768]{3,2,1,0:T(8,128)(2,1)}, bf16[16,384]{1,0:T(8,128)(2,1)}, bf16[16,384]{1,0:T(8,128)(2,1)}, bf16[4,96,768]{2,1,0:T(8,128)(2,1)}, b...) custom-call(s32[1]{0:T(128)} %bitcast.5.refs_0_, s32[4,9]{1,0:T(4,128)} %pad_add_fusion.refs_1_, ...), custom_call_target="tpu_custom_call" | custom-call | tf_op jit(solution)/shard_map/in_grads/pallas_call | solution.py:427
  189.3 8.9 %attention_backward_one.1 = (bf16[416,768]{1,0:T(8,128)(2,1)}, bf16[4,96,1536]{2,1,0:T(8,128)(2,1)}, bf16[4,96,1536]{2,1,0:T(8,128)(2,1)}) custom-call(s32[1]{0:T(128)} %bitcast.5.refs_0_, s32[1,4]{1,0:T(1,128)} %refs_1_.7, bf16[416,2304]{1,0:T(8,128)(2,1)} %get-tuple-element.122.refs_2_.refs_5_, f32[16,416]{1,0:T(8,128)} %get-tuple-element.123.refs_3_.refs_6_, ...), custom_call_target="tpu_custom_call" | custom-call | tf_op jit(solution)/shard_map/attention_backward_one/pallas_call | solution.py:427
  199.7 4.5 %call_pair_in.1 = (bf16[4,3,96,768]{3,2,1,0:T(8,128)(2,1)}, bf16[16,384]{1,0:T(8,128)(2,1)}, bf16[1,192,768]{2,1,0:T(8,128)(2,1)}, bf16[2,192,768]{2,1,0:T(8,128)(2,1)}) custom-call(bf16[4,3,96,768]{3,2,1,0:T(8,128)(2,1)} %get-tuple-element.132.refs_7_.refs_4_.refs_0_, bf16[16,384]{1,0:T(8,128)(2,1)} %get-tuple-element.135.refs_1_, ...), custom_call_target="tpu_custom_call" | custom-call | tf_op jit(solution)/shard_map/call_pair_in/pallas_call | solution.py:427
  204.2 4.1 %all-to-all-start.1 = ((bf16[4,3,96,768]{3,2,1,0:T(8,128)(2,1)}), bf16[4,3,96,768]{3,2,1,0:T(8,128)(2,1)S(1)}, u32[]{:S(2)}, u32[]{:S(2)}) async-start(bf16[4,3,96,768]{3,2,1,0:T(8,128)(2,1)} %get-tuple-element.146.refs_1_.refs_19_), calls=%async_computation.1 | async-start | bytes 3538944 | tf_op jit(solution)/shard_map/all_to_all | solution.py:1418
  208.3 2.3 collective-permute-start.27
  210.6 16.6 %attention_backward_two.1 = (f32[416,768]{1,0:T(8,128)}, bf16[4,96,1664]{2,1,0:T(8,128)(2,1)}, bf16[4,96,1664]{2,1,0:T(8,128)(2,1)}) custom-call(s32[1]{0:T(128)} %bitcast.5.refs_0_, s32[1,4]{1,0:T(1,128)} %refs_1_.7, bf16[416,768]{1,0:T(8,128)(2,1)} %refs_2_.9, f32[16,768]{1,0:T(8,128)} %get-tuple-element.101.refs_3_.refs_5_, ...), custom_call_target="tpu_custom_call" | custom-call | tf_op jit(solution)/shard_map/attention_backward_two/pallas_call | solution.py:427
  229.0 1.5 collective-permute-start.29
  230.5 4.5 %all-to-all-done.1.refs_1_ = bf16[4,3,96,768]{3,2,1,0:T(8,128)(2,1)S(1)} async-done(((bf16[4,3,96,768]{3,2,1,0:T(8,128)(2,1)}), bf16[4,3,96,768]{3,2,1,0:T(8,128)(2,1)S(1)}, u32[]{:S(2)}, u32[]{:S(2)}) %all-to-all-start.1) | async-done | bytes 1769504 | tf_op jit(solution)/shard_map/all_to_all | solution.py:1418
  236.2 2.8 call_split_rows.1
  239.0 1.5 collective-permute-start.30
  242.1 4.4 %call_pair_shares.1.refs_7_.refs_0_ = bf16[4,96,3200]{2,1,0:T(8,128)(2,1)} custom-call(bf16[4,96,1536]{2,1,0:T(8,128)(2,1)} %get-tuple-element.133.refs_0_, bf16[4,96,1536]{2,1,0:T(8,128)(2,1)} %copy-done.18, bf16[4,96,1664]{2,1,0:T(8,128)(2,1)} %get-tuple-element.149.refs_2_.refs_4_, bf16[4,96,1664]{2,1,0:T(8,128)(2,1)} %collective-permute-done.28.refs_3_, ...), custom_call_target="tpu_custom_call" | custom-call | tf_op jit(solution)/shard_map/call_pair_shares/pallas_call | solution.py:427
  247.1 9.1 %collective-permute-done.30.refs_5_ = bf16[2,3,48,768]{3,2,1,0:T(8,128)(2,1)S(1)} collective-permute-done((bf16[2,3,48,768]{3,2,1,0:T(8,128)(2,1)}, bf16[2,3,48,768]{3,2,1,0:T(8,128)(2,1)S(1)}, u32[]{:S(2)}, u32[]{:S(2)}) %collective-permute-start.30) | collective-permute-done | bytes 442400 | tf_op jit(solution)/shard_map/ppermute | solution.py:1428
  256.2 9.4 %collective-permute-done.31.refs_6_ = bf16[2,3,48,768]{3,2,1,0:T(8,128)(2,1)S(1)} collective-permute-done((bf16[2,3,48,768]{3,2,1,0:T(8,128)(2,1)}, bf16[2,3,48,768]{3,2,1,0:T(8,128)(2,1)S(1)}, u32[]{:S(2)}, u32[]{:S(2)}) %collective-permute-start.31) | collective-permute-done | bytes 442400 | tf_op jit(solution)/shard_map/ppermute | solution.py:1428
  266.4 3.4 call_line_sums.1
  269.8 4.2 %all-to-all-start.2 = ((bf16[4,96,3200]{2,1,0:T(8,128)(2,1)}), bf16[4,96,3200]{2,1,0:T(8,128)(2,1)S(1)}, u32[]{:S(2)}, u32[]{:S(2)}) async-start(bf16[4,96,3200]{2,1,0:T(8,128)(2,1)} %hold.13), calls=%async_computation.2 | async-start | bytes 4915200 | tf_op jit(solution)/shard_map/all_to_all | solution.py:1418
  274.0 2.0 collective-permute-start.33
  276.0 26.9 %all-to-all-done.2.refs_1_ = bf16[4,96,3200]{2,1,0:T(8,128)(2,1)S(1)} async-done(((bf16[4,96,3200]{2,1,0:T(8,128)(2,1)}), bf16[4,96,3200]{2,1,0:T(8,128)(2,1)S(1)}, u32[]{:S(2)}, u32[]{:S(2)}) %all-to-all-start.2) | async-done | bytes 2457632 | tf_op jit(solution)/shard_map/all_to_all | solution.py:1418
  303.0 1.4 copy-done.7
  304.4 2.7 call_attention_shares.1
  307.2 3.5 call_down_result.1.refs_2_
  310.6 5.0 %collective-permute-done.33.refs_1_ = bf16[4,3,48,768]{3,2,1,0:T(8,128)(2,1)} collective-permute-done((bf16[4,3,48,768]{3,2,1,0:T(8,128)(2,1)}, bf16[4,3,48,768]{3,2,1,0:T(8,128)(2,1)}, u32[]{:S(2)}, u32[]{:S(2)}) %collective-permute-start.33) | collective-permute-done | bytes 884768 | tf_op jit(solution)/shard_map/ppermute | solution.py:1428
  315.7 2.6 call_sums.3.refs_2_.refs_1_
  318.9 4.2 %collective-permute-done.32.refs_1_ = bf16[64,3200]{1,0:T(8,128)(2,1)S(1)} collective-permute-done((bf16[64,3200]{1,0:T(8,128)(2,1)}, bf16[64,3200]{1,0:T(8,128)(2,1)S(1)}, u32[]{:S(2)}, u32[]{:S(2)}) %collective-permute-start.32) | collective-permute-done | bytes 409632 | tf_op jit(solution)/shard_map/ppermute | solution.py:1428
  323.9 2.0 call_sums.4.refs_0_
  325.8 2.2 collective-permute-start.35
  328.1 22.7 %collective-permute-done.35.refs_1_ = bf16[64,3200]{1,0:T(8,128)(2,1)S(1)} collective-permute-done((bf16[64,3200]{1,0:T(8,128)(2,1)}, bf16[64,3200]{1,0:T(8,128)(2,1)S(1)}, u32[]{:S(2)}, u32[]{:S(2)}) %collective-permute-start.35) | collective-permute-done | bytes 409632 | tf_op jit(solution)/shard_map/ppermute | solution.py:1428
  351.5 2.0 call_sums.5.refs_5_.refs_1_
  353.5 3.1 finish_output.1.refs_3_
  357.5 3.5 call_in_result.1
  361.0 2.8 collective-permute-done.36.refs_2_
  364.5 2.2 call_attention_result.1
  (163 shorter events, 34.7 us)
Async XLA Ops:
  7.2 35.2 %copy-start.35 = (s32[416,1]{0,1:T(1,128)S(1)}, s32[416,1]{0,1:T(1,128)}, u32[]{:S(2)}) copy-start(s32[416,1]{0,1:T(1,128)} %param.21) | copy-start | bytes 4996
  10.7 17.0 %collective-permute-start = (bf16[400,768]{1,0:T(8,128)(2,1)}, bf16[400,768]{1,0:T(8,128)(2,1)S(1)}, u32[]{:S(2)}, u32[]{:S(2)}) collective-permute-start(bf16[400,768]{1,0:T(8,128)(2,1)} %pack.1.refs_0_.refs_3_.refs_5_.refs_11_), channel_id=1, source_target_pairs={{0,8},{4,12},{8,0},{12,4},{16,24},{20,28},{24,16},{28,20},{1,9},{5... | collective-permute-start | bytes 1843208 | tf_op jit(solution)/shard_map/ppermute | solution.py:1404
  13.6 15.5 %collective-permute-start.1 = (bf16[400,768]{1,0:T(8,128)(2,1)}, bf16[400,768]{1,0:T(8,128)(2,1)S(1)}, u32[]{:S(2)}, u32[]{:S(2)}) collective-permute-start(bf16[400,768]{1,0:T(8,128)(2,1)} %pack.1.refs_0_.refs_3_.refs_5_.refs_11_), channel_id=1, source_target_pairs={{0,16},{4,20},{8,24},{12,28},{16,0},{20,4},{24,8},{28,12},{1,17},{... | collective-permute-start | bytes 1843208 | tf_op jit(solution)/shard_map/ppermute | solution.py:1404
  18.4 28.4 %copy-start.38 = (s32[1,9]{1,0:T(1,128)}, s32[1,9]{1,0:T(1,128)S(1)}, u32[]{:S(2)}) copy-start(s32[1,9]{1,0:T(1,128)S(1)} %mul.42.refs_1_) | copy-start | bytes 112
  27.7 1.5 copy-start.3
  32.9 7.8 %collective-permute-start.2 = (bf16[192,768]{1,0:T(8,128)(2,1)}, bf16[192,768]{1,0:T(8,128)(2,1)S(1)}, u32[]{:S(2)}, u32[]{:S(2)}) collective-permute-start(bf16[192,768]{1,0:T(8,128)(2,1)} %get-tuple-element.97.refs_4_), channel_id=1, source_target_pairs={{0,16},{4,20},{8,24},{12,28},{16,0},{20,4},{24,8},{28,12},{1,17},{... | collective-permute-start | bytes 884744 | tf_op jit(solution)/shard_map/ppermute | solution.py:1404
  34.4 8.0 %collective-permute-start.3 = (bf16[208,768]{1,0:T(8,128)(2,1)}, bf16[208,768]{1,0:T(8,128)(2,1)S(1)}, u32[]{:S(2)}, u32[]{:S(2)}) collective-permute-start(bf16[208,768]{1,0:T(8,128)(2,1)} %get-tuple-element.98), channel_id=1, source_target_pairs={{0,8},{4,12},{8,0},{12,4},{16,24},{20,28},{24,16},{28,20},{1,9},{5... | collective-permute-start | bytes 958472 | tf_op jit(solution)/shard_map/ppermute | solution.py:1404
  36.0 15.9 %collective-permute-start.4 = (bf16[3,400,768]{2,1,0:T(8,128)(2,1)}, bf16[3,400,768]{2,1,0:T(8,128)(2,1)}, u32[]{:S(2)}, u32[]{:S(2)}) collective-permute-start(bf16[3,400,768]{2,1,0:T(8,128)(2,1)} %get-tuple-element.99), channel_id=1, source_target_pairs={{0,4},{4,0},{8,12},{12,8},{16,20},{20,16},{24,28},{28,24},{1,5},{5... | collective-permute-start | bytes 5529608 | tf_op jit(solution)/shard_map/ppermute | solution.py:1404
  40.6 7.0 %copy-start.13 = (bf16[192,768]{1,0:T(8,128)(2,1)}, bf16[192,768]{1,0:T(8,128)(2,1)S(1)}, u32[]{:S(2)}) copy-start(bf16[192,768]{1,0:T(8,128)(2,1)S(1)} %collective-permute-done.2.refs_6_.refs_8_.refs_14_) | copy-start | bytes 884740
  40.6 6.1 %collective-permute-start.5 = (bf16[192,768]{1,0:T(8,128)(2,1)S(1)}, bf16[192,768]{1,0:T(8,128)(2,1)S(1)}, u32[]{:S(2)}, u32[]{:S(2)}) collective-permute-start(bf16[192,768]{1,0:T(8,128)(2,1)S(1)} %collective-permute-done.2.refs_6_.refs_8_.refs_14_), channel_id=1, source_target_pairs={{0,4},{4,0},{8,12},{12,8},{16,20},{20,16},{24,28},{28,24},{1,5},{5... | collective-permute-start | bytes 884744 | tf_op jit(solution)/shard_map/ppermute | solution.py:1404
  42.4 5.2 %copy-start.12 = (bf16[208,768]{1,0:T(8,128)(2,1)}, bf16[208,768]{1,0:T(8,128)(2,1)S(1)}, u32[]{:S(2)}) copy-start(bf16[208,768]{1,0:T(8,128)(2,1)S(1)} %collective-permute-done.3.refs_7_.refs_9_.refs_15_) | copy-start | bytes 958468
  42.4 4.4 %collective-permute-start.6 = (bf16[208,768]{1,0:T(8,128)(2,1)S(1)}, bf16[208,768]{1,0:T(8,128)(2,1)S(1)}, u32[]{:S(2)}, u32[]{:S(2)}) collective-permute-start(bf16[208,768]{1,0:T(8,128)(2,1)S(1)} %collective-permute-done.3.refs_7_.refs_9_.refs_15_), channel_id=1, source_target_pairs={{0,4},{4,0},{8,12},{12,8},{16,20},{20,16},{24,28},{28,24},{1,5},{5... | collective-permute-start | bytes 958472 | tf_op jit(solution)/shard_map/ppermute | solution.py:1404
  47.6 3.8 %copy-start.1 = (bf16[3,384,768]{2,1,0:T(8,128)(2,1)S(1)}, bf16[3,384,768]{2,1,0:T(8,128)(2,1)}, u32[]{:S(2)}) copy-start(bf16[3,384,768]{2,1,0:T(8,128)(2,1)} %refs_9_.3) | copy-start | bytes 5308420
  47.6 26.0 %all-to-all-start = ((bf16[4,3,96,768]{3,2,1,0:T(8,128)(2,1)}), bf16[4,3,96,768]{3,2,1,0:T(8,128)(2,1)S(1)}, u32[]{:S(2)}, u32[]{:S(2)}) async-start(bf16[4,3,96,768]{3,2,1,0:T(8,128)(2,1)} %hold.7), calls=%async_computation | async-start | bytes 3538944 | tf_op jit(solution)/shard_map/all_to_all | solution.py:1418
  51.3 302.2 %reduce-scatter.4.cloned.1.call-start = ((), (), s32[]{:S(2)}) async-start(), calls=%async_computation.4 | async-start | bytes 3440640
  51.4 26.9 %collective-permute-start.12 = (bf16[3,384,768]{2,1,0:T(8,128)(2,1)S(1)}, bf16[3,384,768]{2,1,0:T(8,128)(2,1)}, u32[]{:S(2)}, u32[]{:S(2)}) collective-permute-start(bf16[3,384,768]{2,1,0:T(8,128)(2,1)S(1)} %copy-done.1), channel_id=1, source_target_pairs={{0,4},{4,0},{8,12},{12,8},{16,20},{20,16},{24,28},{28,24},{1,5},{5... | collective-permute-start | bytes 5308424 | tf_op jit(solution)/shard_map/ppermute | solution.py:1404
  73.6 1.2 copy-start
  74.8 4.1 %collective-permute-start.11 = (bf16[4,3,96,768]{3,2,1,0:T(8,128)(2,1)}, bf16[4,3,96,768]{3,2,1,0:T(8,128)(2,1)S(1)}, u32[]{:S(2)}, u32[]{:S(2)}) collective-permute-start(bf16[4,3,96,768]{3,2,1,0:T(8,128)(2,1)} %hold.8.refs_5_.refs_7_), channel_id=1, source_target_pairs={{0,4},{4,0},{8,12},{12,8},{16,20},{20,16},{24,28},{28,24},{1,5},{5... | collective-permute-start | bytes 5308424 | tf_op jit(solution)/shard_map/ppermute | solution.py:1404
  74.8 19.1 %collective-permute-start.9 = (bf16[464,768]{1,0:T(8,128)(2,1)}, bf16[464,768]{1,0:T(8,128)(2,1)}, u32[]{:S(2)}, u32[]{:S(2)}) collective-permute-start(bf16[464,768]{1,0:T(8,128)(2,1)} %get-tuple-element.104.refs_4_.refs_2_), channel_id=1, source_target_pairs={{0,8},{4,12},{8,0},{12,4},{16,24},{20,28},{24,16},{28,20},{1,9},{5... | collective-permute-start | bytes 2138120 | tf_op jit(solution)/shard_map/ppermute | solution.py:1404
  76.2 19.1 %collective-permute-start.10 = (bf16[464,768]{1,0:T(8,128)(2,1)}, bf16[464,768]{1,0:T(8,128)(2,1)}, u32[]{:S(2)}, u32[]{:S(2)}) collective-permute-start(bf16[464,768]{1,0:T(8,128)(2,1)} %get-tuple-element.104.refs_4_.refs_2_), channel_id=1, source_target_pairs={{0,16},{4,20},{8,24},{12,28},{16,0},{20,4},{24,8},{28,12},{1,17},{... | collective-permute-start | bytes 2138120 | tf_op jit(solution)/shard_map/ppermute | solution.py:1404
  76.8 31.5 %collective-permute-start.7 = (bf16[448,768]{1,0:T(8,128)(2,1)}, bf16[448,768]{1,0:T(8,128)(2,1)}, u32[]{:S(2)}, u32[]{:S(2)}) collective-permute-start(bf16[448,768]{1,0:T(8,128)(2,1)} %get-tuple-element.103.refs_1_.refs_3_.refs_2_), channel_id=1, source_target_pairs={{0,8},{4,12},{8,0},{12,4},{16,24},{20,28},{24,16},{28,20},{1,9},{5... | collective-permute-start | bytes 2064392 | tf_op jit(solution)/shard_map/ppermute | solution.py:1404
  78.3 31.0 %collective-permute-start.8 = (bf16[448,768]{1,0:T(8,128)(2,1)}, bf16[448,768]{1,0:T(8,128)(2,1)S(1)}, u32[]{:S(2)}, u32[]{:S(2)}) collective-permute-start(bf16[448,768]{1,0:T(8,128)(2,1)} %get-tuple-element.103.refs_1_.refs_3_.refs_2_), channel_id=1, source_target_pairs={{0,16},{4,20},{8,24},{12,28},{16,0},{20,4},{24,8},{28,12},{1,17},{... | collective-permute-start | bytes 2064392 | tf_op jit(solution)/shard_map/ppermute | solution.py:1404
  78.9 1.2 copy-start.2
  113.0 20.2 %collective-permute-start.13 = (bf16[464,768]{1,0:T(8,128)(2,1)}, bf16[464,768]{1,0:T(8,128)(2,1)S(1)}, u32[]{:S(2)}, u32[]{:S(2)}) collective-permute-start(bf16[464,768]{1,0:T(8,128)(2,1)} %get-tuple-element.108), channel_id=1, source_target_pairs={{0,8},{4,12},{8,0},{12,4},{16,24},{20,28},{24,16},{28,20},{1,9},{5... | collective-permute-start | bytes 2138120 | tf_op jit(solution)/shard_map/ppermute | solution.py:1404
  113.6 20.1 %collective-permute-start.14 = (bf16[448,768]{1,0:T(8,128)(2,1)}, bf16[448,768]{1,0:T(8,128)(2,1)S(1)}, u32[]{:S(2)}, u32[]{:S(2)}) collective-permute-start(bf16[448,768]{1,0:T(8,128)(2,1)} %get-tuple-element.109), channel_id=1, source_target_pairs={{0,16},{4,20},{8,24},{12,28},{16,0},{20,4},{24,8},{28,12},{1,17},{... | collective-permute-start | bytes 2064392 | tf_op jit(solution)/shard_map/ppermute | solution.py:1404
  131.1 18.4 %collective-permute-start.15 = (bf16[448,768]{1,0:T(8,128)(2,1)}, bf16[448,768]{1,0:T(8,128)(2,1)S(1)}, u32[]{:S(2)}, u32[]{:S(2)}) collective-permute-start(bf16[448,768]{1,0:T(8,128)(2,1)} %get-tuple-element.114), channel_id=1, source_target_pairs={{0,8},{4,12},{8,0},{12,4},{16,24},{20,28},{24,16},{28,20},{1,9},{5... | collective-permute-start | bytes 2064392 | tf_op jit(solution)/shard_map/ppermute | solution.py:1404
  131.7 31.1 %collective-permute-start.16 = (bf16[448,768]{1,0:T(8,128)(2,1)}, bf16[448,768]{1,0:T(8,128)(2,1)S(1)}, u32[]{:S(2)}, u32[]{:S(2)}) collective-permute-start(bf16[448,768]{1,0:T(8,128)(2,1)} %get-tuple-element.115), channel_id=1, source_target_pairs={{0,16},{4,20},{8,24},{12,28},{16,0},{20,4},{24,8},{28,12},{1,17},{... | collective-permute-start | bytes 2064392 | tf_op jit(solution)/shard_map/ppermute | solution.py:1404
  134.6 11.2 %copy-start.37 = (s32[2,9]{1,0:T(2,128)S(1)}, s32[2,9]{1,0:T(2,128)}, u32[]{:S(2)}) copy-start(s32[2,9]{1,0:T(2,128)} %convert_multiply_fusion.refs_1_) | copy-start | bytes 220
  134.6 11.2 %copy-start.39 = (s32[1,9]{1,0:T(1,128)S(1)}, s32[1,9]{1,0:T(1,128)}, u32[]{:S(2)}) copy-start(s32[1,9]{1,0:T(1,128)} %copy-done.38) | copy-start | bytes 112
  134.6 11.2 %copy-start.40 = (s32[1,9]{1,0:T(1,128)S(1)}, s32[1,9]{1,0:T(1,128)}, u32[]{:S(2)}) copy-start(s32[1,9]{1,0:T(1,128)} %fusion.1.refs_1_) | copy-start | bytes 112
  144.2 18.6 %collective-permute-start.17 = (bf16[448,768]{1,0:T(8,128)(2,1)}, bf16[448,768]{1,0:T(8,128)(2,1)S(1)}, u32[]{:S(2)}, u32[]{:S(2)}) collective-permute-start(bf16[448,768]{1,0:T(8,128)(2,1)} %get-tuple-element.116), channel_id=1, source_target_pairs={{0,24},{4,28},{8,16},{12,20},{16,8},{20,12},{24,0},{28,4},{1,25},{... | collective-permute-start | bytes 2064392 | tf_op jit(solution)/shard_map/ppermute | solution.py:1404
  160.8 10.2 %collective-permute-start.18 = (bf16[384,768]{1,0:T(8,128)(2,1)}, bf16[384,768]{1,0:T(8,128)(2,1)S(1)}, u32[]{:S(2)}, u32[]{:S(2)}) collective-permute-start(bf16[384,768]{1,0:T(8,128)(2,1)} %get-tuple-element.128), channel_id=1, source_target_pairs={{0,4},{4,0},{8,12},{12,8},{16,20},{20,16},{24,28},{28,24},{1,5},{5... | collective-permute-start | bytes 1769480 | tf_op jit(solution)/shard_map/ppermute | solution.py:1404
  160.9 10.2 %collective-permute-start.19 = (bf16[384,768]{1,0:T(8,128)(2,1)}, bf16[384,768]{1,0:T(8,128)(2,1)S(1)}, u32[]{:S(2)}, u32[]{:S(2)}) collective-permute-start(bf16[384,768]{1,0:T(8,128)(2,1)} %get-tuple-element.129), channel_id=1, source_target_pairs={{0,4},{4,0},{8,12},{12,8},{16,20},{20,16},{24,28},{28,24},{1,5},{5... | collective-permute-start | bytes 1769480 | tf_op jit(solution)/shard_map/ppermute | solution.py:1404
  161.4 9.7 %collective-permute-start.20 = (bf16[384,768]{1,0:T(8,128)(2,1)}, bf16[384,768]{1,0:T(8,128)(2,1)S(1)}, u32[]{:S(2)}, u32[]{:S(2)}) collective-permute-start(bf16[384,768]{1,0:T(8,128)(2,1)} %get-tuple-element.130), channel_id=1, source_target_pairs={{0,4},{4,0},{8,12},{12,8},{16,20},{20,16},{24,28},{28,24},{1,5},{5... | collective-permute-start | bytes 1769480 | tf_op jit(solution)/shard_map/ppermute | solution.py:1404
  162.8 1.1 copy-start.22
  171.1 1.2 copy-start.25
  175.7 22.5 %collective-permute-start.22 = (bf16[3,192,768]{2,1,0:T(8,128)(2,1)}, bf16[3,192,768]{2,1,0:T(8,128)(2,1)S(1)}, u32[]{:S(2)}, u32[]{:S(2)}) collective-permute-start(bf16[3,192,768]{2,1,0:T(8,128)(2,1)} %get-tuple-element.131.refs_10_), channel_id=1, source_target_pairs={{0,1},{1,0},{2,3},{3,2},{4,5},{5,4},{6,7},{7,6},{8,9},{9,8},{10,11... | collective-permute-start | bytes 2654216 | tf_op jit(solution)/shard_map/ppermute | solution.py:1428
  188.2 10.0 %collective-permute-start.23 = (bf16[4,96,768]{2,1,0:T(8,128)(2,1)}, bf16[4,96,768]{2,1,0:T(8,128)(2,1)S(1)}, u32[]{:S(2)}, u32[]{:S(2)}) collective-permute-start(bf16[4,96,768]{2,1,0:T(8,128)(2,1)} %get-tuple-element.142), channel_id=1, source_target_pairs={{0,4},{4,0},{8,12},{12,8},{16,20},{20,16},{24,28},{28,24},{1,5},{5... | collective-permute-start | bytes 1769480 | tf_op jit(solution)/shard_map/ppermute | solution.py:1404
  188.2 10.0 %collective-permute-start.24 = (bf16[4,96,768]{2,1,0:T(8,128)(2,1)}, bf16[4,96,768]{2,1,0:T(8,128)(2,1)S(1)}, u32[]{:S(2)}, u32[]{:S(2)}) collective-permute-start(bf16[4,96,768]{2,1,0:T(8,128)(2,1)} %get-tuple-element.143), channel_id=1, source_target_pairs={{0,4},{4,0},{8,12},{12,8},{16,20},{20,16},{24,28},{28,24},{1,5},{5... | collective-permute-start | bytes 1769480 | tf_op jit(solution)/shard_map/ppermute | solution.py:1404
  188.7 9.5 %collective-permute-start.25 = (bf16[4,96,768]{2,1,0:T(8,128)(2,1)}, bf16[4,96,768]{2,1,0:T(8,128)(2,1)S(1)}, u32[]{:S(2)}, u32[]{:S(2)}) collective-permute-start(bf16[4,96,768]{2,1,0:T(8,128)(2,1)} %get-tuple-element.144), channel_id=1, source_target_pairs={{0,4},{4,0},{8,12},{12,8},{16,20},{20,16},{24,28},{28,24},{1,5},{5... | collective-permute-start | bytes 1769480 | tf_op jit(solution)/shard_map/ppermute | solution.py:1404
  188.8 9.4 %collective-permute-start.21 = (bf16[16,384]{1,0:T(8,128)(2,1)}, bf16[16,384]{1,0:T(8,128)(2,1)S(1)}, u32[]{:S(2)}, u32[]{:S(2)}) collective-permute-start(bf16[16,384]{1,0:T(8,128)(2,1)} %get-tuple-element.140), channel_id=1, source_target_pairs={{0,4},{4,0},{8,12},{12,8},{16,20},{20,16},{24,28},{28,24},{1,5},{5... | collective-permute-start | bytes 36872 | tf_op jit(solution)/shard_map/ppermute | solution.py:1404
  198.2 1.2 copy-start.28
  198.3 1.4 copy-start.20
  204.2 4.1 %copy-start.34 = (bf16[1,192,768]{2,1,0:T(8,128)(2,1)S(1)}, bf16[1,192,768]{2,1,0:T(8,128)(2,1)}, u32[]{:S(2)}) copy-start(bf16[1,192,768]{2,1,0:T(8,128)(2,1)} %get-tuple-element.152.refs_0_) | copy-start | bytes 884740
  204.2 30.8 %all-to-all-start.1 = ((bf16[4,3,96,768]{3,2,1,0:T(8,128)(2,1)}), bf16[4,3,96,768]{3,2,1,0:T(8,128)(2,1)S(1)}, u32[]{:S(2)}, u32[]{:S(2)}) async-start(bf16[4,3,96,768]{3,2,1,0:T(8,128)(2,1)} %get-tuple-element.146.refs_1_.refs_19_), calls=%async_computation.1 | async-start | bytes 3538944 | tf_op jit(solution)/shard_map/all_to_all | solution.py:1418
  208.3 18.9 %collective-permute-start.27 = (bf16[1,192,768]{2,1,0:T(8,128)(2,1)S(1)}, bf16[1,192,768]{2,1,0:T(8,128)(2,1)S(1)}, u32[]{:S(2)}, u32[]{:S(2)}) collective-permute-start(bf16[1,192,768]{2,1,0:T(8,128)(2,1)S(1)} %copy-done.34), channel_id=1, source_target_pairs={{0,3},{3,0},{1,2},{2,1},{4,7},{7,4},{5,6},{6,5},{8,11},{11,8},{9,1... | collective-permute-start | bytes 884744 | tf_op jit(solution)/shard_map/ppermute | solution.py:1428
  227.9 13.1 %collective-permute-start.28 = (bf16[4,96,1664]{2,1,0:T(8,128)(2,1)}, bf16[4,96,1664]{2,1,0:T(8,128)(2,1)}, u32[]{:S(2)}, u32[]{:S(2)}) collective-permute-start(bf16[4,96,1664]{2,1,0:T(8,128)(2,1)} %get-tuple-element.153), channel_id=1, source_target_pairs={{0,4},{4,0},{8,12},{12,8},{16,20},{20,16},{24,28},{28,24},{1,5},{5... | collective-permute-start | bytes 3833864 | tf_op jit(solution)/shard_map/ppermute | solution.py:1404
  227.9 1.1 copy-start.16
  227.9 13.1 %collective-permute-start.26 = (bf16[4,96,1536]{2,1,0:T(8,128)(2,1)}, bf16[4,96,1536]{2,1,0:T(8,128)(2,1)S(1)}, u32[]{:S(2)}, u32[]{:S(2)}) collective-permute-start(bf16[4,96,1536]{2,1,0:T(8,128)(2,1)} %hold.11), channel_id=1, source_target_pairs={{0,4},{4,0},{8,12},{12,8},{16,20},{20,16},{24,28},{28,24},{1,5},{5... | collective-permute-start | bytes 3538952 | tf_op jit(solution)/shard_map/ppermute | solution.py:1404
  229.0 18.1 %collective-permute-start.29 = (bf16[2,192,768]{2,1,0:T(8,128)(2,1)S(1)}, bf16[2,192,768]{2,1,0:T(8,128)(2,1)}, u32[]{:S(2)}, u32[]{:S(2)}) collective-permute-start(bf16[2,192,768]{2,1,0:T(8,128)(2,1)S(1)} %copy-done.16), channel_id=1, source_target_pairs={{0,3},{3,0},{1,2},{2,1},{4,7},{7,4},{5,6},{6,5},{8,11},{11,8},{9,1... | collective-permute-start | bytes 1769480 | tf_op jit(solution)/shard_map/ppermute | solution.py:1428
  235.0 1.2 copy-start.10
  239.0 17.2 %collective-permute-start.30 = (bf16[2,3,48,768]{3,2,1,0:T(8,128)(2,1)}, bf16[2,3,48,768]{3,2,1,0:T(8,128)(2,1)S(1)}, u32[]{:S(2)}, u32[]{:S(2)}) collective-permute-start(bf16[2,3,48,768]{3,2,1,0:T(8,128)(2,1)} %get-tuple-element.156), channel_id=1, source_target_pairs={{0,1},{1,0},{2,3},{3,2},{4,5},{5,4},{6,7},{7,6},{8,9},{9,8},{10,11... | collective-permute-start | bytes 1327112 | tf_op jit(solution)/shard_map/ppermute | solution.py:1428
  240.5 25.1 %collective-permute-start.31 = (bf16[2,3,48,768]{3,2,1,0:T(8,128)(2,1)}, bf16[2,3,48,768]{3,2,1,0:T(8,128)(2,1)S(1)}, u32[]{:S(2)}, u32[]{:S(2)}) collective-permute-start(bf16[2,3,48,768]{3,2,1,0:T(8,128)(2,1)} %get-tuple-element.157), channel_id=1, source_target_pairs={{0,1},{1,0},{2,3},{3,2},{4,5},{5,4},{6,7},{7,6},{8,9},{9,8},{10,11... | collective-permute-start | bytes 1327112 | tf_op jit(solution)/shard_map/ppermute | solution.py:1428
  241.1 1.0 copy-start.18
  256.2 9.4 %copy-start.29 = (bf16[2,3,48,768]{3,2,1,0:T(8,128)(2,1)}, bf16[2,3,48,768]{3,2,1,0:T(8,128)(2,1)S(1)}, u32[]{:S(2)}) copy-start(bf16[2,3,48,768]{3,2,1,0:T(8,128)(2,1)S(1)} %collective-permute-done.30.refs_5_) | copy-start | bytes 1327108
  269.8 4.2 %copy-start.14 = (bf16[3,192,768]{2,1,0:T(8,128)(2,1)S(1)}, bf16[3,192,768]{2,1,0:T(8,128)(2,1)}, u32[]{:S(2)}) copy-start(bf16[3,192,768]{2,1,0:T(8,128)(2,1)} %get-tuple-element.158.refs_1_) | copy-start | bytes 2654212
  269.8 33.2 %all-to-all-start.2 = ((bf16[4,96,3200]{2,1,0:T(8,128)(2,1)}), bf16[4,96,3200]{2,1,0:T(8,128)(2,1)S(1)}, u32[]{:S(2)}, u32[]{:S(2)}) async-start(bf16[4,96,3200]{2,1,0:T(8,128)(2,1)} %hold.13), calls=%async_computation.2 | async-start | bytes 4915200 | tf_op jit(solution)/shard_map/all_to_all | solution.py:1418
  274.0 33.2 %collective-permute-start.34 = (bf16[3,192,768]{2,1,0:T(8,128)(2,1)S(1)}, bf16[3,192,768]{2,1,0:T(8,128)(2,1)}, u32[]{:S(2)}, u32[]{:S(2)}) collective-permute-start(bf16[3,192,768]{2,1,0:T(8,128)(2,1)S(1)} %copy-done.14), channel_id=1, source_target_pairs={{0,1},{1,0},{2,3},{3,2},{4,5},{5,4},{6,7},{7,6},{8,9},{9,8},{10,11... | collective-permute-start | bytes 2654216 | tf_op jit(solution)/shard_map/ppermute | solution.py:1428
  274.0 41.7 %collective-permute-start.33 = (bf16[4,3,48,768]{3,2,1,0:T(8,128)(2,1)}, bf16[4,3,48,768]{3,2,1,0:T(8,128)(2,1)}, u32[]{:S(2)}, u32[]{:S(2)}) collective-permute-start(bf16[4,3,48,768]{3,2,1,0:T(8,128)(2,1)} %get-tuple-element.162.refs_0_), channel_id=1, source_target_pairs={{0,3},{3,0},{1,2},{2,1},{4,7},{7,4},{5,6},{6,5},{8,11},{11,8},{9,1... | collective-permute-start | bytes 2654216 | tf_op jit(solution)/shard_map/ppermute | solution.py:1428
  303.0 1.4 copy-start.7
  307.2 15.9 %collective-permute-start.32 = (bf16[64,3200]{1,0:T(8,128)(2,1)}, bf16[64,3200]{1,0:T(8,128)(2,1)S(1)}, u32[]{:S(2)}, u32[]{:S(2)}) collective-permute-start(bf16[64,3200]{1,0:T(8,128)(2,1)} %get-tuple-element.161.refs_3_), channel_id=1, source_target_pairs={{0,1},{1,0},{2,3},{3,2},{4,5},{5,4},{6,7},{7,6},{8,9},{9,8},{10,11... | collective-permute-start | bytes 1228808 | tf_op jit(solution)/shard_map/ppermute | solution.py:1428
  318.3 38.3 %collective-permute-start.37 = (bf16[4,3,48,768]{3,2,1,0:T(8,128)(2,1)}, bf16[4,3,48,768]{3,2,1,0:T(8,128)(2,1)S(1)}, u32[]{:S(2)}, u32[]{:S(2)}) collective-permute-start(bf16[4,3,48,768]{3,2,1,0:T(8,128)(2,1)} %call_sums.3.refs_2_.refs_1_), channel_id=1, source_target_pairs={{0,1},{1,0},{2,3},{3,2},{4,5},{5,4},{6,7},{7,6},{8,9},{9,8},{10,11... | collective-permute-start | bytes 2654216 | tf_op jit(solution)/shard_map/ppermute | solution.py:1428
  325.8 25.0 %collective-permute-start.35 = (bf16[64,3200]{1,0:T(8,128)(2,1)}, bf16[64,3200]{1,0:T(8,128)(2,1)S(1)}, u32[]{:S(2)}, u32[]{:S(2)}) collective-permute-start(bf16[64,3200]{1,0:T(8,128)(2,1)} %call_sums.4.refs_0_), channel_id=1, source_target_pairs={{0,3},{3,0},{1,2},{2,1},{4,7},{7,4},{5,6},{6,5},{8,11},{11,8},{9,1... | collective-permute-start | bytes 1228808 | tf_op jit(solution)/shard_map/ppermute | solution.py:1428
  353.5 10.3 %collective-permute-start.36 = (bf16[64,3200]{1,0:T(8,128)(2,1)}, bf16[64,3200]{1,0:T(8,128)(2,1)S(1)}, u32[]{:S(2)}, u32[]{:S(2)}) collective-permute-start(bf16[64,3200]{1,0:T(8,128)(2,1)} %call_sums.5.refs_5_.refs_1_), channel_id=1, source_target_pairs={{0,1},{1,0},{2,3},{3,2},{4,5},{5,4},{6,7},{7,6},{8,9},{9,8},{10,11... | collective-permute-start | bytes 1228808 | tf_op jit(solution)/shard_map/ppermute | solution.py:1428
  (19 other events, 15.6 us)
Sparse Core Ops, SparseCore 0:
  177.4 54.1 reduce-scatter.3

commit v6 on v5

--- a/solution.py
+++ b/solution.py
@@ -1200,18 +1200,25 @@
     return total
 
 
-def call_halves(own, along, across, deps=()):
+def call_halves(along, across, deps=()):
     rows, width = along.shape
     half = rows // 32 * 16
 
     def body(_, ins, outs):
-        outs[0][...] = ins[1][:half]
-        outs[1][...] = ins[2][half:]
-        for i in range(3):
-            outs[2][i] = ins[i][...]
-
-    shapes = (sds((half, width)), sds((rows - half, width)), sds((3, rows, width)))
-    return join(body, call_halves, shapes, (), (own, along, across), deps)
+        outs[0][...] = ins[0][:half]
+        outs[1][...] = ins[1][half:]
+
+    shapes = (sds((half, width)), sds((rows - half, width)))
+    return join(body, call_halves, shapes, (), (along, across), deps)
+
+
+def call_stack(parts, deps=()):
+    def body(_, ins, outs):
+        for i, ref in enumerate(ins):
+            outs[0][i] = ref[...]
+
+    shapes = (sds((len(parts), *parts[0].shape)),)
+    return join(body, call_stack, shapes, (), parts, deps)[0]
 
 
 def call_two_halves(first, second, deps=()):
@@ -1466,7 +1473,8 @@
         expert_in_bias,
     )
     along, across = swap(payload, n, 2), swap(payload, n, 4)
-    top, bottom, three = call_halves(payload, along, across)
+    top, bottom = call_halves(along, across)
+    three = call_stack((payload, along, across), (top,))
     top_got, bottom_got = swap(top, n, 4), swap(bottom, n, 2)
     rows, half = payload.shape[0], top.shape[0]
     w_attn = [payload, along, across, top_got, bottom_got]

time: 380 us -> 379 us (level)
    pallas_call x34 -> x35, Pallas kernels: 159 us -> 161 us  [kernel_call(): pl.pallas_call(body, out_shape=out_shape, in_specs=in_specs, out_specs=ou...]
  transfers between devices with their start and end apart: 42 -> 42, of which waited for: 20 -> 20; matrix products, arithmetic and copies ran while one was open for 2% -> 2% of each run, Pallas kernels for 39% -> 40%
where the time goes in v6:
time: 379 us; the launch traced here: 373 us
  Pallas kernels  161 us (42%)
  waiting for transfers between devices  125 us (33%)
  starting transfers between devices  44 us (12%)
  local copies, waits for them, and re-layouts  23 us (6%)
  between operations  14.9 us (4%)
  other arithmetic  5.29 us (1%)
    pallas_call x35, Pallas kernels, kernel_call(): pl.pallas_call(body, out_shape=out_shape, in_specs=in_specs, out_specs=ou...  161 us
    ppermute x11, waiting for transfers between devices, line(): return lax.ppermute(v, REP, pairs)  53.8 us
    ppermute x27, waiting for transfers between devices, swap(): return lax.ppermute(v, FSDP, [(i, i ^ mask) for i in range(n)])  38 us
    all_to_all x3, waiting for transfers between devices, exchange(): return lax.all_to_all(v, FSDP, 0, 0, axis_index_groups=groups)  33.2 us
    ppermute x27, starting transfers between devices, swap(): return lax.ppermute(v, FSDP, [(i, i ^ mask) for i in range(n)])  19.6 us
    unnamed x83, local copies, waits for them, and re-layouts  19.3 us
    ppermute x11, starting transfers between devices, line(): return lax.ppermute(v, REP, pairs)  12.3 us
    all_to_all x3, starting transfers between devices, exchange(): return lax.all_to_all(v, FSDP, 0, 0, axis_index_groups=groups)  12 us
  transfers between devices with their start and end apart: 42, of which 20 were waited for; matrix products, arithmetic and copies ran while one was open for 2% of the time, Pallas kernels for 40%

profile of v6, /device:TPU:0, one launch (start us, length us, event | category | flops | bytes accessed | tf_op | source)
XLA Modules:
  0.0 373.2 jit_solution(12072231804059035083)
XLA Ops:
  7.2 1.3 stack.37.refs_4_
  8.5 2.1 pack.1.refs_0_.refs_3_.refs_5_.refs_11_
  10.7 2.9 collective-permute-start
  13.6 1.5 collective-permute-start.1
  18.4 9.2 %collective-permute-done.refs_0_.refs_1_.refs_4_.refs_6_.refs_12_ = bf16[400,768]{1,0:T(8,128)(2,1)S(1)} collective-permute-done((bf16[400,768]{1,0:T(8,128)(2,1)}, bf16[400,768]{1,0:T(8,128)(2,1)S(1)}, u32[]{:S(2)}, u32[]{:S(2)}) %collective-permute-start) | collective-permute-done | bytes 614432 | tf_op jit(solution)/shard_map/ppermute | solution.py:1411
  27.7 1.5 collective-permute-done.1.refs_1_.refs_2_.refs_5_.refs_7_.refs_13_
  29.9 2.1 call_halves.1
  32.0 1.5 collective-permute-start.2
  35.2 2.8 call_stack.1
  38.0 1.8 collective-permute-done.2.refs_6_.refs_8_.refs_14_
  39.8 1.8 collective-permute-done.3.refs_7_.refs_9_.refs_15_
  42.3 3.7 call_columns_and_sort.1
  46.8 3.7 all-to-all-start
  51.2 14.7 %attention_forward.1 = (bf16[416,2304]{1,0:T(8,128)(2,1)}, bf16[416,768]{1,0:T(8,128)(2,1)}, f32[16,416]{1,0:T(8,128)}, bf16[416,768]{1,0:T(8,128)(2,1)}, f32[16,768]{1,0:T(8,128)}, /*index=5*/f32[16,768]{1,0:T(8,128)}) custom-call(s32[1]{0:T(128)} %bitcast.5.refs_0_, s32[1,4]{1,0:T(1,128)} %refs_1_.7, bf16[416,768]{1,0:T(8,128)(2,1)} %refs_2_.9, ...), custom_call_target="tpu_custom_call" | custom-call | tf_op jit(solution)/shard_map/attention_forward/pallas_call | solution.py:427
  65.9 5.2 %mix_out.1 = (f32[416,768]{1,0:T(8,128)}, bf16[448,768]{1,0:T(8,128)(2,1)}) custom-call(s32[1]{0:T(128)} %bitcast.5.refs_0_, bf16[416,768]{1,0:T(8,128)(2,1)} %get-tuple-element.98.refs_1_.refs_6_, bf16[416,768]{1,0:T(8,128)(2,1)} %refs_2_.9, f32[16,768]{1,0:T(8,128)} %get-tuple-element.99.refs_3_.refs_5_, s32[1,416]{1,0:T(1,128)} %bitcast.48, ...), custom_call_target="tpu_custom_call" | custom-call | tf_op jit(solution)/shard_map/mix_out/pallas_call | solution.py:427
  71.1 1.7 all-to-all-done.refs_0_
  74.0 1.4 collective-permute-start.9
  76.0 1.5 collective-permute-start.7
  79.3 9.8 %experts.3 = (bf16[448,768]{1,0:T(8,128)(2,1)}, bf16[4,448,768]{2,1,0:T(8,128)(2,1)}, bf16[3,208,768]{2,1,0:T(8,128)(2,1)}, bf16[3,208,768]{2,1,0:T(8,128)(2,1)}) custom-call(s32[1]{0:T(128)} %bitcast.5.refs_0_, s32[1,9]{1,0:T(1,128)} %copy-done.38, f32[16,768]{1,0:T(8,128)} %get-tuple-element.103.refs_2_, ...), custom_call_target="tpu_custom_call" | custom-call | tf_op jit(solution)/shard_map/experts/pallas_call | solution.py:427
  89.1 3.9 %collective-permute-done.9.refs_2_.refs_5_.refs_3_ = bf16[464,768]{1,0:T(8,128)(2,1)} collective-permute-done((bf16[464,768]{1,0:T(8,128)(2,1)}, bf16[464,768]{1,0:T(8,128)(2,1)}, u32[]{:S(2)}, u32[]{:S(2)}) %collective-permute-start.9) | collective-permute-done | bytes 712736 | tf_op jit(solution)/shard_map/ppermute | solution.py:1411
  93.1 1.5 collective-permute-done.10.refs_3_.refs_6_.refs_4_
  94.5 12.9 %collective-permute-done.7.refs_0_.refs_3_ = bf16[448,768]{1,0:T(8,128)(2,1)} collective-permute-done((bf16[448,768]{1,0:T(8,128)(2,1)}, bf16[448,768]{1,0:T(8,128)(2,1)}, u32[]{:S(2)}, u32[]{:S(2)}) %collective-permute-start.7) | collective-permute-done | bytes 688160 | tf_op jit(solution)/shard_map/ppermute | solution.py:1411
  109.3 2.9 call_two_halves.1
  112.8 1.5 collective-permute-start.14
  116.2 14.1 %experts.4 = (bf16[448,768]{1,0:T(8,128)(2,1)}, bf16[448,768]{1,0:T(8,128)(2,1)}, bf16[4,448,768]{2,1,0:T(8,128)(2,1)}, bf16[3,416,768]{2,1,0:T(8,128)(2,1)}, bf16[3,416,768]{2,1,0:T(8,128)(2,1)}) custom-call(s32[1]{0:T(128)} %bitcast.5.refs_0_, s32[2,9]{1,0:T(2,128)} %convert_multiply_fusion.refs_1_, ...), custom_call_target="tpu_custom_call", output_to_operand_aliasing={{2}: (11, {})} | custom-call | tf_op jit(solution)/shard_map/experts/pallas_call | solution.py:427
  130.9 1.5 collective-permute-start.16
  133.8 9.6 %experts.5 = (bf16[448,768]{1,0:T(8,128)(2,1)}, bf16[4,448,768]{2,1,0:T(8,128)(2,1)}, bf16[3,208,768]{2,1,0:T(8,128)(2,1)}, bf16[3,208,768]{2,1,0:T(8,128)(2,1)}) custom-call(s32[1]{0:T(128)} %bitcast.5.refs_0_, s32[1,9]{1,0:T(1,128)} %fusion.1.refs_1_, f32[16,768]{1,0:T(8,128)} %get-tuple-element.103.refs_2_, ...), custom_call_target="tpu_custom_call", output_to_operand_aliasing={{1}: (11, {})} | custom-call | tf_op jit(solution)/shard_map/experts/pallas_call | solution.py:427
  143.4 1.6 collective-permute-start.17
  145.6 3.1 collective-permute-done.15.refs_10_.refs_8_
  149.6 10.4 %down_grads.1 = (bf16[3,384,768]{2,1,0:T(8,128)(2,1)}, bf16[384,768]{1,0:T(8,128)(2,1)}, bf16[384,768]{1,0:T(8,128)(2,1)}, bf16[384,768]{1,0:T(8,128)(2,1)}) custom-call(s32[1]{0:T(128)} %bitcast.5.refs_0_, s32[4,9]{1,0:T(4,128)} %pad_add_fusion.refs_1_, bf16[464,768]{1,0:T(8,128)(2,1)} %get-tuple-element.102.refs_4_.refs_2_, ...), custom_call_target="tpu_custom_call" | custom-call | tf_op jit(solution)/shard_map/down_grads/pallas_call | solution.py:427
  163.1 7.2 %mix_out_backward.1 = (f32[416,768]{1,0:T(8,128)}, bf16[416,768]{1,0:T(8,128)(2,1)}, f32[16,768]{1,0:T(8,128)}, bf16[768,768]{1,0:T(8,128)(2,1)}) custom-call(s32[1]{0:T(128)} %bitcast.5.refs_0_, s32[1,416]{1,0:T(1,128)} %bitcast.49, s32[1,416]{1,0:T(1,128)} %bitcast.53, f32[416,768]{1,0:T(8,128)} %get-tuple-element.100.refs_3_.refs_1_, ...), custom_call_target="tpu_custom_call" | custom-call | tf_op jit(solution)/shard_map/mix_out_backward/pallas_call | solution.py:427
  171.4 3.5 call_pair_down.1
  174.9 1.6 collective-permute-start.22
  176.5 10.8 %in_grads.1 = (bf16[4,3,96,768]{3,2,1,0:T(8,128)(2,1)}, bf16[16,384]{1,0:T(8,128)(2,1)}, bf16[16,384]{1,0:T(8,128)(2,1)}, bf16[4,96,768]{2,1,0:T(8,128)(2,1)}, b...) custom-call(s32[1]{0:T(128)} %bitcast.5.refs_0_, s32[4,9]{1,0:T(4,128)} %pad_add_fusion.refs_1_, ...), custom_call_target="tpu_custom_call" | custom-call | tf_op jit(solution)/shard_map/in_grads/pallas_call | solution.py:427
  188.5 8.9 %attention_backward_one.1 = (bf16[416,768]{1,0:T(8,128)(2,1)}, bf16[4,96,1536]{2,1,0:T(8,128)(2,1)}, bf16[4,96,1536]{2,1,0:T(8,128)(2,1)}) custom-call(s32[1]{0:T(128)} %bitcast.5.refs_0_, s32[1,4]{1,0:T(1,128)} %refs_1_.7, bf16[416,2304]{1,0:T(8,128)(2,1)} %get-tuple-element.120.refs_2_.refs_5_, f32[16,416]{1,0:T(8,128)} %get-tuple-element.121.refs_3_.refs_6_, ...), custom_call_target="tpu_custom_call" | custom-call | tf_op jit(solution)/shard_map/attention_backward_one/pallas_call | solution.py:427
  198.9 4.5 %call_pair_in.1 = (bf16[4,3,96,768]{3,2,1,0:T(8,128)(2,1)}, bf16[16,384]{1,0:T(8,128)(2,1)}, bf16[1,192,768]{2,1,0:T(8,128)(2,1)}, bf16[2,192,768]{2,1,0:T(8,128)(2,1)}) custom-call(bf16[4,3,96,768]{3,2,1,0:T(8,128)(2,1)} %get-tuple-element.130.refs_7_.refs_4_.refs_0_, bf16[16,384]{1,0:T(8,128)(2,1)} %get-tuple-element.133.refs_1_, ...), custom_call_target="tpu_custom_call" | custom-call | tf_op jit(solution)/shard_map/call_pair_in/pallas_call | solution.py:427
  203.4 4.1 %all-to-all-start.1 = ((bf16[4,3,96,768]{3,2,1,0:T(8,128)(2,1)}), bf16[4,3,96,768]{3,2,1,0:T(8,128)(2,1)S(1)}, u32[]{:S(2)}, u32[]{:S(2)}) async-start(bf16[4,3,96,768]{3,2,1,0:T(8,128)(2,1)} %get-tuple-element.144.refs_1_.refs_19_), calls=%async_computation.1 | async-start | bytes 3538944 | tf_op jit(solution)/shard_map/all_to_all | solution.py:1425
  207.5 2.3 collective-permute-start.27
  209.8 16.6 %attention_backward_two.1 = (f32[416,768]{1,0:T(8,128)}, bf16[4,96,1664]{2,1,0:T(8,128)(2,1)}, bf16[4,96,1664]{2,1,0:T(8,128)(2,1)}) custom-call(s32[1]{0:T(128)} %bitcast.5.refs_0_, s32[1,4]{1,0:T(1,128)} %refs_1_.7, bf16[416,768]{1,0:T(8,128)(2,1)} %refs_2_.9, f32[16,768]{1,0:T(8,128)} %get-tuple-element.99.refs_3_.refs_5_, ...), custom_call_target="tpu_custom_call" | custom-call | tf_op jit(solution)/shard_map/attention_backward_two/pallas_call | solution.py:427
  228.2 1.5 collective-permute-start.29
  229.7 4.5 %all-to-all-done.1.refs_1_ = bf16[4,3,96,768]{3,2,1,0:T(8,128)(2,1)S(1)} async-done(((bf16[4,3,96,768]{3,2,1,0:T(8,128)(2,1)}), bf16[4,3,96,768]{3,2,1,0:T(8,128)(2,1)S(1)}, u32[]{:S(2)}, u32[]{:S(2)}) %all-to-all-start.1) | async-done | bytes 1769504 | tf_op jit(solution)/shard_map/all_to_all | solution.py:1425
  235.4 2.8 call_split_rows.1
  238.2 1.5 collective-permute-start.30
  241.3 4.4 %call_pair_shares.1.refs_7_.refs_0_ = bf16[4,96,3200]{2,1,0:T(8,128)(2,1)} custom-call(bf16[4,96,1536]{2,1,0:T(8,128)(2,1)} %get-tuple-element.131.refs_0_, bf16[4,96,1536]{2,1,0:T(8,128)(2,1)} %copy-done.18, bf16[4,96,1664]{2,1,0:T(8,128)(2,1)} %get-tuple-element.147.refs_2_.refs_4_, bf16[4,96,1664]{2,1,0:T(8,128)(2,1)} %collective-permute-done.28.refs_3_, ...), custom_call_target="tpu_custom_call" | custom-call | tf_op jit(solution)/shard_map/call_pair_shares/pallas_call | solution.py:427
  246.3 9.1 %collective-permute-done.30.refs_5_ = bf16[2,3,48,768]{3,2,1,0:T(8,128)(2,1)S(1)} collective-permute-done((bf16[2,3,48,768]{3,2,1,0:T(8,128)(2,1)}, bf16[2,3,48,768]{3,2,1,0:T(8,128)(2,1)S(1)}, u32[]{:S(2)}, u32[]{:S(2)}) %collective-permute-start.30) | collective-permute-done | bytes 442400 | tf_op jit(solution)/shard_map/ppermute | solution.py:1435
  255.4 9.4 %collective-permute-done.31.refs_6_ = bf16[2,3,48,768]{3,2,1,0:T(8,128)(2,1)S(1)} collective-permute-done((bf16[2,3,48,768]{3,2,1,0:T(8,128)(2,1)}, bf16[2,3,48,768]{3,2,1,0:T(8,128)(2,1)S(1)}, u32[]{:S(2)}, u32[]{:S(2)}) %collective-permute-start.31) | collective-permute-done | bytes 442400 | tf_op jit(solution)/shard_map/ppermute | solution.py:1435
  265.6 3.4 call_line_sums.1
  269.0 4.2 %all-to-all-start.2 = ((bf16[4,96,3200]{2,1,0:T(8,128)(2,1)}), bf16[4,96,3200]{2,1,0:T(8,128)(2,1)S(1)}, u32[]{:S(2)}, u32[]{:S(2)}) async-start(bf16[4,96,3200]{2,1,0:T(8,128)(2,1)} %hold.13), calls=%async_computation.2 | async-start | bytes 4915200 | tf_op jit(solution)/shard_map/all_to_all | solution.py:1425
  273.2 2.0 collective-permute-start.33
  275.3 26.9 %all-to-all-done.2.refs_1_ = bf16[4,96,3200]{2,1,0:T(8,128)(2,1)S(1)} async-done(((bf16[4,96,3200]{2,1,0:T(8,128)(2,1)}), bf16[4,96,3200]{2,1,0:T(8,128)(2,1)S(1)}, u32[]{:S(2)}, u32[]{:S(2)}) %all-to-all-start.2) | async-done | bytes 2457632 | tf_op jit(solution)/shard_map/all_to_all | solution.py:1425
  302.2 1.4 copy-done.7
  303.6 2.7 call_attention_shares.1
  306.4 3.5 call_down_result.1.refs_2_
  309.9 5.0 %collective-permute-done.33.refs_1_ = bf16[4,3,48,768]{3,2,1,0:T(8,128)(2,1)} collective-permute-done((bf16[4,3,48,768]{3,2,1,0:T(8,128)(2,1)}, bf16[4,3,48,768]{3,2,1,0:T(8,128)(2,1)}, u32[]{:S(2)}, u32[]{:S(2)}) %collective-permute-start.33) | collective-permute-done | bytes 884768 | tf_op jit(solution)/shard_map/ppermute | solution.py:1435
  314.9 2.6 call_sums.3.refs_2_.refs_1_
  318.1 4.2 %collective-permute-done.32.refs_1_ = bf16[64,3200]{1,0:T(8,128)(2,1)S(1)} collective-permute-done((bf16[64,3200]{1,0:T(8,128)(2,1)}, bf16[64,3200]{1,0:T(8,128)(2,1)S(1)}, u32[]{:S(2)}, u32[]{:S(2)}) %collective-permute-start.32) | collective-permute-done | bytes 409632 | tf_op jit(solution)/shard_map/ppermute | solution.py:1435
  323.0 2.0 call_sums.4.refs_0_
  325.0 2.3 collective-permute-start.35
  327.3 22.7 %collective-permute-done.35.refs_1_ = bf16[64,3200]{1,0:T(8,128)(2,1)S(1)} collective-permute-done((bf16[64,3200]{1,0:T(8,128)(2,1)}, bf16[64,3200]{1,0:T(8,128)(2,1)S(1)}, u32[]{:S(2)}, u32[]{:S(2)}) %collective-permute-start.35) | collective-permute-done | bytes 409632 | tf_op jit(solution)/shard_map/ppermute | solution.py:1435
  350.8 2.0 call_sums.5.refs_5_.refs_1_
  352.7 3.1 finish_output.1.refs_3_
  356.7 3.5 call_in_result.1
  360.2 2.8 collective-permute-done.36.refs_2_
  363.7 2.2 call_attention_result.1
  (164 shorter events, 36.0 us)
Async XLA Ops:
  10.7 17.0 %collective-permute-start = (bf16[400,768]{1,0:T(8,128)(2,1)}, bf16[400,768]{1,0:T(8,128)(2,1)S(1)}, u32[]{:S(2)}, u32[]{:S(2)}) collective-permute-start(bf16[400,768]{1,0:T(8,128)(2,1)} %pack.1.refs_0_.refs_3_.refs_5_.refs_11_), channel_id=1, source_target_pairs={{0,8},{4,12},{8,0},{12,4},{16,24},{20,28},{24,16},{28,20},{1,9},{5... | collective-permute-start | bytes 1843208 | tf_op jit(solution)/shard_map/ppermute | solution.py:1411
  13.6 15.5 %collective-permute-start.1 = (bf16[400,768]{1,0:T(8,128)(2,1)}, bf16[400,768]{1,0:T(8,128)(2,1)S(1)}, u32[]{:S(2)}, u32[]{:S(2)}) collective-permute-start(bf16[400,768]{1,0:T(8,128)(2,1)} %pack.1.refs_0_.refs_3_.refs_5_.refs_11_), channel_id=1, source_target_pairs={{0,16},{4,20},{8,24},{12,28},{16,0},{20,4},{24,8},{28,12},{1,17},{... | collective-permute-start | bytes 1843208 | tf_op jit(solution)/shard_map/ppermute | solution.py:1411
  18.4 19.7 %copy-start.38 = (s32[1,9]{1,0:T(1,128)}, s32[1,9]{1,0:T(1,128)S(1)}, u32[]{:S(2)}) copy-start(s32[1,9]{1,0:T(1,128)S(1)} %mul.42.refs_1_) | copy-start | bytes 112
  27.7 1.5 copy-start.1
  32.0 7.8 %collective-permute-start.2 = (bf16[192,768]{1,0:T(8,128)(2,1)}, bf16[192,768]{1,0:T(8,128)(2,1)S(1)}, u32[]{:S(2)}, u32[]{:S(2)}) collective-permute-start(bf16[192,768]{1,0:T(8,128)(2,1)} %get-tuple-element.96.refs_3_.refs_4_), channel_id=1, source_target_pairs={{0,16},{4,20},{8,24},{12,28},{16,0},{20,4},{24,8},{28,12},{1,17},{... | collective-permute-start | bytes 884744 | tf_op jit(solution)/shard_map/ppermute | solution.py:1411
  33.6 8.0 %collective-permute-start.3 = (bf16[208,768]{1,0:T(8,128)(2,1)}, bf16[208,768]{1,0:T(8,128)(2,1)S(1)}, u32[]{:S(2)}, u32[]{:S(2)}) collective-permute-start(bf16[208,768]{1,0:T(8,128)(2,1)} %get-tuple-element.97), channel_id=1, source_target_pairs={{0,8},{4,12},{8,0},{12,4},{16,24},{20,28},{24,16},{28,20},{1,9},{5... | collective-permute-start | bytes 958472 | tf_op jit(solution)/shard_map/ppermute | solution.py:1411
  35.2 6.4 %copy-start.35 = (s32[416,1]{0,1:T(1,128)S(1)}, s32[416,1]{0,1:T(1,128)}, u32[]{:S(2)}) copy-start(s32[416,1]{0,1:T(1,128)} %param.21) | copy-start | bytes 4996
  38.0 13.1 %collective-permute-start.4 = (bf16[3,400,768]{2,1,0:T(8,128)(2,1)}, bf16[3,400,768]{2,1,0:T(8,128)(2,1)}, u32[]{:S(2)}, u32[]{:S(2)}) collective-permute-start(bf16[3,400,768]{2,1,0:T(8,128)(2,1)} %call_stack.1), channel_id=1, source_target_pairs={{0,4},{4,0},{8,12},{12,8},{16,20},{20,16},{24,28},{28,24},{1,5},{5... | collective-permute-start | bytes 5529608 | tf_op jit(solution)/shard_map/ppermute | solution.py:1411
  39.8 7.0 %copy-start.13 = (bf16[192,768]{1,0:T(8,128)(2,1)}, bf16[192,768]{1,0:T(8,128)(2,1)S(1)}, u32[]{:S(2)}) copy-start(bf16[192,768]{1,0:T(8,128)(2,1)S(1)} %collective-permute-done.2.refs_6_.refs_8_.refs_14_) | copy-start | bytes 884740
  39.8 6.1 %collective-permute-start.5 = (bf16[192,768]{1,0:T(8,128)(2,1)S(1)}, bf16[192,768]{1,0:T(8,128)(2,1)S(1)}, u32[]{:S(2)}, u32[]{:S(2)}) collective-permute-start(bf16[192,768]{1,0:T(8,128)(2,1)S(1)} %collective-permute-done.2.refs_6_.refs_8_.refs_14_), channel_id=1, source_target_pairs={{0,4},{4,0},{8,12},{12,8},{16,20},{20,16},{24,28},{28,24},{1,5},{5... | collective-permute-start | bytes 884744 | tf_op jit(solution)/shard_map/ppermute | solution.py:1411
  41.6 5.2 %copy-start.12 = (bf16[208,768]{1,0:T(8,128)(2,1)}, bf16[208,768]{1,0:T(8,128)(2,1)S(1)}, u32[]{:S(2)}) copy-start(bf16[208,768]{1,0:T(8,128)(2,1)S(1)} %collective-permute-done.3.refs_7_.refs_9_.refs_15_) | copy-start | bytes 958468
  41.6 4.4 %collective-permute-start.6 = (bf16[208,768]{1,0:T(8,128)(2,1)S(1)}, bf16[208,768]{1,0:T(8,128)(2,1)S(1)}, u32[]{:S(2)}, u32[]{:S(2)}) collective-permute-start(bf16[208,768]{1,0:T(8,128)(2,1)S(1)} %collective-permute-done.3.refs_7_.refs_9_.refs_15_), channel_id=1, source_target_pairs={{0,4},{4,0},{8,12},{12,8},{16,20},{20,16},{24,28},{28,24},{1,5},{5... | collective-permute-start | bytes 958472 | tf_op jit(solution)/shard_map/ppermute | solution.py:1411
  46.8 3.8 %copy-start.3 = (bf16[3,384,768]{2,1,0:T(8,128)(2,1)S(1)}, bf16[3,384,768]{2,1,0:T(8,128)(2,1)}, u32[]{:S(2)}) copy-start(bf16[3,384,768]{2,1,0:T(8,128)(2,1)} %refs_9_.3) | copy-start | bytes 5308420
  46.8 26.0 %all-to-all-start = ((bf16[4,3,96,768]{3,2,1,0:T(8,128)(2,1)}), bf16[4,3,96,768]{3,2,1,0:T(8,128)(2,1)S(1)}, u32[]{:S(2)}, u32[]{:S(2)}) async-start(bf16[4,3,96,768]{3,2,1,0:T(8,128)(2,1)} %hold.7), calls=%async_computation | async-start | bytes 3538944 | tf_op jit(solution)/shard_map/all_to_all | solution.py:1425
  50.5 302.2 %reduce-scatter.4.cloned.1.call-start = ((), (), s32[]{:S(2)}) async-start(), calls=%async_computation.4 | async-start | bytes 3440640
  50.6 26.9 %collective-permute-start.12 = (bf16[3,384,768]{2,1,0:T(8,128)(2,1)S(1)}, bf16[3,384,768]{2,1,0:T(8,128)(2,1)}, u32[]{:S(2)}, u32[]{:S(2)}) collective-permute-start(bf16[3,384,768]{2,1,0:T(8,128)(2,1)S(1)} %copy-done.3), channel_id=1, source_target_pairs={{0,4},{4,0},{8,12},{12,8},{16,20},{20,16},{24,28},{28,24},{1,5},{5... | collective-permute-start | bytes 5308424 | tf_op jit(solution)/shard_map/ppermute | solution.py:1411
  72.8 1.2 copy-start
  74.0 4.1 %collective-permute-start.11 = (bf16[4,3,96,768]{3,2,1,0:T(8,128)(2,1)}, bf16[4,3,96,768]{3,2,1,0:T(8,128)(2,1)S(1)}, u32[]{:S(2)}, u32[]{:S(2)}) collective-permute-start(bf16[4,3,96,768]{3,2,1,0:T(8,128)(2,1)} %hold.8.refs_5_.refs_7_), channel_id=1, source_target_pairs={{0,4},{4,0},{8,12},{12,8},{16,20},{20,16},{24,28},{28,24},{1,5},{5... | collective-permute-start | bytes 5308424 | tf_op jit(solution)/shard_map/ppermute | solution.py:1411
  74.0 19.1 %collective-permute-start.9 = (bf16[464,768]{1,0:T(8,128)(2,1)}, bf16[464,768]{1,0:T(8,128)(2,1)}, u32[]{:S(2)}, u32[]{:S(2)}) collective-permute-start(bf16[464,768]{1,0:T(8,128)(2,1)} %get-tuple-element.102.refs_4_.refs_2_), channel_id=1, source_target_pairs={{0,8},{4,12},{8,0},{12,4},{16,24},{20,28},{24,16},{28,20},{1,9},{5... | collective-permute-start | bytes 2138120 | tf_op jit(solution)/shard_map/ppermute | solution.py:1411
  75.4 19.1 %collective-permute-start.10 = (bf16[464,768]{1,0:T(8,128)(2,1)}, bf16[464,768]{1,0:T(8,128)(2,1)}, u32[]{:S(2)}, u32[]{:S(2)}) collective-permute-start(bf16[464,768]{1,0:T(8,128)(2,1)} %get-tuple-element.102.refs_4_.refs_2_), channel_id=1, source_target_pairs={{0,16},{4,20},{8,24},{12,28},{16,0},{20,4},{24,8},{28,12},{1,17},{... | collective-permute-start | bytes 2138120 | tf_op jit(solution)/shard_map/ppermute | solution.py:1411
  76.0 31.5 %collective-permute-start.7 = (bf16[448,768]{1,0:T(8,128)(2,1)}, bf16[448,768]{1,0:T(8,128)(2,1)}, u32[]{:S(2)}, u32[]{:S(2)}) collective-permute-start(bf16[448,768]{1,0:T(8,128)(2,1)} %get-tuple-element.101.refs_1_.refs_3_.refs_2_), channel_id=1, source_target_pairs={{0,8},{4,12},{8,0},{12,4},{16,24},{20,28},{24,16},{28,20},{1,9},{5... | collective-permute-start | bytes 2064392 | tf_op jit(solution)/shard_map/ppermute | solution.py:1411
  77.5 31.0 %collective-permute-start.8 = (bf16[448,768]{1,0:T(8,128)(2,1)}, bf16[448,768]{1,0:T(8,128)(2,1)S(1)}, u32[]{:S(2)}, u32[]{:S(2)}) collective-permute-start(bf16[448,768]{1,0:T(8,128)(2,1)} %get-tuple-element.101.refs_1_.refs_3_.refs_2_), channel_id=1, source_target_pairs={{0,16},{4,20},{8,24},{12,28},{16,0},{20,4},{24,8},{28,12},{1,17},{... | collective-permute-start | bytes 2064392 | tf_op jit(solution)/shard_map/ppermute | solution.py:1411
  78.1 1.2 copy-start.4
  112.2 20.2 %collective-permute-start.13 = (bf16[464,768]{1,0:T(8,128)(2,1)}, bf16[464,768]{1,0:T(8,128)(2,1)S(1)}, u32[]{:S(2)}, u32[]{:S(2)}) collective-permute-start(bf16[464,768]{1,0:T(8,128)(2,1)} %get-tuple-element.106), channel_id=1, source_target_pairs={{0,8},{4,12},{8,0},{12,4},{16,24},{20,28},{24,16},{28,20},{1,9},{5... | collective-permute-start | bytes 2138120 | tf_op jit(solution)/shard_map/ppermute | solution.py:1411
  112.8 20.2 %collective-permute-start.14 = (bf16[448,768]{1,0:T(8,128)(2,1)}, bf16[448,768]{1,0:T(8,128)(2,1)S(1)}, u32[]{:S(2)}, u32[]{:S(2)}) collective-permute-start(bf16[448,768]{1,0:T(8,128)(2,1)} %get-tuple-element.107), channel_id=1, source_target_pairs={{0,16},{4,20},{8,24},{12,28},{16,0},{20,4},{24,8},{28,12},{1,17},{... | collective-permute-start | bytes 2064392 | tf_op jit(solution)/shard_map/ppermute | solution.py:1411
  130.3 18.4 %collective-permute-start.15 = (bf16[448,768]{1,0:T(8,128)(2,1)}, bf16[448,768]{1,0:T(8,128)(2,1)S(1)}, u32[]{:S(2)}, u32[]{:S(2)}) collective-permute-start(bf16[448,768]{1,0:T(8,128)(2,1)} %get-tuple-element.112), channel_id=1, source_target_pairs={{0,8},{4,12},{8,0},{12,4},{16,24},{20,28},{24,16},{28,20},{1,9},{5... | collective-permute-start | bytes 2064392 | tf_op jit(solution)/shard_map/ppermute | solution.py:1411
  130.9 31.1 %collective-permute-start.16 = (bf16[448,768]{1,0:T(8,128)(2,1)}, bf16[448,768]{1,0:T(8,128)(2,1)S(1)}, u32[]{:S(2)}, u32[]{:S(2)}) collective-permute-start(bf16[448,768]{1,0:T(8,128)(2,1)} %get-tuple-element.113), channel_id=1, source_target_pairs={{0,16},{4,20},{8,24},{12,28},{16,0},{20,4},{24,8},{28,12},{1,17},{... | collective-permute-start | bytes 2064392 | tf_op jit(solution)/shard_map/ppermute | solution.py:1411
  133.8 11.2 %copy-start.37 = (s32[2,9]{1,0:T(2,128)S(1)}, s32[2,9]{1,0:T(2,128)}, u32[]{:S(2)}) copy-start(s32[2,9]{1,0:T(2,128)} %convert_multiply_fusion.refs_1_) | copy-start | bytes 220
  133.8 11.2 %copy-start.39 = (s32[1,9]{1,0:T(1,128)S(1)}, s32[1,9]{1,0:T(1,128)}, u32[]{:S(2)}) copy-start(s32[1,9]{1,0:T(1,128)} %copy-done.38) | copy-start | bytes 112
  133.8 11.2 %copy-start.40 = (s32[1,9]{1,0:T(1,128)S(1)}, s32[1,9]{1,0:T(1,128)}, u32[]{:S(2)}) copy-start(s32[1,9]{1,0:T(1,128)} %fusion.1.refs_1_) | copy-start | bytes 112
  143.4 18.5 %collective-permute-start.17 = (bf16[448,768]{1,0:T(8,128)(2,1)}, bf16[448,768]{1,0:T(8,128)(2,1)S(1)}, u32[]{:S(2)}, u32[]{:S(2)}) collective-permute-start(bf16[448,768]{1,0:T(8,128)(2,1)} %get-tuple-element.114), channel_id=1, source_target_pairs={{0,24},{4,28},{8,16},{12,20},{16,8},{20,12},{24,0},{28,4},{1,25},{... | collective-permute-start | bytes 2064392 | tf_op jit(solution)/shard_map/ppermute | solution.py:1411
  160.0 10.2 %collective-permute-start.18 = (bf16[384,768]{1,0:T(8,128)(2,1)}, bf16[384,768]{1,0:T(8,128)(2,1)S(1)}, u32[]{:S(2)}, u32[]{:S(2)}) collective-permute-start(bf16[384,768]{1,0:T(8,128)(2,1)} %get-tuple-element.126), channel_id=1, source_target_pairs={{0,4},{4,0},{8,12},{12,8},{16,20},{20,16},{24,28},{28,24},{1,5},{5... | collective-permute-start | bytes 1769480 | tf_op jit(solution)/shard_map/ppermute | solution.py:1411
  160.1 10.1 %collective-permute-start.19 = (bf16[384,768]{1,0:T(8,128)(2,1)}, bf16[384,768]{1,0:T(8,128)(2,1)S(1)}, u32[]{:S(2)}, u32[]{:S(2)}) collective-permute-start(bf16[384,768]{1,0:T(8,128)(2,1)} %get-tuple-element.127), channel_id=1, source_target_pairs={{0,4},{4,0},{8,12},{12,8},{16,20},{20,16},{24,28},{28,24},{1,5},{5... | collective-permute-start | bytes 1769480 | tf_op jit(solution)/shard_map/ppermute | solution.py:1411
  160.6 9.7 %collective-permute-start.20 = (bf16[384,768]{1,0:T(8,128)(2,1)}, bf16[384,768]{1,0:T(8,128)(2,1)S(1)}, u32[]{:S(2)}, u32[]{:S(2)}) collective-permute-start(bf16[384,768]{1,0:T(8,128)(2,1)} %get-tuple-element.128), channel_id=1, source_target_pairs={{0,4},{4,0},{8,12},{12,8},{16,20},{20,16},{24,28},{28,24},{1,5},{5... | collective-permute-start | bytes 1769480 | tf_op jit(solution)/shard_map/ppermute | solution.py:1411
  162.0 1.1 copy-start.22
  170.3 1.2 copy-start.25
  174.9 22.5 %collective-permute-start.22 = (bf16[3,192,768]{2,1,0:T(8,128)(2,1)}, bf16[3,192,768]{2,1,0:T(8,128)(2,1)S(1)}, u32[]{:S(2)}, u32[]{:S(2)}) collective-permute-start(bf16[3,192,768]{2,1,0:T(8,128)(2,1)} %get-tuple-element.129.refs_10_), channel_id=1, source_target_pairs={{0,1},{1,0},{2,3},{3,2},{4,5},{5,4},{6,7},{7,6},{8,9},{9,8},{10,11... | collective-permute-start | bytes 2654216 | tf_op jit(solution)/shard_map/ppermute | solution.py:1435
  187.4 10.0 %collective-permute-start.23 = (bf16[4,96,768]{2,1,0:T(8,128)(2,1)}, bf16[4,96,768]{2,1,0:T(8,128)(2,1)S(1)}, u32[]{:S(2)}, u32[]{:S(2)}) collective-permute-start(bf16[4,96,768]{2,1,0:T(8,128)(2,1)} %get-tuple-element.140), channel_id=1, source_target_pairs={{0,4},{4,0},{8,12},{12,8},{16,20},{20,16},{24,28},{28,24},{1,5},{5... | collective-permute-start | bytes 1769480 | tf_op jit(solution)/shard_map/ppermute | solution.py:1411
  187.4 10.0 %collective-permute-start.24 = (bf16[4,96,768]{2,1,0:T(8,128)(2,1)}, bf16[4,96,768]{2,1,0:T(8,128)(2,1)S(1)}, u32[]{:S(2)}, u32[]{:S(2)}) collective-permute-start(bf16[4,96,768]{2,1,0:T(8,128)(2,1)} %get-tuple-element.141), channel_id=1, source_target_pairs={{0,4},{4,0},{8,12},{12,8},{16,20},{20,16},{24,28},{28,24},{1,5},{5... | collective-permute-start | bytes 1769480 | tf_op jit(solution)/shard_map/ppermute | solution.py:1411
  187.9 9.5 %collective-permute-start.25 = (bf16[4,96,768]{2,1,0:T(8,128)(2,1)}, bf16[4,96,768]{2,1,0:T(8,128)(2,1)S(1)}, u32[]{:S(2)}, u32[]{:S(2)}) collective-permute-start(bf16[4,96,768]{2,1,0:T(8,128)(2,1)} %get-tuple-element.142), channel_id=1, source_target_pairs={{0,4},{4,0},{8,12},{12,8},{16,20},{20,16},{24,28},{28,24},{1,5},{5... | collective-permute-start | bytes 1769480 | tf_op jit(solution)/shard_map/ppermute | solution.py:1411
  188.0 9.4 %collective-permute-start.21 = (bf16[16,384]{1,0:T(8,128)(2,1)}, bf16[16,384]{1,0:T(8,128)(2,1)S(1)}, u32[]{:S(2)}, u32[]{:S(2)}) collective-permute-start(bf16[16,384]{1,0:T(8,128)(2,1)} %get-tuple-element.138), channel_id=1, source_target_pairs={{0,4},{4,0},{8,12},{12,8},{16,20},{20,16},{24,28},{28,24},{1,5},{5... | collective-permute-start | bytes 36872 | tf_op jit(solution)/shard_map/ppermute | solution.py:1411
  197.4 1.2 copy-start.28
  197.5 1.4 copy-start.20
  203.4 4.1 %copy-start.34 = (bf16[1,192,768]{2,1,0:T(8,128)(2,1)S(1)}, bf16[1,192,768]{2,1,0:T(8,128)(2,1)}, u32[]{:S(2)}) copy-start(bf16[1,192,768]{2,1,0:T(8,128)(2,1)} %get-tuple-element.150.refs_0_) | copy-start | bytes 884740
  203.4 30.8 %all-to-all-start.1 = ((bf16[4,3,96,768]{3,2,1,0:T(8,128)(2,1)}), bf16[4,3,96,768]{3,2,1,0:T(8,128)(2,1)S(1)}, u32[]{:S(2)}, u32[]{:S(2)}) async-start(bf16[4,3,96,768]{3,2,1,0:T(8,128)(2,1)} %get-tuple-element.144.refs_1_.refs_19_), calls=%async_computation.1 | async-start | bytes 3538944 | tf_op jit(solution)/shard_map/all_to_all | solution.py:1425
  207.5 18.9 %collective-permute-start.27 = (bf16[1,192,768]{2,1,0:T(8,128)(2,1)S(1)}, bf16[1,192,768]{2,1,0:T(8,128)(2,1)S(1)}, u32[]{:S(2)}, u32[]{:S(2)}) collective-permute-start(bf16[1,192,768]{2,1,0:T(8,128)(2,1)S(1)} %copy-done.34), channel_id=1, source_target_pairs={{0,3},{3,0},{1,2},{2,1},{4,7},{7,4},{5,6},{6,5},{8,11},{11,8},{9,1... | collective-permute-start | bytes 884744 | tf_op jit(solution)/shard_map/ppermute | solution.py:1435
  227.1 13.1 %collective-permute-start.28 = (bf16[4,96,1664]{2,1,0:T(8,128)(2,1)}, bf16[4,96,1664]{2,1,0:T(8,128)(2,1)}, u32[]{:S(2)}, u32[]{:S(2)}) collective-permute-start(bf16[4,96,1664]{2,1,0:T(8,128)(2,1)} %get-tuple-element.151), channel_id=1, source_target_pairs={{0,4},{4,0},{8,12},{12,8},{16,20},{20,16},{24,28},{28,24},{1,5},{5... | collective-permute-start | bytes 3833864 | tf_op jit(solution)/shard_map/ppermute | solution.py:1411
  227.1 1.1 copy-start.16
  227.2 13.1 %collective-permute-start.26 = (bf16[4,96,1536]{2,1,0:T(8,128)(2,1)}, bf16[4,96,1536]{2,1,0:T(8,128)(2,1)S(1)}, u32[]{:S(2)}, u32[]{:S(2)}) collective-permute-start(bf16[4,96,1536]{2,1,0:T(8,128)(2,1)} %hold.11), channel_id=1, source_target_pairs={{0,4},{4,0},{8,12},{12,8},{16,20},{20,16},{24,28},{28,24},{1,5},{5... | collective-permute-start | bytes 3538952 | tf_op jit(solution)/shard_map/ppermute | solution.py:1411
  228.2 18.1 %collective-permute-start.29 = (bf16[2,192,768]{2,1,0:T(8,128)(2,1)S(1)}, bf16[2,192,768]{2,1,0:T(8,128)(2,1)}, u32[]{:S(2)}, u32[]{:S(2)}) collective-permute-start(bf16[2,192,768]{2,1,0:T(8,128)(2,1)S(1)} %copy-done.16), channel_id=1, source_target_pairs={{0,3},{3,0},{1,2},{2,1},{4,7},{7,4},{5,6},{6,5},{8,11},{11,8},{9,1... | collective-permute-start | bytes 1769480 | tf_op jit(solution)/shard_map/ppermute | solution.py:1435
  234.2 1.2 copy-start.10
  238.2 17.2 %collective-permute-start.30 = (bf16[2,3,48,768]{3,2,1,0:T(8,128)(2,1)}, bf16[2,3,48,768]{3,2,1,0:T(8,128)(2,1)S(1)}, u32[]{:S(2)}, u32[]{:S(2)}) collective-permute-start(bf16[2,3,48,768]{3,2,1,0:T(8,128)(2,1)} %get-tuple-element.154), channel_id=1, source_target_pairs={{0,1},{1,0},{2,3},{3,2},{4,5},{5,4},{6,7},{7,6},{8,9},{9,8},{10,11... | collective-permute-start | bytes 1327112 | tf_op jit(solution)/shard_map/ppermute | solution.py:1435
  239.7 25.1 %collective-permute-start.31 = (bf16[2,3,48,768]{3,2,1,0:T(8,128)(2,1)}, bf16[2,3,48,768]{3,2,1,0:T(8,128)(2,1)S(1)}, u32[]{:S(2)}, u32[]{:S(2)}) collective-permute-start(bf16[2,3,48,768]{3,2,1,0:T(8,128)(2,1)} %get-tuple-element.155), channel_id=1, source_target_pairs={{0,1},{1,0},{2,3},{3,2},{4,5},{5,4},{6,7},{7,6},{8,9},{9,8},{10,11... | collective-permute-start | bytes 1327112 | tf_op jit(solution)/shard_map/ppermute | solution.py:1435
  240.3 1.0 copy-start.18
  255.4 9.4 %copy-start.29 = (bf16[2,3,48,768]{3,2,1,0:T(8,128)(2,1)}, bf16[2,3,48,768]{3,2,1,0:T(8,128)(2,1)S(1)}, u32[]{:S(2)}) copy-start(bf16[2,3,48,768]{3,2,1,0:T(8,128)(2,1)S(1)} %collective-permute-done.30.refs_5_) | copy-start | bytes 1327108
  269.0 4.2 %copy-start.14 = (bf16[3,192,768]{2,1,0:T(8,128)(2,1)S(1)}, bf16[3,192,768]{2,1,0:T(8,128)(2,1)}, u32[]{:S(2)}) copy-start(bf16[3,192,768]{2,1,0:T(8,128)(2,1)} %get-tuple-element.156.refs_1_) | copy-start | bytes 2654212
  269.0 33.2 %all-to-all-start.2 = ((bf16[4,96,3200]{2,1,0:T(8,128)(2,1)}), bf16[4,96,3200]{2,1,0:T(8,128)(2,1)S(1)}, u32[]{:S(2)}, u32[]{:S(2)}) async-start(bf16[4,96,3200]{2,1,0:T(8,128)(2,1)} %hold.13), calls=%async_computation.2 | async-start | bytes 4915200 | tf_op jit(solution)/shard_map/all_to_all | solution.py:1425
  273.2 33.2 %collective-permute-start.34 = (bf16[3,192,768]{2,1,0:T(8,128)(2,1)S(1)}, bf16[3,192,768]{2,1,0:T(8,128)(2,1)}, u32[]{:S(2)}, u32[]{:S(2)}) collective-permute-start(bf16[3,192,768]{2,1,0:T(8,128)(2,1)S(1)} %copy-done.14), channel_id=1, source_target_pairs={{0,1},{1,0},{2,3},{3,2},{4,5},{5,4},{6,7},{7,6},{8,9},{9,8},{10,11... | collective-permute-start | bytes 2654216 | tf_op jit(solution)/shard_map/ppermute | solution.py:1435
  273.2 41.7 %collective-permute-start.33 = (bf16[4,3,48,768]{3,2,1,0:T(8,128)(2,1)}, bf16[4,3,48,768]{3,2,1,0:T(8,128)(2,1)}, u32[]{:S(2)}, u32[]{:S(2)}) collective-permute-start(bf16[4,3,48,768]{3,2,1,0:T(8,128)(2,1)} %get-tuple-element.160.refs_0_), channel_id=1, source_target_pairs={{0,3},{3,0},{1,2},{2,1},{4,7},{7,4},{5,6},{6,5},{8,11},{11,8},{9,1... | collective-permute-start | bytes 2654216 | tf_op jit(solution)/shard_map/ppermute | solution.py:1435
  302.2 1.4 copy-start.7
  306.4 15.9 %collective-permute-start.32 = (bf16[64,3200]{1,0:T(8,128)(2,1)}, bf16[64,3200]{1,0:T(8,128)(2,1)S(1)}, u32[]{:S(2)}, u32[]{:S(2)}) collective-permute-start(bf16[64,3200]{1,0:T(8,128)(2,1)} %get-tuple-element.159.refs_3_), channel_id=1, source_target_pairs={{0,1},{1,0},{2,3},{3,2},{4,5},{5,4},{6,7},{7,6},{8,9},{9,8},{10,11... | collective-permute-start | bytes 1228808 | tf_op jit(solution)/shard_map/ppermute | solution.py:1435
  317.5 38.3 %collective-permute-start.37 = (bf16[4,3,48,768]{3,2,1,0:T(8,128)(2,1)}, bf16[4,3,48,768]{3,2,1,0:T(8,128)(2,1)S(1)}, u32[]{:S(2)}, u32[]{:S(2)}) collective-permute-start(bf16[4,3,48,768]{3,2,1,0:T(8,128)(2,1)} %call_sums.3.refs_2_.refs_1_), channel_id=1, source_target_pairs={{0,1},{1,0},{2,3},{3,2},{4,5},{5,4},{6,7},{7,6},{8,9},{9,8},{10,11... | collective-permute-start | bytes 2654216 | tf_op jit(solution)/shard_map/ppermute | solution.py:1435
  325.0 25.0 %collective-permute-start.35 = (bf16[64,3200]{1,0:T(8,128)(2,1)}, bf16[64,3200]{1,0:T(8,128)(2,1)S(1)}, u32[]{:S(2)}, u32[]{:S(2)}) collective-permute-start(bf16[64,3200]{1,0:T(8,128)(2,1)} %call_sums.4.refs_0_), channel_id=1, source_target_pairs={{0,3},{3,0},{1,2},{2,1},{4,7},{7,4},{5,6},{6,5},{8,11},{11,8},{9,1... | collective-permute-start | bytes 1228808 | tf_op jit(solution)/shard_map/ppermute | solution.py:1435
  352.7 10.2 %collective-permute-start.36 = (bf16[64,3200]{1,0:T(8,128)(2,1)}, bf16[64,3200]{1,0:T(8,128)(2,1)S(1)}, u32[]{:S(2)}, u32[]{:S(2)}) collective-permute-start(bf16[64,3200]{1,0:T(8,128)(2,1)} %call_sums.5.refs_5_.refs_1_), channel_id=1, source_target_pairs={{0,1},{1,0},{2,3},{3,2},{4,5},{5,4},{6,7},{7,6},{8,9},{9,8},{10,11... | collective-permute-start | bytes 1228808 | tf_op jit(solution)/shard_map/ppermute | solution.py:1435
  (19 other events, 15.6 us)
Sparse Core Ops, SparseCore 0:
  176.6 54.1 reduce-scatter.3
